TPU v7x, 32 devices: a whole 2x2x4 slice. The times are simulated.
32 devices in a mesh: dp: 4 (over y, x), row: 2 (over core), col: 4 (over z).
Axes of the slice: x: 2, y: 2, z: 4, core: 2. Of those that a mesh axis runs over, the one named last changes fastest.
Arguments:
- tokens: bfloat16 [4096, 2048], P(('dp', 'row'), 'col'), may hold values from -6 to 6
- attention_norm_gain: float32 [2048], P('col'), may hold values from 0.5 to 1.5
- attention_norm_bias: float32 [2048], P('col'), may hold values from -3 to 3
- qkv_weight: bfloat16 [2048, 3, 2048], P('col', None, 'row'), may hold values from -0.125 to 0.125
- qkv_bias: float32 [3, 2048], P(None, ('row', 'col')), may hold values from -4 to 4
- out_weight: bfloat16 [2048, 2048], P('row', 'col'), may hold values from -1 to 1
- feedforward_norm_gain: float32 [2048], P('col'), may hold values from 0.5 to 1.5
- feedforward_norm_bias: float32 [2048], P('col'), may hold values from -3 to 3
- gate_up_weight: bfloat16 [2048, 2, 5632], P('col', None, 'row'), may hold values from -0.125 to 0.125
- down_weight: bfloat16 [5632, 2048], P('row', 'col'), may hold values from -0.078125 to 0.078125
- cotangent: bfloat16 [4096, 2048], P(('dp', 'row'), 'col'), may hold values from -6 to 6
Outputs:
- mixed: bfloat16 [4096, 2048], P(('dp', 'row'), 'col')
- input_token_gradient: float32 [4096, 2048], P(('dp', 'row'), 'col')
- grad_first_gain: float32 [2048], P('col')
- grad_first_shift: float32 [2048], P('col')
- grad_qkv_weight: float32 [2048, 3, 2048], P('col', None, 'row')
- grad_qkv_bias: float32 [3, 2048], P(None, ('row', 'col'))
- grad_out_weight: float32 [2048, 2048], P('row', 'col')
- grad_second_gain: float32 [2048], P('col')
- grad_second_shift: float32 [2048], P('col')
- grad_gate_up: float32 [2048, 2, 5632], P('col', None, 'row')
- grad_down: float32 [5632, 2048], P('row', 'col')
All inputs are finite; a program needn't handle non-finite values.
Results may differ from a plain program's by a relative error of at most 0.012.
Values may be sent and summed in bfloat16 or wider, within the bound.
A program may use at most 192 MiB of HBM per device.

v0:
```python
import jax
import jax.numpy as jnp
from jax import lax
from jax.sharding import PartitionSpec as P

MODEL_WIDTH = 2048
HD = 64
ROT = 16
SEQ = 1024


EPSILON = 1e-05
ROPE_BASE = 10000.0
NEG_LARGE = -1e30


def rotate(inputs, positions):
    half_rot = ROT // 2
    inverse = ROPE_BASE ** (-2.0 * jnp.arange(half_rot).astype(jnp.float32) / ROT)
    angles = positions[:, None] * inverse[None, :]
    cosine = jnp.cos(angles)[:, None, :]
    sine_part = jnp.sin(angles)[:, None, :]
    lower_half = inputs[..., :half_rot]
    upper_half = inputs[..., half_rot:ROT]
    return jnp.concatenate(
        [
            lower_half * cosine - upper_half * sine_part,
            upper_half * cosine + lower_half * sine_part,
            inputs[..., ROT:],
        ],
        axis=-1,
    )


def gather_rows(inputs):
    return lax.all_gather(inputs, "row", axis=0, tiled=True)


def sum_rows(inputs):
    return lax.psum_scatter(inputs, "row", scatter_dimension=0, tiled=True)


def sum_cols(inputs):
    return lax.psum_scatter(inputs, "col", scatter_dimension=2, tiled=True)


def gather_cols(inputs):
    return lax.all_gather(inputs, "col", axis=2, tiled=True)


def norm_stats(residual_stream):
    totals = lax.psum(jnp.sum(residual_stream, axis=1), "col")
    row_mean = totals / MODEL_WIDTH
    centered = residual_stream - row_mean[:, None]
    squares = lax.psum(jnp.sum(centered * centered, axis=1), "col")
    spread = squares / MODEL_WIDTH
    return (row_mean, lax.rsqrt(spread + EPSILON))


def layer_norm_pullback(
    normalized_gradient, standardized_input, inverse_deviation, norm_gain_vector
):
    scaled_gradient = normalized_gradient * norm_gain_vector
    attention_residual_sum, feedforward_residual_sum = lax.psum(
        (jnp.sum(scaled_gradient, axis=1), jnp.sum(scaled_gradient * standardized_input, axis=1)),
        "col",
    )
    return inverse_deviation[:, None] * (
        scaled_gradient
        - attention_residual_sum[:, None] / MODEL_WIDTH
        - standardized_input * feedforward_residual_sum[:, None] / MODEL_WIDTH
    )


def block_scores(query_block, key_rows, offset):
    block_rows = query_block.shape[0]
    scores = jnp.einsum(
        "qhd,khd->hqk", query_block, key_rows, preferred_element_type=jnp.float32
    ) * HD ** (-0.5)
    allowed = (offset + jnp.arange(block_rows))[:, None] >= jnp.arange(key_rows.shape[0])[None, :]
    return jnp.where(allowed[None], scores, NEG_LARGE)


def attention_forward(queries, key_rows, value_rows):

    def one_seq(packed):
        seq_queries, seq_keys, seq_values = packed
        length = seq_queries.shape[0]
        block_rows = min(512, length)
        blocks = length // block_rows
        query_blocks = seq_queries.reshape((blocks, block_rows) + seq_queries.shape[1:])
        offsets = jnp.arange(blocks) * block_rows

        def one_block(element):
            query_block, offset = element
            scores = block_scores(query_block, seq_keys, offset)
            row_max = jnp.max(scores, axis=2, keepdims=True)
            expo = jnp.exp(scores - row_max)
            denominator = jnp.sum(expo, axis=2, keepdims=True)
            attn_probs = (expo / denominator).astype(jnp.bfloat16)
            result = jnp.einsum(
                "hqk,khd->qhd", attn_probs, seq_values, preferred_element_type=jnp.float32
            )
            return (result, (row_max + jnp.log(denominator))[:, :, 0])

        results, log_sums = lax.map(one_block, (query_blocks, offsets))
        return (results.reshape(seq_queries.shape), log_sums)

    return lax.map(one_seq, (queries, key_rows, value_rows))


def attention_backward(queries, key_rows, value_rows, log_sums, grad_attn):

    def one_seq(packed):
        seq_queries, seq_keys, seq_values, seq_sums, seq_grad = packed
        length = seq_queries.shape[0]
        block_rows = min(512, length)
        blocks = length // block_rows
        block_shape = (blocks, block_rows) + seq_queries.shape[1:]
        offsets = jnp.arange(blocks) * block_rows

        def advance(running, element):
            query_block, offset, sum_block, grad_block = element
            scores = block_scores(query_block, seq_keys, offset)
            attn_probs = jnp.exp(scores - sum_block[:, :, None])
            grad_probs = jnp.einsum(
                "qhd,khd->hqk", grad_block, seq_values, preferred_element_type=jnp.float32
            )
            delta = jnp.sum(grad_probs * attn_probs, axis=2, keepdims=True)
            grad_scores = (attn_probs * (grad_probs - delta)).astype(jnp.bfloat16)
            grad_query = jnp.einsum(
                "hqk,khd->qhd", grad_scores, seq_keys, preferred_element_type=jnp.float32
            ) * HD ** (-0.5)
            grad_key = jnp.einsum(
                "hqk,qhd->khd", grad_scores, query_block, preferred_element_type=jnp.float32
            ) * HD ** (-0.5)
            grad_value = jnp.einsum(
                "hqk,qhd->khd",
                attn_probs.astype(jnp.bfloat16),
                grad_block,
                preferred_element_type=jnp.float32,
            )
            return ((running[0] + grad_key, running[1] + grad_value), grad_query)

        empty_grad = jnp.zeros(seq_keys.shape, jnp.float32)
        (grad_keys, grad_values), grad_queries = lax.scan(
            advance,
            (empty_grad, empty_grad),
            (seq_queries.reshape(block_shape), offsets, seq_sums, seq_grad.reshape(block_shape)),
        )
        return (grad_queries.reshape(seq_queries.shape), grad_keys, grad_values)

    return lax.map(one_seq, (queries, key_rows, value_rows, log_sums, grad_attn))


def swiglu(gate_up):
    return jax.nn.silu(gate_up[:, 0]) * gate_up[:, 1]


def body(
    tokens,
    attention_norm_gain,
    attention_norm_bias,
    qkv_weight,
    qkv_bias,
    out_weight,
    feedforward_norm_gain,
    feedforward_norm_bias,
    gate_up_weight,
    down_weight,
    cotangent,
):
    residual_stream = tokens.astype(jnp.float32)
    attention_norm_average, attention_inverse_deviation = norm_stats(residual_stream)
    attention_standardized = (
        residual_stream - attention_norm_average[:, None]
    ) * attention_inverse_deviation[:, None]
    attention_normalized = (
        attention_standardized * attention_norm_gain + attention_norm_bias
    ).astype(jnp.bfloat16)
    rows_one = gather_rows(attention_normalized)
    group_rows = rows_one.shape[0]
    heads_local = qkv_bias.shape[1] // HD
    seq_count = group_rows // SEQ
    positions = (jnp.arange(group_rows) % SEQ).astype(jnp.float32)
    head_shape = (group_rows, heads_local, HD)
    seq_shape = (seq_count, SEQ, heads_local, HD)
    qkv = (
        sum_cols(
            jnp.einsum("td,dkf->tkf", rows_one, qkv_weight, preferred_element_type=jnp.float32)
        )
        + qkv_bias[None]
    )

    def turn_heads(inputs):
        return rotate(inputs, positions)

    queries = turn_heads(qkv[:, 0].reshape(head_shape)).astype(jnp.bfloat16).reshape(seq_shape)
    key_rows = turn_heads(qkv[:, 1].reshape(head_shape)).astype(jnp.bfloat16).reshape(seq_shape)
    value_rows = qkv[:, 2].reshape(seq_shape).astype(jnp.bfloat16)
    attn_out, log_sums = attention_forward(queries, key_rows, value_rows)
    attn_low = attn_out.reshape(group_rows, 1, heads_local * HD).astype(jnp.bfloat16)
    attn_cols = gather_cols(attn_low)[:, 0]
    branch = sum_rows(jnp.dot(attn_cols, out_weight, preferred_element_type=jnp.float32))
    middle_state = residual_stream + branch
    feedforward_norm_average, feedforward_inverse_deviation = norm_stats(middle_state)
    feedforward_standardized = (
        middle_state - feedforward_norm_average[:, None]
    ) * feedforward_inverse_deviation[:, None]
    feedforward_normalized = (
        feedforward_standardized * feedforward_norm_gain + feedforward_norm_bias
    ).astype(jnp.bfloat16)
    rows_two = gather_rows(feedforward_normalized)
    gate_up = sum_cols(
        jnp.einsum("td,dkf->tkf", rows_two, gate_up_weight, preferred_element_type=jnp.float32)
    )
    hidden, swiglu_pull = jax.vjp(swiglu, gate_up)
    hidden_low = hidden.astype(jnp.bfloat16)[:, None]
    hidden_cols = gather_cols(hidden_low)[:, 0]
    ffn_branch = sum_rows(jnp.dot(hidden_cols, down_weight, preferred_element_type=jnp.float32))
    mixed = (middle_state + ffn_branch).astype(jnp.bfloat16)
    cotan_rows = gather_rows(cotangent)
    grad_down = jnp.einsum("tf,td->fd", hidden_cols, cotan_rows, preferred_element_type=jnp.float32)
    grad_hidden = sum_cols(
        jnp.einsum("td,fd->tf", cotan_rows, down_weight, preferred_element_type=jnp.float32)[
            :, None
        ]
    )[:, 0]
    (grad_gate_up_f,) = swiglu_pull(grad_hidden)
    grad_gate_up_low = grad_gate_up_f.astype(jnp.bfloat16)
    grad_gu_cols = gather_cols(grad_gate_up_low)
    grad_gate_up = jnp.einsum(
        "td,tkf->dkf", rows_two, grad_gu_cols, preferred_element_type=jnp.float32
    )
    grad_part_two = jnp.einsum(
        "tkf,dkf->td", grad_gu_cols, gate_up_weight, preferred_element_type=jnp.float32
    )
    feedforward_normalized_gradient = sum_rows(grad_part_two)
    feedforward_gain_partial = jnp.sum(
        feedforward_normalized_gradient * feedforward_standardized, axis=0
    )
    shift_two_part = jnp.sum(feedforward_normalized_gradient, axis=0)
    middle_state_gradient = cotangent.astype(jnp.float32) + layer_norm_pullback(
        feedforward_normalized_gradient,
        feedforward_standardized,
        feedforward_inverse_deviation,
        feedforward_norm_gain,
    )
    grad_middle_rows = gather_rows(middle_state_gradient.astype(jnp.bfloat16))
    grad_out_weight = jnp.einsum(
        "tf,td->fd", attn_cols, grad_middle_rows, preferred_element_type=jnp.float32
    )
    grad_attn = sum_cols(
        jnp.einsum("td,fd->tf", grad_middle_rows, out_weight, preferred_element_type=jnp.float32)[
            :, None
        ]
    )[:, 0]
    grad_attn_low = grad_attn.astype(jnp.bfloat16).reshape(seq_shape)
    grad_queries, grad_keys, grad_values = attention_backward(
        queries, key_rows, value_rows, log_sums, grad_attn_low
    )
    unused, rotate_pull = jax.vjp(turn_heads, qkv[:, 0].reshape(head_shape))
    (grad_query_pre,) = rotate_pull(grad_queries.reshape(head_shape))
    (grad_key_pre,) = rotate_pull(grad_keys.reshape(head_shape))
    grad_qkv = jnp.stack([grad_query_pre, grad_key_pre, grad_values.reshape(head_shape)], axis=1)
    grad_qkv_low = grad_qkv.reshape(group_rows, 3, heads_local * HD).astype(jnp.bfloat16)
    grad_qkv_bias = jnp.sum(grad_qkv_low, axis=0, dtype=jnp.float32)
    grad_qkv_cols = gather_cols(grad_qkv_low)
    grad_qkv_weight = jnp.einsum(
        "td,tkf->dkf", rows_one, grad_qkv_cols, preferred_element_type=jnp.float32
    )
    attention_normalized_gradient = sum_rows(
        jnp.einsum("tkf,dkf->td", grad_qkv_cols, qkv_weight, preferred_element_type=jnp.float32)
    )
    attention_gain_partial = jnp.sum(attention_normalized_gradient * attention_standardized, axis=0)
    shift_one_part = jnp.sum(attention_normalized_gradient, axis=0)
    input_token_gradient = middle_state_gradient + layer_norm_pullback(
        attention_normalized_gradient,
        attention_standardized,
        attention_inverse_deviation,
        attention_norm_gain,
    )
    summed = lax.psum(
        (grad_qkv_weight, grad_qkv_bias, grad_out_weight, grad_gate_up, grad_down), "dp"
    )
    norm_grads = lax.psum(
        (attention_gain_partial, shift_one_part, feedforward_gain_partial, shift_two_part),
        ("dp", "row"),
    )
    return (
        mixed,
        input_token_gradient,
        norm_grads[0],
        norm_grads[1],
        summed[0],
        summed[1],
        summed[2],
        norm_grads[2],
        norm_grads[3],
        summed[3],
        summed[4],
    )


def solution(mesh):
    return jax.shard_map(
        body,
        mesh=mesh,
        in_specs=(
            P(("dp", "row"), "col"),
            P("col"),
            P("col"),
            P("col", None, "row"),
            P(None, ("row", "col")),
            P("row", "col"),
            P("col"),
            P("col"),
            P("col", None, "row"),
            P("row", "col"),
            P(("dp", "row"), "col"),
        ),
        out_specs=(
            P(("dp", "row"), "col"),
            P(("dp", "row"), "col"),
            P("col"),
            P("col"),
            P("col", None, "row"),
            P(None, ("row", "col")),
            P("row", "col"),
            P("col"),
            P("col"),
            P("col", None, "row"),
            P("row", "col"),
        ),
        check_vma=False,
    )
```

profile of v0, /device:TPU:0, one launch (start us, length us, event | category | flops | bytes accessed | tf_op | source)
XLA Modules:
  0.0 2179.8 jit_solution(12219122579403285556)
XLA Ops:
  8.6 13.5 psum.119
  23.4 8.4 psum.120
  34.5 8.8 all-gather.9.cloned.1.call-done
  43.3 7.6 fusion.78
  52.3 211.8 %reduce-scatter.9.cloned.1.call-done = f32[1024,3,256]{2,0,1:T(8,128)} async-done(((f32[1024,3,1024]{2,0,1:T(8,128)}), f32[1024,3,256]{2,0,1:T(8,128)}) %reduce-scatter.9.cloned.1.call-update) | async-done | bytes 3145744 | tf_op jit(solution)/shard_map/reduce_scatter | solution.py:44
  268.5 2.5 copy.41
  273.3 2.5 copy.44
  285.3 22.5 %while.47 = (s32[]{:T(128)}, bf16[2,512,4,64]{1,3,2,0:T(8,128)(2,1)}, f32[2,4,512]{2,1,0:T(4,128)S(1)}, s32[2]{0:T(128)}, bf16[2,512,4,64]{1,3,2,0:T(8,128)(2,1)...) while((s32[]{:T(128)}, bf16[2,512,4,64]{1,3,2,0:T(8,128)(2,1)}, ...), condition=%wide.region_8.9_spmd, body=%wide.region_5.8_spmd.sunk | while | flops 562559488 | bytes 35459276 | solution.py:106
  287.6 2.8 fusion.129
  292.7 3.0 fusion.131
  298.8 2.8 fusion.129
  304.0 3.0 fusion.131
  312.5 47.1 %all-gather.11.cloned.1.call-done = bf16[1024,1,1024]{0,2,1:T(8,128)(2,1)} async-done(((bf16[1024,1,256]{0,2,1:T(8,128)(2,1)}), bf16[1024,1,1024]{0,2,1:T(8,128)(2,1)}) %all-gather.11.cloned.1.call-update) | async-done | bytes 2097168 | tf_op jit(solution)/shard_map/all_gather | solution.py:48
  359.6 4.5 fusion.53
  364.7 7.8 reduce-scatter.11.cloned.1.call-done
  375.0 12.2 psum.121
  388.6 8.4 psum.122
  399.4 9.8 convolution_bitcast_fusion
  409.2 13.7 fusion.44
  423.0 184.3 %reduce-scatter.17.cloned.1.call-done = f32[1024,1,704]{0,2,1:T(8,128)} async-done(((f32[1024,1,2816]{0,2,1:T(8,128)}), f32[1024,1,704]{0,2,1:T(8,128)}) %reduce-scatter.17.cloned.1.call-update) | async-done | bytes 2883600 | tf_op jit(solution)/shard_map/reduce_scatter | solution.py:44
  607.2 384.2 %reduce-scatter.13.cloned.1.call-done = f32[1024,2,704]{0,2,1:T(8,128)} async-done(((f32[1024,2,2816]{0,2,1:T(8,128)}), f32[1024,2,704]{0,2,1:T(8,128)}) %reduce-scatter.13.cloned.1.call-update) | async-done | bytes 5767184 | tf_op jit(solution)/shard_map/reduce_scatter | solution.py:44
  991.4 5.3 fusion.80
  999.4 202.4 %all-gather.19.cloned.1.call-done = bf16[1024,2,2816]{0,2,1:T(8,128)(2,1)} async-done(((bf16[1024,2,704]{0,2,1:T(8,128)(2,1)}), bf16[1024,2,2816]{0,2,1:T(8,128)(2,1)}) %all-gather.19.cloned.1.call-update) | async-done | bytes 11534352 | tf_op jit(solution)/shard_map/all_gather | solution.py:48
  1201.8 11.8 fusion.55
  1213.6 10.8 reduce-scatter.15.cloned.1.call-start
  1224.4 84.3 %all-gather.15.cloned.1.call-done = bf16[1024,1,2816]{0,2,1:T(8,128)(2,1)} async-done(((bf16[1024,1,704]{0,2,1:T(8,128)(2,1)}), bf16[1024,1,2816]{0,2,1:T(8,128)(2,1)}) %all-gather.15.cloned.1.call-update) | async-done | bytes 5767184 | tf_op jit(solution)/shard_map/all_gather | solution.py:48
  1308.7 8.0 fusion.42
  1316.8 2.7 reduce-scatter.19.cloned.1.call-done
  1319.4 2.6 multiply_reduce_fusion.1
  1322.1 11.9 all-reduce.10
  1334.0 3.9 fusion.85
  1338.0 9.3 all-gather.21.cloned.1.call-done
  1347.3 4.8 convolution_bitcast_fusion.1
  1352.2 78.0 %reduce-scatter.21.cloned.1.call-done = f32[1024,1,256]{2,0,1:T(8,128)} async-done(((f32[1024,1,1024]{2,0,1:T(8,128)}), f32[1024,1,256]{2,0,1:T(8,128)}) %reduce-scatter.21.cloned.1.call-update) | async-done | bytes 1048592 | tf_op jit(solution)/shard_map/reduce_scatter | solution.py:44
  1432.3 2.8 reshape.248
  1437.4 68.0 %while.48 = (s32[]{:T(128)}, f32[1024,4,64]{0,2,1:T(8,128)}, f32[1024,4,64]{0,2,1:T(8,128)}, f32[2,512,4,64]{1,0,3,2:T(2,128)}, bf16[2,512,4,64]{1,3,2,0:T(8,128...) while((s32[]{:T(128)}, f32[1024,4,64]{0,2,1:T(8,128)}, ...), condition=%wide.region_25.26_spmd.clone, body=%wide.region_23.25_spmd.clone.sunk | while | flops 1375599104 | bytes 170979760 | solution.py:146
  1437.4 2.5 fusion.141
  1441.7 3.2 multiply_reduce_fusion.7
  1444.9 3.7 multiply_convert_fusion.3
  1448.6 4.2 fusion.142
  1453.8 3.5 fusion.143
  1460.1 10.4 dynamic_update_slice.31
  1474.9 3.2 multiply_reduce_fusion.7
  1478.0 3.7 multiply_convert_fusion.3
  1481.7 4.5 fusion.142
  1487.3 4.7 fusion.143
  1494.8 10.4 dynamic_update_slice.31
  1505.4 3.1 reshape.241
  1518.7 2.6 add_convert_fusion.1
  1525.3 2.8 convert_reduce_fusion
  1528.2 115.4 %all-gather.23.cloned.1.call-done = bf16[1024,3,1024]{2,0,1:T(8,128)(2,1)} async-done(((bf16[1024,3,256]{2,0,1:T(8,128)(2,1)}), bf16[1024,3,1024]{2,0,1:T(8,128)(2,1)}) %all-gather.23.cloned.1.call-update) | async-done | bytes 6291472 | tf_op jit(solution)/shard_map/all_gather | solution.py:48
  1643.7 7.5 convolution_bitcast_fusion.2
  1651.3 8.8 fusion.40
  1660.1 22.1 %fusion.73 = f32[512,2,2816]{2,0,1:T(8,128)} fusion(bf16[1024,2,2816]{0,2,1:T(8,128)(2,1)} %all-gather.19.cloned.1.call-done, bf16[1024,512]{1,0:T(8,128)(2,1)S(1)} %copy-done.13), kind=kOutput, calls=%fused_computation.94 | convolution fusion | flops 5905580032 | bytes 24117248 | tf_op jit(solution)/shard_map/td,tkf->dkf/dot_general | solution.py:232
  1682.2 2.7 fusion.51
  1684.9 5.4 fusion.76
  1690.3 10.6 psum.130
  1702.9 13.3 all-reduce.8
  1716.2 9.1 all-reduce.9
  1725.3 3.1 fusion.70
  1728.4 415.1 %all-reduce.14.cloned.1.call-done = (f32[512,3,1024]{2,0,1:T(8,128)}, f32[1024,512]{1,0:T(8,128)}, f32[512,2,2816]{2,0,1:T(8,128)}, f32[2816,512]{1,0:T(8,128)}) async-done(((f32[512,3,1024]{2,0,1:T(8,128)}, f32[1024,512]{1,0:T(8,128)}, f32[512,2,2816]{2,0,1:T(8,128)}, f32[2816,512]{1,0:T(8,128)}), (f32[512,3,1024]{2,0,1:T(8,128)}, f32[1024,512]{1,0:T(8,128)}, f32[512,2,2816]{2,0,1:T(8,128)}, ...) | async-done | bytes 25690128 | tf_op jit(solution)/shard_map/psum | solution.py:283
  2143.6 20.4 copy.61
  2164.0 3.2 copy.128
  2170.3 2.5 copy.130
  (202 shorter events, 85.7 us)
Async XLA Ops:
  7.2 36.2 %copy-start = (bf16[512,3,1024]{2,0,1:T(8,128)(2,1)S(1)}, bf16[512,3,1024]{2,0,1:T(8,128)(2,1)}, u32[]{:S(2)}) copy-start(bf16[512,3,1024]{2,0,1:T(8,128)(2,1)} %param.18) | copy-start | bytes 9437188
  7.2 36.1 %all-gather.9.cloned.1.call-start = ((), (), s32[]{:S(2)}) async-start(), calls=%async_computation.8 | async-start | bytes 1572864 | tf_op jit(solution)/shard_map/all_gather | solution.py:36
  22.0 28.8 %copy-start.16 = (f32[512]{0:T(512)}, f32[512]{0:T(512)S(1)}, u32[]{:S(2)}) copy-start(f32[512]{0:T(512)S(1)} %broadcast_multiply_fusion.3) | copy-start | bytes 6148
  31.8 0.6 copy-start.18
  34.5 229.6 %reduce-scatter.9.cloned.1.call-start = ((), (), s32[]{:S(2)}) async-start(), calls=%async_computation.9 | async-start | bytes 15728640 | tf_op jit(solution)/shard_map/reduce_scatter | solution.py:44
  50.9 213.2 %copy-start.24 = (f32[3,256]{1,0:T(4,128)S(1)}, f32[3,256]{1,0:T(4,128)}, u32[]{:S(2)}) copy-start(f32[3,256]{1,0:T(4,128)} %param.19) | copy-start | bytes 9220
  50.9 308.7 %all-gather.11.cloned.1.call-start = ((), (), s32[]{:S(2)}) async-start(), calls=%async_computation.10 | async-start | bytes 2621440 | tf_op jit(solution)/shard_map/all_gather | solution.py:48
  290.4 2.4 copy-start.7
  290.4 2.4 copy-start.14
  295.8 0.8 copy-start.15
  301.6 2.4 copy-start.7
  301.6 2.4 copy-start.14
  307.0 0.8 copy-start.15
  312.4 84.6 %copy-start.20 = (f32[512]{0:T(512)S(1)}, f32[512]{0:T(512)}, u32[]{:S(2)}) copy-start(f32[512]{0:T(512)} %param.21) | copy-start | bytes 6148
  312.4 84.6 %copy-start.25 = (f32[512]{0:T(512)S(1)}, f32[512]{0:T(512)}, u32[]{:S(2)}) copy-start(f32[512]{0:T(512)} %param.22) | copy-start | bytes 6148
  312.5 60.1 %reduce-scatter.11.cloned.1.call-start = ((), (), s32[]{:S(2)}) async-start(), calls=%async_computation.11 | async-start | bytes 3145728 | tf_op jit(solution)/shard_map/reduce_scatter | solution.py:40
  364.1 35.3 %all-gather.17.cloned.1.call-start = ((), (), s32[]{:S(2)}) async-start(), calls=%async_computation.16 | async-start | bytes 1572864 | tf_op jit(solution)/shard_map/all_gather | solution.py:36
  364.7 44.6 %all-gather.13.cloned.1.call-start = ((), (), s32[]{:S(2)}) async-start(), calls=%async_computation.12 | async-start | bytes 1572864 | tf_op jit(solution)/shard_map/all_gather | solution.py:36
  399.3 208.0 %reduce-scatter.17.cloned.1.call-start = ((), (), s32[]{:S(2)}) async-start(), calls=%async_computation.17 | async-start | bytes 14417920 | tf_op jit(solution)/shard_map/reduce_scatter | solution.py:44
  409.1 582.3 %reduce-scatter.13.cloned.1.call-start = ((), (), s32[]{:S(2)}) async-start(), calls=%async_computation.13 | async-start | bytes 28835840 | tf_op jit(solution)/shard_map/reduce_scatter | solution.py:44
  422.9 778.8 %all-gather.19.cloned.1.call-start = ((), (), s32[]{:S(2)}) async-start(), calls=%async_computation.18 | async-start | bytes 14417920 | tf_op jit(solution)/shard_map/all_gather | solution.py:48
  998.7 309.9 %all-gather.15.cloned.1.call-start = ((), (), s32[]{:S(2)}) async-start(), calls=%async_computation.14 | async-start | bytes 7208960 | tf_op jit(solution)/shard_map/all_gather | solution.py:48
  999.3 320.1 %reduce-scatter.19.cloned.1.call-start = ((), (), s32[]{:S(2)}) async-start(), calls=%async_computation.19 | async-start | bytes 3145728 | tf_op jit(solution)/shard_map/reduce_scatter | solution.py:40
  1213.6 120.4 %reduce-scatter.15.cloned.1.call-start = ((), (), s32[]{:S(2)}) async-start(), calls=%async_computation.15 | async-start | bytes 3145728 | tf_op jit(solution)/shard_map/reduce_scatter | solution.py:40
  1316.7 30.6 %all-gather.21.cloned.1.call-start = ((), (), s32[]{:S(2)}) async-start(), calls=%async_computation.20 | async-start | bytes 1572864 | tf_op jit(solution)/shard_map/all_gather | solution.py:36
  1337.9 92.3 %reduce-scatter.21.cloned.1.call-start = ((), (), s32[]{:S(2)}) async-start(), calls=%async_computation.21 | async-start | bytes 5242880 | tf_op jit(solution)/shard_map/reduce_scatter | solution.py:44
  1352.1 85.2 %copy-start.29 = (s32[2]{0:T(128)S(1)}, s32[2]{0:T(128)}, u32[]{:S(2)}) copy-start(s32[2]{0:T(128)} %get-tuple-element.596) | copy-start | bytes 28
  1352.2 291.5 %all-gather.23.cloned.1.call-start = ((), (), s32[]{:S(2)}) async-start(), calls=%async_computation.22 | async-start | bytes 7864320 | tf_op jit(solution)/shard_map/all_gather | solution.py:48
  1437.4 4.3 copy-start.8
  1437.4 4.3 copy-start.9
  1439.9 5.0 copy-start.1
  1441.6 3.2 copy-start.5
  1448.5 5.1 copy-start.2
  1448.5 5.1 copy-start.6
  1448.5 5.3 copy-start.10
  1453.8 3.5 copy-start.3
  1453.8 3.5 copy-start.4
  1470.6 4.3 copy-start.8
  1470.6 4.3 copy-start.9
  1473.1 5.0 copy-start.1
  1474.8 3.2 copy-start.5
  1481.7 5.4 copy-start.2
  1481.7 5.5 copy-start.6
  1481.7 5.6 copy-start.10
  1487.3 4.7 copy-start.3
  1487.3 4.7 copy-start.4
  1528.2 172.7 %reduce-scatter.23.cloned.1.call-start = ((), (), s32[]{:S(2)}) async-start(), calls=%async_computation.23 | async-start | bytes 3145728 | tf_op jit(solution)/shard_map/reduce_scatter | solution.py:40
  1651.3 492.3 %all-reduce.14.cloned.1.call-start = ((), (), s32[]{:S(2)}) async-start(), calls=%async_computation.24 | async-start | bytes 51380224 | tf_op jit(solution)/shard_map/psum | solution.py:283
  1651.3 8.8 copy-start.13
  1651.3 33.5 %slice-start.2 = ((s8[6291456]{0:T(1024)(128)(4,1)}), s8[4194304]{0:T(1024)(128)(4,1)S(1)}, s32[]{:S(2)}) async-start(s8[6291456]{0:T(1024)(128)(4,1)} %bitcast.162), calls=%async_computation.27 | async-start | bytes 8388608
  1660.1 22.1 %copy-start.26 = (bf16[1024,1,1024]{0,2,1:T(8,128)(2,1)S(1)}, bf16[1024,1,1024]{0,2,1:T(8,128)(2,1)}, u32[]{:S(2)}) copy-start(bf16[1024,1,1024]{0,2,1:T(8,128)(2,1)} %all-gather.11.cloned.1.call-done) | copy-start | bytes 6291460
  1660.1 22.1 %copy-start.28 = (bf16[1024,512]{1,0:T(8,128)(2,1)S(1)}, bf16[1024,512]{1,0:T(8,128)(2,1)}, u32[]{:S(2)}) copy-start(bf16[1024,512]{1,0:T(8,128)(2,1)} %all-gather.21.cloned.1.call-done) | copy-start | bytes 3145732
  1660.1 24.8 %slice-start.3 = ((s8[6291456]{0:T(1024)(128)(4,1)}), s8[2097152]{0:T(1024)(128)(4,1)S(1)}, s32[]{:S(2)}) async-start(s8[6291456]{0:T(1024)(128)(4,1)} %bitcast.162), calls=%async_computation.28 | async-start | bytes 4194304
  1682.2 2.7 copy-start.27
  1690.2 10.7 copy-start.17
  1690.2 10.7 copy-start.19
  1690.2 10.7 copy-start.21
  1690.2 12.6 copy-start.22
  1690.2 12.6 copy-start.23
  2143.6 20.4 copy-start.11
  2163.9 5.8 slice-start
  2163.9 3.3 copy-start.12
  2164.0 6.3 slice-start.1
Sparse Core Ops, SparseCore 0:
  34.6 8.6 all-gather.8
  51.0 213.0 reduce-scatter.8
  312.6 46.9 all-gather.10
  364.2 8.3 reduce-scatter.10
  374.0 10.1 all-gather.16
  399.4 8.6 all-gather.12
  411.1 196.0 reduce-scatter.16
  609.7 381.6 reduce-scatter.12
  998.9 202.8 all-gather.18
  1203.7 104.8 all-gather.14
  1311.5 7.8 reduce-scatter.18
  1322.2 10.7 reduce-scatter.14
  1338.0 9.2 all-gather.20
  1352.3 77.9 reduce-scatter.20
  1528.3 115.3 all-gather.22
  1651.4 7.7 reduce-scatter.22
  1690.4 453.1 all-reduce.13
where the time goes:
time: 2190 us; the launch traced here: 2180 us
  waiting for transfers between devices  1750 us (80%)
  matrix products  149 us (7%)
  local copies, waits for them, and re-layouts  97.8 us (4%)
  blocking collectives  87.4 us (4%)
  other arithmetic  66.1 us (3%)
    reduce_scatter x4, waiting for transfers between devices, sum_cols(): return lax.psum_scatter(inputs, 'col', scatter_dimension=2, tiled=True)  858 us
    all_gather x4, waiting for transfers between devices, gather_cols(): return lax.all_gather(inputs, 'col', axis=2, tiled=True)  449 us
    psum x1, waiting for transfers between devices, body(): lax.psum((grad_qkv_weight, grad_qkv_bias, grad_out_weight, grad_gate_up,...  415 us
  transfers between devices with their start and end apart: 17, of which 13 were waited for; matrix products, arithmetic and copies ran while one was open for 4% of the time, Pallas kernels for 0%

commit v1 on v0

v1 whole, which is shorter than its diff:
```python
import jax
import jax.numpy as jnp
from jax import lax
from jax.sharding import PartitionSpec as P

MODEL_WIDTH = 2048
HD = 64
ROT = 16
SEQ = 1024
EPSILON = 1e-05
ROPE_BASE = 10000.0
NEG_LARGE = -1e30
F32 = jnp.float32
BF16 = jnp.bfloat16


def rope_tables(length):
    half_rot = ROT // 2
    inverse = ROPE_BASE ** (-2.0 * jnp.arange(half_rot).astype(F32) / ROT)
    angles = jnp.arange(length).astype(F32)[:, None] * inverse[None, :]
    return jnp.cos(angles)[:, None, :], jnp.sin(angles)[:, None, :]


def rotate(inputs, cosine, sine):
    half_rot = ROT // 2
    lower_half = inputs[..., :half_rot]
    upper_half = inputs[..., half_rot:ROT]
    return jnp.concatenate(
        [
            lower_half * cosine - upper_half * sine,
            upper_half * cosine + lower_half * sine,
            inputs[..., ROT:],
        ],
        axis=-1,
    )


def dot(spec, a, b):
    return jnp.einsum(spec, a, b, preferred_element_type=F32)


def fetch_columns(block, sizes):
    dp, col = sizes["dp"], sizes["col"]
    depth, k, wide = block.shape
    part = depth // dp
    piece = lax.dynamic_slice_in_dim(block, lax.axis_index("dp") * part, part, 0)
    piece = piece.reshape(part, k, col, wide // col).transpose(2, 0, 1, 3)
    piece = lax.all_to_all(piece, "col", 0, 0, tiled=True)
    whole = lax.all_gather(piece, "dp", axis=0)
    return whole.transpose(1, 0, 2, 3, 4).reshape(col * depth, k, wide // col)


def return_columns(grad, sizes):
    dp, col = sizes["dp"], sizes["col"]
    width, k, narrow = grad.shape
    part = width // col // dp
    pieces = grad.astype(BF16).reshape(col, dp, part, k * narrow).transpose(1, 0, 2, 3)
    piece = lax.psum_scatter(pieces, "dp", scatter_dimension=0, tiled=True)[0]
    piece = lax.all_to_all(piece, "col", 0, 0, tiled=True)
    piece = piece.reshape(col, part, k, narrow).transpose(1, 2, 0, 3).reshape(part, k, col * narrow)
    return lax.all_gather(piece, "dp", axis=0, tiled=True).astype(F32)


def fetch_rows(block, sizes):
    dp, col = sizes["dp"], sizes["col"]
    tall, depth = block.shape
    part = tall // col // dp
    piece = lax.dynamic_index_in_dim(
        block.reshape(col, dp, part, depth), lax.axis_index("dp"), 1, False
    )
    piece = lax.all_to_all(piece, "col", 0, 0, tiled=True)
    piece = piece.transpose(1, 0, 2).reshape(part, col * depth)
    return lax.all_gather(piece, "dp", axis=0, tiled=True)


def return_rows(grad, sizes):
    dp, col = sizes["dp"], sizes["col"]
    short, width = grad.shape
    part, depth = short // dp, width // col
    piece = lax.psum_scatter(grad.astype(BF16), "dp", scatter_dimension=0, tiled=True)
    piece = piece.reshape(part, col, depth).transpose(1, 0, 2)
    piece = lax.all_to_all(piece, "col", 0, 0, tiled=True)
    whole = lax.all_gather(piece, "dp", axis=0)
    return whole.transpose(1, 0, 2, 3).reshape(col * short, depth).astype(F32)


def sum_tokens(partial, sizes):
    half = lax.psum_scatter(partial.astype(BF16), "row", scatter_dimension=0, tiled=True)
    return lax.psum_scatter(half, "col", scatter_dimension=0, tiled=True)


def sum_features(partial, sizes):
    half = lax.psum_scatter(partial.astype(BF16), "row", scatter_dimension=0, tiled=True)
    return lax.psum_scatter(half, "col", scatter_dimension=1, tiled=True)


def gather_tokens(own):
    return lax.all_gather(lax.all_gather(own, "col", axis=0, tiled=True), "row", axis=0, tiled=True)


def stats(rows):
    mean = jnp.mean(rows, axis=1, keepdims=True)
    centered = rows - mean
    return mean, lax.rsqrt(jnp.mean(centered * centered, axis=1, keepdims=True) + EPSILON)


def block_scores(query_block, key_rows, offset):
    block_rows = query_block.shape[0]
    scores = dot("qhd,khd->hqk", query_block, key_rows) * HD ** (-0.5)
    allowed = (offset + jnp.arange(block_rows))[:, None] >= jnp.arange(key_rows.shape[0])[None, :]
    return jnp.where(allowed[None], scores, NEG_LARGE)


def attention_forward(queries, key_rows, value_rows):
    def one_seq(packed):
        seq_queries, seq_keys, seq_values = packed
        length = seq_queries.shape[0]
        block_rows = min(512, length)
        blocks = length // block_rows
        query_blocks = seq_queries.reshape((blocks, block_rows) + seq_queries.shape[1:])
        offsets = jnp.arange(blocks) * block_rows

        def one_block(element):
            query_block, offset = element
            scores = block_scores(query_block, seq_keys, offset)
            row_max = jnp.max(scores, axis=2, keepdims=True)
            expo = jnp.exp(scores - row_max)
            denominator = jnp.sum(expo, axis=2, keepdims=True)
            attn_probs = (expo / denominator).astype(BF16)
            result = dot("hqk,khd->qhd", attn_probs, seq_values)
            return (result, (row_max + jnp.log(denominator))[:, :, 0])

        results, log_sums = lax.map(one_block, (query_blocks, offsets))
        return (results.reshape(seq_queries.shape), log_sums)

    return lax.map(one_seq, (queries, key_rows, value_rows))


def attention_backward(queries, key_rows, value_rows, log_sums, grad_attn):
    def one_seq(packed):
        seq_queries, seq_keys, seq_values, seq_sums, seq_grad = packed
        length = seq_queries.shape[0]
        block_rows = min(512, length)
        blocks = length // block_rows
        block_shape = (blocks, block_rows) + seq_queries.shape[1:]
        offsets = jnp.arange(blocks) * block_rows

        def advance(running, element):
            query_block, offset, sum_block, grad_block = element
            scores = block_scores(query_block, seq_keys, offset)
            attn_probs = jnp.exp(scores - sum_block[:, :, None])
            grad_probs = dot("qhd,khd->hqk", grad_block, seq_values)
            delta = jnp.sum(grad_probs * attn_probs, axis=2, keepdims=True)
            grad_scores = (attn_probs * (grad_probs - delta)).astype(BF16)
            grad_query = dot("hqk,khd->qhd", grad_scores, seq_keys) * HD ** (-0.5)
            grad_key = dot("hqk,qhd->khd", grad_scores, query_block) * HD ** (-0.5)
            grad_value = dot("hqk,qhd->khd", attn_probs.astype(BF16), grad_block)
            return ((running[0] + grad_key, running[1] + grad_value), grad_query)

        empty_grad = jnp.zeros(seq_keys.shape, F32)
        (grad_keys, grad_values), grad_queries = lax.scan(
            advance,
            (empty_grad, empty_grad),
            (seq_queries.reshape(block_shape), offsets, seq_sums, seq_grad.reshape(block_shape)),
        )
        return (grad_queries.reshape(seq_queries.shape), grad_keys, grad_values)

    return lax.map(one_seq, (queries, key_rows, value_rows, log_sums, grad_attn))


def make_body(sizes):
    col = sizes["col"]

    def body(
        tokens,
        attention_norm_gain,
        attention_norm_bias,
        qkv_weight,
        qkv_bias,
        out_weight,
        feedforward_norm_gain,
        feedforward_norm_bias,
        gate_up_weight,
        down_weight,
        cotangent,
    ):
        my_col = lax.axis_index("col")
        depth = tokens.shape[1]
        qkv_w = fetch_columns(qkv_weight, sizes)
        out_w = fetch_rows(out_weight, sizes)
        gate_up_w = fetch_columns(gate_up_weight, sizes)
        down_w = fetch_rows(down_weight, sizes)
        vectors = lax.all_gather(
            jnp.stack(
                [
                    attention_norm_gain,
                    attention_norm_bias,
                    feedforward_norm_gain,
                    feedforward_norm_bias,
                ]
            ),
            "col",
            axis=1,
            tiled=True,
        )
        rows_half = lax.all_gather(tokens, "col", axis=1, tiled=True)
        cotan_half = lax.all_gather(cotangent, "col", axis=1, tiled=True)
        cotan_rows = lax.all_gather(cotan_half, "row", axis=0, tiled=True)
        half_f = rows_half.astype(F32)
        mean_one, rstd_one = stats(half_f)
        normed_half = ((half_f - mean_one) * rstd_one * vectors[0] + vectors[1]).astype(BF16)
        normed_one = lax.all_gather(normed_half, "row", axis=0, tiled=True)
        group_rows = normed_one.shape[0]
        heads = qkv_bias.shape[1] // HD
        seqs = group_rows // SEQ
        head_shape = (group_rows, heads, HD)
        seq_shape = (seqs, SEQ, heads, HD)
        cosine, sine = rope_tables(SEQ)
        cosine, sine = jnp.tile(cosine, (seqs, 1, 1)), jnp.tile(sine, (seqs, 1, 1))
        qkv = dot("td,dkf->tkf", normed_one, qkv_w) + qkv_bias[None]
        queries = rotate(qkv[:, 0].reshape(head_shape), cosine, sine).astype(BF16).reshape(seq_shape)
        keys = rotate(qkv[:, 1].reshape(head_shape), cosine, sine).astype(BF16).reshape(seq_shape)
        values = qkv[:, 2].astype(BF16).reshape(seq_shape)
        attn_out, log_sums = attention_forward(queries, keys, values)
        attn = attn_out.reshape(group_rows, heads * HD).astype(BF16)
        own = group_rows // sizes["row"] // col
        branch = sum_tokens(dot("tf,fd->td", attn, out_w), sizes).astype(F32)

        def own_rows(half):
            return lax.dynamic_slice_in_dim(half, my_col * own, own, 0).astype(F32)

        middle = own_rows(rows_half) + branch
        mean_two, rstd_two = stats(middle)
        xhat_two = (middle - mean_two) * rstd_two
        normed_two = gather_tokens((xhat_two * vectors[2] + vectors[3]).astype(BF16))
        gate_up = dot("td,dkf->tkf", normed_two, gate_up_w)
        gate, up = gate_up[:, 0], gate_up[:, 1]
        sig = jax.nn.sigmoid(gate)
        hidden = (gate * sig * up).astype(BF16)
        mixed_part = dot("tf,fd->td", hidden, down_w)
        start = lax.axis_index("row") * (own * col) + my_col * own
        mine = lax.dynamic_slice_in_dim(mixed_part, start, own, 0)
        mixed_part = lax.dynamic_update_slice_in_dim(mixed_part, mine + middle, start, 0)
        mixed = sum_features(mixed_part, sizes)
        grad_down = return_rows(dot("tf,td->fd", hidden, cotan_rows), sizes)
        grad_hidden = dot("td,fd->tf", cotan_rows, down_w)
        grad_gu = jnp.stack(
            [grad_hidden * up * sig * (1.0 + gate * (1.0 - sig)), grad_hidden * gate * sig], axis=1
        ).astype(BF16)
        grad_gate_up = return_columns(dot("td,tkf->dkf", normed_two, grad_gu), sizes)
        grad_normed_two = sum_tokens(dot("tkf,dkf->td", grad_gu, gate_up_w), sizes).astype(F32)
        second = jnp.stack(
            [jnp.sum(grad_normed_two * xhat_two, axis=0), jnp.sum(grad_normed_two, axis=0)]
        )
        scaled = grad_normed_two * vectors[2]
        grad_middle = own_rows(cotan_half) + rstd_two * (
            scaled
            - jnp.mean(scaled, axis=1, keepdims=True)
            - xhat_two * jnp.mean(scaled * xhat_two, axis=1, keepdims=True)
        )
        grad_middle_rows = gather_tokens(grad_middle.astype(BF16))
        grad_out = return_rows(dot("tf,td->fd", attn, grad_middle_rows), sizes)
        grad_attn = dot("td,fd->tf", grad_middle_rows, out_w).astype(BF16).reshape(seq_shape)
        grad_queries, grad_keys, grad_values = attention_backward(
            queries, keys, values, log_sums, grad_attn
        )
        grad_qkv = jnp.stack(
            [
                rotate(grad_queries.reshape(head_shape), cosine, -sine),
                rotate(grad_keys.reshape(head_shape), cosine, -sine),
                grad_values.reshape(head_shape),
            ],
            axis=1,
        )
        grad_qkv = grad_qkv.reshape(group_rows, 3, heads * HD).astype(BF16)
        bias_part = jnp.sum(grad_qkv, axis=0, dtype=F32)
        grad_qkv_weight = return_columns(dot("td,tkf->dkf", normed_one, grad_qkv), sizes)
        normed_part = dot("tkf,dkf->td", grad_qkv, qkv_w)
        grad_normed_one = sum_features(normed_part, sizes).astype(F32)
        xhat_one = (tokens.astype(F32) - mean_one) * rstd_one
        scaled_one = grad_normed_one * attention_norm_gain
        sums = lax.psum(
            jnp.stack([jnp.sum(scaled_one, axis=1), jnp.sum(scaled_one * xhat_one, axis=1)]), "col"
        )
        own_grad = sum_features_residual(grad_middle_rows, depth, my_col)
        input_grad = own_grad + rstd_one * (
            scaled_one - sums[0][:, None] / MODEL_WIDTH - xhat_one * sums[1][:, None] / MODEL_WIDTH
        )
        first = jnp.stack(
            [jnp.sum(grad_normed_one * xhat_one, axis=0), jnp.sum(grad_normed_one, axis=0)]
        )
        second = lax.psum_scatter(second, "col", scatter_dimension=1, tiled=True)
        norms = lax.psum(jnp.concatenate([first, second]), ("dp", "row"))
        bias = lax.psum(bias_part, "dp")
        return (
            mixed,
            input_grad,
            norms[0],
            norms[1],
            grad_qkv_weight,
            bias,
            grad_out,
            norms[2],
            norms[3],
            grad_gate_up,
            grad_down,
        )

    return body


def sum_features_residual(grad_middle_rows, depth, my_col):
    half = grad_middle_rows.shape[0] // 2
    rows = lax.dynamic_slice_in_dim(grad_middle_rows, lax.axis_index("row") * half, half, 0)
    return lax.dynamic_slice_in_dim(rows, my_col * depth, depth, 1).astype(F32)


def solution(mesh):
    specs = (
        P(("dp", "row"), "col"),
        P("col"),
        P("col"),
        P("col", None, "row"),
        P(None, ("row", "col")),
        P("row", "col"),
        P("col"),
        P("col"),
        P("col", None, "row"),
        P("row", "col"),
    )
    return jax.shard_map(
        make_body(dict(mesh.shape)),
        mesh=mesh,
        in_specs=specs + (P(("dp", "row"), "col"),),
        out_specs=(P(("dp", "row"), "col"),) + specs,
        check_vma=False,
    )
```

time: 2190 us -> 1210 us (0.55)
  waiting for transfers between devices: 1750 us -> 569 us
  blocking collectives: 87.4 us -> 254 us
  local copies, waits for them, and re-layouts: 97.8 us -> 164 us
    reduce_scatter x8 -> x10, waiting for transfers between devices: 869 us -> 170 us  [the longest x2 85.3 us: sum_tokens(): return lax.psum_scatter(half, 'col', scatter_dimension=0, tiled=True)]
    psum x1 -> x0, waiting for transfers between devices: 415 us -> none  [body(): lax.psum((grad_qkv_weight, grad_qkv_bias, grad_out_weight, grad_gate_up,...]
    all_to_all x0 -> x6, blocking collectives: none -> 208 us  [the longest x2 111 us: fetch_columns(): piece = lax.all_to_all(piece, 'col', 0, 0, tiled=True)]
    all_gather x8 -> x16, waiting for transfers between devices: 467 us -> 331 us  [the longest x2 97.2 us: return_columns(): return lax.all_gather(piece, 'dp', axis=0, tiled=True).astype(F32)]
    psum x8 -> x3, blocking collectives: 87.4 us -> 33.5 us  [the longest x1 12.8 us: body(): norms = lax.psum(jnp.concatenate([first, second]), ('dp', 'row'))]
    reshape x1 -> x11, local copies, waits for them, and re-layouts: 3.09 us -> 50 us  [the longest x3 24.8 us: return_columns(): grad.astype(BF16).reshape(col, dp, part, k * narrow).transpose(1, 0, 2, 3)]
    all_to_all x0 -> x2, waiting for transfers between devices: none -> 40.2 us  [the longest x1 32 us: return_columns(): piece = lax.all_to_all(piece, 'col', 0, 0, tiled=True)]
    unnamed x17 -> x32, waiting for transfers between devices: 1.31 us -> 27.8 us
  transfers between devices with their start and end apart: 17 -> 31, of which waited for: 13 -> 21; matrix products, arithmetic and copies ran while one was open for 4% -> 25% of each run, Pallas kernels for 0% -> 0%
where the time goes in v1:
time: 1210 us; the launch traced here: 1200 us
  waiting for transfers between devices  569 us (47%)
  blocking collectives  254 us (21%)
  local copies, waits for them, and re-layouts  164 us (14%)
  matrix products  135 us (11%)
  other arithmetic  52.6 us (4%)
  between operations  15.2 us (1%)
    dot_general x26, matrix products, dot(): return jnp.einsum(spec, a, b, preferred_element_type=F32)  135 us
    all_to_all x2, blocking collectives, fetch_columns(): piece = lax.all_to_all(piece, 'col', 0, 0, tiled=True)  111 us
    all_gather x2, waiting for transfers between devices, return_columns(): return lax.all_gather(piece, 'dp', axis=0, tiled=True).astype(F32)  97.2 us
    all_gather x2, waiting for transfers between devices, fetch_columns(): whole = lax.all_gather(piece, 'dp', axis=0)  90 us
    reduce_scatter x2, waiting for transfers between devices, sum_tokens(): return lax.psum_scatter(half, 'col', scatter_dimension=0, tiled=True)  85.3 us
    reduce_scatter x2, waiting for transfers between devices, sum_features(): return lax.psum_scatter(half, 'col', scatter_dimension=1, tiled=True)  58.3 us
    all_gather x2, waiting for transfers between devices, gather_tokens(): lax.all_gather(own, 'col', axis=0, tiled=True)  45.4 us
    all_to_all x1, blocking collectives, fetch_rows(): piece = lax.all_to_all(piece, 'col', 0, 0, tiled=True)  40.7 us
  transfers between devices with their start and end apart: 31, of which 21 were waited for; matrix products, arithmetic and copies ran while one was open for 25% of the time, Pallas kernels for 0%

profile of v1, /device:TPU:0, one launch (start us, length us, event | category | flops | bytes accessed | tf_op | source)
XLA Modules:
  0.0 1199.1 jit_solution(2412355122726797253)
XLA Ops:
  11.6 45.5 %all_to_all.40 = bf16[4,128,3,256]{1,3,2,0:T(8,128)(2,1)S(1)} all-to-all(bf16[4,128,3,256]{1,3,2,0:T(8,128)(2,1)S(1)} %copy.127), channel_id=1, replica_groups=mesh['dp'=4,'row'=2,'col'=4] {'col'}, dimensions={0} | all-to-all | bytes 1572864 | tf_op jit(solution)/shard_map/all_to_all | solution.py:48
  58.4 13.2 %all_gather.64 = f32[4,2048]{1,0:T(4,128)S(1)} all-gather(f32[4,512]{1,0:T(4,128)S(1)} %pad_maximum_fusion.8), channel_id=1, replica_groups=mesh['dp'=4,'row'=2,'col'=4] {'col'}, dimensions={1}, use_global_device_ids=true | all-gather | bytes 40960 | tf_op jit(solution)/shard_map/all_gather | solution.py:193
  85.3 8.3 all-to-all-done.1
  94.5 23.4 %all-gather.45.cloned.1.call-done = bf16[16,128,3,256]{3,1,2,0:T(8,128)(2,1)} async-done(((bf16[4,128,3,256]{3,1,2,0:T(8,128)(2,1)}), bf16[16,128,3,256]{3,1,2,0:T(8,128)(2,1)}) %all-gather.45.cloned.1.call-update) | async-done | bytes 3145744 | tf_op jit(solution)/shard_map/all_gather | solution.py:49
  118.0 6.2 copy.129
  124.1 6.4 reshape.330
  133.8 6.2 fusion.61
  142.2 22.2 %while.47 = (s32[]{:T(128)}, bf16[2,512,4,64]{1,3,2,0:T(8,128)(2,1)}, f32[2,4,512]{2,1,0:T(4,128)S(1)}, s32[2]{0:T(128)S(1)}, bf16[2,512,4,64]{1,3,2,0:T(8,128)(...) while((s32[]{:T(128)}, bf16[2,512,4,64]{1,3,2,0:T(8,128)(2,1)}, ...), condition=%wide.region_5.6_spmd, body=%wide.region_2.5_spmd.sunk | while | flops 562559488 | bytes 33362096 | solution.py:133
  148.8 3.7 fusion.136
  166.0 4.7 convolution_convert_fusion.1
  170.8 13.3 %reduce-scatter.20.cloned.1.call-done = bf16[512,2048]{1,0:T(8,128)(2,1)} async-done(((bf16[1024,2048]{1,0:T(8,128)(2,1)}), bf16[512,2048]{1,0:T(8,128)(2,1)}) %reduce-scatter.20.cloned.1.call-update) | async-done | bytes 2097168 | tf_op jit(solution)/shard_map/reduce_scatter | solution.py:88
  184.2 47.4 %reduce-scatter.22.cloned.1.call-done = bf16[128,2048]{1,0:T(8,128)(2,1)} async-done(((bf16[512,2048]{1,0:T(8,128)(2,1)}), bf16[128,2048]{1,0:T(8,128)(2,1)}) %reduce-scatter.22.cloned.1.call-update) | async-done | bytes 524304 | tf_op jit(solution)/shard_map/reduce_scatter | solution.py:89
  240.6 4.9 copy.173
  246.9 65.2 %all_to_all.41 = bf16[4,128,2,704]{1,3,2,0:T(8,128)(2,1)} all-to-all(bf16[4,128,2,704]{1,3,2,0:T(8,128)(2,1)S(1)} %copy.137), channel_id=1, replica_groups=mesh['dp'=4,'row'=2,'col'=4] {'col'}, dimensions={0} | all-to-all | bytes 2883584 | tf_op jit(solution)/shard_map/all_to_all | solution.py:48
  314.0 40.7 %all_to_all.42 = bf16[4,176,512]{2,1,0:T(8,128)(2,1)S(1)} all-to-all(bf16[4,176,512]{2,1,0:T(8,128)(2,1)S(1)} %dynamic-slice_bitcast_fusion.1), channel_id=1, replica_groups=mesh['dp'=4,'row'=2,'col'=4] {'col'}, dimensions={0} | all-to-all | bytes 1441792 | tf_op jit(solution)/shard_map/all_to_all | solution.py:71
  355.7 14.4 %all-gather.33.cloned.1.call-done = bf16[512,2048]{1,0:T(8,128)(2,1)} async-done(((bf16[512,512]{1,0:T(8,128)(2,1)}), bf16[512,2048]{1,0:T(8,128)(2,1)}) %all-gather.33.cloned.1.call-update) | async-done | bytes 2097168 | tf_op jit(solution)/shard_map/all_gather | solution.py:207
  370.1 66.6 %all-gather.47.cloned.1.call-done = bf16[16,128,2,704]{1,3,2,0:T(8,128)(2,1)} async-done(((bf16[4,128,2,704]{1,3,2,0:T(8,128)(2,1)}), bf16[16,128,2,704]{1,3,2,0:T(8,128)(2,1)}) %all-gather.47.cloned.1.call-update) | async-done | bytes 5767184 | tf_op jit(solution)/shard_map/all_gather | solution.py:49
  436.7 9.9 copy.138
  446.7 10.7 reshape.334
  457.3 11.0 fusion.47
  468.3 28.9 %all-gather.31.cloned.1.call-done = bf16[704,2048]{1,0:T(8,128)(2,1)} async-done(((bf16[176,2048]{1,0:T(8,128)(2,1)}), bf16[704,2048]{1,0:T(8,128)(2,1)}) %all-gather.31.cloned.1.call-update) | async-done | bytes 2883600 | tf_op jit(solution)/shard_map/all_gather | solution.py:73
  497.3 15.1 %all-gather.35.cloned.1.call-done = bf16[1024,2048]{1,0:T(8,128)(2,1)} async-done(((bf16[512,2048]{1,0:T(8,128)(2,1)}), bf16[1024,2048]{1,0:T(8,128)(2,1)}) %all-gather.35.cloned.1.call-update) | async-done | bytes 4194320 | tf_op jit(solution)/shard_map/all_gather | solution.py:208
  512.4 10.0 fusion.71
  524.0 11.0 bitcast_convert_fusion.1
  535.1 13.3 %reduce-scatter.28.cloned.1.call-done = bf16[512,2048]{1,0:T(8,128)(2,1)} async-done(((bf16[1024,2048]{1,0:T(8,128)(2,1)}), bf16[512,2048]{1,0:T(8,128)(2,1)}) %reduce-scatter.28.cloned.1.call-update) | async-done | bytes 2097168 | tf_op jit(solution)/shard_map/reduce_scatter | solution.py:88
  548.7 9.2 fusion.90
  557.9 38.0 %reduce-scatter.30.cloned.1.call-done = bf16[128,2048]{1,0:T(8,128)(2,1)} async-done(((bf16[512,2048]{1,0:T(8,128)(2,1)}), bf16[128,2048]{1,0:T(8,128)(2,1)}) %reduce-scatter.30.cloned.1.call-update) | async-done | bytes 524304 | tf_op jit(solution)/shard_map/reduce_scatter | solution.py:89
  601.5 45.4 %all-gather.37.cloned.1.call-done = bf16[512,2048]{1,0:T(8,128)(2,1)} async-done(((bf16[128,2048]{1,0:T(8,128)(2,1)}), bf16[512,2048]{1,0:T(8,128)(2,1)}) %all-gather.37.cloned.1.call-update) | async-done | bytes 2097168 | tf_op jit(solution)/shard_map/all_gather | solution.py:98
  646.9 7.4 convolution_convert_fusion.2
  654.5 11.0 convolution_convert_fusion
  665.5 10.4 reshape.343
  675.9 10.6 copy.155
  687.7 4.3 convolution_convert_fusion.4
  695.4 4.5 convolution_convert_fusion.3
  700.0 65.7 %while.48 = (s32[]{:T(128)}, f32[1024,4,64]{0,2,1:T(8,128)S(1)}, f32[1024,4,64]{0,2,1:T(8,128)}, f32[2,512,4,64]{1,0,3,2:T(2,128)}, bf16[2,512,4,64]{1,3,2,0:T(8...) while((s32[]{:T(128)}, f32[1024,4,64]{0,2,1:T(8,128)S(1)}, ...), condition=%wide.region_18.19_spmd.clone, body=%wide.region_16.18_spmd.clone.sunk | while | flops 1375599104 | bytes 166785360 | solution.py:161
  703.0 4.9 multiply_reduce_fusion.3
  707.9 3.7 multiply_convert_fusion.3
  716.6 3.7 fusion.148
  722.3 10.4 dynamic_update_slice.36
  735.8 4.9 multiply_reduce_fusion.3
  740.7 3.7 multiply_convert_fusion.3
  749.4 3.7 fusion.148
  755.1 10.4 dynamic_update_slice.36
  772.7 7.4 fusion.53
  783.3 3.9 reshape.339
  787.1 6.2 copy.150
  793.4 6.4 bitcast_convert_fusion
  799.9 6.1 convert_element_type.201
  807.3 22.3 %all_to_all.43 = bf16[4,176,512]{2,1,0:T(8,128)(2,1)} all-to-all(bf16[4,176,512]{2,1,0:T(8,128)(2,1)S(1)} %bitcast.294), channel_id=1, replica_groups=mesh['dp'=4,'row'=2,'col'=4] {'col'}, dimensions={0} | all-to-all | bytes 1441792 | tf_op jit(solution)/shard_map/all_to_all | solution.py:82
  834.8 32.0 %all-to-all-done.6 = bf16[4,128,1408]{2,1,0:T(8,128)(2,1)S(1)} async-done(((bf16[4,128,1408]{2,1,0:T(8,128)(2,1)}), bf16[4,128,1408]{2,1,0:T(8,128)(2,1)S(1)}, u32[]{:S(2)}, u32[]{:S(2)}) %all-to-all-start.6) | async-done | bytes 1441824 | tf_op jit(solution)/shard_map/all_to_all | solution.py:59
  869.8 11.4 all_to_all.44
  881.4 22.4 %all_to_all.45 = bf16[4,128,768]{2,1,0:T(8,128)(2,1)S(1)} all-to-all(bf16[4,128,768]{2,1,0:T(8,128)(2,1)} %bitcast.310), channel_id=1, replica_groups=mesh['dp'=4,'row'=2,'col'=4] {'col'}, dimensions={0} | all-to-all | bytes 1572864 | tf_op jit(solution)/shard_map/all_to_all | solution.py:59
  906.6 22.7 %all-gather.51.cloned.1.call-done = bf16[16,176,512]{2,1,0:T(8,128)(2,1)} async-done(((bf16[4,176,512]{2,1,0:T(8,128)(2,1)}), bf16[16,176,512]{2,1,0:T(8,128)(2,1)}) %all-gather.51.cloned.1.call-update) | async-done | bytes 2883600 | tf_op jit(solution)/shard_map/all_gather | solution.py:83
  935.2 24.2 %reduce-scatter.40.cloned.1.call-done = f32[512,2]{1,0:T(8,128)} async-done(((f32[2048,2]{1,0:T(8,128)}), f32[512,2]{1,0:T(8,128)}) %reduce-scatter.40.cloned.1.call-update) | async-done | bytes 4112
  960.7 10.7 psum.23
  971.4 54.7 %all-gather.43.cloned.1.call-done = bf16[512,2,2816]{0,2,1:T(8,128)(2,1)} async-done(((bf16[128,2,2816]{0,2,1:T(8,128)(2,1)}), bf16[512,2,2816]{0,2,1:T(8,128)(2,1)}) %all-gather.43.cloned.1.call-update) | async-done | bytes 5767184 | tf_op jit(solution)/shard_map/all_gather | solution.py:61
  1026.1 15.6 %copy.161 = f32[512,2,2816]{2,1,0:T(2,128)} copy(bf16[512,2,2816]{0,2,1:T(8,128)(2,1)} %all-gather.43.cloned.1.call-done) | data formatting | bytes 17301504
  1041.7 12.8 %all-gather.49.cloned.1.call-done = bf16[16,64,512]{2,1,0:T(8,128)(2,1)} async-done(((bf16[4,64,512]{2,1,0:T(8,128)(2,1)}), bf16[16,64,512]{2,1,0:T(8,128)(2,1)}) %all-gather.49.cloned.1.call-update) | async-done | bytes 1048592 | tf_op jit(solution)/shard_map/all_gather | solution.py:83
  1057.5 42.5 %all-gather.41.cloned.1.call-done = bf16[512,3,1024]{0,2,1:T(8,128)(2,1)} async-done(((bf16[128,3,1024]{0,2,1:T(8,128)(2,1)}), bf16[512,3,1024]{0,2,1:T(8,128)(2,1)}) %all-gather.41.cloned.1.call-update) | async-done | bytes 3145744 | tf_op jit(solution)/shard_map/all_gather | solution.py:61
  1100.0 5.5 copy.160
  1105.5 40.7 %reduce-scatter.34.cloned.1.call-done = bf16[512,512]{1,0:T(8,128)(2,1)} async-done(((bf16[512,2048]{1,0:T(8,128)(2,1)}), bf16[512,512]{1,0:T(8,128)(2,1)}) %reduce-scatter.34.cloned.1.call-update) | async-done | bytes 524304 | tf_op jit(solution)/shard_map/reduce_scatter | solution.py:94
  1148.0 9.9 psum.21
  1157.9 12.8 %psum.22 = f32[4,512]{1,0:T(4,128)S(1)} all-reduce(f32[4,512]{1,0:T(4,128)S(1)} %pad_maximum_fusion.9), channel_id=1, replica_groups=mesh['dp'=4,'row'=2,'col'=4] {'dp','row'}, use_global_device_ids=true, to_apply=%region_29.30 | all-reduce | flops 2048 | bytes 16384 | tf_op jit(solution)/shard_map/psum | solution.py:293
  1174.7 17.7 %reduce-scatter.26.cloned.1.call-done = bf16[512,512]{1,0:T(8,128)(2,1)} async-done(((bf16[512,2048]{1,0:T(8,128)(2,1)}), bf16[512,512]{1,0:T(8,128)(2,1)}) %reduce-scatter.26.cloned.1.call-update) | async-done | bytes 524304 | tf_op jit(solution)/shard_map/reduce_scatter | solution.py:94
  (275 shorter events, 129.6 us)
Async XLA Ops:
  7.2 65.3 %all-gather.21.cloned.1.call-start = ((), (), s32[]{:S(2)}) async-start(), calls=%async_computation.21 | async-start | bytes 2621440 | tf_op jit(solution)/shard_map/all_gather | solution.py:206
  7.9 110.0 %all-gather.45.cloned.1.call-start = ((), (), s32[]{:S(2)}) async-start(), calls=%async_computation.43 | async-start | bytes 3932160 | tf_op jit(solution)/shard_map/all_gather | solution.py:49
  9.1 49.2 %copy-start.32 = (f32[512]{0:T(512)S(1)}, f32[512]{0:T(512)}, u32[]{:S(2)}) copy-start(f32[512]{0:T(512)} %param.16) | copy-start | bytes 6148
  9.1 49.2 %copy-start.34 = (f32[512]{0:T(512)S(1)}, f32[512]{0:T(512)}, u32[]{:S(2)}) copy-start(f32[512]{0:T(512)} %param.22) | copy-start | bytes 6148
  9.1 49.2 %copy-start.35 = (f32[512]{0:T(512)S(1)}, f32[512]{0:T(512)}, u32[]{:S(2)}) copy-start(f32[512]{0:T(512)} %param.21) | copy-start | bytes 6148
  9.1 49.2 %copy-start.36 = (f32[512]{0:T(512)S(1)}, f32[512]{0:T(512)}, u32[]{:S(2)}) copy-start(f32[512]{0:T(512)} %param.17) | copy-start | bytes 6148
  58.2 75.6 %all-gather.23.cloned.1.call-start = ((), (), s32[]{:S(2)}) async-start(), calls=%async_computation.22 | async-start | bytes 6291456 | tf_op jit(solution)/shard_map/all_gather | solution.py:212
  72.5 4.4 copy-start.5
  74.6 4.5 copy-start.26
  76.9 3.9 copy-start.28
  80.8 12.8 %all-to-all-start.1 = ((bf16[4,64,512]{2,1,0:T(8,128)(2,1)}), bf16[4,64,512]{2,1,0:T(8,128)(2,1)S(1)}, u32[]{:S(2)}, u32[]{:S(2)}) async-start(bf16[4,64,512]{2,1,0:T(8,128)(2,1)} %dynamic-slice_bitcast_fusion.2), calls=%async_computation.1 | async-start | bytes 524288 | tf_op jit(solution)/shard_map/all_to_all | solution.py:71
  84.4 81.6 %all-gather.25.cloned.1.call-start = ((), (), s32[]{:S(2)}) async-start(), calls=%async_computation.23 | async-start | bytes 1310720 | tf_op jit(solution)/shard_map/all_gather | solution.py:73
  85.3 55.9 %copy-start.23 = (f32[1024,8]{0,1:T(8,128)}, f32[1024,8]{0,1:T(8,128)S(1)}, u32[]{:S(2)}) copy-start(f32[1024,8]{0,1:T(8,128)S(1)} %get-tuple-element.355) | copy-start | bytes 98308
  94.3 89.8 %reduce-scatter.20.cloned.1.call-start = ((), (), s32[]{:S(2)}) async-start(), calls=%async_computation.24 | async-start | bytes 6291456 | tf_op jit(solution)/shard_map/reduce_scatter | solution.py:88
  124.1 9.7 copy-start.37
  166.0 4.8 copy-start.9
  170.7 60.8 %reduce-scatter.22.cloned.1.call-start = ((), (), s32[]{:S(2)}) async-start(), calls=%async_computation.25 | async-start | bytes 2621440 | tf_op jit(solution)/shard_map/reduce_scatter | solution.py:89
  184.1 128.1 %all-gather.27.cloned.1.call-start = ((), (), s32[]{:S(2)}) async-start(), calls=%async_computation.26 | async-start | bytes 2621440 | tf_op jit(solution)/shard_map/all_gather | solution.py:98
  236.3 133.8 %all-gather.33.cloned.1.call-start = ((), (), s32[]{:S(2)}) async-start(), calls=%async_computation.31 | async-start | bytes 2621440 | tf_op jit(solution)/shard_map/all_gather | solution.py:207
  237.1 199.7 %all-gather.47.cloned.1.call-start = ((), (), s32[]{:S(2)}) async-start(), calls=%async_computation.44 | async-start | bytes 7208960 | tf_op jit(solution)/shard_map/all_gather | solution.py:49
  312.2 145.1 %all-gather.29.cloned.1.call-start = ((), (), s32[]{:S(2)}) async-start(), calls=%async_computation.27 | async-start | bytes 6291456 | tf_op jit(solution)/shard_map/all_gather | solution.py:98
  312.8 184.5 %all-gather.31.cloned.1.call-start = ((), (), s32[]{:S(2)}) async-start(), calls=%async_computation.28 | async-start | bytes 3604480 | tf_op jit(solution)/shard_map/all_gather | solution.py:73
  355.6 156.7 %all-gather.35.cloned.1.call-start = ((), (), s32[]{:S(2)}) async-start(), calls=%async_computation.32 | async-start | bytes 6291456 | tf_op jit(solution)/shard_map/all_gather | solution.py:208
  370.1 178.3 %reduce-scatter.28.cloned.1.call-start = ((), (), s32[]{:S(2)}) async-start(), calls=%async_computation.33 | async-start | bytes 6291456 | tf_op jit(solution)/shard_map/reduce_scatter | solution.py:88
  535.0 60.8 %reduce-scatter.30.cloned.1.call-start = ((), (), s32[]{:S(2)}) async-start(), calls=%async_computation.34 | async-start | bytes 2621440 | tf_op jit(solution)/shard_map/reduce_scatter | solution.py:89
  548.4 98.4 %all-gather.37.cloned.1.call-start = ((), (), s32[]{:S(2)}) async-start(), calls=%async_computation.35 | async-start | bytes 2621440 | tf_op jit(solution)/shard_map/all_gather | solution.py:98
  548.7 47.2 %copy-start.8 = (bf16[128,2048]{1,0:T(8,128)(2,1)S(1)}, bf16[128,2048]{1,0:T(8,128)(2,1)}, u32[]{:S(2)}) copy-start(bf16[128,2048]{1,0:T(8,128)(2,1)} %reduce-scatter.22.cloned.1.call-done) | copy-start | bytes 1572868
  601.4 85.6 %all-gather.39.cloned.1.call-start = ((), (), s32[]{:S(2)}) async-start(), calls=%async_computation.36 | async-start | bytes 6291456 | tf_op jit(solution)/shard_map/all_gather | solution.py:98
  646.9 7.6 copy-start.39
  646.9 159.2 %reduce-scatter.38.cloned.1.call-start = ((), (), s32[]{:S(2)}) async-start(), calls=%async_computation.42 | async-start | bytes 3604480 | tf_op jit(solution)/shard_map/reduce_scatter | solution.py:80
  654.4 175.2 %reduce-scatter.44.cloned.1.call-start = ((), (), s32[]{:S(2)}) async-start(), calls=%async_computation.49 | async-start | bytes 7208960
  686.5 182.4 %reduce-scatter.36.cloned.1.call-start = ((), (), s32[]{:S(2)}) async-start(), calls=%async_computation.40 | async-start | bytes 1310720 | tf_op jit(solution)/shard_map/reduce_scatter | solution.py:80
  687.0 8.4 copy-start.10
  695.4 4.6 copy-start.7
  699.9 181.5 %reduce-scatter.42.cloned.1.call-start = ((), (), s32[]{:S(2)}) async-start(), calls=%async_computation.48 | async-start | bytes 3932160
  701.3 6.7 copy-start.2
  711.6 4.6 copy-start.3
  711.6 5.0 copy-start.18
  734.0 6.7 copy-start.2
  744.4 4.8 copy-start.3
  744.4 5.0 copy-start.18
  765.7 4.0 copy-start.24
  765.7 4.0 copy-start.25
  767.2 4.6 copy-start.12
  787.1 6.3 copy-start.11
  793.4 111.8 %reduce-scatter.32.cloned.1.call-start = ((), (), s32[]{:S(2)}) async-start(), calls=%async_computation.37 | async-start | bytes 6291456 | tf_op jit(solution)/shard_map/reduce_scatter | solution.py:93
  799.8 106.1 %reduce-scatter.24.cloned.1.call-start = ((), (), s32[]{:S(2)}) async-start(), calls=%async_computation.29 | async-start | bytes 6291456 | tf_op jit(solution)/shard_map/reduce_scatter | solution.py:93
  806.0 27.3 %copy-start.30 = (f32[2048]{0:T(1024)S(1)}, f32[2048]{0:T(1024)}, u32[]{:S(2)}) copy-start(f32[2048]{0:T(1024)} %get-tuple-element.280) | copy-start | bytes 24580
  806.0 27.3 %copy-start.31 = (f32[2048]{0:T(1024)S(1)}, f32[2048]{0:T(1024)}, u32[]{:S(2)}) copy-start(f32[2048]{0:T(1024)} %get-tuple-element.287) | copy-start | bytes 24580
  806.0 123.3 %all-gather.51.cloned.1.call-start = ((), (), s32[]{:S(2)}) async-start(), calls=%async_computation.46 | async-start | bytes 3604480 | tf_op jit(solution)/shard_map/all_gather | solution.py:83
  829.7 37.1 %all-to-all-start.6 = ((bf16[4,128,1408]{2,1,0:T(8,128)(2,1)}), bf16[4,128,1408]{2,1,0:T(8,128)(2,1)S(1)}, u32[]{:S(2)}, u32[]{:S(2)}) async-start(bf16[4,128,1408]{2,1,0:T(8,128)(2,1)} %bitcast.305), calls=%async_computation.15 | async-start | bytes 2883584 | tf_op jit(solution)/shard_map/all_to_all | solution.py:59
  833.2 126.1 %reduce-scatter.40.cloned.1.call-start = ((), (), s32[]{:S(2)}) async-start(), calls=%async_computation.47 | async-start | bytes 1310720
  834.7 191.3 %all-gather.43.cloned.1.call-start = ((), (), s32[]{:S(2)}) async-start(), calls=%async_computation.41 | async-start | bytes 7208960 | tf_op jit(solution)/shard_map/all_gather | solution.py:61
  868.8 185.6 %all-gather.49.cloned.1.call-start = ((), (), s32[]{:S(2)}) async-start(), calls=%async_computation.45 | async-start | bytes 1310720 | tf_op jit(solution)/shard_map/all_gather | solution.py:83
  881.3 218.7 %all-gather.41.cloned.1.call-start = ((), (), s32[]{:S(2)}) async-start(), calls=%async_computation.39 | async-start | bytes 3932160 | tf_op jit(solution)/shard_map/all_gather | solution.py:61
  905.1 241.0 %reduce-scatter.34.cloned.1.call-start = ((), (), s32[]{:S(2)}) async-start(), calls=%async_computation.38 | async-start | bytes 2621440 | tf_op jit(solution)/shard_map/reduce_scatter | solution.py:94
  905.9 286.4 %reduce-scatter.26.cloned.1.call-start = ((), (), s32[]{:S(2)}) async-start(), calls=%async_computation.30 | async-start | bytes 2621440 | tf_op jit(solution)/shard_map/reduce_scatter | solution.py:94
  931.9 28.4 %copy-start.13 = (bf16[1024,1,256]{2,0,1:T(8,128)(2,1)S(1)}, bf16[1024,1,256]{2,0,1:T(8,128)(2,1)}, u32[]{:S(2)}) copy-start(bf16[1024,1,256]{2,0,1:T(8,128)(2,1)} %copy-done.12) | copy-start | bytes 1572868
  932.0 28.4 %copy-start.15 = (bf16[1024,1,256]{2,0,1:T(8,128)(2,1)S(1)}, bf16[1024,1,256]{2,0,1:T(8,128)(2,1)}, u32[]{:S(2)}) copy-start(bf16[1024,1,256]{2,0,1:T(8,128)(2,1)} %copy-done.14) | copy-start | bytes 1572868
  932.0 28.4 %copy-start.17 = (bf16[1024,1,256]{2,0,1:T(8,128)(2,1)S(1)}, bf16[1024,1,256]{2,0,1:T(8,128)(2,1)}, u32[]{:S(2)}) copy-start(bf16[1024,1,256]{2,0,1:T(8,128)(2,1)} %copy-done.16) | copy-start | bytes 1572868
  1057.5 88.7 %copy-start.27 = (f32[512]{0:T(512)S(1)}, f32[512]{0:T(512)}, u32[]{:S(2)}) copy-start(f32[512]{0:T(512)} %copy-done.26) | copy-start | bytes 6148
  1057.5 88.7 %copy-start.29 = (f32[512]{0:T(512)S(1)}, f32[512]{0:T(512)}, u32[]{:S(2)}) copy-start(f32[512]{0:T(512)} %copy-done.28) | copy-start | bytes 6148
  1057.5 88.7 %copy-start.33 = (f32[512]{0:T(512)S(1)}, f32[512]{0:T(512)}, u32[]{:S(2)}) copy-start(f32[512]{0:T(512)} %param.16) | copy-start | bytes 6148
  1100.0 92.4 %copy-start.1 = (bf16[512,3,1024]{2,0,1:T(8,128)(2,1)S(1)}, bf16[512,3,1024]{2,0,1:T(8,128)(2,1)}, u32[]{:S(2)}) copy-start(bf16[512,3,1024]{2,0,1:T(8,128)(2,1)} %param.18) | copy-start | bytes 9437188
  (15 other events, 25.4 us)
Sparse Core Ops, SparseCore 0:
  9.6 62.8 all-gather.20
  74.9 43.0 all-gather.44
  120.1 13.6 all-gather.22
  136.1 27.7 all-gather.24
  170.9 13.1 reduce-scatter.19
  186.3 45.1 reduce-scatter.21
  236.4 74.2 all-gather.26
  312.3 57.6 all-gather.32
  371.9 64.7 all-gather.46
  438.1 13.6 all-gather.28
  454.2 42.9 all-gather.30
  498.7 13.6 all-gather.34
  535.2 13.2 reduce-scatter.27
  550.7 45.1 reduce-scatter.29
  601.6 45.2 all-gather.36
  648.3 12.3 all-gather.38
  663.6 42.9 reduce-scatter.37
  709.9 65.8 reduce-scatter.43
  778.7 27.7 reduce-scatter.35
  809.5 43.9 reduce-scatter.41
  855.9 12.0 reduce-scatter.31
  870.8 13.3 reduce-scatter.23
  886.2 43.0 all-gather.50
  932.2 27.1 reduce-scatter.39
  961.7 64.2 all-gather.42
  1027.8 26.6 all-gather.48
  1056.1 43.8 all-gather.40
  1102.3 43.8 reduce-scatter.33
  1149.1 43.1 reduce-scatter.25

commit v2 on v1

v2 whole, which is shorter than its diff:
```python
import functools

import jax
import jax.numpy as jnp
from jax import lax
from jax.experimental import pallas as pl
from jax.experimental.pallas import tpu as pltpu
from jax.sharding import PartitionSpec as P

MODEL_WIDTH = 2048
HD = 64
ROT = 16
SEQ = 1024
EPSILON = 1e-05
ROPE_BASE = 10000.0
NEG_LARGE = -1e30
F32 = jnp.float32
BF16 = jnp.bfloat16
MESH = pl.DeviceIdType.MESH
VMEM_LIMIT = 56 * 1024 * 1024
SUBS = 4


def send(src, dst, send_sem, recv_sem, **where):
    return pltpu.make_async_remote_copy(
        src_ref=src,
        dst_ref=dst,
        send_sem=send_sem,
        recv_sem=recv_sem,
        device_id=where,
        device_id_type=MESH,
    )


def enter(cols, everyone=False):
    r, c = lax.axis_index("row"), lax.axis_index("col")
    barrier = pltpu.get_barrier_semaphore()
    pl.semaphore_signal(barrier, inc=1, device_id={"row": 1 - r}, device_id_type=MESH)
    if everyone:
        for k in range(1, cols):
            pl.semaphore_signal(
                barrier, inc=1, device_id={"col": lax.rem(c + k, cols)}, device_id_type=MESH
            )
        pl.semaphore_wait(barrier, cols)
        return

    @pl.when(c > 0)
    def _():
        pl.semaphore_signal(barrier, inc=1, device_id={"col": c - 1}, device_id_type=MESH)

    @pl.when(c < cols - 1)
    def _():
        pl.semaphore_signal(barrier, inc=1, device_id={"col": c + 1}, device_id_type=MESH)

    inner = (c > 0) & (c < cols - 1)

    @pl.when(inner)
    def _():
        pl.semaphore_wait(barrier, 3)

    @pl.when(jnp.logical_not(inner))
    def _():
        pl.semaphore_wait(barrier, 2)


class Reduce:
    def __init__(self, cols, subs, spot, part, twin, going, coming, sems, add=None):
        self.cols, self.subs, self.spot, self.add = cols, subs, spot, add
        self.part, self.twin, self.going, self.coming = part, twin, going, coming
        self.twin_send, self.twin_recv, self.send, self.recv = sems
        self.r, self.c = lax.axis_index("row"), lax.axis_index("col")
        self.half = part.shape[0] // 2

    def in_half(self, r, d, s):
        row, rows, column, columns = self.spot(d, s)
        return pl.ds(pl.multiple_of(r * self.half + row, 16), rows), pl.ds(column, columns)

    def in_twin(self, d, s):
        row, rows, column, columns = self.spot(d, s)
        return pl.ds(row, rows), pl.ds(column, columns)

    def twin_copy(self, d, s):
        return send(
            self.part.at[self.in_half(1 - self.r, d, s)],
            self.twin.at[self.in_twin(d, s)],
            self.twin_send.at[d, s],
            self.twin_recv.at[d, s],
            row=1 - self.r,
        )

    def start(self):
        order = []
        for j in range(self.cols):
            d = self.cols - 1 - j // 2 if j % 2 == 0 else j // 2
            order.append(d)
        for s in range(self.subs):
            for d in order:
                self.twin_copy(d, s).start()

    def hop(self, way, d, s):
        spot = self.in_twin(d, s)
        target = self.c + 1 if way == 0 else self.c - 1
        return send(
            self.going.at[(way,) + spot],
            self.coming.at[(way,) + spot],
            self.send.at[way, d, s],
            self.recv.at[way, d, s],
            col=target,
        )

    def own(self, d, s):
        self.twin_copy(d, s).wait_recv()
        value = self.part[self.in_half(self.r, d, s)].astype(F32)
        value = value + self.twin[self.in_twin(d, s)].astype(F32)
        if self.add is not None:
            value = value + self.add(d, s)
        return value

    def pass_on(self, way, d, s):
        spot = (way,) + self.in_twin(d, s)
        first = 0 if way == 0 else self.cols - 1

        @pl.when(self.c < d if way == 0 else self.c > d)
        def _():
            value = self.own(d, s)

            @pl.when(self.c == first)
            def _():
                self.going[spot] = value.astype(BF16)

            @pl.when(self.c != first)
            def _():
                self.hop(way, d, s).wait_recv()
                self.going[spot] = (value + self.coming[spot].astype(F32)).astype(BF16)

            self.hop(way, d, s).start()

    def relay(self, s):
        for j in range(self.cols - 1):
            self.pass_on(0, self.cols - 1 - j, s)
            self.pass_on(1, j, s)

    def land(self, s, total):
        for d in range(self.cols):

            @pl.when(self.c == d)
            def _():
                value = self.own(d, s)
                spot = self.in_twin(d, s)
                if d > 0:
                    self.hop(0, d, s).wait_recv()
                    value = value + self.coming[(0,) + spot].astype(F32)
                if d < self.cols - 1:
                    self.hop(1, d, s).wait_recv()
                    value = value + self.coming[(1,) + spot].astype(F32)
                total[...] = value

    def finish(self):
        for s in range(self.subs):
            for d in range(self.cols):
                self.twin_copy(d, s).wait_send()

                @pl.when(self.c < d)
                def _():
                    self.hop(0, d, s).wait_send()

                @pl.when(self.c > d)
                def _():
                    self.hop(1, d, s).wait_send()

    @staticmethod
    def scratch(cols, subs, half, width):
        return [
            pltpu.VMEM((half, width), BF16),
            pltpu.VMEM((2, half, width), BF16),
            pltpu.VMEM((2, half, width), BF16),
            pltpu.SemaphoreType.DMA((cols, subs)),
            pltpu.SemaphoreType.DMA((cols, subs)),
            pltpu.SemaphoreType.DMA((2, cols, subs)),
            pltpu.SemaphoreType.DMA((2, cols, subs)),
        ]


class Gather:
    def __init__(self, cols, subs, spot, whole, sems, pair=True):
        self.cols, self.subs, self.spot, self.whole, self.pair = cols, subs, spot, whole, pair
        self.send, self.recv, self.pair_send, self.pair_recv = sems
        self.r, self.c = lax.axis_index("row"), lax.axis_index("col")

    def hop(self, way, source, s):
        where = self.whole.at[self.spot(self.r, source, s)]
        return send(
            where,
            where,
            self.send.at[way, source, s],
            self.recv.at[way, source, s],
            col=self.c + 1 if way == 0 else self.c - 1,
        )

    def across(self, r, source, s):
        where = self.whole.at[self.spot(r, source, s)]
        return send(
            where, where, self.pair_send.at[source, s], self.pair_recv.at[source, s], row=1 - self.r
        )

    def start(self, s):
        @pl.when(self.c < self.cols - 1)
        def _():
            self.hop(0, self.c, s).start()

        @pl.when(self.c > 0)
        def _():
            self.hop(1, self.c, s).start()

        if self.pair:
            self.across(self.r, self.c, s).start()

    def relay(self, s):
        for k in range(1, self.cols):

            @pl.when(self.c >= k)
            def _():
                self.hop(0, self.c - k, s).wait_recv()

                @pl.when(self.c < self.cols - 1)
                def _():
                    self.hop(0, self.c - k, s).start()

                if self.pair:
                    self.across(self.r, self.c - k, s).start()

            @pl.when(self.c + k < self.cols)
            def _():
                self.hop(1, self.c + k, s).wait_recv()

                @pl.when(self.c > 0)
                def _():
                    self.hop(1, self.c + k, s).start()

                if self.pair:
                    self.across(self.r, self.c + k, s).start()

    def finish(self):
        for s in range(self.subs):
            for source in range(self.cols):
                if self.pair:
                    self.across(1 - self.r, source, s).wait_recv()
                    self.across(self.r, source, s).wait_send()

                @pl.when((self.c >= source) & (self.c < self.cols - 1))
                def _():
                    self.hop(0, source, s).wait_send()

                @pl.when((self.c <= source) & (self.c > 0))
                def _():
                    self.hop(1, source, s).wait_send()

    @staticmethod
    def scratch(cols, subs):
        return [
            pltpu.SemaphoreType.DMA((2, cols, subs)),
            pltpu.SemaphoreType.DMA((2, cols, subs)),
            pltpu.SemaphoreType.DMA((cols, subs)),
            pltpu.SemaphoreType.DMA((cols, subs)),
        ]


def moments(rows):
    mean = jnp.mean(rows, axis=1, keepdims=True)
    centered = rows - mean
    return centered, lax.rsqrt(jnp.mean(centered * centered, axis=1, keepdims=True) + EPSILON)


def params(number):
    return pltpu.CompilerParams(
        collective_id=number, has_side_effects=True, vmem_limit_bytes=VMEM_LIMIT
    )


VM = pl.BlockSpec(memory_space=pltpu.VMEM)


def row_spot(own, step, half, width):
    def spot(r, source, s):
        return pl.ds(pl.multiple_of(r * half + source * own + s * step, 16), step), pl.ds(0, width)

    return spot


def norm_two_kernel(cols, part, tokens_own, vectors, normed, middle, *scratch):
    half, width = part.shape[0] // 2, part.shape[1]
    own = half // cols
    step = own // SUBS
    total = scratch[11]
    enter(cols)
    summing = Reduce(
        cols, SUBS, lambda d, s: (d * own + s * step, step, 0, width), part, *scratch[:3], scratch[3:7]
    )
    spread = Gather(cols, SUBS, row_spot(own, step, half, width), normed, scratch[7:11])
    summing.start()
    for s in range(SUBS):
        summing.relay(s)
        if s > 0:
            spread.relay(s - 1)
        summing.land(s, total)
        rows = pl.ds(s * step, step)
        state = tokens_own[rows, :].astype(F32) + total[...]
        middle[rows, :] = state
        centered, rstd = moments(state)
        result = centered * rstd * vectors[2:3, :] + vectors[3:4, :]
        normed[spread.spot(spread.r, spread.c, s)] = result.astype(BF16)
        spread.start(s)
    spread.relay(SUBS - 1)
    spread.finish()
    summing.finish()


def norm_two(cols, part, tokens_own, vectors):
    group, width = part.shape
    return pl.pallas_call(
        functools.partial(norm_two_kernel, cols),
        out_shape=(
            jax.ShapeDtypeStruct((group, width), BF16),
            jax.ShapeDtypeStruct(tokens_own.shape, F32),
        ),
        in_specs=[VM] * 3,
        out_specs=(VM, VM),
        scratch_shapes=Reduce.scratch(cols, SUBS, group // 2, width)
        + Gather.scratch(cols, SUBS)
        + [pltpu.VMEM((group // 2 // cols // SUBS, width), F32)],
        compiler_params=params(2),
        name="out_sum_norm_gather",
    )(part, tokens_own, vectors)


def norm_two_back_kernel(cols, part, middle, cotan_own, vectors, grads, sums, *scratch):
    half, width = part.shape[0] // 2, part.shape[1]
    own = half // cols
    step = own // SUBS
    total = scratch[11]
    enter(cols)
    summing = Reduce(
        cols, SUBS, lambda d, s: (d * own + s * step, step, 0, width), part, *scratch[:3], scratch[3:7]
    )
    spread = Gather(cols, SUBS, row_spot(own, step, half, width), grads, scratch[7:11])
    summing.start()
    sums[...] = jnp.zeros_like(sums)
    for s in range(SUBS):
        summing.relay(s)
        if s > 0:
            spread.relay(s - 1)
        summing.land(s, total)
        rows = pl.ds(s * step, step)
        centered, rstd = moments(middle[rows, :])
        xhat = centered * rstd
        grad = total[...]
        sums[0:1, :] += jnp.sum(grad * xhat, axis=0, keepdims=True)
        sums[1:2, :] += jnp.sum(grad, axis=0, keepdims=True)
        scaled = grad * vectors[2:3, :]
        inner = (
            scaled
            - jnp.mean(scaled, axis=1, keepdims=True)
            - xhat * jnp.mean(scaled * xhat, axis=1, keepdims=True)
        )
        result = cotan_own[rows, :].astype(F32) + rstd * inner
        grads[spread.spot(spread.r, spread.c, s)] = result.astype(BF16)
        spread.start(s)
    spread.relay(SUBS - 1)
    spread.finish()
    summing.finish()


def norm_two_back(cols, part, middle, cotan_own, vectors):
    group, width = part.shape
    return pl.pallas_call(
        functools.partial(norm_two_back_kernel, cols),
        out_shape=(
            jax.ShapeDtypeStruct((group, width), BF16),
            jax.ShapeDtypeStruct((8, width), F32),
        ),
        in_specs=[VM] * 4,
        out_specs=(VM, VM),
        scratch_shapes=Reduce.scratch(cols, SUBS, group // 2, width)
        + Gather.scratch(cols, SUBS)
        + [pltpu.VMEM((group // 2 // cols // SUBS, width), F32)],
        compiler_params=params(3),
        name="grad_sum_norm_gather",
    )(part, middle, cotan_own, vectors)


def mixed_kernel(cols, part, middle, mixed, *scratch):
    half, width = part.shape[0] // 2, part.shape[1]
    step, depth = half // cols, width // cols
    total = scratch[7]
    enter(cols)
    c = lax.axis_index("col")

    def add(d, s):
        return jnp.where(c == s, middle[:, d * depth : (d + 1) * depth], 0.0)

    summing = Reduce(
        cols,
        cols,
        lambda d, s: (s * step, step, d * depth, depth),
        part,
        *scratch[:3],
        scratch[3:7],
        add=add,
    )
    summing.start()
    for s in range(cols):
        summing.relay(s)
        summing.land(s, total)
        mixed[s * step : (s + 1) * step, :] = total[...].astype(BF16)
    summing.finish()


def sum_mixed(cols, part, middle):
    group, width = part.shape
    return pl.pallas_call(
        functools.partial(mixed_kernel, cols),
        out_shape=jax.ShapeDtypeStruct((group // 2, width // cols), BF16),
        in_specs=[VM] * 2,
        out_specs=VM,
        scratch_shapes=Reduce.scratch(cols, cols, group // 2, width)
        + [pltpu.VMEM((group // 2 // cols, width // cols), F32)],
        compiler_params=params(4),
        name="mixed_sum",
    )(part, middle)


def first_kernel(cols, part, xhat, rstd, gain, grad_middle, result, sums, *scratch):
    half, width = part.shape[0] // 2, part.shape[1]
    step, depth = half // cols, width // cols
    total, grad, mine, theirs, out_sem, in_sem = scratch[7:]
    enter(cols, everyone=True)
    c = lax.axis_index("col")
    summing = Reduce(
        cols,
        cols,
        lambda d, s: (s * step, step, d * depth, depth),
        part,
        *scratch[:3],
        scratch[3:7],
    )
    summing.start()
    sums[...] = jnp.zeros_like(sums)
    lanes = lax.broadcasted_iota(jnp.int32, (step, 128), 1)
    for s in range(cols):
        rows = slice(s * step, (s + 1) * step)
        summing.relay(s)
        summing.land(s, total)
        grad[rows, :] = total[...]
        standard = xhat[rows, :]
        sums[0:1, :] += jnp.sum(total[...] * standard, axis=0, keepdims=True)
        sums[1:2, :] += jnp.sum(total[...], axis=0, keepdims=True)
        scaled = total[...] * gain[0:1, :]
        one = jnp.sum(scaled, axis=1, keepdims=True)
        two = jnp.sum(scaled * standard, axis=1, keepdims=True)
        both = jnp.where(lanes == 0, one, jnp.where(lanes == 1, two, 0.0))
        mine[:, rows] = both.T[0:8, :]

    def exchange(k):
        return send(
            mine, theirs.at[k - 1], out_sem.at[k - 1], in_sem.at[k - 1], col=lax.rem(c + k, cols)
        )

    for k in range(1, cols):
        exchange(k).start()
    for k in range(1, cols):
        exchange(k).wait_recv()
    for s in range(cols):
        rows = slice(s * step, (s + 1) * step)
        both = mine[:, rows]
        for k in range(1, cols):
            both = both + theirs[k - 1, :, rows]
        both = jnp.concatenate([both, jnp.zeros((120, step), F32)], axis=0).T / (depth * cols)
        scaled = grad[rows, :] * gain[0:1, :]
        inner = scaled - both[:, 0:1] - xhat[rows, :] * both[:, 1:2]
        result[rows, :] = grad_middle[rows, :].astype(F32) + rstd[rows, 0:1] * inner
    for k in range(1, cols):
        exchange(k).wait_send()
    summing.finish()


def sum_first(cols, part, xhat, rstd, gain, grad_middle):
    group, width = part.shape
    half, depth = group // 2, width // cols
    return pl.pallas_call(
        functools.partial(first_kernel, cols),
        out_shape=(
            jax.ShapeDtypeStruct((half, depth), F32),
            jax.ShapeDtypeStruct((8, depth), F32),
        ),
        in_specs=[VM] * 5,
        out_specs=(VM, VM),
        scratch_shapes=Reduce.scratch(cols, cols, half, width)
        + [
            pltpu.VMEM((half // cols, depth), F32),
            pltpu.VMEM((half, depth), F32),
            pltpu.VMEM((8, half), F32),
            pltpu.VMEM((cols - 1, 8, half), F32),
            pltpu.SemaphoreType.DMA((cols - 1,)),
            pltpu.SemaphoreType.DMA((cols - 1,)),
        ],
        compiler_params=params(5),
        name="input_grad_sum",
    )(part, xhat, rstd, gain, grad_middle)


def norm_one_kernel(cols, tokens, vector, normed, tokens_own, xhat, rstd, vectors, *scratch):
    half, depth = tokens.shape
    width = depth * cols
    step = half // cols
    full = scratch[0]
    enter(cols)
    r, c = lax.axis_index("row"), lax.axis_index("col")

    def columns(source):
        return pl.ds(pl.multiple_of(source * depth, 128), depth)

    names = Gather(
        cols, 1, lambda r, source, s: (pl.ds(0, 8), columns(source)), vectors, scratch[1:5], pair=False
    )
    spread = Gather(
        cols,
        cols,
        lambda r, source, s: (pl.ds(s * step, step), columns(source)),
        full,
        scratch[5:9],
        pair=False,
    )
    pair_send, pair_recv = scratch[9:11]
    vectors[:, columns(c)] = vector[...]
    names.start(0)
    for s in range(cols):
        rows = pl.ds(s * step, step)
        full[rows, columns(c)] = tokens[rows, :]
        spread.start(s)

    def across(r, s):
        where = normed.at[pl.ds(pl.multiple_of(r * half + s * step, 16), step), :]
        return send(
            where,
            where,
            pair_send.at[s],
            pair_recv.at[s],
            row=1 - lax.axis_index("row"),
        )

    names.relay(0)
    for s in range(cols):
        spread.relay(s)
        rows = slice(s * step, (s + 1) * step)
        state = full[rows, :].astype(F32)
        centered, inverse = moments(state)
        standard = centered * inverse
        out = standard * vectors[0:1, :] + vectors[1:2, :]
        normed[pl.ds(pl.multiple_of(r * half + s * step, 16), step), :] = out.astype(BF16)
        across(r, s).start()
        rstd[rows, :] = jnp.broadcast_to(inverse, (step, 128))
        mean = jnp.mean(state, axis=1, keepdims=True)
        xhat[rows, :] = (tokens[rows, :].astype(F32) - mean) * inverse

        @pl.when(c == s)
        def _():
            tokens_own[...] = full[rows, :]

    for s in range(cols):
        across(1 - r, s).wait_recv()
        across(r, s).wait_send()
    names.finish()
    spread.finish()


def norm_one(cols, tokens, vector):
    half, depth = tokens.shape
    width = depth * cols
    return pl.pallas_call(
        functools.partial(norm_one_kernel, cols),
        out_shape=(
            jax.ShapeDtypeStruct((2 * half, width), BF16),
            jax.ShapeDtypeStruct((half // cols, width), BF16),
            jax.ShapeDtypeStruct((half, depth), F32),
            jax.ShapeDtypeStruct((half, 128), F32),
            jax.ShapeDtypeStruct((8, width), F32),
        ),
        in_specs=[VM] * 2,
        out_specs=(VM,) * 5,
        scratch_shapes=[pltpu.VMEM((half, width), BF16)]
        + Gather.scratch(cols, 1)
        + Gather.scratch(cols, cols)
        + [pltpu.SemaphoreType.DMA((cols,)), pltpu.SemaphoreType.DMA((cols,))],
        compiler_params=params(1),
        name="gather_norm_one",
    )(tokens, vector)


def rope_tables(length):
    half_rot = ROT // 2
    lane = jnp.arange(2 * HD) % HD
    inverse = ROPE_BASE ** (-2.0 * (lane % half_rot).astype(F32) / ROT)
    angles = jnp.arange(length).astype(F32)[:, None] * inverse[None, :]
    turning = lane < ROT
    cosine = jnp.where(turning, jnp.cos(angles), 1.0)
    sine = jnp.where(turning, jnp.sin(angles), 0.0)
    lower = jnp.where(lane < half_rot, -sine, 0.0)
    upper = jnp.where(lane >= half_rot, sine, 0.0)
    return jnp.stack([cosine, lower, upper])


def turn(x, tables, back=False):
    half_rot = ROT // 2
    width = x.shape[1]
    sines = pltpu.roll(x, width - half_rot, 1) * tables[1] + pltpu.roll(x, half_rot, 1) * tables[2]
    return x * tables[0] - sines if back else x * tables[0] + sines


def dot_nt(a, b):
    return lax.dot_general(a, b, (((1,), (1,)), ((), ())), preferred_element_type=F32)


def dot_tn(a, b):
    return lax.dot_general(a, b, (((0,), (0,)), ((), ())), preferred_element_type=F32)


def dot_nn(a, b):
    return jnp.dot(a, b, preferred_element_type=F32)


BLOCK = 256


def causal(rows):
    return lax.broadcasted_iota(jnp.int32, (rows, rows), 0) >= lax.broadcasted_iota(
        jnp.int32, (rows, rows), 1
    )


def attend_kernel(qkv, bias, tables, heads_in, attn, logs):
    length, wide = attn.shape
    two = 2 * HD
    first_head = lax.broadcasted_iota(jnp.int32, (BLOCK, two), 1) < HD

    @pl.loop(0, wide // two)
    def _(pair):
        def lanes(k):
            return pl.ds(pl.multiple_of(k * wide + pair * two, two), two)

        for k in range(3):
            x = qkv[:, lanes(k)] + bias[0:1, lanes(k)]
            if k < 2:
                x = turn(x, tables)
            if k == 0:
                x = x * HD ** (-0.5)
            heads_in[:, lanes(k)] = x.astype(BF16)
        for i in range(length // BLOCK):
            keep = (i + 1) * BLOCK
            rows = slice(i * BLOCK, keep)
            query = heads_in[rows, lanes(0)]
            keys = heads_in[0:keep, lanes(1)]
            values = heads_in[0:keep, lanes(2)]
            outs = []
            for h in range(2):
                mine = first_head if h == 0 else ~first_head
                scores = dot_nt(jnp.where(mine, query, jnp.zeros_like(query)), keys)
                last = jnp.where(causal(BLOCK), scores[:, i * BLOCK :], NEG_LARGE)
                scores = last if i == 0 else jnp.concatenate([scores[:, : i * BLOCK], last], axis=1)
                top = jnp.max(scores, axis=1, keepdims=True)
                expo = jnp.exp(scores - top)
                total = jnp.sum(expo, axis=1, keepdims=True)
                probs = (expo * (1.0 / total)).astype(BF16)
                outs.append(dot_nn(probs, values))
                logs[pair, h, rows, :] = jnp.broadcast_to(top + jnp.log(total), (BLOCK, 128))
            attn[rows, pl.ds(pl.multiple_of(pair * two, two), two)] = jnp.where(
                first_head, outs[0], outs[1]
            ).astype(BF16)


def attend(qkv, bias, tables):
    length, wide = qkv.shape[0], qkv.shape[1] // 3
    return pl.pallas_call(
        attend_kernel,
        out_shape=(
            jax.ShapeDtypeStruct(qkv.shape, BF16),
            jax.ShapeDtypeStruct((length, wide), BF16),
            jax.ShapeDtypeStruct((wide // (2 * HD), 2, length, 128), F32),
        ),
        in_specs=[VM] * 3,
        out_specs=(VM,) * 3,
        compiler_params=pltpu.CompilerParams(vmem_limit_bytes=VMEM_LIMIT),
        cost_estimate=pl.CostEstimate(flops=8 * 10**9, bytes_accessed=10**7, transcendentals=4 * 10**6),
        name="attention",
    )(qkv, bias, tables)


def attend_back_kernel(heads_in, logs, grad, tables, result, sums, queries_grad, keys_grad, values_grad):
    length, wide = grad.shape
    two = 2 * HD
    first_head = lax.broadcasted_iota(jnp.int32, (BLOCK, two), 1) < HD

    @pl.loop(0, wide // two)
    def _(pair):
        def lanes(k):
            return pl.ds(pl.multiple_of(k * wide + pair * two, two), two)

        keys_grad[...] = jnp.zeros_like(keys_grad)
        values_grad[...] = jnp.zeros_like(values_grad)
        for i in range(length // BLOCK):
            keep = (i + 1) * BLOCK
            rows = slice(i * BLOCK, keep)
            query = heads_in[rows, lanes(0)]
            keys = heads_in[0:keep, lanes(1)]
            values = heads_in[0:keep, lanes(2)]
            out_grad = grad[rows, lanes(0)]
            outs = []
            for h in range(2):
                mine = first_head if h == 0 else ~first_head
                query_h = jnp.where(mine, query, jnp.zeros_like(query))
                grad_h = jnp.where(mine, out_grad, jnp.zeros_like(out_grad))
                scores = dot_nt(query_h, keys)
                probs = jnp.exp(scores - logs[pair, h, rows, 0:1])
                last = jnp.where(causal(BLOCK), probs[:, i * BLOCK :], 0.0)
                probs = last if i == 0 else jnp.concatenate([probs[:, : i * BLOCK], last], axis=1)
                probs_grad = dot_nt(grad_h, values)
                delta = jnp.sum(probs * probs_grad, axis=1, keepdims=True)
                scores_grad = (probs * (probs_grad - delta)).astype(BF16)
                outs.append(dot_nn(scores_grad, keys))
                keys_grad[0:keep, :] += dot_tn(scores_grad, query_h)
                values_grad[0:keep, :] += dot_tn(probs.astype(BF16), grad_h)
            queries_grad[rows, :] = jnp.where(first_head, outs[0], outs[1]) * HD ** (-0.5)
        grads = (
            turn(queries_grad[...], tables, back=True),
            turn(keys_grad[...], tables, back=True),
            values_grad[...],
        )
        for k in range(3):
            low = grads[k].astype(BF16)
            result[:, lanes(k)] = low
            total = jnp.sum(low.astype(F32), axis=0, keepdims=True)
            sums[:, lanes(k)] = jnp.broadcast_to(total, (8, two))


def attend_back(heads_in, logs, grad, tables):
    length, wide = grad.shape
    return pl.pallas_call(
        attend_back_kernel,
        out_shape=(
            jax.ShapeDtypeStruct(heads_in.shape, BF16),
            jax.ShapeDtypeStruct((8, 3 * wide), F32),
        ),
        in_specs=[VM] * 4,
        out_specs=(VM,) * 2,
        scratch_shapes=[pltpu.VMEM((length, 2 * HD), F32)] * 3,
        compiler_params=pltpu.CompilerParams(vmem_limit_bytes=VMEM_LIMIT),
        cost_estimate=pl.CostEstimate(flops=20 * 10**9, bytes_accessed=10**7, transcendentals=4 * 10**6),
        name="attention_back",
    )(heads_in, logs, grad, tables)


def dot(spec, a, b):
    return jnp.einsum(spec, a, b, preferred_element_type=F32)


def columns_piece(block, sizes):
    dp, col = sizes["dp"], sizes["col"]
    depth, k, wide = block.shape
    part = depth // dp
    piece = lax.dynamic_slice_in_dim(block, lax.axis_index("dp") * part, part, 0)
    piece = piece.reshape(part, k, col, wide // col).transpose(2, 0, 1, 3)
    return piece.reshape(col, part, k * wide // col)


def columns_whole(piece, sizes):
    whole = lax.all_gather(piece, "dp", axis=0)
    return whole.transpose(1, 0, 2, 3).reshape(-1, piece.shape[-1])


def rows_piece(block, sizes):
    dp, col = sizes["dp"], sizes["col"]
    tall, depth = block.shape
    return lax.dynamic_index_in_dim(
        block.reshape(col, dp, tall // col // dp, depth), lax.axis_index("dp"), 1, False
    )


def rows_whole(piece, sizes):
    col, part, depth = piece.shape
    return lax.all_gather(
        piece.transpose(1, 0, 2).reshape(part, col * depth), "dp", axis=0, tiled=True
    )


def exchange(pieces):
    return lax.all_to_all(pieces, "col", 0, 0, tiled=True)


def exchange_later(pieces, cols):
    me = lax.axis_index("col")
    out = jnp.zeros_like(pieces)
    out = lax.dynamic_update_index_in_dim(
        out, lax.dynamic_index_in_dim(pieces, me, 0, True), me, 0
    )
    for k in range(1, cols):
        going = lax.dynamic_index_in_dim(pieces, lax.rem(me + k, cols), 0, True)
        coming = lax.ppermute(going, "col", [(i, (i + k) % cols) for i in range(cols)])
        out = lax.dynamic_update_index_in_dim(out, coming, lax.rem(me + cols - k, cols), 0)
    return out


def columns_sum(grad, sizes):
    dp, col = sizes["dp"], sizes["col"]
    width, narrow = grad.shape
    part = width // col // dp
    pieces = grad.astype(BF16).reshape(col, dp, part, narrow).transpose(1, 0, 2, 3)
    piece = lax.psum_scatter(
        pieces.reshape(width, narrow), "dp", scatter_dimension=0, tiled=True
    )
    return piece.reshape(col, part, narrow)


def columns_return(piece, k):
    col, part, narrow = piece.shape
    piece = piece.reshape(col, part, k, narrow // k).transpose(1, 2, 0, 3)
    piece = piece.reshape(part, k, col * narrow // k)
    return lax.all_gather(piece, "dp", axis=0, tiled=True).astype(F32)


def rows_sum(grad, sizes):
    dp, col = sizes["dp"], sizes["col"]
    short, width = grad.shape
    piece = lax.psum_scatter(grad.astype(BF16), "dp", scatter_dimension=0, tiled=True)
    return piece.reshape(short // dp, col, width // col).transpose(1, 0, 2)


def rows_return(piece):
    col, part, depth = piece.shape
    whole = lax.all_gather(piece, "dp", axis=0)
    return whole.transpose(1, 0, 2, 3).reshape(-1, depth).astype(F32)


def line_gather(block, cols):
    me = lax.axis_index("col")
    right, left = [block], [block]
    for k in range(1, cols):
        right.append(lax.ppermute(right[-1], "col", [(i, i + 1) for i in range(k - 1, cols - 1)]))
        left.append(lax.ppermute(left[-1], "col", [(i + 1, i) for i in range(cols - k)]))
    depth = block.shape[1]
    out = jnp.zeros((block.shape[0], cols * depth), block.dtype)
    for k in range(cols):
        source = lax.rem(me + cols - k, cols)
        value = block if k == 0 else jnp.where(me >= k, right[k], left[cols - k])
        out = lax.dynamic_update_slice_in_dim(out, value, source * depth, 1)
    return out


def pair_gather(half):
    other = lax.ppermute(half, "row", [(0, 1), (1, 0)])
    first = lax.axis_index("row") == 0
    return jnp.concatenate([jnp.where(first, half, other), jnp.where(first, other, half)])


def make_body(sizes):
    cols = sizes["col"]

    def body(
        tokens,
        attention_norm_gain,
        attention_norm_bias,
        qkv_weight,
        qkv_bias,
        out_weight,
        feedforward_norm_gain,
        feedforward_norm_bias,
        gate_up_weight,
        down_weight,
        cotangent,
    ):
        my_row, my_col, my_dp = (lax.axis_index(name) for name in ("row", "col", "dp"))
        half, depth = tokens.shape
        own = half // cols
        heads_wide = qkv_bias.shape[1]
        tables = rope_tables(SEQ)
        vector = jnp.stack(
            [attention_norm_gain, attention_norm_bias, feedforward_norm_gain, feedforward_norm_bias]
        )
        vector = jnp.concatenate([vector, jnp.zeros_like(vector)])
        qkv_piece = exchange(columns_piece(qkv_weight, sizes))
        out_piece = exchange(rows_piece(out_weight, sizes))
        qkv_w = columns_whole(qkv_piece, sizes)
        out_w = rows_whole(out_piece, sizes)
        tokens, qkv_piece = lax.optimization_barrier((tokens, qkv_piece))
        normed_one, tokens_own, xhat_one, rstd_one, vectors = norm_one(cols, tokens, vector)
        gate_up_block, down_block, cotan_block, normed_one = lax.optimization_barrier(
            (gate_up_weight, down_weight, cotangent, normed_one)
        )
        gate_up_w = columns_whole(exchange_later(columns_piece(gate_up_block, sizes), cols), sizes)
        down_w = rows_whole(exchange_later(rows_piece(down_block, sizes), cols), sizes)
        cotan_half = line_gather(cotan_block, cols)
        cotan_rows = pair_gather(cotan_half)
        cotan_own = lax.dynamic_slice_in_dim(cotan_half, my_col * own, own, 0)

        qkv = dot_nn(normed_one, qkv_w)
        heads_in, attn, logs = attend(qkv, qkv_bias.reshape(1, -1), tables)
        normed_two, middle = norm_two(cols, dot_nn(attn, out_w).astype(BF16), tokens_own, vectors)

        gate_up = dot_nn(normed_two, gate_up_w)
        wide = gate_up.shape[1] // 2
        gate, up = gate_up[:, :wide], gate_up[:, wide:]
        sig = jax.nn.sigmoid(gate)
        hidden = (gate * sig * up).astype(BF16)
        grad_hidden = dot_nt(cotan_rows, down_w)
        grad_gu = jnp.concatenate(
            [grad_hidden * up * sig * (1.0 + gate * (1.0 - sig)), grad_hidden * gate * sig], axis=1
        ).astype(BF16)
        grad_middle, second = norm_two_back(
            cols, dot_nt(grad_gu, gate_up_w).astype(BF16), middle, cotan_own, vectors
        )
        mixed = sum_mixed(cols, dot_nn(hidden, down_w).astype(BF16), middle)
        down_piece = exchange_later(rows_sum(dot_tn(hidden, cotan_rows), sizes), cols)
        gate_up_piece = exchange_later(columns_sum(dot_tn(normed_two, grad_gu), sizes), cols)
        out_piece = exchange_later(rows_sum(dot_tn(attn, grad_middle), sizes), cols)
        grad_attn = dot_nt(grad_middle, out_w).astype(BF16)
        grad_qkv, bias_part = attend_back(heads_in, logs, grad_attn, tables)
        qkv_piece = exchange_later(columns_sum(dot_tn(normed_one, grad_qkv), sizes), cols)
        grad_block = lax.dynamic_slice(grad_middle, (my_row * half, my_col * depth), (half, depth))
        input_grad, first = sum_first(
            cols,
            dot_nt(grad_qkv, qkv_w).astype(BF16),
            xhat_one,
            rstd_one,
            attention_norm_gain.reshape(1, -1),
            grad_block,
        )
        mine = jnp.zeros((4, cols * depth), F32)
        mine = lax.dynamic_update_slice(mine, first[:2], (0, my_col * depth))
        mine = lax.dynamic_update_slice(mine, second[:2], (2, 0))
        biases = jnp.zeros((sizes["row"] * cols, 3 * heads_wide), F32)
        biases = lax.dynamic_update_slice(biases, bias_part[:1], (my_row * cols + my_col, 0))
        small = lax.psum(
            jnp.concatenate([mine.reshape(-1), biases.reshape(-1)]), ("dp", "row", "col")
        )
        norms = lax.dynamic_slice_in_dim(
            small[: mine.size].reshape(mine.shape), my_col * depth, depth, 1
        )
        bias = lax.dynamic_index_in_dim(
            small[mine.size :].reshape(biases.shape), my_row * cols + my_col, 0, False
        ).reshape(3, heads_wide)
        return (
            mixed,
            input_grad,
            norms[0],
            norms[1],
            columns_return(qkv_piece, 3),
            bias,
            rows_return(out_piece),
            norms[2],
            norms[3],
            columns_return(gate_up_piece, 2),
            rows_return(down_piece),
        )

    return body


def solution(mesh):
    specs = (
        P(("dp", "row"), "col"),
        P("col"),
        P("col"),
        P("col", None, "row"),
        P(None, ("row", "col")),
        P("row", "col"),
        P("col"),
        P("col"),
        P("col", None, "row"),
        P("row", "col"),
    )
    return jax.shard_map(
        make_body(dict(mesh.shape)),
        mesh=mesh,
        in_specs=specs + (P(("dp", "row"), "col"),),
        out_specs=(P(("dp", "row"), "col"),) + specs,
        check_vma=False,
    )
```

time: 1210 us -> 1020 us (0.84)
  Pallas kernels: 0 us -> 474 us
  waiting for transfers between devices: 569 us -> 196 us
  blocking collectives: 254 us -> 66.2 us
  local copies, waits for them, and re-layouts: 164 us -> 110 us
  matrix products: 135 us -> 83.8 us
  starting transfers between devices: 9.12 us -> 48.8 us
  other arithmetic: 52.6 us -> 19.7 us
    pallas_call x0 -> x7, Pallas kernels: none -> 474 us  [the longest x1 123 us: norm_two(): pl.pallas_call(functools.partial(norm_two_kernel, cols), out_shape=(jax.S...]
    all_gather x16 -> x8, waiting for transfers between devices: 331 us -> 0.03 us  [the longest x2 0.02 us: columns_whole(): whole = lax.all_gather(piece, 'dp', axis=0)]
    all_to_all x6 -> x1, blocking collectives: 208 us -> 26.4 us  [exchange(): return lax.all_to_all(pieces, 'col', 0, 0, tiled=True)]
    ppermute x0 -> x25, waiting for transfers between devices: none -> 102 us  [the longest x18 68.8 us: exchange_later(): lax.ppermute(going, 'col', [(i, (i + k) % cols) for i in range(cols)])]
    reduce_scatter x10 -> x4, waiting for transfers between devices: 170 us -> 86.6 us  [the longest x2 77.3 us: columns_sum(): lax.psum_scatter(pieces.reshape(width, narrow), 'dp', scatter_dimension=0...]
    dot_general x26 -> x12, matrix products: 135 us -> 83.8 us  [the longest x4 29.3 us: dot_nt(): lax.dot_general(a, b, (((1,), (1,)), ((), ())), preferred_element_type=F32)]
    ppermute x0 -> x25, starting transfers between devices: none -> 44.1 us  [the longest x18 28.1 us: exchange_later(): lax.ppermute(going, 'col', [(i, (i + k) % cols) for i in range(cols)])]
    reshape x11 -> x8, local copies, waits for them, and re-layouts: 50 us -> 9.73 us  [the longest x2 5.04 us: columns_sum(): grad.astype(BF16).reshape(col, dp, part, narrow).transpose(1, 0, 2, 3)]
  transfers between devices with their start and end apart: 31 -> 38, of which waited for: 21 -> 17; matrix products, arithmetic and copies ran while one was open for 25% -> 16% of each run, Pallas kernels for 0% -> 36%
where the time goes in v2:
time: 1020 us; the launch traced here: 1010 us
  Pallas kernels  474 us (46%)
  waiting for transfers between devices  196 us (19%)
  local copies, waits for them, and re-layouts  110 us (11%)
  matrix products  83.8 us (8%)
  blocking collectives  66.2 us (6%)
  starting transfers between devices  48.8 us (5%)
  other arithmetic  19.7 us (2%)
  between operations  15.5 us (2%)
    pallas_call x1, Pallas kernels, norm_two(): pl.pallas_call(functools.partial(norm_two_kernel, cols), out_shape=(jax.S...  123 us
    pallas_call x1, Pallas kernels, norm_two_back(): pl.pallas_call(functools.partial(norm_two_back_kernel, cols), out_shape=(...  109 us
    pallas_call x1, Pallas kernels, sum_first(): pl.pallas_call(functools.partial(first_kernel, cols), out_shape=(jax.Shap...  89.7 us
    reduce_scatter x2, waiting for transfers between devices, columns_sum(): lax.psum_scatter(pieces.reshape(width, narrow), 'dp', scatter_dimension=0...  77.3 us
    pallas_call x1, Pallas kernels, sum_mixed(): pl.pallas_call(functools.partial(mixed_kernel, cols), out_shape=jax.Shape...  76.9 us
    ppermute x18, waiting for transfers between devices, exchange_later(): lax.ppermute(going, 'col', [(i, (i + k) % cols) for i in range(cols)])  68.8 us
    pallas_call x1, Pallas kernels, norm_one(): pl.pallas_call(functools.partial(norm_one_kernel, cols), out_shape=(jax.S...  45.2 us
    unnamed x76, local copies, waits for them, and re-layouts  40.7 us
  transfers between devices with their start and end apart: 38, of which 17 were waited for; matrix products, arithmetic and copies ran while one was open for 16% of the time, Pallas kernels for 36%

profile of v2, /device:TPU:0, one launch (start us, length us, event | category | flops | bytes accessed | tf_op | source)
XLA Modules:
  0.0 1013.7 jit_solution(5176261897029720131)
XLA Ops:
  11.6 26.4 %all_to_all.10 = bf16[4,128,768]{1,2,0:T(8,128)(2,1)S(1)} all-to-all(bf16[4,128,768]{1,2,0:T(8,128)(2,1)S(1)} %bitcast.165), channel_id=1, replica_groups=mesh['dp'=4,'row'=2,'col'=4] {'col'}, dimensions={0} | all-to-all | bytes 1572864 | tf_op jit(solution)/shard_map/all_to_all | solution.py:795
  40.8 3.4 all-to-all-start.1
  45.0 7.4 all-to-all-done.1
  53.2 45.2 %gather_norm_one.1 = (bf16[1024,2048]{1,0:T(8,128)(2,1)}, bf16[128,2048]{1,0:T(8,128)(2,1)}, f32[512,512]{1,0:T(8,128)}, f32[512,128]{1,0:T(8,128)}, f32[8,2048]{1,0:T(8,128)}) custom-call(bf16[512,512]{1,0:T(8,128)(2,1)} %tokens, f32[8,512]{1,0:T(8,128)} %concatenate.13.vector), custom_call_target="tpu_custom_call" | custom-call | tf_op jit(solution)/shard_map/gather_norm_one/pallas_call | solution.py:579
  98.4 14.9 %copy.162 = bf16[512,2,2816]{0,2,1:T(8,128)(2,1)} copy(bf16[512,2,2816]{2,1,0:T(2,128)(2,1)} %param.19) | data formatting | bytes 11534336 | tf_op jit(solution)/shard_map/optimization_barrier | solution.py:894
  115.1 2.7 collective-permute-start.1
  119.3 9.1 collective-permute-done
  129.6 13.3 %collective-permute-done.1 = bf16[1,128,1408]{1,2,0:T(8,128)(2,1)} collective-permute-done((bf16[1,128,1408]{1,2,0:T(8,128)(2,1)S(1)}, bf16[1,128,1408]{1,2,0:T(8,128)(2,1)}, u32[]{:S(2)}, u32[]{:S(2)}) %collective-permute-start.1) | collective-permute-done | bytes 360480 | tf_op jit(solution)/shard_map/ppermute | solution.py:806
  148.0 9.9 collective-permute-start.6
  157.9 8.9 collective-permute-done.7
  169.6 12.1 %collective-permute-done.8 = bf16[512,512]{1,0:T(8,128)(2,1)} collective-permute-done((bf16[512,512]{1,0:T(8,128)(2,1)S(1)}, bf16[512,512]{1,0:T(8,128)(2,1)}, u32[]{:S(2)}, u32[]{:S(2)}) %collective-permute-start.8) | collective-permute-done | bytes 524320 | tf_op jit(solution)/shard_map/ppermute | solution.py:847
  184.1 11.8 %collective-permute-done.9 = bf16[512,512]{1,0:T(8,128)(2,1)} collective-permute-done((bf16[512,512]{1,0:T(8,128)(2,1)}, bf16[512,512]{1,0:T(8,128)(2,1)}, u32[]{:S(2)}, u32[]{:S(2)}) %collective-permute-start.9) | collective-permute-done | bytes 524320 | tf_op jit(solution)/shard_map/ppermute | solution.py:847
  198.6 2.1 dynamic-slice_bitcast_fusion.2
  200.7 2.9 collective-permute-start.4
  204.5 3.0 fusion.1
  208.1 2.3 pad_maximum_fusion.6.tables
  210.9 3.0 dynamic_update_slice.113
  215.2 3.0 dynamic_update_slice.114
  219.4 3.0 dynamic_update_slice.115
  223.7 3.0 dynamic_update_slice.116
  229.0 3.9 broadcast_select_fusion.1
  232.9 2.4 copy.159
  237.0 5.1 fusion.18.qkv
  242.0 13.7 %attention.1 = (bf16[1024,768]{1,0:T(8,128)(2,1)}, bf16[1024,256]{1,0:T(8,128)(2,1)}, f32[2,2,1024,128]{3,2,1,0:T(8,128)}) custom-call(f32[1024,768]{1,0:T(8,128)} %fusion.18.qkv, f32[1,768]{1,0:T(1,128)} %bitcast.187, f32[3,1024,128]{2,1,0:T(8,128)} %pad_maximum_fusion.6.tables), custom_call_target="tpu_custom_call" | custom-call | flops 8000000000 | bytes 10000000 | tf_op jit(solution)/shard_map/attention/pallas_call | solution.py:682
  255.7 4.7 convolution_convert_fusion.3.part
  260.4 123.4 %out_sum_norm_gather.1 = (bf16[1024,2048]{1,0:T(8,128)(2,1)}, f32[128,2048]{1,0:T(8,128)}) custom-call(bf16[1024,2048]{1,0:T(8,128)(2,1)} %convolution_convert_fusion.3.part, bf16[128,2048]{1,0:T(8,128)(2,1)} %get-tuple-element.36.tokens_own, f32[8,2048]{1,0:T(8,128)} %get-tuple-element.37.vectors), custom_call_target="tpu_custom_call" | custom-call | tf_op jit(solution)/shard_map/out_sum_norm_gather/pallas_call | solution.py:320
  383.9 11.8 %fusion.19 = f32[1024,1408]{1,0:T(8,128)} fusion(bf16[1024,2048]{1,0:T(8,128)(2,1)} %get-tuple-element.38, bf16[2048,1408]{1,0:T(8,128)(2,1)} %bitcast.195), kind=kOutput, calls=%fused_computation.110 | convolution fusion | flops 5905580032 | bytes 15728640 | tf_op jit(solution)/shard_map/dot_general | solution.py:628
  395.7 9.8 multiply_convert_fusion.1
  405.6 8.3 convolution_convert_fusion.1.part
  413.8 108.9 %grad_sum_norm_gather.1 = (bf16[1024,2048]{1,0:T(8,128)(2,1)}, f32[8,2048]{1,0:T(8,128)}) custom-call(bf16[1024,2048]{1,0:T(8,128)(2,1)} %convolution_convert_fusion.1.part, f32[128,2048]{1,0:T(8,128)} %get-tuple-element.41.middle, bf16[128,2048]{1,0:T(8,128)(2,1)} %constant_dynamic-slice_fusion.18.cotan_own, f32[8,2048]{1,0:T(8,128)} %get-tuple-element.37.vectors), custom_call_target="tpu_custom_call" | custom-call | tf_op jit(solution)/shard_map/grad_sum_norm_gather/pallas_call | solution.py:375
  522.7 4.4 convolution_convert_fusion.7
  527.2 6.8 convolution_convert_fusion.6
  535.3 4.3 convolution_convert_fusion.8.grad
  539.6 15.9 %attention_back.1 = (bf16[1024,768]{1,0:T(8,128)(2,1)}, f32[8,768]{1,0:T(8,128)}) custom-call(bf16[1024,768]{1,0:T(8,128)(2,1)} %get-tuple-element.42.heads_in, f32[2,2,1024,128]{3,2,1,0:T(8,128)} %get-tuple-element.43.logs, bf16[1024,256]{1,0:T(8,128)(2,1)} %convolution_convert_fusion.8.grad, f32[3,1024,128]{2,1,0:T(8,128)} %pad_maximum_fusion.6.tables), custom_call_target="tpu_custom_call" | custom-call | flops 20000000000 | bytes 10000000 | tf_op jit(solution)/shard_map/attention_back/pallas_call | solution.py:746
  555.5 5.2 convolution_convert_fusion.5
  560.7 2.0 copy.175
  565.0 10.1 convolution_convert_fusion
  575.1 3.1 copy.189
  582.2 2.1 collective-permute-start.18
  584.3 2.8 collective-permute-done.16
  587.0 1.9 collective-permute-done.17
  589.8 9.3 reduce-scatter.11.cloned.1.call-done
  599.1 2.2 reshape.455
  604.4 2.5 collective-permute-start.23
  608.4 3.7 collective-permute-done.22
  612.2 6.5 collective-permute-done.23
  619.7 27.1 %reduce-scatter.5.cloned.1.call-done = bf16[512,768]{1,0:T(8,128)(2,1)} async-done(((bf16[2048,768]{1,0:T(8,128)(2,1)}), bf16[512,768]{1,0:T(8,128)(2,1)}) %reduce-scatter.5.cloned.1.call-update) | async-done | bytes 786448 | tf_op jit(solution)/shard_map/reduce_scatter | solution.py:816
  650.2 2.5 collective-permute-start.14
  654.4 3.6 collective-permute-done.13
  658.1 7.2 collective-permute-done.14
  666.4 50.1 %reduce-scatter.9.cloned.1.call-done = bf16[512,1408]{1,0:T(8,128)(2,1)} async-done(((bf16[2048,1408]{1,0:T(8,128)(2,1)}), bf16[512,1408]{1,0:T(8,128)(2,1)}) %reduce-scatter.9.cloned.1.call-update) | async-done | bytes 1441808 | tf_op jit(solution)/shard_map/reduce_scatter | solution.py:816
  721.5 2.4 collective-permute-start.20
  725.9 6.4 collective-permute-done.19
  732.4 14.2 %collective-permute-done.20 = bf16[1,128,1408]{1,2,0:T(8,128)(2,1)S(1)} collective-permute-done((bf16[1,128,1408]{1,2,0:T(8,128)(2,1)}, bf16[1,128,1408]{1,2,0:T(8,128)(2,1)S(1)}, u32[]{:S(2)}, u32[]{:S(2)}) %collective-permute-start.20) | collective-permute-done | bytes 360480 | tf_op jit(solution)/shard_map/ppermute | solution.py:806
  750.7 6.9 convolution_convert_fusion.4.part
  757.5 89.7 %input_grad_sum.1 = (f32[512,512]{1,0:T(8,128)}, f32[8,512]{1,0:T(8,128)}) custom-call(bf16[1024,2048]{1,0:T(8,128)(2,1)} %convolution_convert_fusion.4.part, f32[512,512]{1,0:T(8,128)} %get-tuple-element.47.xhat, f32[512,128]{1,0:T(8,128)} %get-tuple-element.48.rstd, f32[1,512]{1,0:T(1,128)} %bitcast.184, bf16[512,512]{1,0:T(8,128)(2,1)} %dynamic_slice.121.grad_middle), custom_call_target="tpu_custom_call" | custom-call | tf_op jit(solution)/shard_map/input_grad_sum/pallas_call | solution.py:489
  848.9 39.9 %psum.7 = f32[14336]{0:T(1024)S(1)} all-reduce(f32[14336]{0:T(1024)S(1)} %pad_maximum_fusion.7), channel_id=1, replica_groups=mesh['dp'=4,'row'=2,'col'=4] {'dp','row','col'}, use_global_device_ids=true, to_apply=%region_0.1 | all-reduce | flops 14336 | bytes 114688 | tf_op jit(solution)/shard_map/psum | solution.py:940
  888.8 6.3 convolution_convert_fusion.2.part
  895.2 76.9 %mixed_sum.1 = bf16[512,512]{1,0:T(8,128)(2,1)} custom-call(bf16[1024,2048]{1,0:T(8,128)(2,1)} %convolution_convert_fusion.2.part, f32[128,2048]{1,0:T(8,128)} %get-tuple-element.41.middle), custom_call_target="tpu_custom_call" | custom-call | tf_op jit(solution)/shard_map/mixed_sum/pallas_call | solution.py:420
  973.4 2.8 convert_element_type.99
  976.3 5.1 convert_element_type.100
  981.4 5.4 copy.203
  986.8 15.7 %copy.204 = f32[512,2,2816]{2,1,0:T(2,128)} copy(bf16[512,2,2816]{0,2,1:T(8,128)(2,1)} %all-gather.20.cloned.1.call-done) | data formatting | bytes 17301504
  1004.4 2.3 copy.282
  (213 shorter events, 71.2 us)
Async XLA Ops:
  7.2 1.9 copy-start
  7.2 225.7 %all-gather.24.cloned.1.call-start = ((), (), s32[]{:S(2)}) async-start(), calls=%async_computation.17 | async-start | bytes 3932160 | tf_op jit(solution)/shard_map/all_gather | solution.py:775
  11.6 32.8 %copy-start.13 = (f32[512]{0:T(512)S(1)}, f32[512]{0:T(512)}, u32[]{:S(2)}) copy-start(f32[512]{0:T(512)} %param.12) | copy-start | bytes 6148
  11.6 32.8 %copy-start.15 = (f32[512]{0:T(512)S(1)}, f32[512]{0:T(512)}, u32[]{:S(2)}) copy-start(f32[512]{0:T(512)} %param.13) | copy-start | bytes 6148
  11.6 32.8 %copy-start.16 = (f32[512]{0:T(512)S(1)}, f32[512]{0:T(512)}, u32[]{:S(2)}) copy-start(f32[512]{0:T(512)} %param.17) | copy-start | bytes 6148
  11.6 32.8 %copy-start.17 = (f32[512]{0:T(512)S(1)}, f32[512]{0:T(512)}, u32[]{:S(2)}) copy-start(f32[512]{0:T(512)} %param.18) | copy-start | bytes 6148
  40.8 11.6 %all-to-all-start.1 = ((bf16[4,64,512]{2,1,0:T(8,128)(2,1)}), bf16[4,64,512]{2,1,0:T(8,128)(2,1)S(1)}, u32[]{:S(2)}, u32[]{:S(2)}) async-start(bf16[4,64,512]{2,1,0:T(8,128)(2,1)} %dynamic-slice_bitcast_fusion.1), calls=%async_computation.1 | async-start | bytes 524288 | tf_op jit(solution)/shard_map/all_to_all | solution.py:795
  44.3 211.5 %all-gather.10.cloned.1.call-start = ((), (), s32[]{:S(2)}) async-start(), calls=%async_computation.6 | async-start | bytes 1310720 | tf_op jit(solution)/shard_map/all_gather | solution.py:789
  53.2 330.7 %all-gather.12.cloned.1.call-start = ((), (), s32[]{:S(2)}) async-start(), calls=%async_computation.7 | async-start | bytes 7208960 | tf_op jit(solution)/shard_map/all_gather | solution.py:775
  115.0 13.4 %collective-permute-start = (bf16[1,128,1408]{1,2,0:T(8,128)(2,1)S(1)}, bf16[1,128,1408]{1,2,0:T(8,128)(2,1)}, u32[]{:S(2)}, u32[]{:S(2)}) collective-permute-start(bf16[1,128,1408]{1,2,0:T(8,128)(2,1)S(1)} %get-tuple-element.112), channel_id=1, source_target_pairs={{0,1},{1,2},{2,3},{3,0},{4,5},{5,6},{6,7},{7,4},{8,9},{9,10},{10,1... | collective-permute-start | bytes 1081352 | tf_op jit(solution)/shard_map/ppermute | solution.py:806
  115.1 27.8 %collective-permute-start.1 = (bf16[1,128,1408]{1,2,0:T(8,128)(2,1)S(1)}, bf16[1,128,1408]{1,2,0:T(8,128)(2,1)}, u32[]{:S(2)}, u32[]{:S(2)}) collective-permute-start(bf16[1,128,1408]{1,2,0:T(8,128)(2,1)S(1)} %get-tuple-element.111), channel_id=1, source_target_pairs={{0,2},{1,3},{2,0},{3,1},{4,6},{5,7},{6,4},{7,5},{8,10},{9,11},{10,... | collective-permute-start | bytes 1081352 | tf_op jit(solution)/shard_map/ppermute | solution.py:806
  117.8 26.3 %collective-permute-start.2 = (bf16[1,128,1408]{1,2,0:T(8,128)(2,1)S(1)}, bf16[1,128,1408]{1,2,0:T(8,128)(2,1)}, u32[]{:S(2)}, u32[]{:S(2)}) collective-permute-start(bf16[1,128,1408]{1,2,0:T(8,128)(2,1)S(1)} %get-tuple-element.110), channel_id=1, source_target_pairs={{0,3},{1,0},{2,1},{3,2},{4,7},{5,4},{6,5},{7,6},{8,11},{9,8},{10,9... | collective-permute-start | bytes 1081352 | tf_op jit(solution)/shard_map/ppermute | solution.py:806
  128.4 18.3 %copy-start.10 = (bf16[512,512]{1,0:T(8,128)(2,1)S(1)}, bf16[512,512]{1,0:T(8,128)(2,1)}, u32[]{:S(2)}) copy-start(bf16[512,512]{1,0:T(8,128)(2,1)} %param.21) | copy-start | bytes 1572868
  145.4 1.2 copy-start.2
  146.6 249.1 %all-gather.14.cloned.1.call-start = ((), (), s32[]{:S(2)}) async-start(), calls=%async_computation.8 | async-start | bytes 3604480 | tf_op jit(solution)/shard_map/all_gather | solution.py:789
  146.7 20.1 %collective-permute-start.7 = (bf16[512,512]{1,0:T(8,128)(2,1)S(1)}, bf16[512,512]{1,0:T(8,128)(2,1)S(1)}, u32[]{:S(2)}, u32[]{:S(2)}) collective-permute-start(bf16[512,512]{1,0:T(8,128)(2,1)S(1)} %copy-done.10), channel_id=1, source_target_pairs={{1,0},{2,1},{3,2},{5,4},{6,5},{7,6},{9,8},{10,9},{11,10},{13,12},{... | collective-permute-start | bytes 1572872 | tf_op jit(solution)/shard_map/ppermute | solution.py:847
  148.0 20.1 %collective-permute-start.6 = (bf16[512,512]{1,0:T(8,128)(2,1)S(1)}, bf16[512,512]{1,0:T(8,128)(2,1)}, u32[]{:S(2)}, u32[]{:S(2)}) collective-permute-start(bf16[512,512]{1,0:T(8,128)(2,1)S(1)} %copy-done.10), channel_id=1, source_target_pairs={{0,1},{1,2},{2,3},{4,5},{5,6},{6,7},{8,9},{9,10},{10,11},{12,13},{... | collective-permute-start | bytes 1572872 | tf_op jit(solution)/shard_map/ppermute | solution.py:846
  166.8 16.2 %copy-start.11 = (bf16[512,512]{1,0:T(8,128)(2,1)}, bf16[512,512]{1,0:T(8,128)(2,1)S(1)}, u32[]{:S(2)}) copy-start(bf16[512,512]{1,0:T(8,128)(2,1)S(1)} %collective-permute-done.7) | copy-start | bytes 1572868
  166.8 14.9 %collective-permute-start.8 = (bf16[512,512]{1,0:T(8,128)(2,1)S(1)}, bf16[512,512]{1,0:T(8,128)(2,1)}, u32[]{:S(2)}, u32[]{:S(2)}) collective-permute-start(bf16[512,512]{1,0:T(8,128)(2,1)S(1)} %collective-permute-done.7), channel_id=1, source_target_pairs={{1,0},{2,1},{5,4},{6,5},{9,8},{10,9},{13,12},{14,13},{17,16},{18,1... | collective-permute-start | bytes 1572872 | tf_op jit(solution)/shard_map/ppermute | solution.py:847
  168.1 15.3 %collective-permute-start.10 = (bf16[512,512]{1,0:T(8,128)(2,1)}, bf16[512,512]{1,0:T(8,128)(2,1)}, u32[]{:S(2)}, u32[]{:S(2)}) collective-permute-start(bf16[512,512]{1,0:T(8,128)(2,1)} %collective-permute-done.6), channel_id=1, source_target_pairs={{1,2},{2,3},{5,6},{6,7},{9,10},{10,11},{13,14},{14,15},{17,18},{18... | collective-permute-start | bytes 1572872 | tf_op jit(solution)/shard_map/ppermute | solution.py:846
  181.7 14.2 %collective-permute-start.9 = (bf16[512,512]{1,0:T(8,128)(2,1)}, bf16[512,512]{1,0:T(8,128)(2,1)}, u32[]{:S(2)}, u32[]{:S(2)}) collective-permute-start(bf16[512,512]{1,0:T(8,128)(2,1)} %collective-permute-done.8), channel_id=1, source_target_pairs={{1,0},{5,4},{9,8},{13,12},{17,16},{21,20},{25,24},{29,28}} | collective-permute-start | bytes 1572872 | tf_op jit(solution)/shard_map/ppermute | solution.py:847
  183.0 15.3 %copy-start.12 = (bf16[512,512]{1,0:T(8,128)(2,1)S(1)}, bf16[512,512]{1,0:T(8,128)(2,1)}, u32[]{:S(2)}) copy-start(bf16[512,512]{1,0:T(8,128)(2,1)} %copy-done.11) | copy-start | bytes 1572868
  183.4 14.9 %collective-permute-start.11 = (bf16[512,512]{1,0:T(8,128)(2,1)}, bf16[512,512]{1,0:T(8,128)(2,1)S(1)}, u32[]{:S(2)}, u32[]{:S(2)}) collective-permute-start(bf16[512,512]{1,0:T(8,128)(2,1)} %collective-permute-done.10), channel_id=1, source_target_pairs={{2,3},{6,7},{10,11},{14,15},{18,19},{22,23},{26,27},{30,31}} | collective-permute-start | bytes 1572872 | tf_op jit(solution)/shard_map/ppermute | solution.py:846
  197.0 10.5 %copy-start.14 = (f32[3,256]{1,0:T(4,128)S(1)}, f32[3,256]{1,0:T(4,128)}, u32[]{:S(2)}) copy-start(f32[3,256]{1,0:T(4,128)} %param.15) | copy-start | bytes 9220
  198.4 30.6 %collective-permute-start.12 = (bf16[512,2048]{1,0:T(8,128)(2,1)S(1)}, bf16[512,2048]{1,0:T(8,128)(2,1)}, u32[]{:S(2)}, u32[]{:S(2)}) collective-permute-start(bf16[512,2048]{1,0:T(8,128)(2,1)S(1)} %select_dynamic-update-slice_fusion), channel_id=1, source_target_pairs={{0,4},{4,0},{1,5},{5,1},{2,6},{6,2},{3,7},{7,3},{8,12},{12,8},{9,1... | collective-permute-start | bytes 6291464 | tf_op jit(solution)/shard_map/ppermute | solution.py:858
  200.7 13.3 %collective-permute-start.3 = (bf16[1,176,512]{2,1,0:T(8,128)(2,1)}, bf16[1,176,512]{2,1,0:T(8,128)(2,1)}, u32[]{:S(2)}, u32[]{:S(2)}) collective-permute-start(bf16[1,176,512]{2,1,0:T(8,128)(2,1)} %get-tuple-element.104), channel_id=1, source_target_pairs={{0,1},{1,2},{2,3},{3,0},{4,5},{5,6},{6,7},{7,4},{8,9},{9,10},{10,1... | collective-permute-start | bytes 540680 | tf_op jit(solution)/shard_map/ppermute | solution.py:806
  200.7 17.6 %collective-permute-start.4 = (bf16[1,176,512]{2,1,0:T(8,128)(2,1)}, bf16[1,176,512]{2,1,0:T(8,128)(2,1)}, u32[]{:S(2)}, u32[]{:S(2)}) collective-permute-start(bf16[1,176,512]{2,1,0:T(8,128)(2,1)} %get-tuple-element.103), channel_id=1, source_target_pairs={{0,2},{1,3},{2,0},{3,1},{4,6},{5,7},{6,4},{7,5},{8,10},{9,11},{10,... | collective-permute-start | bytes 540680 | tf_op jit(solution)/shard_map/ppermute | solution.py:806
  203.6 18.9 %collective-permute-start.5 = (bf16[1,176,512]{2,1,0:T(8,128)(2,1)}, bf16[1,176,512]{2,1,0:T(8,128)(2,1)}, u32[]{:S(2)}, u32[]{:S(2)}) collective-permute-start(bf16[1,176,512]{2,1,0:T(8,128)(2,1)} %get-tuple-element.102), channel_id=1, source_target_pairs={{0,3},{1,0},{2,1},{3,2},{4,7},{5,4},{6,5},{7,6},{8,11},{9,8},{10,9... | collective-permute-start | bytes 540680 | tf_op jit(solution)/shard_map/ppermute | solution.py:806
  208.1 2.3 copy-start.9
  227.9 350.6 %reduce-scatter.7.cloned.1.call-start = ((), (), s32[]{:S(2)}) async-start(), calls=%async_computation.11 | async-start | bytes 1310720 | tf_op jit(solution)/shard_map/reduce_scatter | solution.py:832
  232.9 4.0 copy-start.19
  235.4 6.7 copy-start.3
  383.8 11.8 %copy-start.5 = (bf16[512,2048]{1,0:T(8,128)(2,1)S(1)}, bf16[512,2048]{1,0:T(8,128)(2,1)}, u32[]{:S(2)}) copy-start(bf16[512,2048]{1,0:T(8,128)(2,1)} %get-tuple-element.100) | copy-start | bytes 6291460
  395.7 9.9 copy-start.18
  405.5 8.3 copy-start.23
  405.6 8.3 copy-start.25
  413.8 108.9 %copy-start.6 = (bf16[1024,256]{1,0:T(8,128)(2,1)S(1)}, bf16[1024,256]{1,0:T(8,128)(2,1)}, u32[]{:S(2)}) copy-start(bf16[1024,256]{1,0:T(8,128)(2,1)} %get-tuple-element.35) | copy-start | bytes 1572868
  527.2 71.9 %reduce-scatter.11.cloned.1.call-start = ((), (), s32[]{:S(2)}) async-start(), calls=%async_computation.15 | async-start | bytes 3604480 | tf_op jit(solution)/shard_map/reduce_scatter | solution.py:832
  534.0 1.2 copy-start.8
  534.1 112.8 %reduce-scatter.5.cloned.1.call-start = ((), (), s32[]{:S(2)}) async-start(), calls=%async_computation.9 | async-start | bytes 3932160 | tf_op jit(solution)/shard_map/reduce_scatter | solution.py:816
  539.6 15.9 %copy-start.20 = (bf16[1024,2048]{1,0:T(8,128)(2,1)S(1)}, bf16[1024,2048]{1,0:T(8,128)(2,1)}, u32[]{:S(2)}) copy-start(bf16[1024,2048]{1,0:T(8,128)(2,1)} %get-tuple-element.34) | copy-start | bytes 12582916
  562.6 1.6 copy-start.24
  562.6 2.4 copy-start.26
  562.6 153.9 %reduce-scatter.9.cloned.1.call-start = ((), (), s32[]{:S(2)}) async-start(), calls=%async_computation.13 | async-start | bytes 7208960 | tf_op jit(solution)/shard_map/reduce_scatter | solution.py:816
  578.2 395.2 %all-gather.18.cloned.1.call-start = ((), (), s32[]{:S(2)}) async-start(), calls=%async_computation.12 | async-start | bytes 1310720 | tf_op jit(solution)/shard_map/all_gather | solution.py:838
  580.2 6.8 collective-permute-start.16
  580.3 8.7 collective-permute-start.17
  582.2 6.8 collective-permute-start.18
  589.7 386.6 %all-gather.22.cloned.1.call-start = ((), (), s32[]{:S(2)}) async-start(), calls=%async_computation.16 | async-start | bytes 3604480 | tf_op jit(solution)/shard_map/all_gather | solution.py:838
  602.8 9.4 collective-permute-start.22
  604.4 14.4 %collective-permute-start.23 = (bf16[1,176,512]{2,1,0:T(8,128)(2,1)S(1)}, bf16[1,176,512]{2,1,0:T(8,128)(2,1)S(1)}, u32[]{:S(2)}, u32[]{:S(2)}) collective-permute-start(bf16[1,176,512]{2,1,0:T(8,128)(2,1)S(1)} %bitcast.175), channel_id=1, source_target_pairs={{0,2},{1,3},{2,0},{3,1},{4,6},{5,7},{6,4},{7,5},{8,10},{9,11},{10,... | collective-permute-start | bytes 540680 | tf_op jit(solution)/shard_map/ppermute | solution.py:806
  606.9 11.9 %collective-permute-start.24 = (bf16[1,176,512]{2,1,0:T(8,128)(2,1)S(1)}, bf16[1,176,512]{2,1,0:T(8,128)(2,1)S(1)}, u32[]{:S(2)}, u32[]{:S(2)}) collective-permute-start(bf16[1,176,512]{2,1,0:T(8,128)(2,1)S(1)} %bitcast.174), channel_id=1, source_target_pairs={{0,3},{1,0},{2,1},{3,2},{4,7},{5,4},{6,5},{7,6},{8,11},{9,8},{10,9... | collective-permute-start | bytes 540680 | tf_op jit(solution)/shard_map/ppermute | solution.py:806
  618.8 0.9 copy-start.4
  619.7 361.7 %all-gather.16.cloned.1.call-start = ((), (), s32[]{:S(2)}) async-start(), calls=%async_computation.10 | async-start | bytes 3932160 | tf_op jit(solution)/shard_map/all_gather | solution.py:826
  648.3 9.7 collective-permute-start.13
  650.2 15.1 %collective-permute-start.14 = (bf16[1,128,768]{1,2,0:T(8,128)(2,1)S(1)}, bf16[1,128,768]{1,2,0:T(8,128)(2,1)S(1)}, u32[]{:S(2)}, u32[]{:S(2)}) collective-permute-start(bf16[1,128,768]{1,2,0:T(8,128)(2,1)S(1)} %copy.212), channel_id=1, source_target_pairs={{0,2},{1,3},{2,0},{3,1},{4,6},{5,7},{6,4},{7,5},{8,10},{9,11},{10,... | collective-permute-start | bytes 589832 | tf_op jit(solution)/shard_map/ppermute | solution.py:806
  652.8 12.5 %collective-permute-start.15 = (bf16[1,128,768]{1,2,0:T(8,128)(2,1)S(1)}, bf16[1,128,768]{1,2,0:T(8,128)(2,1)S(1)}, u32[]{:S(2)}, u32[]{:S(2)}) collective-permute-start(bf16[1,128,768]{1,2,0:T(8,128)(2,1)S(1)} %copy.213), channel_id=1, source_target_pairs={{0,3},{1,0},{2,1},{3,2},{4,7},{5,4},{6,5},{7,6},{8,11},{9,8},{10,9... | collective-permute-start | bytes 589832 | tf_op jit(solution)/shard_map/ppermute | solution.py:806
  666.4 320.4 %all-gather.20.cloned.1.call-start = ((), (), s32[]{:S(2)}) async-start(), calls=%async_computation.14 | async-start | bytes 7208960 | tf_op jit(solution)/shard_map/all_gather | solution.py:826
  718.9 13.5 %collective-permute-start.19 = (bf16[1,128,1408]{1,2,0:T(8,128)(2,1)}, bf16[1,128,1408]{1,2,0:T(8,128)(2,1)S(1)}, u32[]{:S(2)}, u32[]{:S(2)}) collective-permute-start(bf16[1,128,1408]{1,2,0:T(8,128)(2,1)} %copy.219), channel_id=1, source_target_pairs={{0,1},{1,2},{2,3},{3,0},{4,5},{5,6},{6,7},{7,4},{8,9},{9,10},{10,1... | collective-permute-start | bytes 1081352 | tf_op jit(solution)/shard_map/ppermute | solution.py:806
  721.5 25.1 %collective-permute-start.20 = (bf16[1,128,1408]{1,2,0:T(8,128)(2,1)}, bf16[1,128,1408]{1,2,0:T(8,128)(2,1)S(1)}, u32[]{:S(2)}, u32[]{:S(2)}) collective-permute-start(bf16[1,128,1408]{1,2,0:T(8,128)(2,1)} %copy.220), channel_id=1, source_target_pairs={{0,2},{1,3},{2,0},{3,1},{4,6},{5,7},{6,4},{7,5},{8,10},{9,11},{10,... | collective-permute-start | bytes 1081352 | tf_op jit(solution)/shard_map/ppermute | solution.py:806
  724.1 22.5 %collective-permute-start.21 = (bf16[1,128,1408]{1,2,0:T(8,128)(2,1)S(1)}, bf16[1,128,1408]{1,2,0:T(8,128)(2,1)S(1)}, u32[]{:S(2)}, u32[]{:S(2)}) collective-permute-start(bf16[1,128,1408]{1,2,0:T(8,128)(2,1)S(1)} %copy.221), channel_id=1, source_target_pairs={{0,3},{1,0},{2,1},{3,2},{4,7},{5,4},{6,5},{7,6},{8,11},{9,8},{10,9... | collective-permute-start | bytes 1081352 | tf_op jit(solution)/shard_map/ppermute | solution.py:806
  746.7 3.9 copy-start.22
  757.5 131.3 %copy-start.21 = (bf16[704,2048]{1,0:T(8,128)(2,1)S(1)}, bf16[704,2048]{1,0:T(8,128)(2,1)}, u32[]{:S(2)}) copy-start(bf16[704,2048]{1,0:T(8,128)(2,1)} %all-gather.14.cloned.1.call-done) | copy-start | bytes 8650756
  986.8 19.9 %copy-start.1 = (bf16[512,3,1024]{2,0,1:T(8,128)(2,1)S(1)}, bf16[512,3,1024]{2,0,1:T(8,128)(2,1)}, u32[]{:S(2)}) copy-start(bf16[512,3,1024]{2,0,1:T(8,128)(2,1)} %param.14) | copy-start | bytes 9437188
  (1 other events, 0.7 us)
Sparse Core Ops, SparseCore 0:
  39.3 43.0 all-gather.23
  84.3 26.6 all-gather.9
  146.7 69.7 all-gather.11
  228.0 41.8 all-gather.13
  527.3 26.7 reduce-scatter.6
  557.2 41.7 reduce-scatter.10
  602.9 43.9 reduce-scatter.4
  650.7 65.7 reduce-scatter.8
  718.5 26.5 all-gather.17
  747.0 41.7 all-gather.21
  791.4 43.8 all-gather.15
  837.7 67.0 all-gather.19

commit v3 on v2

--- a/solution.py
+++ b/solution.py
@@ -18,7 +18,7 @@
 BF16 = jnp.bfloat16
 MESH = pl.DeviceIdType.MESH
 VMEM_LIMIT = 56 * 1024 * 1024
-SUBS = 4
+SUBS = 8
 
 
 def send(src, dst, send_sem, recv_sem, **where):
@@ -63,6 +63,9 @@
         pl.semaphore_wait(barrier, 2)
 
 
+LAG = 3
+
+
 class Reduce:
     def __init__(self, cols, subs, spot, part, twin, going, coming, sems, add=None):
         self.cols, self.subs, self.spot, self.add = cols, subs, spot, add
@@ -70,93 +73,107 @@
         self.twin_send, self.twin_recv, self.send, self.recv = sems
         self.r, self.c = lax.axis_index("row"), lax.axis_index("col")
         self.half = part.shape[0] // 2
-
-    def in_half(self, r, d, s):
+        self.per_sub = cols - 1
+        self.landing = LAG * (cols - 1)
+        self.slots = self.per_sub * (subs - 1) + self.landing + 1
+
+    def place(self, d, s, base=0):
         row, rows, column, columns = self.spot(d, s)
-        return pl.ds(pl.multiple_of(r * self.half + row, 16), rows), pl.ds(column, columns)
-
-    def in_twin(self, d, s):
-        row, rows, column, columns = self.spot(d, s)
-        return pl.ds(row, rows), pl.ds(column, columns)
+        if not isinstance(column, int):
+            column = pl.multiple_of(column, 128)
+        return pl.ds(pl.multiple_of(base + row, 16), rows), pl.ds(column, columns)
 
     def twin_copy(self, d, s):
         return send(
-            self.part.at[self.in_half(1 - self.r, d, s)],
-            self.twin.at[self.in_twin(d, s)],
+            self.part.at[self.place(d, s, (1 - self.r) * self.half)],
+            self.twin.at[self.place(d, s)],
             self.twin_send.at[d, s],
             self.twin_recv.at[d, s],
             row=1 - self.r,
         )
 
     def start(self):
-        order = []
-        for j in range(self.cols):
-            d = self.cols - 1 - j // 2 if j % 2 == 0 else j // 2
-            order.append(d)
-        for s in range(self.subs):
-            for d in order:
-                self.twin_copy(d, s).start()
+        @pl.loop(0, self.subs)
+        def _(s):
+            for j in range(self.cols):
+                self.twin_copy(self.cols - 1 - j // 2 if j % 2 == 0 else j // 2, s).start()
 
     def hop(self, way, d, s):
-        spot = self.in_twin(d, s)
-        target = self.c + 1 if way == 0 else self.c - 1
+        place = self.place(d, s)
         return send(
-            self.going.at[(way,) + spot],
-            self.coming.at[(way,) + spot],
+            self.going.at[(way,) + place],
+            self.coming.at[(way,) + place],
             self.send.at[way, d, s],
             self.recv.at[way, d, s],
-            col=target,
+            col=self.c + 1 if way == 0 else self.c - 1,
         )
 
     def own(self, d, s):
         self.twin_copy(d, s).wait_recv()
-        value = self.part[self.in_half(self.r, d, s)].astype(F32)
-        value = value + self.twin[self.in_twin(d, s)].astype(F32)
+        value = self.part[self.place(d, s, self.r * self.half)].astype(F32)
+        value = value + self.twin[self.place(d, s)].astype(F32)
         if self.add is not None:
             value = value + self.add(d, s)
         return value
 
     def pass_on(self, way, d, s):
-        spot = (way,) + self.in_twin(d, s)
+        place = (way,) + self.place(d, s)
         first = 0 if way == 0 else self.cols - 1
 
-        @pl.when(self.c < d if way == 0 else self.c > d)
+        @pl.when(self.c == first)
+        def _():
+            self.going[place] = self.own(d, s).astype(BF16)
+
+        @pl.when(self.c != first)
         def _():
             value = self.own(d, s)
-
-            @pl.when(self.c == first)
+            self.hop(way, d, s).wait_recv()
+            self.going[place] = (value + self.coming[place].astype(F32)).astype(BF16)
+
+        self.hop(way, d, s).start()
+
+    def slot(self, t):
+        for way in range(2):
+            made = self.c if way == 0 else self.cols - 1 - self.c
+            event = t - LAG * made
+
+            @pl.when((event >= 0) & (event < self.per_sub * self.subs))
             def _():
-                self.going[spot] = value.astype(BF16)
-
-            @pl.when(self.c != first)
+                s, j = lax.div(event, self.per_sub), lax.rem(event, self.per_sub)
+                d = self.cols - 1 - j if way == 0 else j
+
+                @pl.when(self.c < d if way == 0 else self.c > d)
+                def _():
+                    self.pass_on(way, d, s)
+
+    def landed(self, t, do):
+        after = t - self.landing
+
+        @pl.when((after >= 0) & (lax.rem(after + self.per_sub * self.cols, self.per_sub) == 0))
+        def _():
+            s = lax.div(after, self.per_sub)
+
+            @pl.when(s < self.subs)
             def _():
-                self.hop(way, d, s).wait_recv()
-                self.going[spot] = (value + self.coming[spot].astype(F32)).astype(BF16)
-
-            self.hop(way, d, s).start()
-
-    def relay(self, s):
-        for j in range(self.cols - 1):
-            self.pass_on(0, self.cols - 1 - j, s)
-            self.pass_on(1, j, s)
+                do(s)
 
     def land(self, s, total):
-        for d in range(self.cols):
-
-            @pl.when(self.c == d)
-            def _():
-                value = self.own(d, s)
-                spot = self.in_twin(d, s)
-                if d > 0:
-                    self.hop(0, d, s).wait_recv()
-                    value = value + self.coming[(0,) + spot].astype(F32)
-                if d < self.cols - 1:
-                    self.hop(1, d, s).wait_recv()
-                    value = value + self.coming[(1,) + spot].astype(F32)
-                total[...] = value
+        place = self.place(self.c, s)
+        total[...] = self.own(self.c, s)
+
+        @pl.when(self.c > 0)
+        def _():
+            self.hop(0, self.c, s).wait_recv()
+            total[...] += self.coming[(0,) + place].astype(F32)
+
+        @pl.when(self.c < self.cols - 1)
+        def _():
+            self.hop(1, self.c, s).wait_recv()
+            total[...] += self.coming[(1,) + place].astype(F32)
 
     def finish(self):
-        for s in range(self.subs):
+        @pl.loop(0, self.subs)
+        def _(s):
             for d in range(self.cols):
                 self.twin_copy(d, s).wait_send()
 
@@ -215,33 +232,44 @@
         if self.pair:
             self.across(self.r, self.c, s).start()
 
-    def relay(self, s):
+    def relay(self, s, k):
+        @pl.when(self.c >= k)
+        def _():
+            self.hop(0, self.c - k, s).wait_recv()
+
+            @pl.when(self.c < self.cols - 1)
+            def _():
+                self.hop(0, self.c - k, s).start()
+
+            if self.pair:
+                self.across(self.r, self.c - k, s).start()
+
+        @pl.when(self.c + k < self.cols)
+        def _():
+            self.hop(1, self.c + k, s).wait_recv()
+
+            @pl.when(self.c > 0)
+            def _():
+                self.hop(1, self.c + k, s).start()
+
+            if self.pair:
+                self.across(self.r, self.c + k, s).start()
+
+    def slot(self, t, begin, step):
         for k in range(1, self.cols):
-
-            @pl.when(self.c >= k)
+            after = t - begin - LAG * k
+
+            @pl.when((after >= 0) & (lax.rem(after + step * LAG * self.cols * 8, step) == 0))
             def _():
-                self.hop(0, self.c - k, s).wait_recv()
-
-                @pl.when(self.c < self.cols - 1)
+                s = lax.div(after, step)
+
+                @pl.when(s < self.subs)
                 def _():
-                    self.hop(0, self.c - k, s).start()
-
-                if self.pair:
-                    self.across(self.r, self.c - k, s).start()
-
-            @pl.when(self.c + k < self.cols)
-            def _():
-                self.hop(1, self.c + k, s).wait_recv()
-
-                @pl.when(self.c > 0)
-                def _():
-                    self.hop(1, self.c + k, s).start()
-
-                if self.pair:
-                    self.across(self.r, self.c + k, s).start()
+                    self.relay(s, k)
 
     def finish(self):
-        for s in range(self.subs):
+        @pl.loop(0, self.subs)
+        def _(s):
             for source in range(self.cols):
                 if self.pair:
                     self.across(1 - self.r, source, s).wait_recv()
@@ -271,6 +299,10 @@
     return centered, lax.rsqrt(jnp.mean(centered * centered, axis=1, keepdims=True) + EPSILON)
 
 
+def cost(us):
+    return pl.CostEstimate(flops=us * 10**9, bytes_accessed=10**7, transcendentals=0)
+
+
 def params(number):
     return pltpu.CompilerParams(
         collective_id=number, has_side_effects=True, vmem_limit_bytes=VMEM_LIMIT
@@ -298,19 +330,23 @@
     )
     spread = Gather(cols, SUBS, row_spot(own, step, half, width), normed, scratch[7:11])
     summing.start()
-    for s in range(SUBS):
-        summing.relay(s)
-        if s > 0:
-            spread.relay(s - 1)
+
+    def land(s):
         summing.land(s, total)
-        rows = pl.ds(s * step, step)
+        rows = pl.ds(pl.multiple_of(s * step, step), step)
         state = tokens_own[rows, :].astype(F32) + total[...]
         middle[rows, :] = state
         centered, rstd = moments(state)
         result = centered * rstd * vectors[2:3, :] + vectors[3:4, :]
         normed[spread.spot(spread.r, spread.c, s)] = result.astype(BF16)
         spread.start(s)
-    spread.relay(SUBS - 1)
+
+    @pl.loop(0, summing.slots + LAG * (cols - 1))
+    def _(t):
+        summing.slot(t)
+        summing.landed(t, land)
+        spread.slot(t, summing.landing, summing.per_sub)
+
     spread.finish()
     summing.finish()
 
@@ -329,6 +365,7 @@
         + Gather.scratch(cols, SUBS)
         + [pltpu.VMEM((group // 2 // cols // SUBS, width), F32)],
         compiler_params=params(2),
+        cost_estimate=cost(60),
         name="out_sum_norm_gather",
     )(part, tokens_own, vectors)
 
@@ -345,12 +382,10 @@
     spread = Gather(cols, SUBS, row_spot(own, step, half, width), grads, scratch[7:11])
     summing.start()
     sums[...] = jnp.zeros_like(sums)
-    for s in range(SUBS):
-        summing.relay(s)
-        if s > 0:
-            spread.relay(s - 1)
+
+    def land(s):
         summing.land(s, total)
-        rows = pl.ds(s * step, step)
+        rows = pl.ds(pl.multiple_of(s * step, step), step)
         centered, rstd = moments(middle[rows, :])
         xhat = centered * rstd
         grad = total[...]
@@ -365,7 +400,13 @@
         result = cotan_own[rows, :].astype(F32) + rstd * inner
         grads[spread.spot(spread.r, spread.c, s)] = result.astype(BF16)
         spread.start(s)
-    spread.relay(SUBS - 1)
+
+    @pl.loop(0, summing.slots + LAG * (cols - 1))
+    def _(t):
+        summing.slot(t)
+        summing.landed(t, land)
+        spread.slot(t, summing.landing, summing.per_sub)
+
     spread.finish()
     summing.finish()
 
@@ -384,60 +425,42 @@
         + Gather.scratch(cols, SUBS)
         + [pltpu.VMEM((group // 2 // cols // SUBS, width), F32)],
         compiler_params=params(3),
+        cost_estimate=cost(60),
         name="grad_sum_norm_gather",
     )(part, middle, cotan_own, vectors)
 
 
-def mixed_kernel(cols, part, middle, mixed, *scratch):
+def mixed_sum(cols, part, middle, scratch):
     half, width = part.shape[0] // 2, part.shape[1]
-    step, depth = half // cols, width // cols
-    total = scratch[7]
-    enter(cols)
+    step, depth, own = half // SUBS, width // cols, half // cols
     c = lax.axis_index("col")
 
     def add(d, s):
-        return jnp.where(c == s, middle[:, d * depth : (d + 1) * depth], 0.0)
-
-    summing = Reduce(
+        inside = s * step - c * own
+        rows = pl.ds(pl.multiple_of(lax.rem(s * step, own), step), step)
+        mine = middle[rows, pl.ds(pl.multiple_of(d * depth, 128), depth)]
+        return jnp.where((inside >= 0) & (inside < own), mine, 0.0)
+
+    return Reduce(
         cols,
-        cols,
+        SUBS,
         lambda d, s: (s * step, step, d * depth, depth),
         part,
         *scratch[:3],
         scratch[3:7],
         add=add,
     )
-    summing.start()
-    for s in range(cols):
-        summing.relay(s)
-        summing.land(s, total)
-        mixed[s * step : (s + 1) * step, :] = total[...].astype(BF16)
-    summing.finish()
-
-
-def sum_mixed(cols, part, middle):
-    group, width = part.shape
-    return pl.pallas_call(
-        functools.partial(mixed_kernel, cols),
-        out_shape=jax.ShapeDtypeStruct((group // 2, width // cols), BF16),
-        in_specs=[VM] * 2,
-        out_specs=VM,
-        scratch_shapes=Reduce.scratch(cols, cols, group // 2, width)
-        + [pltpu.VMEM((group // 2 // cols, width // cols), F32)],
-        compiler_params=params(4),
-        name="mixed_sum",
-    )(part, middle)
 
 
 def first_kernel(cols, part, xhat, rstd, gain, grad_middle, result, sums, *scratch):
     half, width = part.shape[0] // 2, part.shape[1]
-    step, depth = half // cols, width // cols
+    step, depth = half // SUBS, width // cols
     total, grad, mine, theirs, out_sem, in_sem = scratch[7:]
     enter(cols, everyone=True)
     c = lax.axis_index("col")
     summing = Reduce(
         cols,
-        cols,
+        SUBS,
         lambda d, s: (s * step, step, d * depth, depth),
         part,
         *scratch[:3],
@@ -445,18 +468,26 @@
     )
     summing.start()
     sums[...] = jnp.zeros_like(sums)
-    lanes = lax.broadcasted_iota(jnp.int32, (step, 128), 1)
-    for s in range(cols):
-        rows = slice(s * step, (s + 1) * step)
-        summing.relay(s)
+
+    def land(s):
         summing.land(s, total)
+        rows = pl.ds(pl.multiple_of(s * step, step), step)
         grad[rows, :] = total[...]
         standard = xhat[rows, :]
         sums[0:1, :] += jnp.sum(total[...] * standard, axis=0, keepdims=True)
         sums[1:2, :] += jnp.sum(total[...], axis=0, keepdims=True)
-        scaled = total[...] * gain[0:1, :]
+
+    @pl.loop(0, summing.slots)
+    def _(t):
+        summing.slot(t)
+        summing.landed(t, land)
+
+    lanes = lax.broadcasted_iota(jnp.int32, (128, 128), 1)
+    for s in range(half // 128):
+        rows = slice(s * 128, (s + 1) * 128)
+        scaled = grad[rows, :] * gain[0:1, :]
         one = jnp.sum(scaled, axis=1, keepdims=True)
-        two = jnp.sum(scaled * standard, axis=1, keepdims=True)
+        two = jnp.sum(scaled * xhat[rows, :], axis=1, keepdims=True)
         both = jnp.where(lanes == 0, one, jnp.where(lanes == 1, two, 0.0))
         mine[:, rows] = both.T[0:8, :]
 
@@ -469,12 +500,12 @@
         exchange(k).start()
     for k in range(1, cols):
         exchange(k).wait_recv()
-    for s in range(cols):
-        rows = slice(s * step, (s + 1) * step)
+    for s in range(half // 128):
+        rows = slice(s * 128, (s + 1) * 128)
         both = mine[:, rows]
         for k in range(1, cols):
             both = both + theirs[k - 1, :, rows]
-        both = jnp.concatenate([both, jnp.zeros((120, step), F32)], axis=0).T / (depth * cols)
+        both = jnp.concatenate([both, jnp.zeros((120, 128), F32)], axis=0).T / (depth * cols)
         scaled = grad[rows, :] * gain[0:1, :]
         inner = scaled - both[:, 0:1] - xhat[rows, :] * both[:, 1:2]
         result[rows, :] = grad_middle[rows, :].astype(F32) + rstd[rows, 0:1] * inner
@@ -494,9 +525,9 @@
         ),
         in_specs=[VM] * 5,
         out_specs=(VM, VM),
-        scratch_shapes=Reduce.scratch(cols, cols, half, width)
+        scratch_shapes=Reduce.scratch(cols, SUBS, half, width)
         + [
-            pltpu.VMEM((half // cols, depth), F32),
+            pltpu.VMEM((half // SUBS, depth), F32),
             pltpu.VMEM((half, depth), F32),
             pltpu.VMEM((8, half), F32),
             pltpu.VMEM((cols - 1, 8, half), F32),
@@ -504,6 +535,7 @@
             pltpu.SemaphoreType.DMA((cols - 1,)),
         ],
         compiler_params=params(5),
+        cost_estimate=cost(45),
         name="input_grad_sum",
     )(part, xhat, rstd, gain, grad_middle)
 
@@ -548,9 +580,13 @@
             row=1 - lax.axis_index("row"),
         )
 
-    names.relay(0)
+    for k in range(1, cols):
+        names.relay(0, k)
+        for s in range(cols):
+            if k < cols - 1:
+                spread.relay(s, k)
     for s in range(cols):
-        spread.relay(s)
+        spread.relay(s, cols - 1)
         rows = slice(s * step, (s + 1) * step)
         state = full[rows, :].astype(F32)
         centered, inverse = moments(state)
@@ -592,6 +628,7 @@
         + Gather.scratch(cols, cols)
         + [pltpu.SemaphoreType.DMA((cols,)), pltpu.SemaphoreType.DMA((cols,))],
         compiler_params=params(1),
+        cost_estimate=cost(40),
         name="gather_norm_one",
     )(tokens, vector)
 
@@ -629,6 +666,7 @@
 
 
 BLOCK = 256
+PACE = 2
 
 
 def causal(rows):
@@ -637,9 +675,22 @@
     )
 
 
-def attend_kernel(qkv, bias, tables, heads_in, attn, logs):
+def attend_kernel(cols, qkv, bias, tables, cotan, heads_in, attn, logs, cotan_rows, *sems):
     length, wide = attn.shape
     two = 2 * HD
+    half, depth = cotan.shape
+    subs = 2 * (wide // two)
+    step = half // subs
+
+    def spot(r, source, s):
+        rows = pl.ds(pl.multiple_of(r * half + s * step, 16), step)
+        return rows, pl.ds(pl.multiple_of(source * depth, 128), depth)
+
+    enter(cols)
+    spread = Gather(cols, subs, spot, cotan_rows, sems)
+    for s in range(subs):
+        cotan_rows[spot(spread.r, spread.c, s)] = cotan[s * step : (s + 1) * step, :]
+        spread.start(s)
     first_head = lax.broadcasted_iota(jnp.int32, (BLOCK, two), 1) < HD
 
     @pl.loop(0, wide // two)
@@ -675,28 +726,59 @@
             attn[rows, pl.ds(pl.multiple_of(pair * two, two), two)] = jnp.where(
                 first_head, outs[0], outs[1]
             ).astype(BF16)
-
-
-def attend(qkv, bias, tables):
+            if i % 2 == 1:
+                spread.relay(2 * pair + i // 2, 1)
+
+    for k in range(2, cols):
+
+        @pl.loop(0, subs)
+        def _(s):
+            spread.relay(s, k)
+
+    spread.finish()
+
+
+def attend(cols, qkv, bias, tables, cotan):
     length, wide = qkv.shape[0], qkv.shape[1] // 3
+    subs = wide // HD
     return pl.pallas_call(
-        attend_kernel,
+        functools.partial(attend_kernel, cols),
         out_shape=(
             jax.ShapeDtypeStruct(qkv.shape, BF16),
             jax.ShapeDtypeStruct((length, wide), BF16),
             jax.ShapeDtypeStruct((wide // (2 * HD), 2, length, 128), F32),
+            jax.ShapeDtypeStruct((2 * cotan.shape[0], cols * cotan.shape[1]), BF16),
         ),
-        in_specs=[VM] * 3,
-        out_specs=(VM,) * 3,
-        compiler_params=pltpu.CompilerParams(vmem_limit_bytes=VMEM_LIMIT),
-        cost_estimate=pl.CostEstimate(flops=8 * 10**9, bytes_accessed=10**7, transcendentals=4 * 10**6),
-        name="attention",
-    )(qkv, bias, tables)
-
-
-def attend_back_kernel(heads_in, logs, grad, tables, result, sums, queries_grad, keys_grad, values_grad):
+        in_specs=[VM] * 4,
+        out_specs=(VM,) * 4,
+        scratch_shapes=Gather.scratch(cols, subs),
+        compiler_params=params(6),
+        cost_estimate=cost(40),
+        name="attention_cotangent_gather",
+    )(qkv, bias, tables, cotan)
+
+
+def attend_back_kernel(
+    cols, heads_in, logs, grad, tables, part, middle, result, sums, mixed, *scratch
+):
     length, wide = grad.shape
     two = 2 * HD
+    queries_grad, keys_grad, values_grad, total = scratch[:4]
+    step = part.shape[0] // 2 // SUBS
+    enter(cols)
+    summing = mixed_sum(cols, part, middle, scratch[4:])
+    summing.start()
+
+    def land(s):
+        summing.land(s, total)
+        mixed[pl.ds(pl.multiple_of(s * step, step), step), :] = total[...].astype(BF16)
+
+    def slot(t):
+        summing.slot(t)
+        summing.landed(t, land)
+
+    blocks = length // BLOCK
+    done = wide // two * blocks * PACE
     first_head = lax.broadcasted_iota(jnp.int32, (BLOCK, two), 1) < HD
 
     @pl.loop(0, wide // two)
@@ -729,6 +811,11 @@
                 keys_grad[0:keep, :] += dot_tn(scores_grad, query_h)
                 values_grad[0:keep, :] += dot_tn(probs.astype(BF16), grad_h)
             queries_grad[rows, :] = jnp.where(first_head, outs[0], outs[1]) * HD ** (-0.5)
+
+            @pl.loop(0, PACE)
+            def _(u):
+                slot((pair * blocks + i) * PACE + u)
+
         grads = (
             turn(queries_grad[...], tables, back=True),
             turn(keys_grad[...], tables, back=True),
@@ -737,25 +824,35 @@
         for k in range(3):
             low = grads[k].astype(BF16)
             result[:, lanes(k)] = low
-            total = jnp.sum(low.astype(F32), axis=0, keepdims=True)
-            sums[:, lanes(k)] = jnp.broadcast_to(total, (8, two))
-
-
-def attend_back(heads_in, logs, grad, tables):
+            column_sum = jnp.sum(low.astype(F32), axis=0, keepdims=True)
+            sums[:, lanes(k)] = jnp.broadcast_to(column_sum, (8, two))
+
+    @pl.loop(done, max(done, summing.slots))
+    def _(t):
+        slot(t)
+
+    summing.finish()
+
+
+def attend_back(cols, heads_in, logs, grad, tables, part, middle):
     length, wide = grad.shape
+    group, width = part.shape
     return pl.pallas_call(
-        attend_back_kernel,
+        functools.partial(attend_back_kernel, cols),
         out_shape=(
             jax.ShapeDtypeStruct(heads_in.shape, BF16),
             jax.ShapeDtypeStruct((8, 3 * wide), F32),
+            jax.ShapeDtypeStruct((group // 2, width // cols), BF16),
         ),
-        in_specs=[VM] * 4,
-        out_specs=(VM,) * 2,
-        scratch_shapes=[pltpu.VMEM((length, 2 * HD), F32)] * 3,
-        compiler_params=pltpu.CompilerParams(vmem_limit_bytes=VMEM_LIMIT),
-        cost_estimate=pl.CostEstimate(flops=20 * 10**9, bytes_accessed=10**7, transcendentals=4 * 10**6),
-        name="attention_back",
-    )(heads_in, logs, grad, tables)
+        in_specs=[VM] * 6,
+        out_specs=(VM,) * 3,
+        scratch_shapes=[pltpu.VMEM((length, 2 * HD), F32)] * 3
+        + [pltpu.VMEM((group // 2 // SUBS, width // cols), F32)]
+        + Reduce.scratch(cols, SUBS, group // 2, width),
+        compiler_params=params(4),
+        cost_estimate=cost(45),
+        name="attention_back_mixed_sum",
+    )(heads_in, logs, grad, tables, part, middle)
 
 
 def dot(spec, a, b):
@@ -795,19 +892,6 @@
     return lax.all_to_all(pieces, "col", 0, 0, tiled=True)
 
 
-def exchange_later(pieces, cols):
-    me = lax.axis_index("col")
-    out = jnp.zeros_like(pieces)
-    out = lax.dynamic_update_index_in_dim(
-        out, lax.dynamic_index_in_dim(pieces, me, 0, True), me, 0
-    )
-    for k in range(1, cols):
-        going = lax.dynamic_index_in_dim(pieces, lax.rem(me + k, cols), 0, True)
-        coming = lax.ppermute(going, "col", [(i, (i + k) % cols) for i in range(cols)])
-        out = lax.dynamic_update_index_in_dim(out, coming, lax.rem(me + cols - k, cols), 0)
-    return out
-
-
 def columns_sum(grad, sizes):
     dp, col = sizes["dp"], sizes["col"]
     width, narrow = grad.shape
@@ -837,27 +921,6 @@
     col, part, depth = piece.shape
     whole = lax.all_gather(piece, "dp", axis=0)
     return whole.transpose(1, 0, 2, 3).reshape(-1, depth).astype(F32)
-
-
-def line_gather(block, cols):
-    me = lax.axis_index("col")
-    right, left = [block], [block]
-    for k in range(1, cols):
-        right.append(lax.ppermute(right[-1], "col", [(i, i + 1) for i in range(k - 1, cols - 1)]))
-        left.append(lax.ppermute(left[-1], "col", [(i + 1, i) for i in range(cols - k)]))
-    depth = block.shape[1]
-    out = jnp.zeros((block.shape[0], cols * depth), block.dtype)
-    for k in range(cols):
-        source = lax.rem(me + cols - k, cols)
-        value = block if k == 0 else jnp.where(me >= k, right[k], left[cols - k])
-        out = lax.dynamic_update_slice_in_dim(out, value, source * depth, 1)
-    return out
-
-
-def pair_gather(half):
-    other = lax.ppermute(half, "row", [(0, 1), (1, 0)])
-    first = lax.axis_index("row") == 0
-    return jnp.concatenate([jnp.where(first, half, other), jnp.where(first, other, half)])
 
 
 def make_body(sizes):
@@ -887,21 +950,23 @@
         vector = jnp.concatenate([vector, jnp.zeros_like(vector)])
         qkv_piece = exchange(columns_piece(qkv_weight, sizes))
         out_piece = exchange(rows_piece(out_weight, sizes))
+        tokens, qkv_piece, out_piece = lax.optimization_barrier((tokens, qkv_piece, out_piece))
         qkv_w = columns_whole(qkv_piece, sizes)
         out_w = rows_whole(out_piece, sizes)
-        tokens, qkv_piece = lax.optimization_barrier((tokens, qkv_piece))
+        gate_up_piece = columns_piece(gate_up_weight, sizes)
+        down_piece = rows_piece(down_weight, sizes)
+        gate_up_piece, down_piece, qkv_piece = lax.optimization_barrier(
+            (gate_up_piece, down_piece, qkv_piece)
+        )
+        gate_up_w = columns_whole(exchange(gate_up_piece), sizes)
+        down_w = rows_whole(exchange(down_piece), sizes)
         normed_one, tokens_own, xhat_one, rstd_one, vectors = norm_one(cols, tokens, vector)
-        gate_up_block, down_block, cotan_block, normed_one = lax.optimization_barrier(
-            (gate_up_weight, down_weight, cotangent, normed_one)
-        )
-        gate_up_w = columns_whole(exchange_later(columns_piece(gate_up_block, sizes), cols), sizes)
-        down_w = rows_whole(exchange_later(rows_piece(down_block, sizes), cols), sizes)
-        cotan_half = line_gather(cotan_block, cols)
-        cotan_rows = pair_gather(cotan_half)
-        cotan_own = lax.dynamic_slice_in_dim(cotan_half, my_col * own, own, 0)
 
         qkv = dot_nn(normed_one, qkv_w)
-        heads_in, attn, logs = attend(qkv, qkv_bias.reshape(1, -1), tables)
+        heads_in, attn, logs, cotan_rows = attend(
+            cols, qkv, qkv_bias.reshape(1, -1), tables, cotangent
+        )
+        cotan_own = lax.dynamic_slice_in_dim(cotan_rows, my_row * half + my_col * own, own, 0)
         normed_two, middle = norm_two(cols, dot_nn(attn, out_w).astype(BF16), tokens_own, vectors)
 
         gate_up = dot_nn(normed_two, gate_up_w)
@@ -909,20 +974,28 @@
         gate, up = gate_up[:, :wide], gate_up[:, wide:]
         sig = jax.nn.sigmoid(gate)
         hidden = (gate * sig * up).astype(BF16)
+        grad_down = dot_tn(hidden, cotan_rows).astype(BF16)
+        cotan_rows, grad_down = lax.optimization_barrier((cotan_rows, grad_down))
+        down_piece = exchange(rows_sum(grad_down, sizes))
         grad_hidden = dot_nt(cotan_rows, down_w)
         grad_gu = jnp.concatenate(
             [grad_hidden * up * sig * (1.0 + gate * (1.0 - sig)), grad_hidden * gate * sig], axis=1
         ).astype(BF16)
+        grad_gate_up = dot_tn(normed_two, grad_gu).astype(BF16)
+        grad_gu, grad_gate_up = lax.optimization_barrier((grad_gu, grad_gate_up))
+        gate_up_piece = exchange(columns_sum(grad_gate_up, sizes))
         grad_middle, second = norm_two_back(
             cols, dot_nt(grad_gu, gate_up_w).astype(BF16), middle, cotan_own, vectors
         )
-        mixed = sum_mixed(cols, dot_nn(hidden, down_w).astype(BF16), middle)
-        down_piece = exchange_later(rows_sum(dot_tn(hidden, cotan_rows), sizes), cols)
-        gate_up_piece = exchange_later(columns_sum(dot_tn(normed_two, grad_gu), sizes), cols)
-        out_piece = exchange_later(rows_sum(dot_tn(attn, grad_middle), sizes), cols)
         grad_attn = dot_nt(grad_middle, out_w).astype(BF16)
-        grad_qkv, bias_part = attend_back(heads_in, logs, grad_attn, tables)
-        qkv_piece = exchange_later(columns_sum(dot_tn(normed_one, grad_qkv), sizes), cols)
+        grad_out = dot_tn(attn, grad_middle).astype(BF16)
+        grad_qkv, bias_part, mixed = attend_back(
+            cols, heads_in, logs, grad_attn, tables, dot_nn(hidden, down_w).astype(BF16), middle
+        )
+        grad_qkv_weight = dot_tn(normed_one, grad_qkv).astype(BF16)
+        grad_qkv, grad_qkv_weight = lax.optimization_barrier((grad_qkv, grad_qkv_weight))
+        out_piece = exchange(rows_sum(grad_out, sizes))
+        qkv_piece = exchange(columns_sum(grad_qkv_weight, sizes))
         grad_block = lax.dynamic_slice(grad_middle, (my_row * half, my_col * depth), (half, depth))
         input_grad, first = sum_first(
             cols,

time: 1020 us -> 833 us (0.82)
  Pallas kernels: 474 us -> 342 us
  blocking collectives: 66.2 us -> 154 us
  waiting for transfers between devices: 196 us -> 123 us
  starting transfers between devices: 48.8 us -> 13.8 us
  local copies, waits for them, and re-layouts: 110 us -> 82.8 us
  other arithmetic: 19.7 us -> 9.11 us
    ppermute x25 -> x0, waiting for transfers between devices: 102 us -> none  [the longest x18 68.8 us: exchange_later(): lax.ppermute(going, 'col', [(i, (i + k) % cols) for i in range(cols)])]
    all_to_all x1 -> x5, blocking collectives: 26.4 us -> 114 us  [exchange(): return lax.all_to_all(pieces, 'col', 0, 0, tiled=True)]
    pallas_call x1, Pallas kernels: 123 us -> 70.7 us  [norm_two(): pl.pallas_call(functools.partial(norm_two_kernel, cols), out_shape=(jax.S...]
    ppermute x25 -> x0, starting transfers between devices: 44.1 us -> none  [the longest x18 28.1 us: exchange_later(): lax.ppermute(going, 'col', [(i, (i + k) % cols) for i in range(cols)])]
    pallas_call x1, Pallas kernels: 109 us -> 70.6 us  [norm_two_back(): pl.pallas_call(functools.partial(norm_two_back_kernel, cols), out_shape=(...]
    pallas_call x1, Pallas kernels: 89.7 us -> 52.4 us  [sum_first(): pl.pallas_call(functools.partial(first_kernel, cols), out_shape=(jax.Shap...]
    all_to_all x1 -> x3, waiting for transfers between devices: 7.39 us -> 38.7 us  [exchange(): return lax.all_to_all(pieces, 'col', 0, 0, tiled=True)]
    all_gather x2, waiting for transfers between devices: 0.01 us -> 26.9 us  [columns_return(): return lax.all_gather(piece, 'dp', axis=0, tiled=True).astype(F32)]
  transfers between devices with their start and end apart: 38 -> 15, of which waited for: 17 -> 5; matrix products, arithmetic and copies ran while one was open for 16% -> 14% of each run, Pallas kernels for 36% -> 33%
where the time goes in v3:
time: 833 us; the launch traced here: 822 us
  Pallas kernels  342 us (41%)
  blocking collectives  154 us (18%)
  waiting for transfers between devices  123 us (15%)
  matrix products  83.5 us (10%)
  local copies, waits for them, and re-layouts  82.8 us (10%)
  between operations  15.2 us (2%)
  starting transfers between devices  13.8 us (2%)
  other arithmetic  9.11 us (1%)
    all_to_all x5, blocking collectives, exchange(): return lax.all_to_all(pieces, 'col', 0, 0, tiled=True)  114 us
    pallas_call x1, Pallas kernels, norm_two(): pl.pallas_call(functools.partial(norm_two_kernel, cols), out_shape=(jax.S...  70.7 us
    pallas_call x1, Pallas kernels, norm_two_back(): pl.pallas_call(functools.partial(norm_two_back_kernel, cols), out_shape=(...  70.6 us
    reduce_scatter x2, waiting for transfers between devices, columns_sum(): lax.psum_scatter(pieces.reshape(width, narrow), 'dp', scatter_dimension=0...  56.4 us
    pallas_call x1, Pallas kernels, norm_one(): pl.pallas_call(functools.partial(norm_one_kernel, cols), out_shape=(jax.S...  53.7 us
    pallas_call x1, Pallas kernels, sum_first(): pl.pallas_call(functools.partial(first_kernel, cols), out_shape=(jax.Shap...  52.4 us
    pallas_call x1, Pallas kernels, attend_back(): pl.pallas_call(functools.partial(attend_back_kernel, cols), out_shape=(ja...  49.7 us
    pallas_call x1, Pallas kernels, attend(): pl.pallas_call(functools.partial(attend_kernel, cols), out_shape=(jax.Sha...  44.6 us
  transfers between devices with their start and end apart: 15, of which 5 were waited for; matrix products, arithmetic and copies ran while one was open for 14% of the time, Pallas kernels for 33%

profile of v3, /device:TPU:0, one launch (start us, length us, event | category | flops | bytes accessed | tf_op | source)
XLA Modules:
  0.0 822.5 jit_solution(10514561255108295379)
XLA Ops:
  7.2 1.8 dynamic-slice_bitcast_fusion.1
  9.0 6.3 all-to-all-start.1
  16.3 1.5 copy.113
  17.9 6.4 all-to-all-done.1
  24.3 21.8 %all_to_all.40 = bf16[4,128,768]{1,2,0:T(8,128)(2,1)S(1)} all-to-all(bf16[4,128,768]{1,2,0:T(8,128)(2,1)S(1)} %bitcast.128), channel_id=1, replica_groups=mesh['dp'=4,'row'=2,'col'=4] {'col'}, dimensions={0} | all-to-all | bytes 1572864 | tf_op jit(solution)/shard_map/all_to_all | solution.py:892
  46.1 1.2 copy.89
  47.3 2.4 constant_dynamic-slice_fusion.2
  49.6 1.9 copy.115
  51.6 1.2 copy.93
  52.8 2.1 dynamic-slice_bitcast_fusion
  54.8 3.6 all-to-all-start.2
  59.3 32.3 %all-to-all-done.2 = bf16[4,128,1408]{1,2,0:T(8,128)(2,1)S(1)} async-done(((bf16[4,128,1408]{1,2,0:T(8,128)(2,1)}), bf16[4,128,1408]{1,2,0:T(8,128)(2,1)S(1)}, u32[]{:S(2)}, u32[]{:S(2)}) %all-to-all-start.2) | async-done | bytes 1441824 | tf_op jit(solution)/shard_map/all_to_all | solution.py:892
  91.6 1.5 copy.95
  94.4 2.0 fusion
  96.4 1.2 pad_maximum_fusion.1.tables
  97.6 3.5 all-to-all-start.3
  101.2 53.7 %gather_norm_one.1 = (bf16[1024,2048]{1,0:T(8,128)(2,1)}, bf16[128,2048]{1,0:T(8,128)(2,1)}, f32[512,512]{1,0:T(8,128)}, f32[512,128]{1,0:T(8,128)}, f32[8,2048]{1,0:T(8,128)}) custom-call(bf16[512,512]{1,0:T(8,128)(2,1)} %tokens, f32[8,512]{1,0:T(8,128)} %concatenate.10.vector), custom_call_target="tpu_custom_call" | custom-call | flops 40000000000 | bytes 10000000 | tf_op jit(solution)/shard_map/gather_norm_one/pallas_call | solution.py:615
  154.9 1.0 copy.120
  156.0 2.3 copy.90
  159.1 5.1 fusion.10.qkv
  164.2 44.6 %attention_cotangent_gather.1 = (bf16[1024,768]{1,0:T(8,128)(2,1)}, bf16[1024,256]{1,0:T(8,128)(2,1)}, f32[2,2,1024,128]{3,2,1,0:T(8,128)}, bf16[1024,2048]{1,0:T(8,128)(2,1)}) custom-call(f32[1024,768]{1,0:T(8,128)} %fusion.10.qkv, f32[1,768]{1,0:T(1,128)} %bitcast.149, f32[3,1024,128]{2,1,0:T(8,128)} %pad_maximum_fusion.1.tables, bf16[512,512]{1,0:T(8,128)(2,1)} %cotan.1), custom_call_target="tpu_custom_call" | custom-call | flops 40000000000 | bytes 10000000 | tf_op jit(solution)/shard_map/attention_cotangent_gather/pallas_call | solution.py:744
  208.8 4.7 convolution_convert_fusion.3.part
  213.5 70.7 %out_sum_norm_gather.1 = (bf16[1024,2048]{1,0:T(8,128)(2,1)}, f32[128,2048]{1,0:T(8,128)}) custom-call(bf16[1024,2048]{1,0:T(8,128)(2,1)} %convolution_convert_fusion.3.part, bf16[128,2048]{1,0:T(8,128)(2,1)} %get-tuple-element.48.tokens_own, f32[8,2048]{1,0:T(8,128)} %get-tuple-element.49.vectors), custom_call_target="tpu_custom_call" | custom-call | flops 60000002048 | bytes 10000000 | tf_op jit(solution)/shard_map/out_sum_norm_gather/pallas_call | solution.py:356
  284.2 1.9 constant_dynamic-slice_fusion.1.cotan_own
  286.1 3.4 copy.96
  290.0 6.6 fusion.11
  297.5 2.0 copy-done.2
  299.6 1.4 copy-done.9
  300.9 14.9 %convolution_convert_fusion.6 = bf16[704,2048]{1,0:T(8,128)(2,1)} fusion(bf16[1024,704]{1,0:T(8,128)(2,1)S(1)} %multiply_convert_fusion.2, bf16[1024,2048]{1,0:T(8,128)(2,1)S(1)} %copy-done.9), kind=kOutput, calls=%fused_computation.7 | convolution fusion | flops 2954231808 | bytes 8519680 | tf_op jit(solution)/shard_map/dot_general | solution.py:661
  315.9 9.2 %multiply_convert_fusion.1 = (bf16[1024,704]{1,0:T(8,128)(2,1)S(1)}, bf16[1024,704]{1,0:T(8,128)(2,1)S(1)}) fusion(f32[1024,1408]{1,0:T(8,128)} %copy-done.2, bf16[1024,2048]{1,0:T(8,128)(2,1)} %get-tuple-element.52, bf16[704,2048]{1,0:T(8,128)(2,1)} %all-gather.15.cloned.1.call-done), kind=kOutput, calls=%fused_computation.9 | convolution fusion | flops 2962161664 | bytes 15728640 | tf_op jit(solution)/shard_map/dot_general | solution.py:657
  326.0 1.3 copy-done.20
  327.3 8.6 %convolution_convert_fusion = bf16[2048,1408]{1,0:T(8,128)(2,1)} fusion(bf16[1024,2048]{1,0:T(8,128)(2,1)S(1)} %copy-done.20, bf16[1024,1408]{1,0:T(8,128)(2,1)S(1)} %pad_maximum_fusion), kind=kOutput, calls=%fused_computation | convolution fusion | flops 5908463616 | bytes 12845056 | tf_op jit(solution)/shard_map/dot_general | solution.py:661
  335.9 8.2 %convolution_convert_fusion.2.part = bf16[1024,2048]{1,0:T(8,128)(2,1)} fusion(bf16[1024,1408]{1,0:T(8,128)(2,1)S(1)} %pad_maximum_fusion, bf16[2048,1408]{1,0:T(8,128)(2,1)S(1)} %bitcast.119), kind=kOutput, calls=%fused_computation.3 | convolution fusion | flops 5907677184 | bytes 12845056 | tf_op jit(solution)/shard_map/dot_general | solution.py:657
  344.1 70.6 %grad_sum_norm_gather.1 = (bf16[1024,2048]{1,0:T(8,128)(2,1)}, f32[8,2048]{1,0:T(8,128)}) custom-call(bf16[1024,2048]{1,0:T(8,128)(2,1)} %convolution_convert_fusion.2.part, f32[128,2048]{1,0:T(8,128)} %get-tuple-element.55.middle, bf16[128,2048]{1,0:T(8,128)(2,1)} %constant_dynamic-slice_fusion.1.cotan_own, f32[8,2048]{1,0:T(8,128)} %get-tuple-element.49.vectors), custom_call_target="tpu_custom_call" | custom-call | flops 60000002048 | bytes 10000000 | tf_op jit(solution)/shard_map/grad_sum_norm_gather/pallas_call | solution.py:416
  414.7 4.4 convolution_convert_fusion.7
  420.4 4.4 convolution_convert_fusion.8.grad
  424.8 4.9 convolution_convert_fusion.1.part
  429.8 49.7 %attention_back_mixed_sum.1 = (bf16[1024,768]{1,0:T(8,128)(2,1)}, f32[8,768]{1,0:T(8,128)}, bf16[512,512]{1,0:T(8,128)(2,1)}) custom-call(bf16[1024,768]{1,0:T(8,128)(2,1)} %get-tuple-element.43.heads_in, f32[2,2,1024,128]{3,2,1,0:T(8,128)} %get-tuple-element.44.logs, bf16[1024,256]{1,0:T(8,128)(2,1)} %convolution_convert_fusion.8.grad, ...), custom_call_target="tpu_custom_call" | custom-call | flops 44999999488 | bytes 10000000 | tf_op jit(solution)/shard_map/attention_back_mixed_sum/pallas_call | solution.py:840
  479.4 5.3 convolution_convert_fusion.5
  484.7 1.9 copy.100
  486.7 5.9 copy.105
  493.7 10.6 %all_to_all.41 = bf16[4,64,512]{2,1,0:T(8,128)(2,1)} all-to-all(bf16[4,64,512]{2,1,0:T(8,128)(2,1)S(1)} %bitcast.140), channel_id=1, replica_groups=mesh['dp'=4,'row'=2,'col'=4] {'col'}, dimensions={0} | all-to-all | bytes 524288 | tf_op jit(solution)/shard_map/all_to_all | solution.py:892
  504.4 1.2 copy.125
  505.6 18.7 %all_to_all.42 = bf16[4,176,512]{2,1,0:T(8,128)(2,1)} all-to-all(bf16[4,176,512]{2,1,0:T(8,128)(2,1)S(1)} %bitcast.134), channel_id=1, replica_groups=mesh['dp'=4,'row'=2,'col'=4] {'col'}, dimensions={0} | all-to-all | bytes 1441792 | tf_op jit(solution)/shard_map/all_to_all | solution.py:892
  524.3 13.8 %reduce-scatter.5.cloned.1.call-done = bf16[512,768]{1,0:T(8,128)(2,1)} async-done(((bf16[2048,768]{1,0:T(8,128)(2,1)}), bf16[512,768]{1,0:T(8,128)(2,1)}) %reduce-scatter.5.cloned.1.call-update) | async-done | bytes 786448 | tf_op jit(solution)/shard_map/reduce_scatter | solution.py:900
  538.1 1.5 copy.101
  539.6 24.5 %all_to_all.43 = bf16[4,128,768]{1,2,0:T(8,128)(2,1)S(1)} all-to-all(bf16[4,128,768]{1,2,0:T(8,128)(2,1)S(1)} %copy.101), channel_id=1, replica_groups=mesh['dp'=4,'row'=2,'col'=4] {'col'}, dimensions={0} | all-to-all | bytes 1572864 | tf_op jit(solution)/shard_map/all_to_all | solution.py:892
  565.1 42.6 %reduce-scatter.9.cloned.1.call-done = bf16[512,1408]{1,0:T(8,128)(2,1)} async-done(((bf16[2048,1408]{1,0:T(8,128)(2,1)}), bf16[512,1408]{1,0:T(8,128)(2,1)}) %reduce-scatter.9.cloned.1.call-update) | async-done | bytes 1441808 | tf_op jit(solution)/shard_map/reduce_scatter | solution.py:900
  607.7 1.8 copy.106
  609.6 38.5 %all_to_all.44 = bf16[4,128,1408]{1,2,0:T(8,128)(2,1)S(1)} all-to-all(bf16[4,128,1408]{1,2,0:T(8,128)(2,1)S(1)} %copy.106), channel_id=1, replica_groups=mesh['dp'=4,'row'=2,'col'=4] {'col'}, dimensions={0} | all-to-all | bytes 2883584 | tf_op jit(solution)/shard_map/all_to_all | solution.py:892
  648.1 1.2 copy.107
  650.2 1.9 dynamic_slice.32.grad_middle
  652.1 7.1 convolution_convert_fusion.4.part
  659.2 52.4 %input_grad_sum.1 = (f32[512,512]{1,0:T(8,128)}, f32[8,512]{1,0:T(8,128)}) custom-call(bf16[1024,2048]{1,0:T(8,128)(2,1)} %convolution_convert_fusion.4.part, f32[512,512]{1,0:T(8,128)} %get-tuple-element.60.xhat, f32[512,128]{1,0:T(8,128)} %get-tuple-element.61.rstd, f32[1,512]{1,0:T(1,128)} %bitcast.153, bf16[512,512]{1,0:T(8,128)(2,1)} %dynamic_slice.32.grad_middle), custom_call_target="tpu_custom_call" | custom-call | flops 44999999488 | bytes 10000000 | tf_op jit(solution)/shard_map/input_grad_sum/pallas_call | solution.py:520
  713.2 39.5 %psum.7 = f32[14336]{0:T(1024)S(1)} all-reduce(f32[14336]{0:T(1024)S(1)} %pad_maximum_fusion.2), channel_id=1, replica_groups=mesh['dp'=4,'row'=2,'col'=4] {'dp','row','col'}, use_global_device_ids=true, to_apply=%region_0.1 | all-reduce | flops 14336 | bytes 114688 | tf_op jit(solution)/shard_map/psum | solution.py:1013
  754.1 1.5 convert_bitcast_fusion.1
  755.6 1.6 copy.104
  757.2 2.6 convert_bitcast_fusion
  759.8 3.2 copy.109
  763.0 5.5 copy.110
  768.5 26.9 %all-gather.19.cloned.1.call-done = bf16[512,2,2816]{0,2,1:T(8,128)(2,1)} async-done(((bf16[128,2,2816]{0,2,1:T(8,128)(2,1)}), bf16[512,2,2816]{0,2,1:T(8,128)(2,1)}) %all-gather.19.cloned.1.call-update) | async-done | bytes 5767184 | tf_op jit(solution)/shard_map/all_gather | solution.py:910
  795.3 15.7 %copy.111 = f32[512,2,2816]{2,1,0:T(2,128)} copy(bf16[512,2,2816]{0,2,1:T(8,128)(2,1)} %all-gather.19.cloned.1.call-done) | data formatting | bytes 17301504
  811.0 1.9 copy.132
  812.9 2.3 copy.133
  (108 shorter events, 13.5 us)
Async XLA Ops:
  7.2 8.2 copy-start
  9.0 15.2 %all-to-all-start.1 = ((bf16[4,64,512]{2,1,0:T(8,128)(2,1)}), bf16[4,64,512]{2,1,0:T(8,128)(2,1)S(1)}, u32[]{:S(2)}, u32[]{:S(2)}) async-start(bf16[4,64,512]{2,1,0:T(8,128)(2,1)} %dynamic-slice_bitcast_fusion.1), calls=%async_computation.1 | async-start | bytes 524288 | tf_op jit(solution)/shard_map/all_to_all | solution.py:892
  15.3 140.7 %all-gather.21.cloned.1.call-start = ((), (), s32[]{:S(2)}) async-start(), calls=%async_computation.20 | async-start | bytes 3932160 | tf_op jit(solution)/shard_map/all_gather | solution.py:872
  54.8 36.7 %all-to-all-start.2 = ((bf16[4,128,1408]{1,2,0:T(8,128)(2,1)}), bf16[4,128,1408]{1,2,0:T(8,128)(2,1)S(1)}, u32[]{:S(2)}, u32[]{:S(2)}) async-start(bf16[4,128,1408]{1,2,0:T(8,128)(2,1)} %bitcast.15), calls=%async_computation.2 | async-start | bytes 2883584 | tf_op jit(solution)/shard_map/all_to_all | solution.py:892
  58.4 34.7 %copy-start.10 = (f32[3,256]{1,0:T(4,128)S(1)}, f32[3,256]{1,0:T(4,128)}, u32[]{:S(2)}) copy-start(f32[3,256]{1,0:T(4,128)} %param.15) | copy-start | bytes 9220
  58.4 35.3 %copy-start.11 = (f32[512]{0:T(512)S(1)}, f32[512]{0:T(512)}, u32[]{:S(2)}) copy-start(f32[512]{0:T(512)} %param.13) | copy-start | bytes 6148
  58.4 35.3 %copy-start.12 = (f32[512]{0:T(512)S(1)}, f32[512]{0:T(512)}, u32[]{:S(2)}) copy-start(f32[512]{0:T(512)} %param.17) | copy-start | bytes 6148
  58.4 35.3 %copy-start.13 = (f32[512]{0:T(512)S(1)}, f32[512]{0:T(512)}, u32[]{:S(2)}) copy-start(f32[512]{0:T(512)} %param.18) | copy-start | bytes 6148
  58.4 35.3 %copy-start.14 = (f32[512]{0:T(512)S(1)}, f32[512]{0:T(512)}, u32[]{:S(2)}) copy-start(f32[512]{0:T(512)} %param.12) | copy-start | bytes 6148
  58.5 150.4 %all-gather.13.cloned.1.call-start = ((), (), s32[]{:S(2)}) async-start(), calls=%async_computation.12 | async-start | bytes 1310720 | tf_op jit(solution)/shard_map/all_gather | solution.py:886
  59.3 226.9 %all-gather.23.cloned.1.call-start = ((), (), s32[]{:S(2)}) async-start(), calls=%async_computation.21 | async-start | bytes 7208960 | tf_op jit(solution)/shard_map/all_gather | solution.py:872
  97.6 57.3 %all-to-all-start.3 = ((bf16[4,176,512]{2,1,0:T(8,128)(2,1)}), bf16[4,176,512]{2,1,0:T(8,128)(2,1)S(1)}, u32[]{:S(2)}, u32[]{:S(2)}) async-start(bf16[4,176,512]{2,1,0:T(8,128)(2,1)} %dynamic-slice_bitcast_fusion), calls=%async_computation.3 | async-start | bytes 1441792 | tf_op jit(solution)/shard_map/all_to_all | solution.py:892
  101.1 214.7 %all-gather.15.cloned.1.call-start = ((), (), s32[]{:S(2)}) async-start(), calls=%async_computation.13 | async-start | bytes 3604480 | tf_op jit(solution)/shard_map/all_gather | solution.py:886
  155.9 336.8 %reduce-scatter.7.cloned.1.call-start = ((), (), s32[]{:S(2)}) async-start(), calls=%async_computation.16 | async-start | bytes 1310720 | tf_op jit(solution)/shard_map/reduce_scatter | solution.py:916
  156.0 3.1 copy-start.16
  158.3 5.9 copy-start.4
  286.1 3.9 copy-start.19
  289.5 7.1 copy-start.3
  296.6 2.9 copy-start.2
  296.7 4.3 copy-start.9
  300.9 14.9 %copy-start.5 = (bf16[1024,704]{1,0:T(8,128)(2,1)}, bf16[1024,704]{1,0:T(8,128)(2,1)S(1)}, u32[]{:S(2)}) copy-start(bf16[1024,704]{1,0:T(8,128)(2,1)S(1)} %multiply_convert_fusion.2) | copy-start | bytes 4325380
  325.1 2.2 copy-start.20
  325.1 10.8 %slice-start = ((s8[5767168]{0:T(1024)(128)(4,1)}), s8[4194304]{0:T(1024)(128)(4,1)S(1)}, s32[]{:S(2)}) async-start(s8[5767168]{0:T(1024)(128)(4,1)} %bitcast.117), calls=%async_computation.24 | async-start | bytes 8388608
  327.3 8.6 %slice-start.1 = ((s8[5767168]{0:T(1024)(128)(4,1)}), s8[1572864]{0:T(1024)(128)(4,1)S(1)}, s32[]{:S(2)}) async-start(s8[5767168]{0:T(1024)(128)(4,1)} %bitcast.117), calls=%async_computation.25 | async-start | bytes 3145728
  344.1 70.6 %copy-start.7 = (bf16[1024,256]{1,0:T(8,128)(2,1)S(1)}, bf16[1024,256]{1,0:T(8,128)(2,1)}, u32[]{:S(2)}) copy-start(bf16[1024,256]{1,0:T(8,128)(2,1)} %get-tuple-element.46) | copy-start | bytes 1572868
  419.2 1.2 copy-start.8
  419.2 85.2 %reduce-scatter.11.cloned.1.call-start = ((), (), s32[]{:S(2)}) async-start(), calls=%async_computation.19 | async-start | bytes 3604480 | tf_op jit(solution)/shard_map/reduce_scatter | solution.py:916
  419.8 5.1 copy-start.6
  419.8 118.3 %reduce-scatter.5.cloned.1.call-start = ((), (), s32[]{:S(2)}) async-start(), calls=%async_computation.14 | async-start | bytes 3932160 | tf_op jit(solution)/shard_map/reduce_scatter | solution.py:900
  420.4 4.4 copy-start.15
  429.8 49.7 %copy-start.17 = (bf16[1024,2048]{1,0:T(8,128)(2,1)S(1)}, bf16[1024,2048]{1,0:T(8,128)(2,1)}, u32[]{:S(2)}) copy-start(bf16[1024,2048]{1,0:T(8,128)(2,1)} %get-tuple-element.41) | copy-start | bytes 12582916
  486.7 121.1 %reduce-scatter.9.cloned.1.call-start = ((), (), s32[]{:S(2)}) async-start(), calls=%async_computation.17 | async-start | bytes 7208960 | tf_op jit(solution)/shard_map/reduce_scatter | solution.py:900
  492.6 261.5 %all-gather.25.cloned.1.call-start = ((), (), s32[]{:S(2)}) async-start(), calls=%async_computation.22 | async-start | bytes 1310720 | tf_op jit(solution)/shard_map/all_gather | solution.py:922
  504.3 252.8 %all-gather.27.cloned.1.call-start = ((), (), s32[]{:S(2)}) async-start(), calls=%async_computation.23 | async-start | bytes 3604480 | tf_op jit(solution)/shard_map/all_gather | solution.py:922
  524.3 238.7 %all-gather.17.cloned.1.call-start = ((), (), s32[]{:S(2)}) async-start(), calls=%async_computation.15 | async-start | bytes 3932160 | tf_op jit(solution)/shard_map/all_gather | solution.py:910
  565.1 230.3 %all-gather.19.cloned.1.call-start = ((), (), s32[]{:S(2)}) async-start(), calls=%async_computation.18 | async-start | bytes 7208960 | tf_op jit(solution)/shard_map/all_gather | solution.py:910
  648.1 4.0 copy-start.18
  795.3 19.9 %copy-start.1 = (bf16[512,3,1024]{2,0,1:T(8,128)(2,1)S(1)}, bf16[512,3,1024]{2,0,1:T(8,128)(2,1)}, u32[]{:S(2)}) copy-start(bf16[512,3,1024]{2,0,1:T(8,128)(2,1)} %param.14) | copy-start | bytes 9437188
Sparse Core Ops, SparseCore 0:
  47.4 43.0 all-gather.20
  92.9 26.6 all-gather.12
  122.0 65.7 all-gather.22
  189.5 41.8 all-gather.14
  419.3 26.4 reduce-scatter.6
  449.0 41.7 reduce-scatter.10
  494.1 43.9 reduce-scatter.4
  541.9 65.7 reduce-scatter.8
  609.7 26.5 all-gather.24
  638.2 41.7 all-gather.26
  682.6 44.4 all-gather.16
  728.9 66.3 all-gather.18

commit v4 on v3

--- a/solution.py
+++ b/solution.py
@@ -2,6 +2,7 @@
 
 import jax
 import jax.numpy as jnp
+import numpy as np
 from jax import lax
 from jax.experimental import pallas as pl
 from jax.experimental.pallas import tpu as pltpu
@@ -32,7 +33,7 @@
     )
 
 
-def enter(cols, everyone=False):
+def enter(cols, everyone=False, dp=1):
     r, c = lax.axis_index("row"), lax.axis_index("col")
     barrier = pltpu.get_barrier_semaphore()
     pl.semaphore_signal(barrier, inc=1, device_id={"row": 1 - r}, device_id_type=MESH)
@@ -41,7 +42,14 @@
             pl.semaphore_signal(
                 barrier, inc=1, device_id={"col": lax.rem(c + k, cols)}, device_id_type=MESH
             )
-        pl.semaphore_wait(barrier, cols)
+        for k in range(1, dp):
+            pl.semaphore_signal(
+                barrier,
+                inc=1,
+                device_id={"dp": lax.rem(lax.axis_index("dp") + k, dp)},
+                device_id_type=MESH,
+            )
+        pl.semaphore_wait(barrier, cols + dp - 1)
         return
 
     @pl.when(c > 0)
@@ -64,6 +72,8 @@
 
 
 LAG = 3
+BLOCK = 256
+PACE = 6
 
 
 class Reduce:
@@ -291,6 +301,134 @@
             pltpu.SemaphoreType.DMA((cols, subs)),
             pltpu.SemaphoreType.DMA((cols, subs)),
         ]
+
+
+class Exchange:
+    def __init__(self, axis, size, source, target, sems):
+        self.axis, self.size, self.source, self.target = axis, size, source, target
+        self.send, self.recv, self.local = sems
+        self.c = lax.axis_index(axis)
+
+    def hop(self, k):
+        to = lax.rem(self.c + k, self.size)
+        return send(
+            self.source.at[to],
+            self.target.at[self.c],
+            self.send.at[k - 1],
+            self.recv.at[k - 1],
+            **{self.axis: to},
+        )
+
+    def own(self):
+        return pltpu.make_async_copy(
+            self.source.at[self.c], self.target.at[self.c], self.local.at[0]
+        )
+
+    def start(self):
+        for k in range(1, self.size):
+            self.hop(k).start()
+        self.own().start()
+
+    def finish(self):
+        self.own().wait()
+        for k in range(1, self.size):
+            self.hop(k).wait_recv()
+        for k in range(1, self.size):
+            self.hop(k).wait_send()
+
+    @staticmethod
+    def scratch(size):
+        return [
+            pltpu.SemaphoreType.DMA((size - 1,)),
+            pltpu.SemaphoreType.DMA((size - 1,)),
+            pltpu.SemaphoreType.DMA((1,)),
+        ]
+
+
+class Broadcast:
+    def __init__(self, source, target, sems):
+        self.dp, self.source, self.target = target.shape[0], source, target
+        self.send, self.recv, self.local = sems
+        self.me = lax.axis_index("dp")
+
+    def hop(self, k):
+        return send(
+            self.source,
+            self.target.at[self.me],
+            self.send.at[k - 1],
+            self.recv.at[k - 1],
+            dp=lax.rem(self.me + k, self.dp),
+        )
+
+    def own(self):
+        return pltpu.make_async_copy(self.source, self.target.at[self.me], self.local.at[0])
+
+    def start(self):
+        for k in range(1, self.dp):
+            self.hop(k).start()
+        self.own().start()
+
+    def finish(self):
+        self.own().wait()
+        for k in range(1, self.dp):
+            self.hop(k).wait()
+
+
+ANY = pl.BlockSpec(memory_space=pl.ANY)
+
+
+def exchange_kernel(cols, count, *refs):
+    enter(cols, everyone=True)
+    sems = refs[2 * count :]
+    riders = [
+        Exchange("col", cols, refs[i], refs[count + i], sems[3 * i : 3 * i + 3]) for i in range(count)
+    ]
+    for rider in riders:
+        rider.start()
+    for rider in riders:
+        rider.finish()
+
+
+def exchange(cols, number, *pieces):
+    count = len(pieces)
+    return pl.pallas_call(
+        functools.partial(exchange_kernel, cols, count),
+        out_shape=tuple(jax.ShapeDtypeStruct(p.shape, p.dtype) for p in pieces),
+        in_specs=[ANY] * count,
+        out_specs=(ANY,) * count,
+        scratch_shapes=Exchange.scratch(cols) * count,
+        compiler_params=params(number),
+        cost_estimate=cost(25),
+        name="exchange",
+    )(*pieces)
+
+
+def load_columns(weight, whole, sem):
+    dp, cols, part, _ = weight.shape
+    copies = [
+        pltpu.make_async_copy(
+            weight.at[p, j],
+            whole.at[pl.ds((j * dp + p) * part, part), :],
+            sem.at[p, j],
+        )
+        for p in range(dp)
+        for j in range(cols)
+    ]
+    for copy in copies:
+        copy.start()
+    return copies
+
+
+def dot_nt(a, b):
+    return lax.dot_general(a, b, (((1,), (1,)), ((), ())), preferred_element_type=F32)
+
+
+def dot_tn(a, b):
+    return lax.dot_general(a, b, (((0,), (0,)), ((), ())), preferred_element_type=F32)
+
+
+def dot_nn(a, b):
+    return jnp.dot(a, b, preferred_element_type=F32)
 
 
 def moments(rows):
@@ -370,7 +508,23 @@
     )(part, tokens_own, vectors)
 
 
-def norm_two_back_kernel(cols, part, middle, cotan_own, vectors, grads, sums, *scratch):
+def norm_two_back_kernel(
+    cols,
+    part,
+    middle,
+    cotan_own,
+    vectors,
+    hidden,
+    weight,
+    grads,
+    sums,
+    mixed_part,
+    down,
+    sem,
+    *scratch
+):
+    narrow = hidden.shape[1]
+    copies = load_columns(weight, down, sem)
     half, width = part.shape[0] // 2, part.shape[1]
     own = half // cols
     step = own // SUBS
@@ -381,6 +535,9 @@
     )
     spread = Gather(cols, SUBS, row_spot(own, step, half, width), grads, scratch[7:11])
     summing.start()
+    blocks = part.shape[0] // BLOCK
+    for copy in copies:
+        copy.wait()
     sums[...] = jnp.zeros_like(sums)
 
     def land(s):
@@ -407,27 +564,36 @@
         summing.landed(t, land)
         spread.slot(t, summing.landing, summing.per_sub)
 
+        @pl.when((lax.rem(t, PACE) == PACE - 1) & (t < PACE * blocks))
+        def _():
+            rows = pl.ds(pl.multiple_of(lax.div(t, PACE) * BLOCK, BLOCK), BLOCK)
+            result = dot_nt(hidden[rows, :], down[:, :narrow])
+            mixed_part[rows, :] = result.astype(BF16)
+
     spread.finish()
     summing.finish()
 
 
-def norm_two_back(cols, part, middle, cotan_own, vectors):
+def norm_two_back(cols, part, middle, cotan_own, vectors, hidden, weight):
     group, width = part.shape
+    tall = weight.shape[3]
     return pl.pallas_call(
         functools.partial(norm_two_back_kernel, cols),
         out_shape=(
             jax.ShapeDtypeStruct((group, width), BF16),
             jax.ShapeDtypeStruct((8, width), F32),
+            jax.ShapeDtypeStruct((group, width), BF16),
         ),
-        in_specs=[VM] * 4,
-        out_specs=(VM, VM),
-        scratch_shapes=Reduce.scratch(cols, SUBS, group // 2, width)
+        in_specs=[VM] * 5 + [ANY],
+        out_specs=(VM,) * 3,
+        scratch_shapes=[pltpu.VMEM((width, tall), BF16), pltpu.SemaphoreType.DMA(weight.shape[:2])]
+        + Reduce.scratch(cols, SUBS, group // 2, width)
         + Gather.scratch(cols, SUBS)
         + [pltpu.VMEM((group // 2 // cols // SUBS, width), F32)],
         compiler_params=params(3),
         cost_estimate=cost(60),
         name="grad_sum_norm_gather",
-    )(part, middle, cotan_own, vectors)
+    )(part, middle, cotan_own, vectors, hidden, weight)
 
 
 def mixed_sum(cols, part, middle, scratch):
@@ -452,11 +618,57 @@
     )
 
 
-def first_kernel(cols, part, xhat, rstd, gain, grad_middle, result, sums, *scratch):
+def mixed_kernel(cols, part, middle, piece, mixed, pieces, *scratch):
+    half = part.shape[0] // 2
+    step = half // SUBS
+    total = scratch[7]
+    enter(cols, everyone=True, dp=pieces.shape[0])
+    rider = Broadcast(piece, pieces, scratch[8:])
+    rider.start()
+    summing = mixed_sum(cols, part, middle, scratch[:7])
+    summing.start()
+
+    def land(s):
+        summing.land(s, total)
+        mixed[pl.ds(pl.multiple_of(s * step, step), step), :] = total[...].astype(BF16)
+
+    @pl.loop(0, summing.slots)
+    def _(t):
+        summing.slot(t)
+        summing.landed(t, land)
+
+    summing.finish()
+    rider.finish()
+
+
+def sum_mixed(cols, part, middle, piece, dp):
+    group, width = part.shape
+    return pl.pallas_call(
+        functools.partial(mixed_kernel, cols),
+        out_shape=(
+            jax.ShapeDtypeStruct((group // 2, width // cols), BF16),
+            jax.ShapeDtypeStruct((dp,) + piece.shape, BF16),
+        ),
+        in_specs=[VM] * 2 + [ANY],
+        out_specs=(VM, ANY),
+        scratch_shapes=Reduce.scratch(cols, SUBS, group // 2, width)
+        + [pltpu.VMEM((group // 2 // SUBS, width // cols), F32)]
+        + Exchange.scratch(dp),
+        compiler_params=params(4),
+        cost_estimate=cost(45),
+        name="mixed_sum",
+    )(part, middle, piece)
+
+
+def first_kernel(
+    cols, part, xhat, rstd, gain, grad_middle, pieces_from, result, sums, pieces_to, *scratch
+):
+    dp = pieces_from.shape[0]
     half, width = part.shape[0] // 2, part.shape[1]
     step, depth = half // SUBS, width // cols
-    total, grad, mine, theirs, out_sem, in_sem = scratch[7:]
-    enter(cols, everyone=True)
+    total, grad, mine, theirs, out_sem, in_sem = scratch[7:13]
+    enter(cols, everyone=True, dp=dp)
+    rider = Exchange("dp", dp, pieces_from, pieces_to, scratch[13:])
     c = lax.axis_index("col")
     summing = Reduce(
         cols,
@@ -467,6 +679,7 @@
         scratch[3:7],
     )
     summing.start()
+    rider.start()
     sums[...] = jnp.zeros_like(sums)
 
     def land(s):
@@ -512,9 +725,10 @@
     for k in range(1, cols):
         exchange(k).wait_send()
     summing.finish()
-
-
-def sum_first(cols, part, xhat, rstd, gain, grad_middle):
+    rider.finish()
+
+
+def sum_first(cols, part, xhat, rstd, gain, grad_middle, pieces):
     group, width = part.shape
     half, depth = group // 2, width // cols
     return pl.pallas_call(
@@ -522,9 +736,10 @@
         out_shape=(
             jax.ShapeDtypeStruct((half, depth), F32),
             jax.ShapeDtypeStruct((8, depth), F32),
+            jax.ShapeDtypeStruct(pieces.shape, BF16),
         ),
-        in_specs=[VM] * 5,
-        out_specs=(VM, VM),
+        in_specs=[VM] * 5 + [ANY],
+        out_specs=(VM, VM, ANY),
         scratch_shapes=Reduce.scratch(cols, SUBS, half, width)
         + [
             pltpu.VMEM((half // SUBS, depth), F32),
@@ -533,11 +748,12 @@
             pltpu.VMEM((cols - 1, 8, half), F32),
             pltpu.SemaphoreType.DMA((cols - 1,)),
             pltpu.SemaphoreType.DMA((cols - 1,)),
-        ],
+        ]
+        + Exchange.scratch(pieces.shape[0]),
         compiler_params=params(5),
         cost_estimate=cost(45),
         name="input_grad_sum",
-    )(part, xhat, rstd, gain, grad_middle)
+    )(part, xhat, rstd, gain, grad_middle, pieces)
 
 
 def norm_one_kernel(cols, tokens, vector, normed, tokens_own, xhat, rstd, vectors, *scratch):
@@ -633,17 +849,105 @@
     )(tokens, vector)
 
 
+def finish_kernel(
+    cols, pieces, second, first, bias, arranged, small, sums, landed, slices, mine, both, pair, all_dp, *sems
+):
+    dp, _, _, wide = pieces.shape
+    depth = first.shape[1]
+    narrow = wide // 4
+    enter(cols, everyone=True, dp=dp)
+    r, c, me = (lax.axis_index(name) for name in ("row", "col", "dp"))
+    names = Exchange("col", cols, second, slices, sems[:3])
+    names.start()
+    rider = Exchange("col", cols, sums, landed, sems[3:6])
+
+    def total(to):
+        value = pieces[0, to].astype(F32)
+        for p in range(1, dp):
+            value = value + pieces[p, to].astype(F32)
+        return value.astype(BF16)
+
+    for k in range(1, cols):
+        to = lax.rem(c + k, cols)
+        sums[to] = total(to)
+        rider.hop(k).start()
+    landed[c] = total(c)
+    names.finish()
+    mine[...] = jnp.zeros_like(mine)
+    mine[0:2, :depth] = first[0:2, :]
+    shift = slices[0]
+    for j in range(1, cols):
+        shift = shift + slices[j]
+    mine[2:4, :depth] = shift[0:2, :]
+    mine[0:1, depth:] = bias[0:1, :]
+    across = send(mine, pair, sems[6].at[0], sems[6].at[1], row=1 - r)
+    across.start()
+    across.wait()
+    both[:, depth:] = mine[:, depth:]
+    both[:, :depth] = mine[:, :depth] + pair[:, :depth]
+
+    def hop(k):
+        to = lax.rem(me + k, dp)
+        return send(both, all_dp.at[me], sems[7].at[k - 1], sems[8].at[k - 1], dp=to)
+
+    for k in range(1, dp):
+        hop(k).start()
+    all_dp[me] = both[...]
+    for k in range(1, dp):
+        hop(k).wait()
+    value = all_dp[0]
+    for p in range(1, dp):
+        value = value + all_dp[p]
+    small[...] = value
+    for k in range(1, cols):
+        rider.hop(k).wait()
+    for k in range(4):
+        for j in range(cols):
+            arranged[k, :, j * narrow : (j + 1) * narrow] = landed[
+                j, :, k * narrow : (k + 1) * narrow
+            ]
+
+
+def finish(cols, pieces, second, first, bias):
+    dp, _, part, wide = pieces.shape
+    depth, biases = first.shape[1], bias.shape[1]
+    dma = pltpu.SemaphoreType.DMA
+    return pl.pallas_call(
+        functools.partial(finish_kernel, cols),
+        out_shape=(
+            jax.ShapeDtypeStruct((4, part, cols * wide // 4), BF16),
+            jax.ShapeDtypeStruct((8, depth + biases), F32),
+        ),
+        in_specs=[VM] * 4,
+        out_specs=(VM,) * 2,
+        scratch_shapes=[
+            pltpu.VMEM((cols, part, wide), BF16),
+            pltpu.VMEM((cols, part, wide), BF16),
+            pltpu.VMEM((cols, 8, depth), F32),
+            pltpu.VMEM((8, depth + biases), F32),
+            pltpu.VMEM((8, depth + biases), F32),
+            pltpu.VMEM((8, depth + biases), F32),
+            pltpu.VMEM((dp, 8, depth + biases), F32),
+        ]
+        + Exchange.scratch(cols) * 2
+        + [dma((2,)), dma((max(dp - 1, 1),)), dma((max(dp - 1, 1),))],
+        compiler_params=params(10),
+        cost_estimate=cost(25),
+        name="attention_grad_exchange",
+    )(pieces, second, first, bias)
+
+
 def rope_tables(length):
     half_rot = ROT // 2
-    lane = jnp.arange(2 * HD) % HD
-    inverse = ROPE_BASE ** (-2.0 * (lane % half_rot).astype(F32) / ROT)
-    angles = jnp.arange(length).astype(F32)[:, None] * inverse[None, :]
+    lane = np.arange(2 * HD) % HD
+    inverse = (ROPE_BASE ** (-2.0 * (lane % half_rot) / ROT)).astype(np.float32)
+    angles = np.arange(length).astype(np.float32)[:, None] * inverse[None, :]
     turning = lane < ROT
-    cosine = jnp.where(turning, jnp.cos(angles), 1.0)
-    sine = jnp.where(turning, jnp.sin(angles), 0.0)
-    lower = jnp.where(lane < half_rot, -sine, 0.0)
-    upper = jnp.where(lane >= half_rot, sine, 0.0)
-    return jnp.stack([cosine, lower, upper])
+    cosine = np.where(turning, np.cos(angles), 1.0)
+    sine = np.where(turning, np.sin(angles), 0.0)
+    lower = np.where(lane < half_rot, -sine, 0.0)
+    upper = np.where(lane >= half_rot, sine, 0.0)
+    return np.stack([cosine, lower, upper]).astype(np.float32)
 
 
 def turn(x, tables, back=False):
@@ -653,45 +957,49 @@
     return x * tables[0] - sines if back else x * tables[0] + sines
 
 
-def dot_nt(a, b):
-    return lax.dot_general(a, b, (((1,), (1,)), ((), ())), preferred_element_type=F32)
-
-
-def dot_tn(a, b):
-    return lax.dot_general(a, b, (((0,), (0,)), ((), ())), preferred_element_type=F32)
-
-
-def dot_nn(a, b):
-    return jnp.dot(a, b, preferred_element_type=F32)
-
-
-BLOCK = 256
-PACE = 2
-
-
 def causal(rows):
     return lax.broadcasted_iota(jnp.int32, (rows, rows), 0) >= lax.broadcasted_iota(
         jnp.int32, (rows, rows), 1
     )
 
 
-def attend_kernel(cols, qkv, bias, tables, cotan, heads_in, attn, logs, cotan_rows, *sems):
+def attend_kernel(
+    cols,
+    normed,
+    weight,
+    bias,
+    tables,
+    one_from,
+    two_from,
+    heads_in,
+    attn,
+    logs,
+    part,
+    one_to,
+    two_to,
+    whole,
+    sem,
+    qkv,
+    *sems
+):
     length, wide = attn.shape
     two = 2 * HD
-    half, depth = cotan.shape
-    subs = 2 * (wide // two)
-    step = half // subs
-
-    def spot(r, source, s):
-        rows = pl.ds(pl.multiple_of(r * half + s * step, 16), step)
-        return rows, pl.ds(pl.multiple_of(source * depth, 128), depth)
-
-    enter(cols)
-    spread = Gather(cols, subs, spot, cotan_rows, sems)
-    for s in range(subs):
-        cotan_rows[spot(spread.r, spread.c, s)] = cotan[s * step : (s + 1) * step, :]
-        spread.start(s)
+    copies = load_columns(weight, whole, sem)
+    enter(cols, everyone=True)
+    riders = (
+        Exchange("col", cols, one_from, one_to, sems[:3]),
+        Exchange("col", cols, two_from, two_to, sems[3:]),
+    )
+    for rider in riders:
+        rider.start()
+    for copy in copies:
+        copy.wait()
     first_head = lax.broadcasted_iota(jnp.int32, (BLOCK, two), 1) < HD
+
+    @pl.loop(0, length // BLOCK)
+    def _(m):
+        rows = pl.ds(pl.multiple_of(m * BLOCK, BLOCK), BLOCK)
+        qkv[rows, :] = dot_nn(normed[rows, :], whole[:, : 3 * wide]) + bias[0:1, :]
 
     @pl.loop(0, wide // two)
     def _(pair):
@@ -699,7 +1007,7 @@
             return pl.ds(pl.multiple_of(k * wide + pair * two, two), two)
 
         for k in range(3):
-            x = qkv[:, lanes(k)] + bias[0:1, lanes(k)]
+            x = qkv[:, lanes(k)]
             if k < 2:
                 x = turn(x, tables)
             if k == 0:
@@ -726,60 +1034,83 @@
             attn[rows, pl.ds(pl.multiple_of(pair * two, two), two)] = jnp.where(
                 first_head, outs[0], outs[1]
             ).astype(BF16)
-            if i % 2 == 1:
-                spread.relay(2 * pair + i // 2, 1)
-
-    for k in range(2, cols):
-
-        @pl.loop(0, subs)
-        def _(s):
-            spread.relay(s, k)
-
-    spread.finish()
-
-
-def attend(cols, qkv, bias, tables, cotan):
-    length, wide = qkv.shape[0], qkv.shape[1] // 3
-    subs = wide // HD
+
+    @pl.loop(0, length // BLOCK)
+    def _(m):
+        rows = pl.ds(pl.multiple_of(m * BLOCK, BLOCK), BLOCK)
+        part[rows, :] = dot_nt(attn[rows, :], whole[:, 3 * wide :]).astype(BF16)
+
+    for rider in riders:
+        rider.finish()
+
+
+def attend(cols, normed, weight, bias, tables, one, two):
+    length, width = normed.shape
+    dp = weight.shape[0]
+    wide = weight.shape[3] // 4
     return pl.pallas_call(
         functools.partial(attend_kernel, cols),
         out_shape=(
-            jax.ShapeDtypeStruct(qkv.shape, BF16),
+            jax.ShapeDtypeStruct((length, 3 * wide), BF16),
             jax.ShapeDtypeStruct((length, wide), BF16),
             jax.ShapeDtypeStruct((wide // (2 * HD), 2, length, 128), F32),
-            jax.ShapeDtypeStruct((2 * cotan.shape[0], cols * cotan.shape[1]), BF16),
+            jax.ShapeDtypeStruct((length, width), BF16),
+            jax.ShapeDtypeStruct(one.shape, BF16),
+            jax.ShapeDtypeStruct(two.shape, BF16),
         ),
-        in_specs=[VM] * 4,
-        out_specs=(VM,) * 4,
-        scratch_shapes=Gather.scratch(cols, subs),
+        in_specs=[VM, ANY, VM, VM, ANY, ANY],
+        out_specs=(VM,) * 4 + (ANY,) * 2,
+        scratch_shapes=[
+            pltpu.VMEM((width, 4 * wide), BF16),
+            pltpu.SemaphoreType.DMA((dp, cols)),
+            pltpu.VMEM((length, 3 * wide), F32),
+        ]
+        + Exchange.scratch(cols) * 2,
         compiler_params=params(6),
-        cost_estimate=cost(40),
-        name="attention_cotangent_gather",
-    )(qkv, bias, tables, cotan)
+        cost_estimate=cost(50),
+        name="attention_weight_exchange",
+    )(normed, weight, bias, tables, one, two)
 
 
 def attend_back_kernel(
-    cols, heads_in, logs, grad, tables, part, middle, result, sums, mixed, *scratch
+    cols,
+    heads_in,
+    logs,
+    grad_middle,
+    tables,
+    weight,
+    normed,
+    attn,
+    pieces_from,
+    weight_grad,
+    normed_grad,
+    sums,
+    arranged,
+    queries_grad,
+    keys_grad,
+    values_grad,
+    whole,
+    sem,
+    grad,
+    result,
+    pieces_to,
+    *sems
 ):
-    length, wide = grad.shape
+    length, wide = attn.shape
     two = 2 * HD
-    queries_grad, keys_grad, values_grad, total = scratch[:4]
-    step = part.shape[0] // 2 // SUBS
-    enter(cols)
-    summing = mixed_sum(cols, part, middle, scratch[4:])
-    summing.start()
-
-    def land(s):
-        summing.land(s, total)
-        mixed[pl.ds(pl.multiple_of(s * step, step), step), :] = total[...].astype(BF16)
-
-    def slot(t):
-        summing.slot(t)
-        summing.landed(t, land)
-
-    blocks = length // BLOCK
-    done = wide // two * blocks * PACE
+    dp, _, part_rows, _ = weight.shape
+    copies = load_columns(weight, whole, sem)
+    enter(cols, everyone=True)
+    rider = Exchange("col", cols, pieces_from, pieces_to, sems)
+    rider.start()
+    for copy in copies:
+        copy.wait()
     first_head = lax.broadcasted_iota(jnp.int32, (BLOCK, two), 1) < HD
+
+    @pl.loop(0, length // BLOCK)
+    def _(m):
+        rows = pl.ds(pl.multiple_of(m * BLOCK, BLOCK), BLOCK)
+        grad[rows, :] = dot_nn(grad_middle[rows, :], whole[:, 3 * wide :]).astype(BF16)
 
     @pl.loop(0, wide // two)
     def _(pair):
@@ -811,11 +1142,6 @@
                 keys_grad[0:keep, :] += dot_tn(scores_grad, query_h)
                 values_grad[0:keep, :] += dot_tn(probs.astype(BF16), grad_h)
             queries_grad[rows, :] = jnp.where(first_head, outs[0], outs[1]) * HD ** (-0.5)
-
-            @pl.loop(0, PACE)
-            def _(u):
-                slot((pair * blocks + i) * PACE + u)
-
         grads = (
             turn(queries_grad[...], tables, back=True),
             turn(keys_grad[...], tables, back=True),
@@ -827,100 +1153,343 @@
             column_sum = jnp.sum(low.astype(F32), axis=0, keepdims=True)
             sums[:, lanes(k)] = jnp.broadcast_to(column_sum, (8, two))
 
-    @pl.loop(done, max(done, summing.slots))
-    def _(t):
-        slot(t)
-
-    summing.finish()
-
-
-def attend_back(cols, heads_in, logs, grad, tables, part, middle):
-    length, wide = grad.shape
-    group, width = part.shape
+    depth = normed.shape[1] // cols
+
+    @pl.loop(0, cols)
+    def _(j):
+        columns = pl.ds(pl.multiple_of(j * depth, depth), depth)
+        heads_grad = dot_tn(normed[:, columns], result[...]).astype(BF16)
+        out_grad = dot_tn(grad_middle[:, columns], attn[...]).astype(BF16)
+        for p in range(dp):
+            rows = slice(p * part_rows, (p + 1) * part_rows)
+            weight_grad[p, j, :, : 3 * wide] = heads_grad[rows, :]
+            weight_grad[p, j, :, 3 * wide :] = out_grad[rows, :]
+
+    @pl.loop(0, length // BLOCK)
+    def _(m):
+        rows = pl.ds(pl.multiple_of(m * BLOCK, BLOCK), BLOCK)
+        normed_grad[rows, :] = dot_nt(result[rows, :], whole[:, : 3 * wide]).astype(BF16)
+
+    rider.finish()
+    share = arranged.shape[2] // cols
+    for k in range(arranged.shape[0]):
+        arranged[k] = jnp.concatenate(
+            [pieces_to[j, :, k * share : (k + 1) * share] for j in range(cols)], axis=1
+        )
+
+
+def attend_back(cols, heads_in, logs, grad_middle, tables, weight, normed, attn, pieces, share):
+    length, wide = attn.shape
+    width = normed.shape[1]
     return pl.pallas_call(
         functools.partial(attend_back_kernel, cols),
         out_shape=(
-            jax.ShapeDtypeStruct(heads_in.shape, BF16),
+            jax.ShapeDtypeStruct(weight.shape, BF16),
+            jax.ShapeDtypeStruct((length, width), BF16),
             jax.ShapeDtypeStruct((8, 3 * wide), F32),
-            jax.ShapeDtypeStruct((group // 2, width // cols), BF16),
+            jax.ShapeDtypeStruct((3, pieces.shape[1], cols * share), BF16),
         ),
-        in_specs=[VM] * 6,
-        out_specs=(VM,) * 3,
+        in_specs=[VM] * 4 + [ANY, VM, VM, ANY],
+        out_specs=(VM,) * 4,
         scratch_shapes=[pltpu.VMEM((length, 2 * HD), F32)] * 3
-        + [pltpu.VMEM((group // 2 // SUBS, width // cols), F32)]
-        + Reduce.scratch(cols, SUBS, group // 2, width),
-        compiler_params=params(4),
-        cost_estimate=cost(45),
-        name="attention_back_mixed_sum",
-    )(heads_in, logs, grad, tables, part, middle)
-
-
-def dot(spec, a, b):
-    return jnp.einsum(spec, a, b, preferred_element_type=F32)
+        + [
+            pltpu.VMEM((width, 4 * wide), BF16),
+            pltpu.SemaphoreType.DMA(weight.shape[:2]),
+            pltpu.VMEM((length, wide), BF16),
+            pltpu.VMEM((length, 3 * wide), BF16),
+            pltpu.VMEM(pieces.shape, BF16),
+        ]
+        + Exchange.scratch(cols),
+        compiler_params=params(8),
+        cost_estimate=cost(50),
+        name="attention_back_exchange",
+    )(heads_in, logs, grad_middle, tables, weight, normed, attn, pieces)
+
+
+def gate_up_kernel(cols, normed, weight, cotan, hidden, gate_part, up_part, cotan_rows, *scratch):
+    group, narrow = hidden.shape
+    half, depth = cotan.shape
+    step = half // SUBS
+    whole, sem = scratch[:2]
+    copies = load_columns(weight, whole, sem)
+    enter(cols)
+
+    def spot(r, source, s):
+        rows = pl.ds(pl.multiple_of(r * half + s * step, 16), step)
+        return rows, pl.ds(pl.multiple_of(source * depth, 128), depth)
+
+    spread = Gather(cols, SUBS, spot, cotan_rows, scratch[2:])
+    for s in range(SUBS):
+        cotan_rows[spot(spread.r, spread.c, s)] = cotan[s * step : (s + 1) * step, :]
+        spread.start(s)
+    for copy in copies:
+        copy.wait()
+    blocks = group // BLOCK
+    each = SUBS // blocks
+
+    @pl.loop(0, blocks)
+    def _(m):
+        rows = pl.ds(pl.multiple_of(m * BLOCK, BLOCK), BLOCK)
+        both = dot_nn(normed[rows, :], whole[...])
+        gate, up = both[:, :narrow], both[:, narrow:]
+        sig = 1.0 / (1.0 + jnp.exp(-gate))
+        active = gate * sig
+        hidden[rows, :] = (active * up).astype(BF16)
+        up_part[rows, :] = active
+        gate_part[rows, :] = up * sig * (1.0 + gate * (1.0 - sig))
+        for u in range(each):
+            spread.relay(m * each + u, 1)
+
+    for k in range(2, cols):
+
+        @pl.loop(0, SUBS)
+        def _(s):
+            spread.relay(s, k)
+
+    spread.finish()
+
+
+def gate_up(cols, normed, weight, cotan):
+    group, width = normed.shape
+    dp = weight.shape[0]
+    narrow = weight.shape[3] // 2
+    return pl.pallas_call(
+        functools.partial(gate_up_kernel, cols),
+        out_shape=(
+            jax.ShapeDtypeStruct((group, narrow), BF16),
+            jax.ShapeDtypeStruct((group, narrow), F32),
+            jax.ShapeDtypeStruct((group, narrow), F32),
+            jax.ShapeDtypeStruct((group, width), BF16),
+        ),
+        in_specs=[VM, ANY, VM],
+        out_specs=(VM,) * 4,
+        scratch_shapes=[
+            pltpu.VMEM((width, weight.shape[3]), BF16),
+            pltpu.SemaphoreType.DMA((dp, cols)),
+        ]
+        + Gather.scratch(cols, SUBS),
+        compiler_params=params(7),
+        cost_estimate=cost(35),
+        name="gate_up_cotangent_gather",
+    )(normed, weight, cotan)
+
+
+def hidden_back_kernel(
+    hidden_from,
+    gate_from,
+    up_from,
+    cotan_from,
+    gate_up_from,
+    down_from,
+    normed_from,
+    weight_to,
+    normed_to,
+    hidden,
+    gate_part,
+    up_part,
+    cotan,
+    gate_up,
+    down,
+    normed,
+    grads,
+    weight_grad,
+    normed_grad,
+    gate_up_sem,
+    down_sem,
+    block_sem,
+    whole_sem,
+    out_sem,
+    grad_sem,
+):
+    group, narrow = hidden.shape
+    dp, cols, part_rows, _ = gate_up_from.shape
+    wide = weight_grad.shape[3]
+    blocks = group // BLOCK
+    depth = normed.shape[1] // cols
+
+    def rows_of(m):
+        return pl.ds(pl.multiple_of(m * BLOCK, BLOCK), BLOCK)
+
+    def block_copies(m):
+        rows = rows_of(m)
+        pairs = ((cotan_from, cotan), (gate_from, gate_part), (up_from, up_part))
+        return [
+            pltpu.make_async_copy(a.at[rows, :], b.at[rows, :], block_sem.at[i, m])
+            for i, (a, b) in enumerate(pairs)
+        ]
+
+    down_copies = load_columns(down_from, down, down_sem)
+    for copy in block_copies(0):
+        copy.start()
+    gate_up_copies = load_columns(gate_up_from, gate_up, gate_up_sem)
+    for m in range(1, blocks):
+        for copy in block_copies(m):
+            copy.start()
+    whole_copies = [
+        pltpu.make_async_copy(hidden_from, hidden, whole_sem.at[0]),
+        pltpu.make_async_copy(normed_from, normed, whole_sem.at[1]),
+    ]
+    for copy in whole_copies:
+        copy.start()
+    for copy in down_copies:
+        copy.wait()
+
+    def normed_out(m):
+        rows = rows_of(m)
+        return pltpu.make_async_copy(normed_grad.at[rows, :], normed_to.at[rows, :], out_sem.at[m])
+
+    def weight_out(p, j):
+        return pltpu.make_async_copy(weight_grad.at[p, j], weight_to.at[p, j], grad_sem.at[p, j])
+
+    @pl.loop(0, blocks)
+    def _(m):
+        rows = rows_of(m)
+        for copy in block_copies(m):
+            copy.wait()
+        grad = dot_nn(cotan[rows, :], down[:, :narrow])
+        both = jnp.concatenate([grad * gate_part[rows, :], grad * up_part[rows, :]], axis=1)
+        grads[rows, :] = both.astype(BF16)
+
+    for copy in gate_up_copies:
+        copy.wait()
+
+    @pl.loop(0, blocks)
+    def _(m):
+        rows = rows_of(m)
+        normed_grad[rows, :] = dot_nt(grads[rows, :], gate_up[...]).astype(BF16)
+        normed_out(m).start()
+
+    for copy in whole_copies:
+        copy.wait()
+
+    @pl.loop(0, cols)
+    def _(j):
+        columns = pl.ds(pl.multiple_of(j * depth, depth), depth)
+        gate_up_grad = dot_tn(normed[:, columns], grads[...]).astype(BF16)
+        down_grad = dot_tn(cotan[:, columns], hidden[...]).astype(BF16)
+        for p in range(dp):
+            rows = slice(p * part_rows, (p + 1) * part_rows)
+            weight_grad[p, j, :, : 2 * narrow] = gate_up_grad[rows, :]
+            weight_grad[p, j, :, 2 * narrow : 3 * narrow] = down_grad[rows, :]
+            if wide > 3 * narrow:
+                weight_grad[p, j, :, 3 * narrow :] = jnp.zeros((part_rows, wide - 3 * narrow), BF16)
+            weight_out(p, j).start()
+
+    for m in range(blocks):
+        normed_out(m).wait()
+    for p in range(dp):
+        for j in range(cols):
+            weight_out(p, j).wait()
+
+
+def hidden_back(hidden, gate_part, up_part, cotan, gate_up, down, normed):
+    group, width = normed.shape
+    dp, cols, part, double = gate_up.shape
+    grad_shape = (dp, cols, part, double + down.shape[3])
+    blocks = group // BLOCK
+    dma = pltpu.SemaphoreType.DMA
+    return pl.pallas_call(
+        hidden_back_kernel,
+        out_shape=(
+            jax.ShapeDtypeStruct(grad_shape, BF16),
+            jax.ShapeDtypeStruct((group, width), BF16),
+        ),
+        in_specs=[ANY] * 7,
+        out_specs=(ANY,) * 2,
+        scratch_shapes=[
+            pltpu.VMEM(hidden.shape, BF16),
+            pltpu.VMEM(gate_part.shape, F32),
+            pltpu.VMEM(up_part.shape, F32),
+            pltpu.VMEM(cotan.shape, BF16),
+            pltpu.VMEM((width, double), BF16),
+            pltpu.VMEM((width, down.shape[3]), BF16),
+            pltpu.VMEM(normed.shape, BF16),
+            pltpu.VMEM((group, double), BF16),
+            pltpu.VMEM(grad_shape, BF16),
+            pltpu.VMEM((group, width), BF16),
+            dma((dp, cols)),
+            dma((dp, cols)),
+            dma((3, blocks)),
+            dma((2,)),
+            dma((blocks,)),
+            dma((dp, cols)),
+        ],
+        compiler_params=pltpu.CompilerParams(vmem_limit_bytes=VMEM_LIMIT),
+        cost_estimate=cost(30),
+        name="hidden_back",
+    )(hidden, gate_part, up_part, cotan, gate_up, down, normed)
+
+
+def split_kernel(whole, first, last):
+    count, rows = whole.shape[1] - 1, whole.shape[0] * whole.shape[2]
+    inner = first.shape[1] == count
+
+    def part(k):
+        return whole[:, k].reshape(rows, whole.shape[3]).astype(F32)
+
+    for k in range(count):
+        if inner:
+            first[:, k, :] = part(k)
+        else:
+            first[k] = part(k)
+    last[...] = part(count).T
+
+
+def weights_split(whole, inner):
+    dp, count, part, wide = whole.shape
+    rows = min(part, 128)
+    per = 128 // rows
+    depth = dp * part
+    count = count - 1
+    if inner:
+        shape, block, place = (depth, count, wide), (128, count, wide), lambda b: (b, 0, 0)
+    else:
+        shape, block, place = (count, depth, wide), (count, 128, wide), lambda b: (0, b, 0)
+    return pl.pallas_call(
+        split_kernel,
+        grid=(depth // 128,),
+        out_shape=(jax.ShapeDtypeStruct(shape, F32), jax.ShapeDtypeStruct((wide, depth), F32)),
+        in_specs=[
+            pl.BlockSpec(
+                (per, count + 1, rows, wide),
+                lambda b: (b * 128 // (per * part), 0, lax.rem(b, max(part // 128, 1)), 0),
+            )
+        ],
+        out_specs=(pl.BlockSpec(block, place), pl.BlockSpec((wide, 128), lambda b: (0, b))),
+        compiler_params=pltpu.CompilerParams(vmem_limit_bytes=VMEM_LIMIT),
+        cost_estimate=cost(8),
+        name="weight_gradients",
+    )(whole)
 
 
 def columns_piece(block, sizes):
-    dp, col = sizes["dp"], sizes["col"]
+    dp, cols = sizes["dp"], sizes["col"]
     depth, k, wide = block.shape
     part = depth // dp
     piece = lax.dynamic_slice_in_dim(block, lax.axis_index("dp") * part, part, 0)
-    piece = piece.reshape(part, k, col, wide // col).transpose(2, 0, 1, 3)
-    return piece.reshape(col, part, k * wide // col)
-
-
-def columns_whole(piece, sizes):
-    whole = lax.all_gather(piece, "dp", axis=0)
-    return whole.transpose(1, 0, 2, 3).reshape(-1, piece.shape[-1])
+    piece = piece.reshape(part, k, cols, wide // cols).transpose(2, 0, 1, 3)
+    return piece.reshape(cols, part, k * wide // cols)
 
 
 def rows_piece(block, sizes):
-    dp, col = sizes["dp"], sizes["col"]
-    tall, depth = block.shape
-    return lax.dynamic_index_in_dim(
-        block.reshape(col, dp, tall // col // dp, depth), lax.axis_index("dp"), 1, False
+    dp, cols = sizes["dp"], sizes["col"]
+    wide, depth = block.shape
+    part, narrow = depth // dp, wide // cols
+    piece = lax.dynamic_slice_in_dim(block, lax.axis_index("dp") * part, part, 1)
+    piece = piece.reshape(cols, narrow, part).transpose(0, 2, 1)
+    return jnp.pad(piece, ((0, 0), (0, 0), (0, -narrow % 128)))
+
+
+def weights_whole(piece):
+    return lax.all_gather(piece, "dp", axis=0)
+
+
+def weights_sum(pieces):
+    dp, cols, part, wide = pieces.shape
+    piece = lax.psum_scatter(
+        pieces.reshape(dp * cols * part, wide), "dp", scatter_dimension=0, tiled=True
     )
-
-
-def rows_whole(piece, sizes):
-    col, part, depth = piece.shape
-    return lax.all_gather(
-        piece.transpose(1, 0, 2).reshape(part, col * depth), "dp", axis=0, tiled=True
-    )
-
-
-def exchange(pieces):
-    return lax.all_to_all(pieces, "col", 0, 0, tiled=True)
-
-
-def columns_sum(grad, sizes):
-    dp, col = sizes["dp"], sizes["col"]
-    width, narrow = grad.shape
-    part = width // col // dp
-    pieces = grad.astype(BF16).reshape(col, dp, part, narrow).transpose(1, 0, 2, 3)
-    piece = lax.psum_scatter(
-        pieces.reshape(width, narrow), "dp", scatter_dimension=0, tiled=True
-    )
-    return piece.reshape(col, part, narrow)
-
-
-def columns_return(piece, k):
-    col, part, narrow = piece.shape
-    piece = piece.reshape(col, part, k, narrow // k).transpose(1, 2, 0, 3)
-    piece = piece.reshape(part, k, col * narrow // k)
-    return lax.all_gather(piece, "dp", axis=0, tiled=True).astype(F32)
-
-
-def rows_sum(grad, sizes):
-    dp, col = sizes["dp"], sizes["col"]
-    short, width = grad.shape
-    piece = lax.psum_scatter(grad.astype(BF16), "dp", scatter_dimension=0, tiled=True)
-    return piece.reshape(short // dp, col, width // col).transpose(1, 0, 2)
-
-
-def rows_return(piece):
-    col, part, depth = piece.shape
-    whole = lax.all_gather(piece, "dp", axis=0)
-    return whole.transpose(1, 0, 2, 3).reshape(-1, depth).astype(F32)
+    return piece.reshape(cols, part, wide)
 
 
 def make_body(sizes):
@@ -942,95 +1511,84 @@
         my_row, my_col, my_dp = (lax.axis_index(name) for name in ("row", "col", "dp"))
         half, depth = tokens.shape
         own = half // cols
-        heads_wide = qkv_bias.shape[1]
         tables = rope_tables(SEQ)
         vector = jnp.stack(
             [attention_norm_gain, attention_norm_bias, feedforward_norm_gain, feedforward_norm_bias]
         )
         vector = jnp.concatenate([vector, jnp.zeros_like(vector)])
-        qkv_piece = exchange(columns_piece(qkv_weight, sizes))
-        out_piece = exchange(rows_piece(out_weight, sizes))
-        tokens, qkv_piece, out_piece = lax.optimization_barrier((tokens, qkv_piece, out_piece))
-        qkv_w = columns_whole(qkv_piece, sizes)
-        out_w = rows_whole(out_piece, sizes)
+        attention_piece = jnp.concatenate(
+            [columns_piece(qkv_weight, sizes), rows_piece(out_weight, sizes)], axis=2
+        )
+        (attention_piece,) = exchange(cols, 9, attention_piece)
+        tokens, attention_piece = lax.optimization_barrier((tokens, attention_piece))
+        attention_w = weights_whole(attention_piece)
         gate_up_piece = columns_piece(gate_up_weight, sizes)
         down_piece = rows_piece(down_weight, sizes)
-        gate_up_piece, down_piece, qkv_piece = lax.optimization_barrier(
-            (gate_up_piece, down_piece, qkv_piece)
-        )
-        gate_up_w = columns_whole(exchange(gate_up_piece), sizes)
-        down_w = rows_whole(exchange(down_piece), sizes)
         normed_one, tokens_own, xhat_one, rstd_one, vectors = norm_one(cols, tokens, vector)
-
-        qkv = dot_nn(normed_one, qkv_w)
-        heads_in, attn, logs, cotan_rows = attend(
-            cols, qkv, qkv_bias.reshape(1, -1), tables, cotangent
-        )
+        heads_in, attn, logs, branch_part, gate_up_piece, down_piece = attend(
+            cols,
+            normed_one,
+            attention_w,
+            qkv_bias.reshape(1, -1),
+            tables,
+            gate_up_piece,
+            down_piece,
+        )
+        gate_up_w = weights_whole(gate_up_piece)
+        narrow = down_weight.shape[0] // cols
+        normed_two, middle = norm_two(cols, branch_part, tokens_own, vectors)
+        down_piece, normed_two = lax.optimization_barrier((down_piece, normed_two))
+        down_w = weights_whole(down_piece)
+        hidden, gate_part, up_part, cotan_rows = gate_up(cols, normed_two, gate_up_w, cotangent)
         cotan_own = lax.dynamic_slice_in_dim(cotan_rows, my_row * half + my_col * own, own, 0)
-        normed_two, middle = norm_two(cols, dot_nn(attn, out_w).astype(BF16), tokens_own, vectors)
-
-        gate_up = dot_nn(normed_two, gate_up_w)
-        wide = gate_up.shape[1] // 2
-        gate, up = gate_up[:, :wide], gate_up[:, wide:]
-        sig = jax.nn.sigmoid(gate)
-        hidden = (gate * sig * up).astype(BF16)
-        grad_down = dot_tn(hidden, cotan_rows).astype(BF16)
-        cotan_rows, grad_down = lax.optimization_barrier((cotan_rows, grad_down))
-        down_piece = exchange(rows_sum(grad_down, sizes))
-        grad_hidden = dot_nt(cotan_rows, down_w)
-        grad_gu = jnp.concatenate(
-            [grad_hidden * up * sig * (1.0 + gate * (1.0 - sig)), grad_hidden * gate * sig], axis=1
-        ).astype(BF16)
-        grad_gate_up = dot_tn(normed_two, grad_gu).astype(BF16)
-        grad_gu, grad_gate_up = lax.optimization_barrier((grad_gu, grad_gate_up))
-        gate_up_piece = exchange(columns_sum(grad_gate_up, sizes))
-        grad_middle, second = norm_two_back(
-            cols, dot_nt(grad_gu, gate_up_w).astype(BF16), middle, cotan_own, vectors
-        )
-        grad_attn = dot_nt(grad_middle, out_w).astype(BF16)
-        grad_out = dot_tn(attn, grad_middle).astype(BF16)
-        grad_qkv, bias_part, mixed = attend_back(
-            cols, heads_in, logs, grad_attn, tables, dot_nn(hidden, down_w).astype(BF16), middle
-        )
-        grad_qkv_weight = dot_tn(normed_one, grad_qkv).astype(BF16)
-        grad_qkv, grad_qkv_weight = lax.optimization_barrier((grad_qkv, grad_qkv_weight))
-        out_piece = exchange(rows_sum(grad_out, sizes))
-        qkv_piece = exchange(columns_sum(grad_qkv_weight, sizes))
+        hidden_grad, normed_part = hidden_back(
+            hidden, gate_part, up_part, cotan_rows, gate_up_w, down_w, normed_two
+        )
+        hidden_sum = weights_sum(hidden_grad)
+        grad_middle, second, mixed_part = norm_two_back(
+            cols, normed_part, middle, cotan_own, vectors, hidden, down_w
+        )
+        second = second.reshape(8, cols, depth).transpose(1, 0, 2)
         grad_block = lax.dynamic_slice(grad_middle, (my_row * half, my_col * depth), (half, depth))
-        input_grad, first = sum_first(
+        attention_grad, normed_part, bias_part, hidden_sum = attend_back(
             cols,
-            dot_nt(grad_qkv, qkv_w).astype(BF16),
+            heads_in,
+            logs,
+            grad_middle,
+            tables,
+            attention_w,
+            normed_one,
+            attn,
+            hidden_sum,
+            narrow,
+        )
+        hidden_sum = lax.all_gather(hidden_sum, "dp", axis=0)
+        input_grad, first, attention_grad = sum_first(
+            cols,
+            normed_part,
             xhat_one,
             rstd_one,
             attention_norm_gain.reshape(1, -1),
             grad_block,
-        )
-        mine = jnp.zeros((4, cols * depth), F32)
-        mine = lax.dynamic_update_slice(mine, first[:2], (0, my_col * depth))
-        mine = lax.dynamic_update_slice(mine, second[:2], (2, 0))
-        biases = jnp.zeros((sizes["row"] * cols, 3 * heads_wide), F32)
-        biases = lax.dynamic_update_slice(biases, bias_part[:1], (my_row * cols + my_col, 0))
-        small = lax.psum(
-            jnp.concatenate([mine.reshape(-1), biases.reshape(-1)]), ("dp", "row", "col")
-        )
-        norms = lax.dynamic_slice_in_dim(
-            small[: mine.size].reshape(mine.shape), my_col * depth, depth, 1
-        )
-        bias = lax.dynamic_index_in_dim(
-            small[mine.size :].reshape(biases.shape), my_row * cols + my_col, 0, False
-        ).reshape(3, heads_wide)
+            attention_grad,
+        )
+        attention_sum, small = finish(cols, attention_grad, second, first, bias_part)
+        mixed, attention_sum = sum_mixed(cols, mixed_part, middle, attention_sum, sizes["dp"])
+        grad_gate_up, grad_down = weights_split(hidden_sum, True)
+        grad_qkv_weight, grad_out = weights_split(attention_sum, False)
+        grad_qkv_weight = grad_qkv_weight.transpose(1, 0, 2)
         return (
             mixed,
             input_grad,
-            norms[0],
-            norms[1],
-            columns_return(qkv_piece, 3),
-            bias,
-            rows_return(out_piece),
-            norms[2],
-            norms[3],
-            columns_return(gate_up_piece, 2),
-            rows_return(down_piece),
+            small[0, :depth],
+            small[1, :depth],
+            grad_qkv_weight,
+            small[0, depth:].reshape(3, -1),
+            grad_out,
+            small[2, :depth],
+            small[3, :depth],
+            grad_gate_up,
+            grad_down,
         )
 
     return body

time: 833 us -> 669 us (0.80)
  Pallas kernels: 342 us -> 607 us
  blocking collectives: 154 us -> 0 us
  waiting for transfers between devices: 123 us -> 13.6 us
  matrix products: 83.5 us -> 0 us
  local copies, waits for them, and re-layouts: 82.8 us -> 23.6 us
  starting transfers between devices: 13.8 us -> 0.38 us
    pallas_call x0 -> x7, Pallas kernels: none -> 216 us  [the longest x1 72 us: sum_mixed(): pl.pallas_call(functools.partial(mixed_kernel, cols), out_shape=(jax.Shap...]
    all_to_all x5 -> x0, blocking collectives: 114 us -> none  [exchange(): return lax.all_to_all(pieces, 'col', 0, 0, tiled=True)]
    dot_general x12 -> x0, matrix products: 83.5 us -> none  [the longest x4 33.2 us: dot_tn(): lax.dot_general(a, b, (((0,), (0,)), ((), ())), preferred_element_type=F32)]
    reduce_scatter x4 -> x1, waiting for transfers between devices: 56.4 us -> 13.4 us  [weights_sum(): lax.psum_scatter(pieces.reshape(dp * cols * part, wide), 'dp', scatter_di...]
    psum x1 -> x0, blocking collectives: 39.5 us -> none  [body(): lax.psum(jnp.concatenate([mine.reshape(-1), biases.reshape(-1)]), ('dp',...]
    all_to_all x3 -> x0, waiting for transfers between devices: 38.7 us -> none  [exchange(): return lax.all_to_all(pieces, 'col', 0, 0, tiled=True)]
    pallas_call x1, Pallas kernels: 52.4 us -> 88.7 us  [sum_first(): pl.pallas_call(functools.partial(first_kernel, cols), out_shape=(jax.Shap...]
    unnamed x54 -> x23, local copies, waits for them, and re-layouts: 35.9 us -> 7.66 us
  transfers between devices with their start and end apart: 15 -> 5, of which waited for: 5 -> 1; matrix products, arithmetic and copies ran while one was open for 14% -> 2% of each run, Pallas kernels for 33% -> 66%
where the time goes in v4:
time: 669 us; the launch traced here: 660 us
  Pallas kernels  607 us (91%)
  local copies, waits for them, and re-layouts  23.6 us (4%)
  between operations  14.5 us (2%)
  waiting for transfers between devices  13.6 us (2%)
    pallas_call x1, Pallas kernels, sum_first(): pl.pallas_call(functools.partial(first_kernel, cols), out_shape=(jax.Shap...  88.7 us
    pallas_call x1, Pallas kernels, norm_two(): pl.pallas_call(functools.partial(norm_two_kernel, cols), out_shape=(jax.S...  74.3 us
    pallas_call x1, Pallas kernels, norm_two_back(): pl.pallas_call(functools.partial(norm_two_back_kernel, cols), out_shape=(...  73.6 us
    pallas_call x1, Pallas kernels, sum_mixed(): pl.pallas_call(functools.partial(mixed_kernel, cols), out_shape=(jax.Shap...  72 us
    pallas_call x1, Pallas kernels, attend(): pl.pallas_call(functools.partial(attend_kernel, cols), out_shape=(jax.Sha...  55.2 us
    pallas_call x1, Pallas kernels, attend_back(): pl.pallas_call(functools.partial(attend_back_kernel, cols), out_shape=(ja...  50.1 us
    pallas_call x1, Pallas kernels, norm_one(): pl.pallas_call(functools.partial(norm_one_kernel, cols), out_shape=(jax.S...  48.5 us
    pallas_call x1, Pallas kernels, gate_up(): pl.pallas_call(functools.partial(gate_up_kernel, cols), out_shape=(jax.Sh...  45.9 us
  transfers between devices with their start and end apart: 5, of which 1 were waited for; matrix products, arithmetic and copies ran while one was open for 2% of the time, Pallas kernels for 66%

profile of v4, /device:TPU:0, one launch (start us, length us, event | category | flops | bytes accessed | tf_op | source)
XLA Modules:
  0.0 659.8 jit_solution(11314251767665676990)
XLA Ops:
  7.2 0.0 copy-start
  7.2 0.0 all-gather.9.cloned.1.call-start
  7.2 1.8 copy-done
  9.1 0.9 constant_dynamic-slice_fusion.4
  10.0 1.5 copy.39
  11.5 0.1 copy.32
  11.6 0.3 copy.34
  11.9 1.0 constant_dynamic-slice_fusion.3
  12.8 0.1 copy.33
  13.0 1.1 pad_maximum_fusion.refs_0_
  14.1 23.8 %exchange.1 = bf16[4,128,1024]{2,1,0:T(8,128)(2,1)} custom-call(bf16[4,128,1024]{2,1,0:T(8,128)(2,1)} %pad_maximum_fusion.refs_0_), custom_call_target="tpu_custom_call" | custom-call | flops 24999999488 | bytes 10000000 | tf_op jit(solution)/shard_map/exchange/pallas_call | solution.py:394
  37.9 0.0 all-gather.9.cloned.1.call-update
  37.9 0.0 all-gather.11.cloned.1.call-start
  38.0 2.4 constant_dynamic-slice_fusion.2
  40.3 1.9 copy.40
  42.3 0.1 copy.36
  42.4 0.0 copy-start.4
  42.4 0.0 copy-start.5
  42.4 0.0 copy-start.6
  42.4 0.0 copy-start.7
  42.4 0.0 copy-start.8
  42.4 1.5 copy.38.one_from
  44.0 1.2 constant_dynamic-slice_fusion.1
  45.1 0.3 copy.37
  45.4 0.0 copy-done.4
  45.4 0.6 copy.41
  46.0 0.9 pad.4.two_from
  47.0 0.0 copy-done.5
  47.0 0.0 copy-done.6
  47.0 0.0 copy-done.7
  47.0 0.0 copy-done.8
  47.0 0.6 concatenate.7.vector
  47.6 48.5 %gather_norm_one.1 = (bf16[1024,2048]{1,0:T(8,128)(2,1)}, bf16[128,2048]{1,0:T(8,128)(2,1)}, f32[512,512]{1,0:T(8,128)}, f32[512,128]{1,0:T(8,128)}, f32[8,2048]{1,0:T(8,128)}) custom-call(bf16[512,512]{1,0:T(8,128)(2,1)} %tokens, f32[8,512]{1,0:T(8,128)} %concatenate.7.vector), custom_call_target="tpu_custom_call" | custom-call | flops 40000000000 | bytes 10000000 | tf_op jit(solution)/shard_map/gather_norm_one/pallas_call | solution.py:831
  96.1 0.0 all-gather.9.cloned.1.call-done
  96.2 55.2 %attention_weight_exchange.1 = (bf16[1024,768]{1,0:T(8,128)(2,1)}, bf16[1024,256]{1,0:T(8,128)(2,1)}, f32[2,2,1024,128]{3,2,1,0:T(8,128)}, bf16[1024,2048]{1,0:T...) custom-call(bf16[1024,2048]{1,0:T(8,128)(2,1)} %get-tuple-element.53.normed, ...), custom_call_target="tpu_custom_call" | custom-call | flops 49999998976 | bytes 10000000 | tf_op jit(solution)/shard_map/attention_weight_exchange/pallas_call | solution.py:1051
  151.4 0.0 all-gather.11.cloned.1.call-update
  151.4 0.2 all-gather.13.cloned.1.call-start
  151.6 74.3 %out_sum_norm_gather.1 = (bf16[1024,2048]{1,0:T(8,128)(2,1)}, f32[128,2048]{1,0:T(8,128)}) custom-call(bf16[1024,2048]{1,0:T(8,128)(2,1)} %get-tuple-element.56.part, bf16[128,2048]{1,0:T(8,128)(2,1)} %get-tuple-element.57.tokens_own, f32[8,2048]{1,0:T(8,128)} %get-tuple-element.58.vectors), custom_call_target="tpu_custom_call" | custom-call | flops 60000002048 | bytes 10000000 | tf_op jit(solution)/shard_map/out_sum_norm_gather/pallas_call | solution.py:494
  225.9 0.0 all-gather.13.cloned.1.call-update
  225.9 0.0 reduce-scatter.2.cloned.1.call-start
  226.0 0.0 all-gather.11.cloned.1.call-done
  226.0 45.9 %gate_up_cotangent_gather.1 = (bf16[1024,704]{1,0:T(8,128)(2,1)}, f32[1024,704]{1,0:T(8,128)}, f32[1024,704]{1,0:T(8,128)}, bf16[1024,2048]{1,0:T(8,128)(2,1)}) custom-call(bf16[1024,2048]{1,0:T(8,128)(2,1)} %get-tuple-element.60.normed.normed_from, bf16[4,4,128,1408]{3,2,1,0:T(8,128)(2,1)} %bitcast.54, bf16[512,512]{1,0:T(8,128)(2,1)} %cotan.1), custom_call_target="tpu_custom_call" | custom-call | flops 35000000512 | bytes 10000000 | tf_op jit(solution)/shard_map/gate_up_cotangent_gather/pallas_call | solution.py:1256
  271.9 0.0 all-gather.13.cloned.1.call-done
  272.0 31.0 %hidden_back.1 = (bf16[4,4,128,2176]{3,2,1,0:T(8,128)(2,1)}, bf16[1024,2048]{1,0:T(8,128)(2,1)}) custom-call(bf16[1024,704]{1,0:T(8,128)(2,1)} %get-tuple-element.62.hidden_from.hidden, f32[1024,704]{1,0:T(8,128)} %get-tuple-element.63.gate_from, f32[1024,704]{1,0:T(8,128)} %get-tuple-element.64.up_from, bf16[1024,2048]{1,0:T(8,128)(2,1)} %get-tuple-element.65.cotan_from, ...), custom_call_target="tpu_custom_call" | custom-call | flops 30000001024 | bytes 10000000 | tf_op jit(solution)/shard_map/hidden_back/pallas_call | solution.py:1391
  303.0 0.0 reduce-scatter.2.cloned.1.call-update
  303.0 0.0 all-gather.15.cloned.1.call-start
  303.1 1.9 constant_dynamic-slice_fusion.cotan_own
  305.0 73.6 %grad_sum_norm_gather.1 = (bf16[1024,2048]{1,0:T(8,128)(2,1)}, f32[8,2048]{1,0:T(8,128)}, bf16[1024,2048]{1,0:T(8,128)(2,1)}) custom-call(bf16[1024,2048]{1,0:T(8,128)(2,1)} %get-tuple-element.67.part, f32[128,2048]{1,0:T(8,128)} %get-tuple-element.68.middle, bf16[128,2048]{1,0:T(8,128)(2,1)} %constant_dynamic-slice_fusion.cotan_own, ...), custom_call_target="tpu_custom_call" | custom-call | flops 60000002048 | bytes 10000000 | tf_op jit(solution)/shard_map/grad_sum_norm_gather/pallas_call | solution.py:580
  378.6 13.4 %reduce-scatter.2.cloned.1.call-done = bf16[512,2176]{1,0:T(8,128)(2,1)} async-done(((bf16[2048,2176]{1,0:T(8,128)(2,1)}), bf16[512,2176]{1,0:T(8,128)(2,1)}) %reduce-scatter.2.cloned.1.call-update) | async-done | bytes 2228240 | tf_op jit(solution)/shard_map/reduce_scatter | solution.py:1489
  392.0 50.1 %attention_back_exchange.1 = (bf16[4,4,128,1024]{3,2,1,0:T(8,128)(2,1)}, bf16[1024,2048]{1,0:T(8,128)(2,1)}, f32[8,768]{1,0:T(8,128)}, bf16[3,128,2816]{2,1,0:T(8,128)(2,1)}) custom-call(bf16[1024,768]{1,0:T(8,128)(2,1)} %get-tuple-element.70.heads_in, f32[2,2,1024,128]{3,2,1,0:T(8,128)} %get-tuple-element.71.logs, ...), custom_call_target="tpu_custom_call" | custom-call | flops 49999998976 | bytes 10000000 | tf_op jit(solution)/shard_map/attention_back_exchange/pallas_call | solution.py:1184
  442.1 0.0 all-gather.15.cloned.1.call-update
  442.2 1.9 dynamic_slice.23.grad_middle
  444.0 88.7 %input_grad_sum.1 = (f32[512,512]{1,0:T(8,128)}, f32[8,512]{1,0:T(8,128)}, bf16[4,4,128,1024]{3,2,1,0:T(8,128)(2,1)}) custom-call(bf16[1024,2048]{1,0:T(8,128)(2,1)} %get-tuple-element.75.part, f32[512,512]{1,0:T(8,128)} %get-tuple-element.76.xhat, f32[512,128]{1,0:T(8,128)} %get-tuple-element.77.rstd, f32[1,512]{1,0:T(1,128)} %bitcast.47, ...), custom_call_target="tpu_custom_call" | custom-call | flops 44999999488 | bytes 10000000 | tf_op jit(solution)/shard_map/input_grad_sum/pallas_call | solution.py:734
  532.7 26.1 %attention_grad_exchange.1 = (bf16[4,128,1024]{2,1,0:T(8,128)(2,1)}, f32[8,1280]{1,0:T(8,128)}) custom-call(bf16[4,4,128,1024]{3,2,1,0:T(8,128)(2,1)} %get-tuple-element.79.pieces, f32[4,8,512]{2,1,0:T(8,128)} %bitcast.62, f32[8,512]{1,0:T(8,128)} %get-tuple-element.81.first, f32[8,768]{1,0:T(8,128)} %get-tuple-element.82.bias), custom_call_target="tpu_custom_call" | custom-call | flops 24999999488 | bytes 10000000 | tf_op jit(solution)/shard_map/attention_grad_exchange/pallas_call | solution.py:915
  558.8 72.0 %mixed_sum.1 = (bf16[512,512]{1,0:T(8,128)(2,1)}, bf16[4,4,128,1024]{3,2,1,0:T(8,128)(2,1)}) custom-call(bf16[1024,2048]{1,0:T(8,128)(2,1)} %get-tuple-element.69.part, f32[128,2048]{1,0:T(8,128)} %get-tuple-element.68.middle, bf16[4,128,1024]{2,1,0:T(8,128)(2,1)} %get-tuple-element.83.piece), custom_call_target="tpu_custom_call" | custom-call | flops 44999999488 | bytes 10000000 | tf_op jit(solution)/shard_map/mixed_sum/pallas_call | solution.py:646
  630.9 0.8 slice_reduce_fusion
  631.6 0.6 reshape_squeeze.3
  632.2 1.5 fusion
  633.7 6.0 weight_gradients.2
  639.7 0.0 copy-start.1
  639.7 11.3 %weight_gradients.3 = (f32[512,2,2816]{2,1,0:T(2,128)}, f32[2816,512]{1,0:T(8,128)}) custom-call(bf16[4,3,128,2816]{3,2,1,0:T(8,128)(2,1)} %bitcast.53), custom_call_target="tpu_custom_call" | custom-call | flops 8000000000 | bytes 10000000 | tf_op jit(solution)/shard_map/weight_gradients/pallas_call | solution.py:1448
  651.0 0.0 copy-done.3
  651.0 0.8 copy.44
  651.8 1.0 copy.45
  (6 shorter events, 0.0 us)
Async XLA Ops:
  7.2 1.9 copy-start
  7.2 89.0 %all-gather.9.cloned.1.call-start = ((), (), s32[]{:S(2)}) async-start(), calls=%async_computation.2 | async-start | bytes 5242880 | tf_op jit(solution)/shard_map/all_gather | solution.py:1484
  37.9 188.1 %all-gather.11.cloned.1.call-start = ((), (), s32[]{:S(2)}) async-start(), calls=%async_computation.3 | async-start | bytes 7208960 | tf_op jit(solution)/shard_map/all_gather | solution.py:1484
  42.4 3.0 copy-start.4
  42.4 4.6 copy-start.5
  42.4 4.6 copy-start.6
  42.4 4.6 copy-start.7
  42.4 4.6 copy-start.8
  151.4 120.6 %all-gather.13.cloned.1.call-start = ((), (), s32[]{:S(2)}) async-start(), calls=%async_computation.4 | async-start | bytes 3932160 | tf_op jit(solution)/shard_map/all_gather | solution.py:1484
  225.9 166.1 %reduce-scatter.2.cloned.1.call-start = ((), (), s32[]{:S(2)}) async-start(), calls=%async_computation.1 | async-start | bytes 11141120 | tf_op jit(solution)/shard_map/reduce_scatter | solution.py:1489
  303.0 336.7 %all-gather.15.cloned.1.call-start = ((), (), s32[]{:S(2)}) async-start(), calls=%async_computation.5 | async-start | bytes 10813440 | tf_op jit(solution)/shard_map/all_gather | solution.py:1565
  639.7 11.3 %copy-start.3 = (bf16[512,512]{1,0:T(8,128)(2,1)S(1)}, bf16[512,512]{1,0:T(8,128)(2,1)}, u32[]{:S(2)}) copy-start(bf16[512,512]{1,0:T(8,128)(2,1)} %get-tuple-element.108) | copy-start | bytes 1572868
  639.7 12.1 %copy-start.2 = (f32[512,512]{1,0:T(8,128)S(1)}, f32[512,512]{1,0:T(8,128)}, u32[]{:S(2)}) copy-start(f32[512,512]{1,0:T(8,128)} %get-tuple-element.109) | copy-start | bytes 3145732
  639.7 13.1 %copy-start.1 = (bf16[512,3,1024]{2,0,1:T(8,128)(2,1)S(1)}, bf16[512,3,1024]{2,0,1:T(8,128)(2,1)}, u32[]{:S(2)}) copy-start(bf16[512,3,1024]{2,0,1:T(8,128)(2,1)} %param.15) | copy-start | bytes 9437188
Sparse Core Ops, SparseCore 0:
  38.0 57.7 all-gather.8
  151.5 68.5 all-gather.10
  226.0 42.0 all-gather.12
  303.2 88.8 reduce-scatter.1
  442.3 180.3 all-gather.14

commit v5 on v4

--- a/solution.py
+++ b/solution.py
@@ -309,8 +309,13 @@
         self.send, self.recv, self.local = sems
         self.c = lax.axis_index(axis)
 
+    def peer(self, k):
+        if self.size == 4 and k != 2:
+            return self.c + 1 - 2 * lax.rem(self.c, 2) if k == 1 else 3 - self.c
+        return lax.rem(self.c + k, self.size)
+
     def hop(self, k):
-        to = lax.rem(self.c + k, self.size)
+        to = self.peer(k)
         return send(
             self.source.at[to],
             self.target.at[self.c],
@@ -346,61 +351,67 @@
 
 
 class Broadcast:
-    def __init__(self, source, target, sems):
-        self.dp, self.source, self.target = target.shape[0], source, target
-        self.send, self.recv, self.local = sems
+    def __init__(self, dp, units, source, target, sems):
+        self.dp, self.units, self.source, self.target = dp, units, source, target
+        self.send, self.recv = sems
         self.me = lax.axis_index("dp")
-
-    def hop(self, k):
+        self.near = self.me + 1 - 2 * lax.rem(self.me, 2)
+        self.far = lax.rem(self.me + 2, dp)
+        self.square = dp == 4
+
+    def hop(self, i, u):
+        if self.square:
+            to = self.near if i == 0 else self.far
+        else:
+            to = lax.rem(self.me + i + 1, self.dp)
         return send(
-            self.source,
-            self.target.at[self.me],
-            self.send.at[k - 1],
-            self.recv.at[k - 1],
-            dp=lax.rem(self.me + k, self.dp),
-        )
-
-    def own(self):
-        return pltpu.make_async_copy(self.source, self.target.at[self.me], self.local.at[0])
-
-    def start(self):
-        for k in range(1, self.dp):
-            self.hop(k).start()
-        self.own().start()
+            self.source(u), self.target(self.me, u), self.send.at[i, u], self.recv.at[i, u], dp=to
+        )
+
+    def across(self, u):
+        low = u < self.units // 2
+        where = self.target(self.near if low else self.far, u)
+        return send(
+            where,
+            where,
+            self.send.at[2, u],
+            self.recv.at[2, u],
+            dp=self.far if low else self.near,
+        )
+
+    def hops(self):
+        return 2 if self.square else self.dp - 1
+
+    def start(self, units=None):
+        half = self.units // 2
+        for n in range(self.units) if units is None else units:
+            for i in range(self.hops()):
+                u = (n + half) % self.units if self.square and i == 1 and units is None else n
+                self.hop(i, u).start()
+
+    def forward(self, u):
+        if self.square:
+            self.hop(0 if u < self.units // 2 else 1, u).wait_recv()
+            self.across(u).start()
 
     def finish(self):
-        self.own().wait()
-        for k in range(1, self.dp):
-            self.hop(k).wait()
+        for u in range(self.units):
+            for i in range(self.hops()):
+                if not self.square or (i == 0) != (u < self.units // 2):
+                    self.hop(i, u).wait_recv()
+                self.hop(i, u).wait_send()
+            if self.square:
+                self.across(u).wait()
+
+    @staticmethod
+    def scratch(dp, units):
+        return [
+            pltpu.SemaphoreType.DMA((max(dp - 1, 1), units)),
+            pltpu.SemaphoreType.DMA((max(dp - 1, 1), units)),
+        ]
 
 
 ANY = pl.BlockSpec(memory_space=pl.ANY)
-
-
-def exchange_kernel(cols, count, *refs):
-    enter(cols, everyone=True)
-    sems = refs[2 * count :]
-    riders = [
-        Exchange("col", cols, refs[i], refs[count + i], sems[3 * i : 3 * i + 3]) for i in range(count)
-    ]
-    for rider in riders:
-        rider.start()
-    for rider in riders:
-        rider.finish()
-
-
-def exchange(cols, number, *pieces):
-    count = len(pieces)
-    return pl.pallas_call(
-        functools.partial(exchange_kernel, cols, count),
-        out_shape=tuple(jax.ShapeDtypeStruct(p.shape, p.dtype) for p in pieces),
-        in_specs=[ANY] * count,
-        out_specs=(ANY,) * count,
-        scratch_shapes=Exchange.scratch(cols) * count,
-        compiler_params=params(number),
-        cost_estimate=cost(25),
-        name="exchange",
-    )(*pieces)
 
 
 def load_columns(weight, whole, sem):
@@ -457,17 +468,69 @@
     return spot
 
 
-def norm_two_kernel(cols, part, tokens_own, vectors, normed, middle, *scratch):
-    half, width = part.shape[0] // 2, part.shape[1]
+COTANGENT_SLOT = 14
+
+
+def middle_kernel(
+    cols,
+    part,
+    tokens_own,
+    vectors,
+    piece,
+    cotan,
+    normed_to,
+    middle_to,
+    hidden_to,
+    gate_to,
+    up_to,
+    weight_to,
+    cotan_to,
+    normed,
+    middle,
+    hidden,
+    gate_part,
+    up_part,
+    weight,
+    cotan_rows,
+    total,
+    own_sem,
+    out_sem,
+    block_sem,
+    *scratch
+):
+    group, width = part.shape
+    half = group // 2
     own = half // cols
     step = own // SUBS
-    total = scratch[11]
-    enter(cols)
+    depth = cotan.shape[1]
+    rows_each = half // SUBS
+    _, part_rows, double = piece.shape
+    narrow = double // 2
+    dp = weight.shape[0] // cols // part_rows
+    me = lax.axis_index("dp")
+    enter(cols, everyone=True, dp=dp)
     summing = Reduce(
         cols, SUBS, lambda d, s: (d * own + s * step, step, 0, width), part, *scratch[:3], scratch[3:7]
     )
+    summing.start()
     spread = Gather(cols, SUBS, row_spot(own, step, half, width), normed, scratch[7:11])
-    summing.start()
+
+    def cotan_spot(r, source, s):
+        rows = pl.ds(pl.multiple_of(r * half + s * rows_each, 16), rows_each)
+        return rows, pl.ds(pl.multiple_of(source * depth, 128), depth)
+
+    cotan_spread = Gather(cols, SUBS, cotan_spot, cotan_rows, scratch[11:15])
+
+    def weight_rows(p, j):
+        return weight.at[pl.ds(pl.multiple_of((j * dp + p) * part_rows, 16), part_rows), :]
+
+    rider = Broadcast(dp, cols, lambda u: piece.at[u], weight_rows, scratch[15:17])
+    rider.start()
+    own_copies = [
+        pltpu.make_async_copy(piece.at[j], weight_rows(me, j), own_sem.at[j]) for j in range(cols)
+    ]
+    for copy in own_copies:
+        copy.start()
 
     def land(s):
         summing.land(s, total)
@@ -479,33 +542,115 @@
         normed[spread.spot(spread.r, spread.c, s)] = result.astype(BF16)
         spread.start(s)
 
-    @pl.loop(0, summing.slots + LAG * (cols - 1))
+    def cotan_slot(t):
+        after = t - COTANGENT_SLOT
+
+        @pl.when((after >= 0) & (lax.rem(after + 60, 3) == 0) & (after < 3 * SUBS))
+        def _():
+            s = lax.div(after, 3)
+            rows = pl.ds(pl.multiple_of(s * rows_each, 16), rows_each)
+            cotan_rows[cotan_spot(spread.r, spread.c, s)] = cotan[rows, :]
+            cotan_spread.start(s)
+
+        cotan_spread.slot(t, COTANGENT_SLOT, 3)
+
+    first = summing.slots + LAG * (cols - 1)
+    last = COTANGENT_SLOT + 3 * (SUBS - 1) + LAG * (cols - 1) + 1
+    blocks = group // BLOCK
+
+    @pl.loop(0, first)
     def _(t):
         summing.slot(t)
         summing.landed(t, land)
         spread.slot(t, summing.landing, summing.per_sub)
+        cotan_slot(t)
+        for u in range(cols):
+
+            @pl.when(t == 8 + 6 * (u % 2))
+            def _():
+                rider.forward(u)
 
     spread.finish()
+    normed_out = pltpu.make_async_copy(normed, normed_to, out_sem.at[0])
+    normed_out.start()
+    middle_out = pltpu.make_async_copy(middle, middle_to, out_sem.at[1])
+    middle_out.start()
+    for copy in own_copies:
+        copy.wait()
+    rider.finish()
+    weight_out = pltpu.make_async_copy(weight, weight_to, out_sem.at[2])
+    weight_out.start()
+
+    def block_out(m):
+        rows = pl.ds(pl.multiple_of(m * BLOCK, BLOCK), BLOCK)
+        pairs = ((hidden, hidden_to), (gate_part, gate_to), (up_part, up_to))
+        return [
+            pltpu.make_async_copy(a.at[rows, :], b.at[rows, :], block_sem.at[i, m])
+            for i, (a, b) in enumerate(pairs)
+        ]
+
+    @pl.loop(0, max(last - first, blocks))
+    def _(m):
+        @pl.when(m < blocks)
+        def _():
+            rows = pl.ds(pl.multiple_of(m * BLOCK, BLOCK), BLOCK)
+            both = dot_nn(normed[rows, :], weight[...])
+            gate, up = both[:, :narrow], both[:, narrow:]
+            sig = 1.0 / (1.0 + jnp.exp(-gate))
+            active = gate * sig
+            hidden[rows, :] = (active * up).astype(BF16)
+            up_part[rows, :] = active
+            gate_part[rows, :] = up * sig * (1.0 + gate * (1.0 - sig))
+            for copy in block_out(m):
+                copy.start()
+
+        cotan_slot(first + m)
+
+    cotan_spread.finish()
+    cotan_out = pltpu.make_async_copy(cotan_rows, cotan_to, out_sem.at[3])
+    cotan_out.start()
     summing.finish()
-
-
-def norm_two(cols, part, tokens_own, vectors):
+    for m in range(blocks):
+        for copy in block_out(m):
+            copy.wait()
+    for copy in (normed_out, middle_out, weight_out, cotan_out):
+        copy.wait()
+
+
+def middle_part(cols, part, tokens_own, vectors, piece, cotan, dp):
     group, width = part.shape
+    _, part_rows, double = piece.shape
+    narrow = double // 2
+    blocks = group // BLOCK
+    dma = pltpu.SemaphoreType.DMA
+    outs = (
+        ((group, width), BF16),
+        (tokens_own.shape, F32),
+        ((group, narrow), BF16),
+        ((group, narrow), F32),
+        ((group, narrow), F32),
+        ((dp * cols * part_rows, double), BF16),
+        ((group, width), BF16),
+    )
     return pl.pallas_call(
-        functools.partial(norm_two_kernel, cols),
-        out_shape=(
-            jax.ShapeDtypeStruct((group, width), BF16),
-            jax.ShapeDtypeStruct(tokens_own.shape, F32),
-        ),
-        in_specs=[VM] * 3,
-        out_specs=(VM, VM),
-        scratch_shapes=Reduce.scratch(cols, SUBS, group // 2, width)
-        + Gather.scratch(cols, SUBS)
-        + [pltpu.VMEM((group // 2 // cols // SUBS, width), F32)],
+        functools.partial(middle_kernel, cols),
+        out_shape=tuple(jax.ShapeDtypeStruct(*out) for out in outs),
+        in_specs=[VM] * 3 + [ANY, VM],
+        out_specs=(ANY,) * len(outs),
+        scratch_shapes=[pltpu.VMEM(*out) for out in outs]
+        + [
+            pltpu.VMEM((group // 2 // cols // SUBS, width), F32),
+            dma((cols,)),
+            dma((4,)),
+            dma((3, blocks)),
+        ]
+        + Reduce.scratch(cols, SUBS, group // 2, width)
+        + Gather.scratch(cols, SUBS) * 2
+        + Broadcast.scratch(dp, cols),
         compiler_params=params(2),
-        cost_estimate=cost(60),
-        name="out_sum_norm_gather",
-    )(part, tokens_own, vectors)
+        cost_estimate=cost(95),
+        name="middle_gate_up",
+    )(part, tokens_own, vectors, piece, cotan)
 
 
 def norm_two_back_kernel(
@@ -618,15 +763,33 @@
     )
 
 
-def mixed_kernel(cols, part, middle, piece, mixed, pieces, *scratch):
+def mixed_kernel(
+    cols, part, middle, piece, norms, bias, mixed, pieces, small, total, mine, all_dp, *sems
+):
     half = part.shape[0] // 2
     step = half // SUBS
-    total = scratch[7]
-    enter(cols, everyone=True, dp=pieces.shape[0])
-    rider = Broadcast(piece, pieces, scratch[8:])
+    dp = pieces.shape[0]
+    depth = norms.shape[1]
+    me = lax.axis_index("dp")
+    enter(cols, everyone=True, dp=dp)
+    summing = mixed_sum(cols, part, middle, sems[:7])
+    summing.start()
+    mine[:, :depth] = norms[...]
+    mine[:, depth:] = bias[...]
+    all_dp[me] = mine[...]
+
+    def hop(k):
+        to = lax.rem(me + k, dp)
+        return send(mine, all_dp.at[me], sems[7].at[k - 1], sems[8].at[k - 1], dp=to)
+
+    for k in range(1, dp):
+        hop(k).start()
+    rider = Broadcast(
+        dp, piece.shape[0], lambda u: piece.at[u], lambda p, u: pieces.at[p, u], sems[9:11]
+    )
     rider.start()
-    summing = mixed_sum(cols, part, middle, scratch[:7])
-    summing.start()
+    own = pltpu.make_async_copy(piece, pieces.at[me], sems[11].at[0])
+    own.start()
 
     def land(s):
         summing.land(s, total)
@@ -636,59 +799,124 @@
     def _(t):
         summing.slot(t)
         summing.landed(t, land)
-
+        for u in range(rider.units):
+
+            @pl.when(t == 14 + 7 * (u % 2))
+            def _():
+                rider.forward(u)
+
+    for k in range(1, dp):
+        hop(k).wait()
+    value = all_dp[0]
+    for p in range(1, dp):
+        value = value + all_dp[p]
+    small[...] = value
     summing.finish()
+    own.wait()
     rider.finish()
 
 
-def sum_mixed(cols, part, middle, piece, dp):
+def sum_mixed(cols, part, middle, piece, norms, bias, dp):
     group, width = part.shape
+    small = (8, norms.shape[1] + bias.shape[1])
+    hops = max(dp - 1, 1)
     return pl.pallas_call(
         functools.partial(mixed_kernel, cols),
         out_shape=(
             jax.ShapeDtypeStruct((group // 2, width // cols), BF16),
             jax.ShapeDtypeStruct((dp,) + piece.shape, BF16),
+            jax.ShapeDtypeStruct(small, F32),
         ),
-        in_specs=[VM] * 2 + [ANY],
-        out_specs=(VM, ANY),
-        scratch_shapes=Reduce.scratch(cols, SUBS, group // 2, width)
-        + [pltpu.VMEM((group // 2 // SUBS, width // cols), F32)]
-        + Exchange.scratch(dp),
+        in_specs=[VM] * 2 + [ANY] + [VM] * 2,
+        out_specs=(VM, ANY, VM),
+        scratch_shapes=[
+            pltpu.VMEM((group // 2 // SUBS, width // cols), F32),
+            pltpu.VMEM(small, F32),
+            pltpu.VMEM((dp,) + small, F32),
+        ]
+        + Reduce.scratch(cols, SUBS, group // 2, width)
+        + [pltpu.SemaphoreType.DMA((hops,)), pltpu.SemaphoreType.DMA((hops,))]
+        + Broadcast.scratch(dp, piece.shape[0])
+        + [pltpu.SemaphoreType.DMA((1,))],
         compiler_params=params(4),
         cost_estimate=cost(45),
         name="mixed_sum",
-    )(part, middle, piece)
+    )(part, middle, piece, norms, bias)
 
 
 def first_kernel(
-    cols, part, xhat, rstd, gain, grad_middle, pieces_from, result, sums, pieces_to, *scratch
+    cols,
+    part,
+    xhat,
+    rstd,
+    gain,
+    grad_middle,
+    heads_grad,
+    out_grad,
+    second,
+    result,
+    norms,
+    arranged,
+    total,
+    grad,
+    mine,
+    theirs,
+    sums,
+    landed,
+    slices,
+    own_norms,
+    pair_norms,
+    *sems
 ):
-    dp = pieces_from.shape[0]
     half, width = part.shape[0] // 2, part.shape[1]
     step, depth = half // SUBS, width // cols
-    total, grad, mine, theirs, out_sem, in_sem = scratch[7:13]
-    enter(cols, everyone=True, dp=dp)
-    rider = Exchange("dp", dp, pieces_from, pieces_to, scratch[13:])
-    c = lax.axis_index("col")
+    pairs, dp = heads_grad.shape[:2]
+    two = heads_grad.shape[4] // 3
+    narrow = sums.shape[2] // 4
+    enter(cols, everyone=True)
+    r, c = lax.axis_index("row"), lax.axis_index("col")
     summing = Reduce(
         cols,
         SUBS,
         lambda d, s: (s * step, step, d * depth, depth),
         part,
-        *scratch[:3],
-        scratch[3:7],
+        *sems[:3],
+        sems[3:7],
     )
     summing.start()
-    rider.start()
-    sums[...] = jnp.zeros_like(sums)
+    out_sem, in_sem, pair_sem = sems[7:10]
+    rider = Exchange("col", cols, sums, landed, sems[10:13])
+    names = Exchange("col", cols, second, slices, sems[13:16])
+    names.start()
+
+    def over_dp(ref, to):
+        value = ref[0, to].astype(F32)
+        for p in range(1, dp):
+            value = value + ref[p, to].astype(F32)
+        return value.astype(BF16)
+
+    def fill(to, target):
+        for pair in range(pairs):
+            value = over_dp(heads_grad.at[pair], to)
+            for k in range(3):
+                first = k * narrow + pair * two
+                target[:, first : first + two] = value[:, k * two : (k + 1) * two]
+        target[:, 3 * narrow :] = over_dp(out_grad, to)
+
+    for k in range(1, cols):
+        to = rider.peer(k)
+        fill(to, sums.at[to])
+        rider.hop(k).start()
+    fill(c, landed.at[c])
+    own_norms[...] = jnp.zeros_like(own_norms)
 
     def land(s):
         summing.land(s, total)
         rows = pl.ds(pl.multiple_of(s * step, step), step)
         grad[rows, :] = total[...]
         standard = xhat[rows, :]
-        sums[0:1, :] += jnp.sum(total[...] * standard, axis=0, keepdims=True)
-        sums[1:2, :] += jnp.sum(total[...], axis=0, keepdims=True)
+        own_norms[0:1, :] += jnp.sum(total[...] * standard, axis=0, keepdims=True)
+        own_norms[1:2, :] += jnp.sum(total[...], axis=0, keepdims=True)
 
     @pl.loop(0, summing.slots)
     def _(t):
@@ -700,19 +928,26 @@
         rows = slice(s * 128, (s + 1) * 128)
         scaled = grad[rows, :] * gain[0:1, :]
         one = jnp.sum(scaled, axis=1, keepdims=True)
-        two = jnp.sum(scaled * xhat[rows, :], axis=1, keepdims=True)
-        both = jnp.where(lanes == 0, one, jnp.where(lanes == 1, two, 0.0))
+        two_sum = jnp.sum(scaled * xhat[rows, :], axis=1, keepdims=True)
+        both = jnp.where(lanes == 0, one, jnp.where(lanes == 1, two_sum, 0.0))
         mine[:, rows] = both.T[0:8, :]
 
-    def exchange(k):
+    def exchange_sums(k):
         return send(
             mine, theirs.at[k - 1], out_sem.at[k - 1], in_sem.at[k - 1], col=lax.rem(c + k, cols)
         )
 
     for k in range(1, cols):
-        exchange(k).start()
+        exchange_sums(k).start()
+    names.finish()
+    shift = slices[0]
+    for j in range(1, cols):
+        shift = shift + slices[j]
+    own_norms[2:4, :] = shift[0:2, :]
+    across = send(own_norms, pair_norms, pair_sem.at[0], pair_sem.at[1], row=1 - r)
+    across.start()
     for k in range(1, cols):
-        exchange(k).wait_recv()
+        exchange_sums(k).wait_recv()
     for s in range(half // 128):
         rows = slice(s * 128, (s + 1) * 128)
         both = mine[:, rows]
@@ -723,182 +958,10 @@
         inner = scaled - both[:, 0:1] - xhat[rows, :] * both[:, 1:2]
         result[rows, :] = grad_middle[rows, :].astype(F32) + rstd[rows, 0:1] * inner
     for k in range(1, cols):
-        exchange(k).wait_send()
+        exchange_sums(k).wait_send()
+    across.wait()
+    norms[...] = own_norms[...] + pair_norms[...]
     summing.finish()
-    rider.finish()
-
-
-def sum_first(cols, part, xhat, rstd, gain, grad_middle, pieces):
-    group, width = part.shape
-    half, depth = group // 2, width // cols
-    return pl.pallas_call(
-        functools.partial(first_kernel, cols),
-        out_shape=(
-            jax.ShapeDtypeStruct((half, depth), F32),
-            jax.ShapeDtypeStruct((8, depth), F32),
-            jax.ShapeDtypeStruct(pieces.shape, BF16),
-        ),
-        in_specs=[VM] * 5 + [ANY],
-        out_specs=(VM, VM, ANY),
-        scratch_shapes=Reduce.scratch(cols, SUBS, half, width)
-        + [
-            pltpu.VMEM((half // SUBS, depth), F32),
-            pltpu.VMEM((half, depth), F32),
-            pltpu.VMEM((8, half), F32),
-            pltpu.VMEM((cols - 1, 8, half), F32),
-            pltpu.SemaphoreType.DMA((cols - 1,)),
-            pltpu.SemaphoreType.DMA((cols - 1,)),
-        ]
-        + Exchange.scratch(pieces.shape[0]),
-        compiler_params=params(5),
-        cost_estimate=cost(45),
-        name="input_grad_sum",
-    )(part, xhat, rstd, gain, grad_middle, pieces)
-
-
-def norm_one_kernel(cols, tokens, vector, normed, tokens_own, xhat, rstd, vectors, *scratch):
-    half, depth = tokens.shape
-    width = depth * cols
-    step = half // cols
-    full = scratch[0]
-    enter(cols)
-    r, c = lax.axis_index("row"), lax.axis_index("col")
-
-    def columns(source):
-        return pl.ds(pl.multiple_of(source * depth, 128), depth)
-
-    names = Gather(
-        cols, 1, lambda r, source, s: (pl.ds(0, 8), columns(source)), vectors, scratch[1:5], pair=False
-    )
-    spread = Gather(
-        cols,
-        cols,
-        lambda r, source, s: (pl.ds(s * step, step), columns(source)),
-        full,
-        scratch[5:9],
-        pair=False,
-    )
-    pair_send, pair_recv = scratch[9:11]
-    vectors[:, columns(c)] = vector[...]
-    names.start(0)
-    for s in range(cols):
-        rows = pl.ds(s * step, step)
-        full[rows, columns(c)] = tokens[rows, :]
-        spread.start(s)
-
-    def across(r, s):
-        where = normed.at[pl.ds(pl.multiple_of(r * half + s * step, 16), step), :]
-        return send(
-            where,
-            where,
-            pair_send.at[s],
-            pair_recv.at[s],
-            row=1 - lax.axis_index("row"),
-        )
-
-    for k in range(1, cols):
-        names.relay(0, k)
-        for s in range(cols):
-            if k < cols - 1:
-                spread.relay(s, k)
-    for s in range(cols):
-        spread.relay(s, cols - 1)
-        rows = slice(s * step, (s + 1) * step)
-        state = full[rows, :].astype(F32)
-        centered, inverse = moments(state)
-        standard = centered * inverse
-        out = standard * vectors[0:1, :] + vectors[1:2, :]
-        normed[pl.ds(pl.multiple_of(r * half + s * step, 16), step), :] = out.astype(BF16)
-        across(r, s).start()
-        rstd[rows, :] = jnp.broadcast_to(inverse, (step, 128))
-        mean = jnp.mean(state, axis=1, keepdims=True)
-        xhat[rows, :] = (tokens[rows, :].astype(F32) - mean) * inverse
-
-        @pl.when(c == s)
-        def _():
-            tokens_own[...] = full[rows, :]
-
-    for s in range(cols):
-        across(1 - r, s).wait_recv()
-        across(r, s).wait_send()
-    names.finish()
-    spread.finish()
-
-
-def norm_one(cols, tokens, vector):
-    half, depth = tokens.shape
-    width = depth * cols
-    return pl.pallas_call(
-        functools.partial(norm_one_kernel, cols),
-        out_shape=(
-            jax.ShapeDtypeStruct((2 * half, width), BF16),
-            jax.ShapeDtypeStruct((half // cols, width), BF16),
-            jax.ShapeDtypeStruct((half, depth), F32),
-            jax.ShapeDtypeStruct((half, 128), F32),
-            jax.ShapeDtypeStruct((8, width), F32),
-        ),
-        in_specs=[VM] * 2,
-        out_specs=(VM,) * 5,
-        scratch_shapes=[pltpu.VMEM((half, width), BF16)]
-        + Gather.scratch(cols, 1)
-        + Gather.scratch(cols, cols)
-        + [pltpu.SemaphoreType.DMA((cols,)), pltpu.SemaphoreType.DMA((cols,))],
-        compiler_params=params(1),
-        cost_estimate=cost(40),
-        name="gather_norm_one",
-    )(tokens, vector)
-
-
-def finish_kernel(
-    cols, pieces, second, first, bias, arranged, small, sums, landed, slices, mine, both, pair, all_dp, *sems
-):
-    dp, _, _, wide = pieces.shape
-    depth = first.shape[1]
-    narrow = wide // 4
-    enter(cols, everyone=True, dp=dp)
-    r, c, me = (lax.axis_index(name) for name in ("row", "col", "dp"))
-    names = Exchange("col", cols, second, slices, sems[:3])
-    names.start()
-    rider = Exchange("col", cols, sums, landed, sems[3:6])
-
-    def total(to):
-        value = pieces[0, to].astype(F32)
-        for p in range(1, dp):
-            value = value + pieces[p, to].astype(F32)
-        return value.astype(BF16)
-
-    for k in range(1, cols):
-        to = lax.rem(c + k, cols)
-        sums[to] = total(to)
-        rider.hop(k).start()
-    landed[c] = total(c)
-    names.finish()
-    mine[...] = jnp.zeros_like(mine)
-    mine[0:2, :depth] = first[0:2, :]
-    shift = slices[0]
-    for j in range(1, cols):
-        shift = shift + slices[j]
-    mine[2:4, :depth] = shift[0:2, :]
-    mine[0:1, depth:] = bias[0:1, :]
-    across = send(mine, pair, sems[6].at[0], sems[6].at[1], row=1 - r)
-    across.start()
-    across.wait()
-    both[:, depth:] = mine[:, depth:]
-    both[:, :depth] = mine[:, :depth] + pair[:, :depth]
-
-    def hop(k):
-        to = lax.rem(me + k, dp)
-        return send(both, all_dp.at[me], sems[7].at[k - 1], sems[8].at[k - 1], dp=to)
-
-    for k in range(1, dp):
-        hop(k).start()
-    all_dp[me] = both[...]
-    for k in range(1, dp):
-        hop(k).wait()
-    value = all_dp[0]
-    for p in range(1, dp):
-        value = value + all_dp[p]
-    small[...] = value
     for k in range(1, cols):
         rider.hop(k).wait()
     for k in range(4):
@@ -908,33 +971,241 @@
             ]
 
 
-def finish(cols, pieces, second, first, bias):
-    dp, _, part, wide = pieces.shape
-    depth, biases = first.shape[1], bias.shape[1]
+def sum_first(cols, part, xhat, rstd, gain, grad_middle, heads_grad, out_grad, second):
+    group, width = part.shape
+    half, depth = group // 2, width // cols
+    rows, narrow = out_grad.shape[2:]
     dma = pltpu.SemaphoreType.DMA
     return pl.pallas_call(
-        functools.partial(finish_kernel, cols),
+        functools.partial(first_kernel, cols),
         out_shape=(
-            jax.ShapeDtypeStruct((4, part, cols * wide // 4), BF16),
-            jax.ShapeDtypeStruct((8, depth + biases), F32),
+            jax.ShapeDtypeStruct((half, depth), F32),
+            jax.ShapeDtypeStruct((8, depth), F32),
+            jax.ShapeDtypeStruct((4, rows, cols * narrow), BF16),
         ),
-        in_specs=[VM] * 4,
-        out_specs=(VM,) * 2,
+        in_specs=[VM] * 8,
+        out_specs=(VM,) * 3,
         scratch_shapes=[
-            pltpu.VMEM((cols, part, wide), BF16),
-            pltpu.VMEM((cols, part, wide), BF16),
+            pltpu.VMEM((half // SUBS, depth), F32),
+            pltpu.VMEM((half, depth), F32),
+            pltpu.VMEM((8, half), F32),
+            pltpu.VMEM((cols - 1, 8, half), F32),
+            pltpu.VMEM((cols, rows, 4 * narrow), BF16),
+            pltpu.VMEM((cols, rows, 4 * narrow), BF16),
             pltpu.VMEM((cols, 8, depth), F32),
-            pltpu.VMEM((8, depth + biases), F32),
-            pltpu.VMEM((8, depth + biases), F32),
-            pltpu.VMEM((8, depth + biases), F32),
-            pltpu.VMEM((dp, 8, depth + biases), F32),
+            pltpu.VMEM((8, depth), F32),
+            pltpu.VMEM((8, depth), F32),
         ]
-        + Exchange.scratch(cols) * 2
-        + [dma((2,)), dma((max(dp - 1, 1),)), dma((max(dp - 1, 1),))],
-        compiler_params=params(10),
-        cost_estimate=cost(25),
-        name="attention_grad_exchange",
-    )(pieces, second, first, bias)
+        + Reduce.scratch(cols, SUBS, half, width)
+        + [dma((cols - 1,)), dma((cols - 1,)), dma((2,))]
+        + Exchange.scratch(cols) * 2,
+        compiler_params=params(5),
+        cost_estimate=cost(60),
+        name="input_grad_sum",
+    )(part, xhat, rstd, gain, grad_middle, heads_grad, out_grad, second)
+
+
+def start_kernel(
+    cols,
+    tokens,
+    vector,
+    heads_from,
+    out_from,
+    gate_up_from,
+    down_from,
+    normed,
+    tokens_own,
+    xhat,
+    rstd,
+    vectors,
+    gate_up_piece,
+    down_piece,
+    attention_w,
+    heads,
+    out,
+    gate_up,
+    down,
+    pieces,
+    landed,
+    full,
+    in_sem,
+    own_sem,
+    pair_send,
+    pair_recv,
+    *sems
+):
+    half, depth = tokens.shape
+    width = depth * cols
+    step = half // cols
+    dp, _, part, wide = attention_w.shape
+    narrow = wide // 4
+    tall = down.shape[0] // cols
+    r, c, me = (lax.axis_index(name) for name in ("row", "col", "dp"))
+    begin = pl.multiple_of(me * part, part)
+    rows_in = pl.ds(begin, part)
+
+    def share_of(ref):
+        return ref if ref.shape[1] == part else ref.at[:, rows_in]
+
+    loads = [
+        pltpu.make_async_copy(heads_from.at[:, rows_in], heads, in_sem.at[0]),
+        pltpu.make_async_copy(share_of(out_from), out, in_sem.at[1]),
+        pltpu.make_async_copy(gate_up_from.at[rows_in], gate_up, in_sem.at[2]),
+        pltpu.make_async_copy(share_of(down_from), down, in_sem.at[3]),
+    ]
+    for load in loads:
+        load.start()
+    enter(cols, everyone=True, dp=dp)
+    loads[0].wait()
+    loads[1].wait()
+    for j in range(cols):
+        share = slice(j * narrow, (j + 1) * narrow)
+        for k in range(3):
+            pieces[j, :, k * narrow : (k + 1) * narrow] = heads[k, :, share]
+        pieces[j, :, 3 * narrow :] = out[share, :].T
+    rider = Exchange("col", cols, pieces, landed, sems[:3])
+    assert cols == 4
+    landed[c] = pieces[c]
+    units = [c] + [rider.peer(k) for k in range(1, cols)]
+    cast = Broadcast(
+        dp, cols, lambda k: landed.at[units[k]], lambda p, k: attention_w.at[p, units[k]], sems[11:13]
+    )
+    cast.start((0,))
+    for k in range(1, cols):
+        rider.hop(k).start()
+
+    def columns(source):
+        return pl.ds(pl.multiple_of(source * depth, 128), depth)
+
+    names = Gather(
+        cols, 1, lambda r, source, s: (pl.ds(0, 8), columns(source)), vectors, sems[3:7], pair=False
+    )
+    spread = Gather(
+        cols,
+        cols,
+        lambda r, source, s: (pl.ds(s * step, step), columns(source)),
+        full,
+        sems[7:11],
+        pair=False,
+    )
+    vectors[:, columns(c)] = vector[...]
+    names.start(0)
+    for s in range(cols):
+        rows = pl.ds(s * step, step)
+        full[rows, columns(c)] = tokens[rows, :]
+        spread.start(s)
+    loads[2].wait()
+    for i in range(2):
+        values = gate_up[:, i, :]
+        for j in range(cols):
+            gate_up_piece[j, :, i * tall : (i + 1) * tall] = values[:, j * tall : (j + 1) * tall]
+    loads[3].wait()
+    for j in range(cols):
+        down_piece[j, :, :tall] = down[j * tall : (j + 1) * tall, :].T
+        if down_piece.shape[2] > tall:
+            down_piece[j, :, tall:] = jnp.zeros((part, down_piece.shape[2] - tall), BF16)
+
+    def across(r, s):
+        where = normed.at[pl.ds(pl.multiple_of(r * half + s * step, 16), step), :]
+        return send(where, where, pair_send.at[s], pair_recv.at[s], row=1 - lax.axis_index("row"))
+
+    def own(k):
+        u = units[k]
+        return pltpu.make_async_copy(landed.at[u], attention_w.at[me, u], own_sem.at[k])
+
+    def take(k):
+        rider.hop(k).wait_recv()
+        cast.start((k,))
+        own(k).start()
+
+    def norm(s):
+        rows = slice(s * step, (s + 1) * step)
+        state = full[rows, :].astype(F32)
+        centered, inverse = moments(state)
+        result = centered * inverse * vectors[0:1, :] + vectors[1:2, :]
+        normed[pl.ds(pl.multiple_of(r * half + s * step, 16), step), :] = result.astype(BF16)
+        across(r, s).start()
+        rstd[rows, :] = jnp.broadcast_to(inverse, (step, 128))
+        mean = jnp.mean(state, axis=1, keepdims=True)
+        xhat[rows, :] = (tokens[rows, :].astype(F32) - mean) * inverse
+
+        @pl.when(c == s)
+        def _():
+            tokens_own[...] = full[rows, :]
+
+    own(0).start()
+    take(1)
+    for k in range(1, cols):
+        names.relay(0, k)
+    for s in range(cols):
+        spread.relay(s, 1)
+    cast.forward(0)
+    take(2)
+    take(3)
+    for s in range(cols):
+        spread.relay(s, 2)
+    cast.forward(1)
+    cast.forward(2)
+    for s in range(cols):
+        spread.relay(s, 3)
+        norm(s)
+        if s == 1:
+            cast.forward(3)
+
+    for s in range(cols):
+        across(1 - r, s).wait_recv()
+        across(r, s).wait_send()
+    for u in range(cols):
+        own(u).wait()
+    cast.finish()
+    for k in range(1, cols):
+        rider.hop(k).wait_send()
+    names.finish()
+    spread.finish()
+
+
+def start_part(tokens, vector, heads, out, gate_up, down, sizes):
+    dp, cols = sizes["dp"], sizes["col"]
+    half, depth = tokens.shape
+    width = depth * cols
+    part, wide, tall = depth // dp, heads.shape[2], down.shape[0]
+    each = tall // cols
+    dma = pltpu.SemaphoreType.DMA
+    return pl.pallas_call(
+        functools.partial(start_kernel, cols),
+        out_shape=(
+            jax.ShapeDtypeStruct((2 * half, width), BF16),
+            jax.ShapeDtypeStruct((half // cols, width), BF16),
+            jax.ShapeDtypeStruct((half, depth), F32),
+            jax.ShapeDtypeStruct((half, 128), F32),
+            jax.ShapeDtypeStruct((8, width), F32),
+            jax.ShapeDtypeStruct((cols, part, 2 * each), BF16),
+            jax.ShapeDtypeStruct((cols, part, each + -each % 128), BF16),
+            jax.ShapeDtypeStruct((dp, cols, part, 4 * wide // cols), BF16),
+        ),
+        in_specs=[VM] * 2 + [ANY] * 4,
+        out_specs=(VM,) * 7 + (ANY,),
+        scratch_shapes=[
+            pltpu.VMEM((3, part, wide), BF16),
+            pltpu.VMEM((wide, part), BF16),
+            pltpu.VMEM((part, 2, tall), BF16),
+            pltpu.VMEM((tall, part), BF16),
+            pltpu.VMEM((cols, part, 4 * wide // cols), BF16),
+            pltpu.VMEM((cols, part, 4 * wide // cols), BF16),
+            pltpu.VMEM((half, width), BF16),
+            dma((4,)),
+            dma((cols,)),
+            dma((cols,)),
+            dma((cols,)),
+        ]
+        + Exchange.scratch(cols)
+        + Gather.scratch(cols, 1)
+        + Gather.scratch(cols, cols)
+        + Broadcast.scratch(dp, cols),
+        compiler_params=params(1),
+        cost_estimate=cost(60),
+        name="tokens_norm_weights",
+    )(tokens, vector, heads, out, gate_up, down)
 
 
 def rope_tables(length):
@@ -1082,7 +1353,8 @@
     normed,
     attn,
     pieces_from,
-    weight_grad,
+    heads_to,
+    out_to,
     normed_grad,
     sums,
     arranged,
@@ -1093,18 +1365,40 @@
     sem,
     grad,
     result,
+    own,
     pieces_to,
+    heads_from,
+    out_from,
     *sems
 ):
     length, wide = attn.shape
     two = 2 * HD
     dp, _, part_rows, _ = weight.shape
     copies = load_columns(weight, whole, sem)
-    enter(cols, everyone=True)
-    rider = Exchange("col", cols, pieces_from, pieces_to, sems)
+    enter(cols, everyone=True, dp=dp)
+    rider = Exchange("col", cols, pieces_from, pieces_to, sems[:3])
     rider.start()
+    out_rider = Exchange("dp", dp, out_from, out_to, sems[3:6])
+    depth = normed.shape[1] // cols
+
+    def heads_rider(pair):
+        return Exchange(
+            "dp", dp, heads_from.at[pair], heads_to.at[pair], [sem.at[pair] for sem in sems[6:]]
+        )
+
+    def parts(j):
+        return pl.ds(pl.multiple_of(j * depth, depth), depth)
+
+    @pl.loop(0, cols)
+    def _(j):
+        out_grad = dot_tn(grad_middle[:, parts(j)], attn[...]).astype(BF16)
+        for p in range(dp):
+            out_from[p, j] = out_grad[p * part_rows : (p + 1) * part_rows, :]
+
+    out_rider.start()
     for copy in copies:
         copy.wait()
+    sums[...] = jnp.zeros_like(sums)
     first_head = lax.broadcasted_iota(jnp.int32, (BLOCK, two), 1) < HD
 
     @pl.loop(0, length // BLOCK)
@@ -1150,26 +1444,26 @@
         for k in range(3):
             low = grads[k].astype(BF16)
             result[:, lanes(k)] = low
+            own[:, k * two : (k + 1) * two] = low
             column_sum = jnp.sum(low.astype(F32), axis=0, keepdims=True)
-            sums[:, lanes(k)] = jnp.broadcast_to(column_sum, (8, two))
-
-    depth = normed.shape[1] // cols
-
-    @pl.loop(0, cols)
-    def _(j):
-        columns = pl.ds(pl.multiple_of(j * depth, depth), depth)
-        heads_grad = dot_tn(normed[:, columns], result[...]).astype(BF16)
-        out_grad = dot_tn(grad_middle[:, columns], attn[...]).astype(BF16)
-        for p in range(dp):
-            rows = slice(p * part_rows, (p + 1) * part_rows)
-            weight_grad[p, j, :, : 3 * wide] = heads_grad[rows, :]
-            weight_grad[p, j, :, 3 * wide :] = out_grad[rows, :]
+            sums[0:1, lanes(k)] = column_sum
+
+        @pl.loop(0, cols)
+        def _(j):
+            heads_grad = dot_tn(normed[:, parts(j)], own[...]).astype(BF16)
+            for p in range(dp):
+                heads_from[pair, p, j] = heads_grad[p * part_rows : (p + 1) * part_rows, :]
+
+        heads_rider(pair).start()
 
     @pl.loop(0, length // BLOCK)
     def _(m):
         rows = pl.ds(pl.multiple_of(m * BLOCK, BLOCK), BLOCK)
         normed_grad[rows, :] = dot_nt(result[rows, :], whole[:, : 3 * wide]).astype(BF16)
 
+    out_rider.finish()
+    for pair in range(wide // two):
+        heads_rider(pair).finish()
     rider.finish()
     share = arranged.shape[2] // cols
     for k in range(arranged.shape[0]):
@@ -1181,97 +1475,41 @@
 def attend_back(cols, heads_in, logs, grad_middle, tables, weight, normed, attn, pieces, share):
     length, wide = attn.shape
     width = normed.shape[1]
+    dp, _, part, _ = weight.shape
+    pairs = wide // (2 * HD)
+    heads = (pairs, dp, cols, part, 6 * HD)
+    out = (dp, cols, part, wide)
+    hops = max(dp - 1, 1)
+    dma = pltpu.SemaphoreType.DMA
     return pl.pallas_call(
         functools.partial(attend_back_kernel, cols),
         out_shape=(
-            jax.ShapeDtypeStruct(weight.shape, BF16),
+            jax.ShapeDtypeStruct(heads, BF16),
+            jax.ShapeDtypeStruct(out, BF16),
             jax.ShapeDtypeStruct((length, width), BF16),
             jax.ShapeDtypeStruct((8, 3 * wide), F32),
             jax.ShapeDtypeStruct((3, pieces.shape[1], cols * share), BF16),
         ),
         in_specs=[VM] * 4 + [ANY, VM, VM, ANY],
-        out_specs=(VM,) * 4,
+        out_specs=(ANY,) * 2 + (VM,) * 3,
         scratch_shapes=[pltpu.VMEM((length, 2 * HD), F32)] * 3
         + [
             pltpu.VMEM((width, 4 * wide), BF16),
             pltpu.SemaphoreType.DMA(weight.shape[:2]),
             pltpu.VMEM((length, wide), BF16),
             pltpu.VMEM((length, 3 * wide), BF16),
+            pltpu.VMEM((length, 6 * HD), BF16),
             pltpu.VMEM(pieces.shape, BF16),
+            pltpu.VMEM(heads, BF16),
+            pltpu.VMEM(out, BF16),
         ]
-        + Exchange.scratch(cols),
+        + Exchange.scratch(cols)
+        + Exchange.scratch(dp)
+        + [dma((pairs, hops)), dma((pairs, hops)), dma((pairs, 1))],
         compiler_params=params(8),
         cost_estimate=cost(50),
         name="attention_back_exchange",
     )(heads_in, logs, grad_middle, tables, weight, normed, attn, pieces)
-
-
-def gate_up_kernel(cols, normed, weight, cotan, hidden, gate_part, up_part, cotan_rows, *scratch):
-    group, narrow = hidden.shape
-    half, depth = cotan.shape
-    step = half // SUBS
-    whole, sem = scratch[:2]
-    copies = load_columns(weight, whole, sem)
-    enter(cols)
-
-    def spot(r, source, s):
-        rows = pl.ds(pl.multiple_of(r * half + s * step, 16), step)
-        return rows, pl.ds(pl.multiple_of(source * depth, 128), depth)
-
-    spread = Gather(cols, SUBS, spot, cotan_rows, scratch[2:])
-    for s in range(SUBS):
-        cotan_rows[spot(spread.r, spread.c, s)] = cotan[s * step : (s + 1) * step, :]
-        spread.start(s)
-    for copy in copies:
-        copy.wait()
-    blocks = group // BLOCK
-    each = SUBS // blocks
-
-    @pl.loop(0, blocks)
-    def _(m):
-        rows = pl.ds(pl.multiple_of(m * BLOCK, BLOCK), BLOCK)
-        both = dot_nn(normed[rows, :], whole[...])
-        gate, up = both[:, :narrow], both[:, narrow:]
-        sig = 1.0 / (1.0 + jnp.exp(-gate))
-        active = gate * sig
-        hidden[rows, :] = (active * up).astype(BF16)
-        up_part[rows, :] = active
-        gate_part[rows, :] = up * sig * (1.0 + gate * (1.0 - sig))
-        for u in range(each):
-            spread.relay(m * each + u, 1)
-
-    for k in range(2, cols):
-
-        @pl.loop(0, SUBS)
-        def _(s):
-            spread.relay(s, k)
-
-    spread.finish()
-
-
-def gate_up(cols, normed, weight, cotan):
-    group, width = normed.shape
-    dp = weight.shape[0]
-    narrow = weight.shape[3] // 2
-    return pl.pallas_call(
-        functools.partial(gate_up_kernel, cols),
-        out_shape=(
-            jax.ShapeDtypeStruct((group, narrow), BF16),
-            jax.ShapeDtypeStruct((group, narrow), F32),
-            jax.ShapeDtypeStruct((group, narrow), F32),
-            jax.ShapeDtypeStruct((group, width), BF16),
-        ),
-        in_specs=[VM, ANY, VM],
-        out_specs=(VM,) * 4,
-        scratch_shapes=[
-            pltpu.VMEM((width, weight.shape[3]), BF16),
-            pltpu.SemaphoreType.DMA((dp, cols)),
-        ]
-        + Gather.scratch(cols, SUBS),
-        compiler_params=params(7),
-        cost_estimate=cost(35),
-        name="gate_up_cotangent_gather",
-    )(normed, weight, cotan)
 
 
 def hidden_back_kernel(
@@ -1302,7 +1540,7 @@
     grad_sem,
 ):
     group, narrow = hidden.shape
-    dp, cols, part_rows, _ = gate_up_from.shape
+    dp, cols, part_rows, _ = down_from.shape
     wide = weight_grad.shape[3]
     blocks = group // BLOCK
     depth = normed.shape[1] // cols
@@ -1321,7 +1559,8 @@
     down_copies = load_columns(down_from, down, down_sem)
     for copy in block_copies(0):
         copy.start()
-    gate_up_copies = load_columns(gate_up_from, gate_up, gate_up_sem)
+    gate_up_copy = pltpu.make_async_copy(gate_up_from, gate_up, gate_up_sem.at[0])
+    gate_up_copy.start()
     for m in range(1, blocks):
         for copy in block_copies(m):
             copy.start()
@@ -1350,8 +1589,7 @@
         both = jnp.concatenate([grad * gate_part[rows, :], grad * up_part[rows, :]], axis=1)
         grads[rows, :] = both.astype(BF16)
 
-    for copy in gate_up_copies:
-        copy.wait()
+    gate_up_copy.wait()
 
     @pl.loop(0, blocks)
     def _(m):
@@ -1384,7 +1622,8 @@
 
 def hidden_back(hidden, gate_part, up_part, cotan, gate_up, down, normed):
     group, width = normed.shape
-    dp, cols, part, double = gate_up.shape
+    dp, cols, part, _ = down.shape
+    double = gate_up.shape[1]
     grad_shape = (dp, cols, part, double + down.shape[3])
     blocks = group // BLOCK
     dma = pltpu.SemaphoreType.DMA
@@ -1407,7 +1646,7 @@
             pltpu.VMEM((group, double), BF16),
             pltpu.VMEM(grad_shape, BF16),
             pltpu.VMEM((group, width), BF16),
-            dma((dp, cols)),
+            dma((1,)),
             dma((dp, cols)),
             dma((3, blocks)),
             dma((2,)),
@@ -1462,24 +1701,6 @@
     )(whole)
 
 
-def columns_piece(block, sizes):
-    dp, cols = sizes["dp"], sizes["col"]
-    depth, k, wide = block.shape
-    part = depth // dp
-    piece = lax.dynamic_slice_in_dim(block, lax.axis_index("dp") * part, part, 0)
-    piece = piece.reshape(part, k, cols, wide // cols).transpose(2, 0, 1, 3)
-    return piece.reshape(cols, part, k * wide // cols)
-
-
-def rows_piece(block, sizes):
-    dp, cols = sizes["dp"], sizes["col"]
-    wide, depth = block.shape
-    part, narrow = depth // dp, wide // cols
-    piece = lax.dynamic_slice_in_dim(block, lax.axis_index("dp") * part, part, 1)
-    piece = piece.reshape(cols, narrow, part).transpose(0, 2, 1)
-    return jnp.pad(piece, ((0, 0), (0, 0), (0, -narrow % 128)))
-
-
 def weights_whole(piece):
     return lax.all_gather(piece, "dp", axis=0)
 
@@ -1516,15 +1737,29 @@
             [attention_norm_gain, attention_norm_bias, feedforward_norm_gain, feedforward_norm_bias]
         )
         vector = jnp.concatenate([vector, jnp.zeros_like(vector)])
-        attention_piece = jnp.concatenate(
-            [columns_piece(qkv_weight, sizes), rows_piece(out_weight, sizes)], axis=2
-        )
-        (attention_piece,) = exchange(cols, 9, attention_piece)
-        tokens, attention_piece = lax.optimization_barrier((tokens, attention_piece))
-        attention_w = weights_whole(attention_piece)
-        gate_up_piece = columns_piece(gate_up_weight, sizes)
-        down_piece = rows_piece(down_weight, sizes)
-        normed_one, tokens_own, xhat_one, rstd_one, vectors = norm_one(cols, tokens, vector)
+        part = depth // sizes["dp"]
+
+        def share_of(rows):
+            return rows if part % 128 == 0 else lax.dynamic_slice_in_dim(rows, my_dp * part, part, 1)
+
+        (
+            normed_one,
+            tokens_own,
+            xhat_one,
+            rstd_one,
+            vectors,
+            gate_up_piece,
+            down_piece,
+            attention_w,
+        ) = start_part(
+            tokens,
+            vector,
+            qkv_weight.transpose(1, 0, 2),
+            share_of(out_weight),
+            gate_up_weight,
+            share_of(down_weight),
+            sizes,
+        )
         heads_in, attn, logs, branch_part, gate_up_piece, down_piece = attend(
             cols,
             normed_one,
@@ -1534,12 +1769,11 @@
             gate_up_piece,
             down_piece,
         )
-        gate_up_w = weights_whole(gate_up_piece)
+        down_w = weights_whole(down_piece)
         narrow = down_weight.shape[0] // cols
-        normed_two, middle = norm_two(cols, branch_part, tokens_own, vectors)
-        down_piece, normed_two = lax.optimization_barrier((down_piece, normed_two))
-        down_w = weights_whole(down_piece)
-        hidden, gate_part, up_part, cotan_rows = gate_up(cols, normed_two, gate_up_w, cotangent)
+        normed_two, middle, hidden, gate_part, up_part, gate_up_w, cotan_rows = middle_part(
+            cols, branch_part, tokens_own, vectors, gate_up_piece, cotangent, sizes["dp"]
+        )
         cotan_own = lax.dynamic_slice_in_dim(cotan_rows, my_row * half + my_col * own, own, 0)
         hidden_grad, normed_part = hidden_back(
             hidden, gate_part, up_part, cotan_rows, gate_up_w, down_w, normed_two
@@ -1550,7 +1784,7 @@
         )
         second = second.reshape(8, cols, depth).transpose(1, 0, 2)
         grad_block = lax.dynamic_slice(grad_middle, (my_row * half, my_col * depth), (half, depth))
-        attention_grad, normed_part, bias_part, hidden_sum = attend_back(
+        heads_grad, out_grad, normed_part, bias_part, hidden_sum = attend_back(
             cols,
             heads_in,
             logs,
@@ -1563,17 +1797,20 @@
             narrow,
         )
         hidden_sum = lax.all_gather(hidden_sum, "dp", axis=0)
-        input_grad, first, attention_grad = sum_first(
+        input_grad, norms, attention_sum = sum_first(
             cols,
             normed_part,
             xhat_one,
             rstd_one,
             attention_norm_gain.reshape(1, -1),
             grad_block,
-            attention_grad,
-        )
-        attention_sum, small = finish(cols, attention_grad, second, first, bias_part)
-        mixed, attention_sum = sum_mixed(cols, mixed_part, middle, attention_sum, sizes["dp"])
+            heads_grad,
+            out_grad,
+            second,
+        )
+        mixed, attention_sum, small = sum_mixed(
+            cols, mixed_part, middle, attention_sum, norms, bias_part, sizes["dp"]
+        )
         grad_gate_up, grad_down = weights_split(hidden_sum, True)
         grad_qkv_weight, grad_out = weights_split(attention_sum, False)
         grad_qkv_weight = grad_qkv_weight.transpose(1, 0, 2)

time: 669 us -> 596 us (0.89)
  Pallas kernels: 607 us -> 550 us
  local copies, waits for them, and re-layouts: 23.6 us -> 11 us
    pallas_call x5 -> x2, Pallas kernels: 219 us -> 192 us  [the longest x1 116 us: middle_part(): pl.pallas_call(functools.partial(middle_kernel, cols), out_shape=tuple((j...]
    pallas_call x1, Pallas kernels: 72 us -> 52.5 us  [sum_mixed(): pl.pallas_call(functools.partial(mixed_kernel, cols), out_shape=(jax.Shap...]
    pallas_call x1, Pallas kernels: 88.7 us -> 71.8 us  [sum_first(): pl.pallas_call(functools.partial(first_kernel, cols), out_shape=(jax.Shap...]
    pallas_call x1, Pallas kernels: 50.1 us -> 60.5 us  [attend_back(): pl.pallas_call(functools.partial(attend_back_kernel, cols), out_shape=(ja...]
  transfers between devices with their start and end apart: 5 -> 3, of which waited for: 1 -> 1; matrix products, arithmetic and copies ran while one was open for 2% -> 1% of each run, Pallas kernels for 66% -> 54%
where the time goes in v5:
time: 596 us; the launch traced here: 589 us
  Pallas kernels  550 us (92%)
  waiting for transfers between devices  14.1 us (2%)
  between operations  14.1 us (2%)
  local copies, waits for them, and re-layouts  11 us (2%)
    pallas_call x1, Pallas kernels, middle_part(): pl.pallas_call(functools.partial(middle_kernel, cols), out_shape=tuple((j...  116 us
    pallas_call x1, Pallas kernels, start_part(): pl.pallas_call(functools.partial(start_kernel, cols), out_shape=(jax.Shap...  75.5 us
    pallas_call x1, Pallas kernels, norm_two_back(): pl.pallas_call(functools.partial(norm_two_back_kernel, cols), out_shape=(...  73.3 us
    pallas_call x1, Pallas kernels, sum_first(): pl.pallas_call(functools.partial(first_kernel, cols), out_shape=(jax.Shap...  71.8 us
    pallas_call x1, Pallas kernels, attend_back(): pl.pallas_call(functools.partial(attend_back_kernel, cols), out_shape=(ja...  60.5 us
    pallas_call x1, Pallas kernels, attend(): pl.pallas_call(functools.partial(attend_kernel, cols), out_shape=(jax.Sha...  53.4 us
    pallas_call x1, Pallas kernels, sum_mixed(): pl.pallas_call(functools.partial(mixed_kernel, cols), out_shape=(jax.Shap...  52.5 us
    pallas_call x1, Pallas kernels, hidden_back(): pl.pallas_call(hidden_back_kernel, out_shape=(jax.ShapeDtypeStruct(grad_s...  29.4 us
  transfers between devices with their start and end apart: 3, of which 1 were waited for; matrix products, arithmetic and copies ran while one was open for 1% of the time, Pallas kernels for 54%

profile of v5, /device:TPU:0, one launch (start us, length us, event | category | flops | bytes accessed | tf_op | source)
XLA Modules:
  0.0 589.2 jit_solution(18414904049827582052)
XLA Ops:
  7.2 0.0 all-gather.5.cloned.1.call-start
  7.2 1.3 copy.23
  8.5 1.4 concatenate.3.vector
  9.8 75.5 %tokens_norm_weights.1 = (bf16[1024,2048]{1,0:T(8,128)(2,1)}, bf16[128,2048]{1,0:T(8,128)(2,1)}, f32[512,512]{1,0:T(8,128)}, f32[512,128]{1,0:T(8,128)}, f32[8,2...) custom-call(bf16[512,512]{1,0:T(8,128)(2,1)} %tokens.1, ...), custom_call_target="tpu_custom_call" | custom-call | flops 60000002048 | bytes 10000000 | tf_op jit(solution)/shard_map/tokens_norm_weights/pallas_call | solution.py:1174
  85.4 53.4 %attention_weight_exchange.1 = (bf16[1024,768]{1,0:T(8,128)(2,1)}, bf16[1024,256]{1,0:T(8,128)(2,1)}, f32[2,2,1024,128]{3,2,1,0:T(8,128)}, bf16[1024,2048]{1,0:T...) custom-call(bf16[1024,2048]{1,0:T(8,128)(2,1)} %get-tuple-element.52.normed, ...), custom_call_target="tpu_custom_call" | custom-call | flops 49999998976 | bytes 10000000 | tf_op jit(solution)/shard_map/attention_weight_exchange/pallas_call | solution.py:1322
  138.8 0.0 all-gather.5.cloned.1.call-update
  138.8 0.2 reduce-scatter.2.cloned.1.call-start
  139.0 116.4 %middle_gate_up.1 = (bf16[1024,2048]{1,0:T(8,128)(2,1)}, f32[128,2048]{1,0:T(8,128)}, bf16[1024,704]{1,0:T(8,128)(2,1)}, f32[1024,704]{1,0:T(8,128)}, f32[1024,7...) custom-call(bf16[1024,2048]{1,0:T(8,128)(2,1)} %get-tuple-element.56.part, ...), custom_call_target="tpu_custom_call" | custom-call | flops 95000002560 | bytes 10000000 | tf_op jit(solution)/shard_map/middle_gate_up/pallas_call | solution.py:635
  255.4 0.0 all-gather.5.cloned.1.call-done
  255.5 29.4 %hidden_back.1 = (bf16[4,4,128,2176]{3,2,1,0:T(8,128)(2,1)}, bf16[1024,2048]{1,0:T(8,128)(2,1)}) custom-call(bf16[1024,704]{1,0:T(8,128)(2,1)} %get-tuple-element.60.hidden_from.hidden, f32[1024,704]{1,0:T(8,128)} %get-tuple-element.61.gate_from, f32[1024,704]{1,0:T(8,128)} %get-tuple-element.62.up_from, bf16[1024,2048]{1,0:T(8,128)(2,1)} %get-tuple-element.63.cotan_from, ...), custom_call_target="tpu_custom_call" | custom-call | flops 30000001024 | bytes 10000000 | tf_op jit(solution)/shard_map/hidden_back/pallas_call | solution.py:1630
  284.9 0.0 reduce-scatter.2.cloned.1.call-update
  284.9 0.0 all-gather.7.cloned.1.call-start
  285.0 1.9 constant_dynamic-slice_fusion.cotan_own
  286.9 73.3 %grad_sum_norm_gather.1 = (bf16[1024,2048]{1,0:T(8,128)(2,1)}, f32[8,2048]{1,0:T(8,128)}, bf16[1024,2048]{1,0:T(8,128)(2,1)}) custom-call(bf16[1024,2048]{1,0:T(8,128)(2,1)} %get-tuple-element.67.part, f32[128,2048]{1,0:T(8,128)} %get-tuple-element.68.middle, bf16[128,2048]{1,0:T(8,128)(2,1)} %constant_dynamic-slice_fusion.cotan_own, ...), custom_call_target="tpu_custom_call" | custom-call | flops 60000002048 | bytes 10000000 | tf_op jit(solution)/shard_map/grad_sum_norm_gather/pallas_call | solution.py:725
  360.2 14.1 %reduce-scatter.2.cloned.1.call-done = bf16[512,2176]{1,0:T(8,128)(2,1)} async-done(((bf16[2048,2176]{1,0:T(8,128)(2,1)}), bf16[512,2176]{1,0:T(8,128)(2,1)}) %reduce-scatter.2.cloned.1.call-update) | async-done | bytes 2228240 | tf_op jit(solution)/shard_map/reduce_scatter | solution.py:1710
  374.3 60.5 %attention_back_exchange.1 = (bf16[2,4,4,128,384]{4,3,2,1,0:T(8,128)(2,1)}, bf16[4,4,128,256]{3,2,1,0:T(8,128)(2,1)}, bf16[1024,2048]{1,0:T(8,128)(2,1)}, f32[8,768]{1,0:T(8,128)}, bf16[3,128,2816]{2,1,0:T(8,128)(2,1)}) custom-call(bf16[1024,768]{1,0:T(8,128)(2,1)} %get-tuple-element.70.heads_in, f32[2,2,1024,128]{3,2,1,0:T(8,128)} %get-tuple-element.71.logs, ...), custom_call_target="tpu_custom_call" | custom-call | flops 49999998976 | bytes 10000000 | tf_op jit(solution)/shard_map/attention_back_exchange/pallas_call | solution.py:1484
  434.8 0.0 all-gather.7.cloned.1.call-update
  434.9 1.9 dynamic_slice.7.grad_middle
  436.7 71.8 %input_grad_sum.1 = (f32[512,512]{1,0:T(8,128)}, f32[8,512]{1,0:T(8,128)}, bf16[4,128,1024]{2,1,0:T(8,128)(2,1)}) custom-call(bf16[1024,2048]{1,0:T(8,128)(2,1)} %get-tuple-element.75.part, f32[512,512]{1,0:T(8,128)} %get-tuple-element.76.xhat, f32[512,128]{1,0:T(8,128)} %get-tuple-element.77.rstd, f32[1,512]{1,0:T(1,128)} %bitcast.27, ...), custom_call_target="tpu_custom_call" | custom-call | flops 60000002048 | bytes 10000000 | tf_op jit(solution)/shard_map/input_grad_sum/pallas_call | solution.py:979
  508.5 52.5 %mixed_sum.1 = (bf16[512,512]{1,0:T(8,128)(2,1)}, bf16[4,4,128,1024]{3,2,1,0:T(8,128)(2,1)}, f32[8,1280]{1,0:T(8,128)}) custom-call(bf16[1024,2048]{1,0:T(8,128)(2,1)} %get-tuple-element.69.part, f32[128,2048]{1,0:T(8,128)} %get-tuple-element.68.middle, bf16[4,128,1024]{2,1,0:T(8,128)(2,1)} %get-tuple-element.81.piece, f32[8,512]{1,0:T(8,128)} %get-tuple-element.82.norms, ...), custom_call_target="tpu_custom_call" | custom-call | flops 44999999488 | bytes 10000000 | tf_op jit(solution)/shard_map/mixed_sum/pallas_call | solution.py:823
  561.0 0.8 slice_reduce_fusion
  561.8 0.6 reshape_squeeze.3
  562.4 1.5 fusion
  563.8 6.0 %weight_gradients.2 = (f32[3,512,1024]{2,1,0:T(8,128)}, f32[1024,512]{1,0:T(8,128)}) custom-call(bf16[4,4,128,1024]{3,2,1,0:T(8,128)(2,1)} %get-tuple-element.87.whole), custom_call_target="tpu_custom_call" | custom-call | flops 8000000000 | bytes 10000000 | tf_op jit(solution)/shard_map/weight_gradients/pallas_call | solution.py:1687
  569.9 0.0 all-gather.7.cloned.1.call-done
  569.9 0.0 copy-start.1
  569.9 0.0 copy-start
  569.9 10.8 %weight_gradients.3 = (f32[512,2,2816]{2,1,0:T(2,128)}, f32[2816,512]{1,0:T(8,128)}) custom-call(bf16[4,3,128,2816]{3,2,1,0:T(8,128)(2,1)} %bitcast.32), custom_call_target="tpu_custom_call" | custom-call | flops 8000000000 | bytes 10000000 | tf_op jit(solution)/shard_map/weight_gradients/pallas_call | solution.py:1687
  580.7 0.0 copy-done.1
  580.7 0.8 copy.26
  581.5 0.0 copy-done
  581.5 1.0 copy.27
  (1 shorter events, 0.0 us)
Async XLA Ops:
  7.2 248.3 %all-gather.5.cloned.1.call-start = ((), (), s32[]{:S(2)}) async-start(), calls=%async_computation.2 | async-start | bytes 3932160 | tf_op jit(solution)/shard_map/all_gather | solution.py:1705
  138.8 235.5 %reduce-scatter.2.cloned.1.call-start = ((), (), s32[]{:S(2)}) async-start(), calls=%async_computation.1 | async-start | bytes 11141120 | tf_op jit(solution)/shard_map/reduce_scatter | solution.py:1710
  284.9 284.9 %all-gather.7.cloned.1.call-start = ((), (), s32[]{:S(2)}) async-start(), calls=%async_computation.3 | async-start | bytes 10813440 | tf_op jit(solution)/shard_map/all_gather | solution.py:1799
  569.9 10.8 %copy-start.1 = (bf16[512,512]{1,0:T(8,128)(2,1)S(1)}, bf16[512,512]{1,0:T(8,128)(2,1)}, u32[]{:S(2)}) copy-start(bf16[512,512]{1,0:T(8,128)(2,1)} %get-tuple-element.108) | copy-start | bytes 1572868
  569.9 11.6 %copy-start = (f32[512,512]{1,0:T(8,128)S(1)}, f32[512,512]{1,0:T(8,128)}, u32[]{:S(2)}) copy-start(f32[512,512]{1,0:T(8,128)} %get-tuple-element.109) | copy-start | bytes 3145732
Sparse Core Ops, SparseCore 0:
  138.9 69.8 all-gather.4
  285.0 89.1 reduce-scatter.1
  435.0 97.0 all-gather.6

commit v6 on v5

--- a/solution.py
+++ b/solution.py
@@ -412,6 +412,57 @@
 
 
 ANY = pl.BlockSpec(memory_space=pl.ANY)
+
+
+def staged_call(kernel, args, out_shape, in_specs, out_specs, scratch_shapes, loads, stores, **kinds):
+    counts = len(args), len(out_shape)
+    dma = pltpu.SemaphoreType.DMA
+    buffers = [pltpu.VMEM(shape, args[i].dtype) for i, shape, _ in loads]
+    buffers += [pltpu.VMEM(out_shape[j].shape, out_shape[j].dtype) for j in stores]
+    in_specs, out_specs = list(in_specs), list(out_specs)
+    for i, _, _ in loads:
+        in_specs[i] = ANY
+    for j in stores:
+        out_specs[j] = ANY
+
+    def run(*refs):
+        ins, outs = list(refs[: counts[0]]), list(refs[counts[0] : sum(counts)])
+        own = refs[len(refs) - len(buffers) - 2 :]
+        in_sem, out_sem = own[-2:]
+        coming, going = {}, {}
+        for n, (i, _, part) in enumerate(loads):
+            source = ins[i] if part is None else ins[i].at[part()]
+            coming[i] = pltpu.make_async_copy(source, own[n], in_sem.at[n])
+            ins[i] = own[n]
+        for n, j in enumerate(stores):
+            buffer = own[len(loads) + n]
+            going[j] = pltpu.make_async_copy(buffer, outs[j], out_sem.at[n])
+            outs[j] = buffer
+        for copy in coming.values():
+            copy.start()
+
+        def load(*which):
+            for i in which:
+                coming[i].wait()
+
+        def store(*which):
+            for j in which:
+                going[j].start()
+
+        kernel(*ins, *outs, *refs[sum(counts) : len(refs) - len(own)], load=load, store=store)
+        for copy in going.values():
+            copy.wait()
+
+    return pl.pallas_call(
+        run,
+        out_shape=tuple(out_shape),
+        in_specs=in_specs,
+        out_specs=tuple(out_specs),
+        scratch_shapes=list(scratch_shapes)
+        + buffers
+        + [dma((max(len(loads), 1),)), dma((max(len(stores), 1),))],
+        **kinds,
+    )(*args)
 
 
 def load_columns(weight, whole, sem):
@@ -496,7 +547,9 @@
     own_sem,
     out_sem,
     block_sem,
-    *scratch
+    *scratch,
+    load,
+    store
 ):
     group, width = part.shape
     half = group // 2
@@ -509,6 +562,7 @@
     dp = weight.shape[0] // cols // part_rows
     me = lax.axis_index("dp")
     enter(cols, everyone=True, dp=dp)
+    load(0)
     summing = Reduce(
         cols, SUBS, lambda d, s: (d * own + s * step, step, 0, width), part, *scratch[:3], scratch[3:7]
     )
@@ -531,6 +585,7 @@
     ]
     for copy in own_copies:
         copy.start()
+    load(1, 2, 4)
 
     def land(s):
         summing.land(s, total)
@@ -632,11 +687,15 @@
         ((dp * cols * part_rows, double), BF16),
         ((group, width), BF16),
     )
-    return pl.pallas_call(
+    args = (part, tokens_own, vectors, piece, cotan)
+    return staged_call(
         functools.partial(middle_kernel, cols),
+        args,
         out_shape=tuple(jax.ShapeDtypeStruct(*out) for out in outs),
         in_specs=[VM] * 3 + [ANY, VM],
-        out_specs=(ANY,) * len(outs),
+        out_specs=[ANY] * len(outs),
+        loads=[(i, args[i].shape, None) for i in (0, 1, 2, 4)],
+        stores=(),
         scratch_shapes=[pltpu.VMEM(*out) for out in outs]
         + [
             pltpu.VMEM((group // 2 // cols // SUBS, width), F32),
@@ -650,7 +709,7 @@
         compiler_params=params(2),
         cost_estimate=cost(95),
         name="middle_gate_up",
-    )(part, tokens_own, vectors, piece, cotan)
+    )
 
 
 def norm_two_back_kernel(
@@ -666,7 +725,9 @@
     mixed_part,
     down,
     sem,
-    *scratch
+    *scratch,
+    load,
+    store
 ):
     narrow = hidden.shape[1]
     copies = load_columns(weight, down, sem)
@@ -675,6 +736,7 @@
     step = own // SUBS
     total = scratch[11]
     enter(cols)
+    load(0)
     summing = Reduce(
         cols, SUBS, lambda d, s: (d * own + s * step, step, 0, width), part, *scratch[:3], scratch[3:7]
     )
@@ -683,6 +745,7 @@
     blocks = part.shape[0] // BLOCK
     for copy in copies:
         copy.wait()
+    load(1, 2, 3, 4)
     sums[...] = jnp.zeros_like(sums)
 
     def land(s):
@@ -715,22 +778,36 @@
             result = dot_nt(hidden[rows, :], down[:, :narrow])
             mixed_part[rows, :] = result.astype(BF16)
 
+    store(2)
     spread.finish()
+    store(0)
     summing.finish()
 
 
-def norm_two_back(cols, part, middle, cotan_own, vectors, hidden, weight):
+def norm_two_back(cols, part, middle, cotan, vectors, hidden, weight):
     group, width = part.shape
     tall = weight.shape[3]
-    return pl.pallas_call(
+    own = group // 2 // cols
+
+    def own_rows():
+        row = lax.axis_index("row") * (group // 2) + lax.axis_index("col") * own
+        return pl.ds(pl.multiple_of(row, own), own)
+
+    args = (part, middle, cotan, vectors, hidden, weight)
+    return staged_call(
         functools.partial(norm_two_back_kernel, cols),
+        args,
         out_shape=(
             jax.ShapeDtypeStruct((group, width), BF16),
             jax.ShapeDtypeStruct((8, width), F32),
             jax.ShapeDtypeStruct((group, width), BF16),
         ),
         in_specs=[VM] * 5 + [ANY],
-        out_specs=(VM,) * 3,
+        out_specs=[VM] * 3,
+        loads=[(i, args[i].shape, None) for i in (0, 1)]
+        + [(2, (own, width), own_rows)]
+        + [(i, args[i].shape, None) for i in (3, 4)],
+        stores=(0, 2),
         scratch_shapes=[pltpu.VMEM((width, tall), BF16), pltpu.SemaphoreType.DMA(weight.shape[:2])]
         + Reduce.scratch(cols, SUBS, group // 2, width)
         + Gather.scratch(cols, SUBS)
@@ -738,7 +815,7 @@
         compiler_params=params(3),
         cost_estimate=cost(60),
         name="grad_sum_norm_gather",
-    )(part, middle, cotan_own, vectors, hidden, weight)
+    )
 
 
 def mixed_sum(cols, part, middle, scratch):
@@ -763,88 +840,11 @@
     )
 
 
-def mixed_kernel(
-    cols, part, middle, piece, norms, bias, mixed, pieces, small, total, mine, all_dp, *sems
-):
-    half = part.shape[0] // 2
-    step = half // SUBS
-    dp = pieces.shape[0]
-    depth = norms.shape[1]
-    me = lax.axis_index("dp")
-    enter(cols, everyone=True, dp=dp)
-    summing = mixed_sum(cols, part, middle, sems[:7])
-    summing.start()
-    mine[:, :depth] = norms[...]
-    mine[:, depth:] = bias[...]
-    all_dp[me] = mine[...]
-
-    def hop(k):
-        to = lax.rem(me + k, dp)
-        return send(mine, all_dp.at[me], sems[7].at[k - 1], sems[8].at[k - 1], dp=to)
-
-    for k in range(1, dp):
-        hop(k).start()
-    rider = Broadcast(
-        dp, piece.shape[0], lambda u: piece.at[u], lambda p, u: pieces.at[p, u], sems[9:11]
-    )
-    rider.start()
-    own = pltpu.make_async_copy(piece, pieces.at[me], sems[11].at[0])
-    own.start()
-
-    def land(s):
-        summing.land(s, total)
-        mixed[pl.ds(pl.multiple_of(s * step, step), step), :] = total[...].astype(BF16)
-
-    @pl.loop(0, summing.slots)
-    def _(t):
-        summing.slot(t)
-        summing.landed(t, land)
-        for u in range(rider.units):
-
-            @pl.when(t == 14 + 7 * (u % 2))
-            def _():
-                rider.forward(u)
-
-    for k in range(1, dp):
-        hop(k).wait()
-    value = all_dp[0]
-    for p in range(1, dp):
-        value = value + all_dp[p]
-    small[...] = value
-    summing.finish()
-    own.wait()
-    rider.finish()
-
-
-def sum_mixed(cols, part, middle, piece, norms, bias, dp):
-    group, width = part.shape
-    small = (8, norms.shape[1] + bias.shape[1])
-    hops = max(dp - 1, 1)
-    return pl.pallas_call(
-        functools.partial(mixed_kernel, cols),
-        out_shape=(
-            jax.ShapeDtypeStruct((group // 2, width // cols), BF16),
-            jax.ShapeDtypeStruct((dp,) + piece.shape, BF16),
-            jax.ShapeDtypeStruct(small, F32),
-        ),
-        in_specs=[VM] * 2 + [ANY] + [VM] * 2,
-        out_specs=(VM, ANY, VM),
-        scratch_shapes=[
-            pltpu.VMEM((group // 2 // SUBS, width // cols), F32),
-            pltpu.VMEM(small, F32),
-            pltpu.VMEM((dp,) + small, F32),
-        ]
-        + Reduce.scratch(cols, SUBS, group // 2, width)
-        + [pltpu.SemaphoreType.DMA((hops,)), pltpu.SemaphoreType.DMA((hops,))]
-        + Broadcast.scratch(dp, piece.shape[0])
-        + [pltpu.SemaphoreType.DMA((1,))],
-        compiler_params=params(4),
-        cost_estimate=cost(45),
-        name="mixed_sum",
-    )(part, middle, piece, norms, bias)
-
-
-def first_kernel(
+MIXED_SLOT = 22
+ARRANGE_SLOT = 24
+
+
+def last_kernel(
     cols,
     part,
     xhat,
@@ -854,9 +854,15 @@
     heads_grad,
     out_grad,
     second,
+    mixed_part,
+    middle,
+    hidden_piece,
+    bias,
     result,
-    norms,
-    arranged,
+    mixed,
+    small,
+    attention_all,
+    hidden_all,
     total,
     grad,
     mine,
@@ -866,28 +872,55 @@
     slices,
     own_norms,
     pair_norms,
-    *sems
+    arranged,
+    own_small,
+    all_small,
+    out_sem,
+    in_sem,
+    pair_sem,
+    small_send,
+    small_recv,
+    own_sem,
+    *sems,
+    load,
+    store
 ):
     half, width = part.shape[0] // 2, part.shape[1]
     step, depth = half // SUBS, width // cols
     pairs, dp = heads_grad.shape[:2]
     two = heads_grad.shape[4] // 3
     narrow = sums.shape[2] // 4
-    enter(cols, everyone=True)
-    r, c = lax.axis_index("row"), lax.axis_index("col")
+    rows_each = hidden_piece.shape[1] // 2
+    weights = hidden_piece.shape[0]
+    enter(cols, everyone=True, dp=dp)
+    r, c, me = (lax.axis_index(name) for name in ("row", "col", "dp"))
+    load(0)
     summing = Reduce(
-        cols,
-        SUBS,
-        lambda d, s: (s * step, step, d * depth, depth),
-        part,
-        *sems[:3],
-        sems[3:7],
+        cols, SUBS, lambda d, s: (s * step, step, d * depth, depth), part, *sems[:3], sems[3:7]
     )
     summing.start()
-    out_sem, in_sem, pair_sem = sems[7:10]
-    rider = Exchange("col", cols, sums, landed, sems[10:13])
-    names = Exchange("col", cols, second, slices, sems[13:16])
+    rider = Exchange("col", cols, sums, landed, sems[14:17])
+    names = Exchange("col", cols, second, slices, sems[17:20])
     names.start()
+
+    def hidden_rows(u):
+        return u % weights, pl.ds(u // weights * rows_each, rows_each)
+
+    hidden_cast = Broadcast(
+        dp,
+        2 * weights,
+        lambda u: hidden_piece.at[hidden_rows(u)],
+        lambda p, u: hidden_all.at[(p,) + hidden_rows(u)],
+        sems[20:22],
+    )
+    attention_cast = Broadcast(
+        dp, 4, lambda u: arranged.at[u], lambda p, u: attention_all.at[p, u], sems[22:24]
+    )
+    hidden_own = pltpu.make_async_copy(hidden_piece, hidden_all.at[me], own_sem.at[0])
+    attention_own = pltpu.make_async_copy(arranged, attention_all.at[me], own_sem.at[1])
+    hidden_cast.start()
+    hidden_own.start()
+    load(5, 6)
 
     def over_dp(ref, to):
         value = ref[0, to].astype(F32)
@@ -909,6 +942,10 @@
         rider.hop(k).start()
     fill(c, landed.at[c])
     own_norms[...] = jnp.zeros_like(own_norms)
+    load(8, 9)
+    mixing = mixed_sum(cols, mixed_part, middle, sems[7:14])
+    mixing.start()
+    load(1, 2, 4)
 
     def land(s):
         summing.land(s, total)
@@ -918,10 +955,37 @@
         own_norms[0:1, :] += jnp.sum(total[...] * standard, axis=0, keepdims=True)
         own_norms[1:2, :] += jnp.sum(total[...], axis=0, keepdims=True)
 
+    def land_mixed(s):
+        mixing.land(s, total)
+        mixed[pl.ds(pl.multiple_of(s * step, step), step), :] = total[...].astype(BF16)
+
+    def arrange():
+        for k in range(1, cols):
+            rider.hop(k).wait_recv()
+        for k in range(4):
+            for j in range(cols):
+                arranged[k, :, j * narrow : (j + 1) * narrow] = landed[
+                    j, :, k * narrow : (k + 1) * narrow
+                ]
+        attention_cast.start()
+        attention_own.start()
+
     @pl.loop(0, summing.slots)
     def _(t):
         summing.slot(t)
         summing.landed(t, land)
+        mixing.slot(t - MIXED_SLOT)
+        mixing.landed(t - MIXED_SLOT, land_mixed)
+        for u in range(weights):
+
+            @pl.when(t == 8 + 6 * u)
+            def _():
+                hidden_cast.forward(u)
+                hidden_cast.forward(weights + u)
+
+        @pl.when(t == ARRANGE_SLOT)
+        def _():
+            arrange()
 
     lanes = lax.broadcasted_iota(jnp.int32, (128, 128), 1)
     for s in range(half // 128):
@@ -946,6 +1010,31 @@
     own_norms[2:4, :] = shift[0:2, :]
     across = send(own_norms, pair_norms, pair_sem.at[0], pair_sem.at[1], row=1 - r)
     across.start()
+
+    @pl.loop(summing.slots, MIXED_SLOT + mixing.slots)
+    def _(t):
+        mixing.slot(t - MIXED_SLOT)
+        mixing.landed(t - MIXED_SLOT, land_mixed)
+        for u in range(2):
+
+            @pl.when(t == summing.slots + 6 + 8 * u)
+            def _():
+                attention_cast.forward(u)
+                attention_cast.forward(2 + u)
+
+    across.wait()
+    own_small[:, :depth] = own_norms[...] + pair_norms[...]
+    own_small[:, depth:] = bias[...]
+    all_small[me] = own_small[...]
+
+    def hop(k):
+        to = lax.rem(me + k, dp)
+        return send(
+            own_small, all_small.at[me], small_send.at[k - 1], small_recv.at[k - 1], dp=to
+        )
+
+    for k in range(1, dp):
+        hop(k).start()
     for k in range(1, cols):
         exchange_sums(k).wait_recv()
     for s in range(half // 128):
@@ -957,34 +1046,68 @@
         scaled = grad[rows, :] * gain[0:1, :]
         inner = scaled - both[:, 0:1] - xhat[rows, :] * both[:, 1:2]
         result[rows, :] = grad_middle[rows, :].astype(F32) + rstd[rows, 0:1] * inner
+    store(0, 1)
+    for k in range(1, dp):
+        hop(k).wait()
+    value = all_small[0]
+    for p in range(1, dp):
+        value = value + all_small[p]
+    small[...] = value
     for k in range(1, cols):
         exchange_sums(k).wait_send()
-    across.wait()
-    norms[...] = own_norms[...] + pair_norms[...]
+        rider.hop(k).wait_send()
     summing.finish()
-    for k in range(1, cols):
-        rider.hop(k).wait()
-    for k in range(4):
-        for j in range(cols):
-            arranged[k, :, j * narrow : (j + 1) * narrow] = landed[
-                j, :, k * narrow : (k + 1) * narrow
-            ]
-
-
-def sum_first(cols, part, xhat, rstd, gain, grad_middle, heads_grad, out_grad, second):
+    mixing.finish()
+    hidden_own.wait()
+    attention_own.wait()
+    hidden_cast.finish()
+    attention_cast.finish()
+
+
+def last_part(
+    cols, part, xhat, rstd, gain, grad_middle, heads_grad, out_grad, second, mixed_part, middle, piece, bias
+):
     group, width = part.shape
     half, depth = group // 2, width // cols
-    rows, narrow = out_grad.shape[2:]
+    dp, _, rows, narrow = out_grad.shape
+    small = (8, depth + bias.shape[1])
+    hops = max(dp - 1, 1)
     dma = pltpu.SemaphoreType.DMA
-    return pl.pallas_call(
-        functools.partial(first_kernel, cols),
+
+    def own_block():
+        row = lax.axis_index("row") * half
+        column = lax.axis_index("col") * depth
+        return pl.ds(pl.multiple_of(row, half), half), pl.ds(pl.multiple_of(column, 128), depth)
+
+    args = (
+        part,
+        xhat,
+        rstd,
+        gain,
+        grad_middle,
+        heads_grad,
+        out_grad,
+        second,
+        mixed_part,
+        middle,
+        piece,
+        bias,
+    )
+    return staged_call(
+        functools.partial(last_kernel, cols),
+        args,
         out_shape=(
             jax.ShapeDtypeStruct((half, depth), F32),
-            jax.ShapeDtypeStruct((8, depth), F32),
-            jax.ShapeDtypeStruct((4, rows, cols * narrow), BF16),
+            jax.ShapeDtypeStruct((half, depth), BF16),
+            jax.ShapeDtypeStruct(small, F32),
+            jax.ShapeDtypeStruct((dp, 4, rows, cols * narrow), BF16),
+            jax.ShapeDtypeStruct((dp,) + piece.shape, BF16),
         ),
-        in_specs=[VM] * 8,
-        out_specs=(VM,) * 3,
+        in_specs=[VM] * 10 + [ANY, VM],
+        out_specs=[VM] * 3 + [ANY] * 2,
+        loads=[(i, args[i].shape, None) for i in (0, 5, 6, 8, 9, 1, 2)]
+        + [(4, (half, depth), own_block)],
+        stores=(0, 1),
         scratch_shapes=[
             pltpu.VMEM((half // SUBS, depth), F32),
             pltpu.VMEM((half, depth), F32),
@@ -995,14 +1118,24 @@
             pltpu.VMEM((cols, 8, depth), F32),
             pltpu.VMEM((8, depth), F32),
             pltpu.VMEM((8, depth), F32),
+            pltpu.VMEM((4, rows, cols * narrow), BF16),
+            pltpu.VMEM(small, F32),
+            pltpu.VMEM((dp,) + small, F32),
+            dma((cols - 1,)),
+            dma((cols - 1,)),
+            dma((2,)),
+            dma((hops,)),
+            dma((hops,)),
+            dma((2,)),
         ]
-        + Reduce.scratch(cols, SUBS, half, width)
-        + [dma((cols - 1,)), dma((cols - 1,)), dma((2,))]
-        + Exchange.scratch(cols) * 2,
+        + Reduce.scratch(cols, SUBS, half, width) * 2
+        + Exchange.scratch(cols) * 2
+        + Broadcast.scratch(dp, 2 * piece.shape[0])
+        + Broadcast.scratch(dp, 4),
         compiler_params=params(5),
-        cost_estimate=cost(60),
-        name="input_grad_sum",
-    )(part, xhat, rstd, gain, grad_middle, heads_grad, out_grad, second)
+        cost_estimate=cost(110),
+        name="input_grad_mixed_sum",
+    )
 
 
 def start_kernel(
@@ -1251,7 +1384,9 @@
     whole,
     sem,
     qkv,
-    *sems
+    *sems,
+    load,
+    store
 ):
     length, wide = attn.shape
     two = 2 * HD
@@ -1265,6 +1400,7 @@
         rider.start()
     for copy in copies:
         copy.wait()
+    load(0, 3)
     first_head = lax.broadcasted_iota(jnp.int32, (BLOCK, two), 1) < HD
 
     @pl.loop(0, length // BLOCK)
@@ -1306,11 +1442,14 @@
                 first_head, outs[0], outs[1]
             ).astype(BF16)
 
+    store(0, 1, 2)
+
     @pl.loop(0, length // BLOCK)
     def _(m):
         rows = pl.ds(pl.multiple_of(m * BLOCK, BLOCK), BLOCK)
         part[rows, :] = dot_nt(attn[rows, :], whole[:, 3 * wide :]).astype(BF16)
 
+    store(3)
     for rider in riders:
         rider.finish()
 
@@ -1319,8 +1458,10 @@
     length, width = normed.shape
     dp = weight.shape[0]
     wide = weight.shape[3] // 4
-    return pl.pallas_call(
+    args = (normed, weight, bias, tables, one, two)
+    return staged_call(
         functools.partial(attend_kernel, cols),
+        args,
         out_shape=(
             jax.ShapeDtypeStruct((length, 3 * wide), BF16),
             jax.ShapeDtypeStruct((length, wide), BF16),
@@ -1330,7 +1471,9 @@
             jax.ShapeDtypeStruct(two.shape, BF16),
         ),
         in_specs=[VM, ANY, VM, VM, ANY, ANY],
-        out_specs=(VM,) * 4 + (ANY,) * 2,
+        out_specs=[VM] * 4 + [ANY] * 2,
+        loads=[(i, args[i].shape, None) for i in (0, 3)],
+        stores=(0, 1, 2, 3),
         scratch_shapes=[
             pltpu.VMEM((width, 4 * wide), BF16),
             pltpu.SemaphoreType.DMA((dp, cols)),
@@ -1340,7 +1483,7 @@
         compiler_params=params(6),
         cost_estimate=cost(50),
         name="attention_weight_exchange",
-    )(normed, weight, bias, tables, one, two)
+    )
 
 
 def attend_back_kernel(
@@ -1369,7 +1512,9 @@
     pieces_to,
     heads_from,
     out_from,
-    *sems
+    *sems,
+    load,
+    store
 ):
     length, wide = attn.shape
     two = 2 * HD
@@ -1380,6 +1525,7 @@
     rider.start()
     out_rider = Exchange("dp", dp, out_from, out_to, sems[3:6])
     depth = normed.shape[1] // cols
+    load(2, 6)
 
     def heads_rider(pair):
         return Exchange(
@@ -1398,6 +1544,7 @@
     out_rider.start()
     for copy in copies:
         copy.wait()
+    load(0, 1, 3, 5)
     sums[...] = jnp.zeros_like(sums)
     first_head = lax.broadcasted_iota(jnp.int32, (BLOCK, two), 1) < HD
 
@@ -1461,6 +1608,7 @@
         rows = pl.ds(pl.multiple_of(m * BLOCK, BLOCK), BLOCK)
         normed_grad[rows, :] = dot_nt(result[rows, :], whole[:, : 3 * wide]).astype(BF16)
 
+    store(2)
     out_rider.finish()
     for pair in range(wide // two):
         heads_rider(pair).finish()
@@ -1481,8 +1629,10 @@
     out = (dp, cols, part, wide)
     hops = max(dp - 1, 1)
     dma = pltpu.SemaphoreType.DMA
-    return pl.pallas_call(
+    args = (heads_in, logs, grad_middle, tables, weight, normed, attn, pieces)
+    return staged_call(
         functools.partial(attend_back_kernel, cols),
+        args,
         out_shape=(
             jax.ShapeDtypeStruct(heads, BF16),
             jax.ShapeDtypeStruct(out, BF16),
@@ -1491,7 +1641,9 @@
             jax.ShapeDtypeStruct((3, pieces.shape[1], cols * share), BF16),
         ),
         in_specs=[VM] * 4 + [ANY, VM, VM, ANY],
-        out_specs=(ANY,) * 2 + (VM,) * 3,
+        out_specs=[ANY] * 2 + [VM] * 3,
+        loads=[(i, args[i].shape, None) for i in (2, 6, 0, 1, 3, 5)],
+        stores=(2,),
         scratch_shapes=[pltpu.VMEM((length, 2 * HD), F32)] * 3
         + [
             pltpu.VMEM((width, 4 * wide), BF16),
@@ -1509,7 +1661,7 @@
         compiler_params=params(8),
         cost_estimate=cost(50),
         name="attention_back_exchange",
-    )(heads_in, logs, grad_middle, tables, weight, normed, attn, pieces)
+    )
 
 
 def hidden_back_kernel(
@@ -1729,9 +1881,8 @@
         down_weight,
         cotangent,
     ):
-        my_row, my_col, my_dp = (lax.axis_index(name) for name in ("row", "col", "dp"))
-        half, depth = tokens.shape
-        own = half // cols
+        my_dp = lax.axis_index("dp")
+        depth = tokens.shape[1]
         tables = rope_tables(SEQ)
         vector = jnp.stack(
             [attention_norm_gain, attention_norm_bias, feedforward_norm_gain, feedforward_norm_bias]
@@ -1774,16 +1925,14 @@
         normed_two, middle, hidden, gate_part, up_part, gate_up_w, cotan_rows = middle_part(
             cols, branch_part, tokens_own, vectors, gate_up_piece, cotangent, sizes["dp"]
         )
-        cotan_own = lax.dynamic_slice_in_dim(cotan_rows, my_row * half + my_col * own, own, 0)
         hidden_grad, normed_part = hidden_back(
             hidden, gate_part, up_part, cotan_rows, gate_up_w, down_w, normed_two
         )
         hidden_sum = weights_sum(hidden_grad)
         grad_middle, second, mixed_part = norm_two_back(
-            cols, normed_part, middle, cotan_own, vectors, hidden, down_w
+            cols, normed_part, middle, cotan_rows, vectors, hidden, down_w
         )
         second = second.reshape(8, cols, depth).transpose(1, 0, 2)
-        grad_block = lax.dynamic_slice(grad_middle, (my_row * half, my_col * depth), (half, depth))
         heads_grad, out_grad, normed_part, bias_part, hidden_sum = attend_back(
             cols,
             heads_in,
@@ -1796,20 +1945,20 @@
             hidden_sum,
             narrow,
         )
-        hidden_sum = lax.all_gather(hidden_sum, "dp", axis=0)
-        input_grad, norms, attention_sum = sum_first(
+        input_grad, mixed, small, attention_sum, hidden_sum = last_part(
             cols,
             normed_part,
             xhat_one,
             rstd_one,
             attention_norm_gain.reshape(1, -1),
-            grad_block,
+            grad_middle,
             heads_grad,
             out_grad,
             second,
-        )
-        mixed, attention_sum, small = sum_mixed(
-            cols, mixed_part, middle, attention_sum, norms, bias_part, sizes["dp"]
+            mixed_part,
+            middle,
+            hidden_sum,
+            bias_part,
         )
         grad_gate_up, grad_down = weights_split(hidden_sum, True)
         grad_qkv_weight, grad_out = weights_split(attention_sum, False)

time: 596 us -> 573 us (0.961)
  Pallas kernels: 550 us -> 526 us
    pallas_call x6 -> x5, Pallas kernels: 428 us -> 405 us  [staged_call(): pl.pallas_call(run, out_shape=tuple(out_shape), in_specs=in_specs, out_sp...]
  transfers between devices with their start and end apart: 3 -> 2, of which waited for: 1 -> 1; matrix products, arithmetic and copies ran while one was open for 1% -> 0% of each run, Pallas kernels for 54% -> 33%
where the time goes in v6:
time: 573 us; the launch traced here: 567 us
  Pallas kernels  526 us (92%)
  waiting for transfers between devices  18.6 us (3%)
  between operations  14.4 us (3%)
  local copies, waits for them, and re-layouts  7.21 us (1%)
    pallas_call x5, Pallas kernels, staged_call(): pl.pallas_call(run, out_shape=tuple(out_shape), in_specs=in_specs, out_sp...  405 us
    pallas_call x1, Pallas kernels, start_part(): pl.pallas_call(functools.partial(start_kernel, cols), out_shape=(jax.Shap...  75.6 us
    pallas_call x1, Pallas kernels, hidden_back(): pl.pallas_call(hidden_back_kernel, out_shape=(jax.ShapeDtypeStruct(grad_s...  29.4 us
    reduce_scatter x1, waiting for transfers between devices, weights_sum(): lax.psum_scatter(pieces.reshape(dp * cols * part, wide), 'dp', scatter_di...  18.6 us
    pallas_call x2, Pallas kernels, weights_split(): pl.pallas_call(split_kernel, grid=(depth // 128,), out_shape=(jax.ShapeDt...  16.8 us
  transfers between devices with their start and end apart: 2, of which 1 were waited for; matrix products, arithmetic and copies ran while one was open for 0% of the time, Pallas kernels for 33%

profile of v6, /device:TPU:0, one launch (start us, length us, event | category | flops | bytes accessed | tf_op | source)
XLA Modules:
  0.0 566.9 jit_solution(8884715635213869399)
XLA Ops:
  7.2 0.0 all-gather.3.cloned.1.call-start
  7.2 1.3 copy.23
  8.5 1.4 concatenate.3.vector
  9.8 75.6 %tokens_norm_weights.1 = (bf16[1024,2048]{1,0:T(8,128)(2,1)}, bf16[128,2048]{1,0:T(8,128)(2,1)}, f32[512,512]{1,0:T(8,128)}, f32[512,128]{1,0:T(8,128)}, f32[8,2...) custom-call(bf16[512,512]{1,0:T(8,128)(2,1)} %tokens.1, ...), custom_call_target="tpu_custom_call" | custom-call | flops 60000002048 | bytes 10000000 | tf_op jit(solution)/shard_map/tokens_norm_weights/pallas_call | solution.py:1307
  85.4 48.2 %attention_weight_exchange.1 = (bf16[1024,768]{1,0:T(8,128)(2,1)}, bf16[1024,256]{1,0:T(8,128)(2,1)}, f32[2,2,1024,128]{3,2,1,0:T(8,128)}, bf16[1024,2048]{1,0:T...) custom-call(bf16[1024,2048]{1,0:T(8,128)(2,1)} %get-tuple-element.51.refs_0_.refs_5_, ...), custom_call_target="tpu_custom_call" | custom-call | flops 49999998976 | bytes 10000000 | tf_op jit(solution)/shard_map/attention_weight_exchange/pallas_call | solution.py:456
  133.6 0.0 all-gather.3.cloned.1.call-update
  133.6 0.2 reduce-scatter.2.cloned.1.call-start
  133.9 113.6 %middle_gate_up.1 = (bf16[1024,2048]{1,0:T(8,128)(2,1)}, f32[128,2048]{1,0:T(8,128)}, bf16[1024,704]{1,0:T(8,128)(2,1)}, f32[1024,704]{1,0:T(8,128)}, f32[1024,7...) custom-call(bf16[1024,2048]{1,0:T(8,128)(2,1)} %get-tuple-element.57.refs_0_, ...), custom_call_target="tpu_custom_call" | custom-call | flops 95000002560 | bytes 10000000 | tf_op jit(solution)/shard_map/middle_gate_up/pallas_call | solution.py:456
  247.5 0.0 all-gather.3.cloned.1.call-done
  247.5 29.4 %hidden_back.1 = (bf16[4,4,128,2176]{3,2,1,0:T(8,128)(2,1)}, bf16[1024,2048]{1,0:T(8,128)(2,1)}) custom-call(bf16[1024,704]{1,0:T(8,128)(2,1)} %get-tuple-element.61.hidden_from.refs_4_, f32[1024,704]{1,0:T(8,128)} %get-tuple-element.62.gate_from, f32[1024,704]{1,0:T(8,128)} %get-tuple-element.63.up_from, ...), custom_call_target="tpu_custom_call" | custom-call | flops 30000001024 | bytes 10000000 | tf_op jit(solution)/shard_map/hidden_back/pallas_call | solution.py:1782
  277.0 0.0 reduce-scatter.2.cloned.1.call-update
  277.0 71.5 %grad_sum_norm_gather.1 = (bf16[1024,2048]{1,0:T(8,128)(2,1)}, f32[8,2048]{1,0:T(8,128)}, bf16[1024,2048]{1,0:T(8,128)(2,1)}) custom-call(bf16[1024,2048]{1,0:T(8,128)(2,1)} %get-tuple-element.68.refs_0_, f32[128,2048]{1,0:T(8,128)} %get-tuple-element.69.refs_1_.refs_9_, bf16[1024,2048]{1,0:T(8,128)(2,1)} %get-tuple-element.64.cotan_from.refs_2_, ...), custom_call_target="tpu_custom_call" | custom-call | flops 60000002048 | bytes 10000000 | tf_op jit(solution)/shard_map/grad_sum_norm_gather/pallas_call | solution.py:456
  348.5 18.6 %reduce-scatter.2.cloned.1.call-done = bf16[512,2176]{1,0:T(8,128)(2,1)} async-done(((bf16[2048,2176]{1,0:T(8,128)(2,1)}), bf16[512,2176]{1,0:T(8,128)(2,1)}) %reduce-scatter.2.cloned.1.call-update) | async-done | bytes 2228240 | tf_op jit(solution)/shard_map/reduce_scatter | solution.py:1862
  367.1 55.1 %attention_back_exchange.1 = (bf16[2,4,4,128,384]{4,3,2,1,0:T(8,128)(2,1)}, bf16[4,4,128,256]{3,2,1,0:T(8,128)(2,1)}, bf16[1024,2048]{1,0:T(8,128)(2,1)}, f32[8,768]{1,0:T(8,128)}, bf16[3,128,2816]{2,1,0:T(8,128)(2,1)}) custom-call(bf16[1024,768]{1,0:T(8,128)(2,1)} %get-tuple-element.55.refs_0_, f32[2,2,1024,128]{3,2,1,0:T(8,128)} %get-tuple-element.56.refs_1_, ...), custom_call_target="tpu_custom_call" | custom-call | flops 49999998976 | bytes 10000000 | tf_op jit(solution)/shard_map/attention_back_exchange/pallas_call | solution.py:456
  422.2 116.1 %input_grad_mixed_sum.1 = (f32[512,512]{1,0:T(8,128)}, bf16[512,512]{1,0:T(8,128)(2,1)}, f32[8,1280]{1,0:T(8,128)}, bf16[4,4,128,1024]{3,2,1,0:T(8,128)(2,1)}, bf16[4,3,128,2816]{3,2,1,0:T(8,128)(2,1)}) custom-call(bf16[1024,2048]{1,0:T(8,128)(2,1)} %get-tuple-element.73.refs_0_, f32[512,512]{1,0:T(8,128)} %get-tuple-element.74.refs_1_, ...), custom_call_target="tpu_custom_call" | custom-call | flops 109999996928 | bytes 10000000 | tf_op jit(solution)/shard_map/input_grad_mixed_sum/pallas_call | solution.py:456
  538.4 0.8 slice_reduce_fusion
  539.1 1.5 fusion
  540.6 0.6 reshape_squeeze.3
  541.2 6.0 %weight_gradients.2 = (f32[3,512,1024]{2,1,0:T(8,128)}, f32[1024,512]{1,0:T(8,128)}) custom-call(bf16[4,4,128,1024]{3,2,1,0:T(8,128)(2,1)} %get-tuple-element.85.whole), custom_call_target="tpu_custom_call" | custom-call | flops 8000000000 | bytes 10000000 | tf_op jit(solution)/shard_map/weight_gradients/pallas_call | solution.py:1839
  547.2 0.0 copy-start.1
  547.2 0.0 copy-start
  547.2 10.8 %weight_gradients.3 = (f32[512,2,2816]{2,1,0:T(2,128)}, f32[2816,512]{1,0:T(8,128)}) custom-call(bf16[4,3,128,2816]{3,2,1,0:T(8,128)(2,1)} %get-tuple-element.88.whole), custom_call_target="tpu_custom_call" | custom-call | flops 8000000000 | bytes 10000000 | tf_op jit(solution)/shard_map/weight_gradients/pallas_call | solution.py:1839
  558.0 0.0 copy-done.1
  558.0 0.8 copy.26
  558.8 0.0 copy-done
  558.8 1.0 copy.27
  (1 shorter events, 0.0 us)
Async XLA Ops:
  7.2 240.3 %all-gather.3.cloned.1.call-start = ((), (), s32[]{:S(2)}) async-start(), calls=%async_computation.2 | async-start | bytes 3932160 | tf_op jit(solution)/shard_map/all_gather | solution.py:1857
  133.6 233.5 %reduce-scatter.2.cloned.1.call-start = ((), (), s32[]{:S(2)}) async-start(), calls=%async_computation.1 | async-start | bytes 11141120 | tf_op jit(solution)/shard_map/reduce_scatter | solution.py:1862
  547.2 10.8 %copy-start.1 = (bf16[512,512]{1,0:T(8,128)(2,1)S(1)}, bf16[512,512]{1,0:T(8,128)(2,1)}, u32[]{:S(2)}) copy-start(bf16[512,512]{1,0:T(8,128)(2,1)} %get-tuple-element.106) | copy-start | bytes 1572868
  547.2 11.6 %copy-start = (f32[512,512]{1,0:T(8,128)S(1)}, f32[512,512]{1,0:T(8,128)}, u32[]{:S(2)}) copy-start(f32[512,512]{1,0:T(8,128)} %get-tuple-element.107) | copy-start | bytes 3145732
Sparse Core Ops, SparseCore 0:
  133.8 69.8 all-gather.2
  277.1 89.9 reduce-scatter.1

commit v7 on v6

--- a/solution.py
+++ b/solution.py
@@ -519,7 +519,7 @@
     return spot
 
 
-COTANGENT_SLOT = 14
+COTANGENT_SLOT = 0
 
 
 def middle_kernel(
@@ -621,7 +621,7 @@
         cotan_slot(t)
         for u in range(cols):
 
-            @pl.when(t == 8 + 6 * (u % 2))
+            @pl.when(t == 14 + 8 * (u % 2))
             def _():
                 rider.forward(u)
 
@@ -654,8 +654,8 @@
             sig = 1.0 / (1.0 + jnp.exp(-gate))
             active = gate * sig
             hidden[rows, :] = (active * up).astype(BF16)
-            up_part[rows, :] = active
-            gate_part[rows, :] = up * sig * (1.0 + gate * (1.0 - sig))
+            up_part[rows, :] = active.astype(BF16)
+            gate_part[rows, :] = (up * sig * (1.0 + gate * (1.0 - sig))).astype(BF16)
             for copy in block_out(m):
                 copy.start()
 
@@ -682,8 +682,8 @@
         ((group, width), BF16),
         (tokens_own.shape, F32),
         ((group, narrow), BF16),
-        ((group, narrow), F32),
-        ((group, narrow), F32),
+        ((group, narrow), BF16),
+        ((group, narrow), BF16),
         ((dp * cols * part_rows, double), BF16),
         ((group, width), BF16),
     )
@@ -714,7 +714,8 @@
 
 def norm_two_back_kernel(
     cols,
-    part,
+    gate_up_grad,
+    gate_up,
     middle,
     cotan_own,
     vectors,
@@ -723,6 +724,7 @@
     grads,
     sums,
     mixed_part,
+    part,
     down,
     sem,
     *scratch,
@@ -736,16 +738,26 @@
     step = own // SUBS
     total = scratch[11]
     enter(cols)
-    load(0)
+    load(0, 1)
     summing = Reduce(
         cols, SUBS, lambda d, s: (d * own + s * step, step, 0, width), part, *scratch[:3], scratch[3:7]
     )
     spread = Gather(cols, SUBS, row_spot(own, step, half, width), grads, scratch[7:11])
+    blocks = part.shape[0] // BLOCK
+    row = lax.axis_index("row")
+
+    def product(r):
+        @pl.loop(0, blocks // 2)
+        def _(m):
+            rows = pl.ds(pl.multiple_of(r * half + m * BLOCK, BLOCK), BLOCK)
+            part[rows, :] = dot_nt(gate_up_grad[rows, :], gate_up[...]).astype(BF16)
+
+    product(1 - row)
     summing.start()
-    blocks = part.shape[0] // BLOCK
+    product(row)
     for copy in copies:
         copy.wait()
-    load(1, 2, 3, 4)
+    load(2, 3, 4, 5)
     sums[...] = jnp.zeros_like(sums)
 
     def land(s):
@@ -784,8 +796,8 @@
     summing.finish()
 
 
-def norm_two_back(cols, part, middle, cotan, vectors, hidden, weight):
-    group, width = part.shape
+def norm_two_back(cols, gate_up_grad, gate_up, middle, cotan, vectors, hidden, weight):
+    group, width = cotan.shape
     tall = weight.shape[3]
     own = group // 2 // cols
 
@@ -793,7 +805,7 @@
         row = lax.axis_index("row") * (group // 2) + lax.axis_index("col") * own
         return pl.ds(pl.multiple_of(row, own), own)
 
-    args = (part, middle, cotan, vectors, hidden, weight)
+    args = (gate_up_grad, gate_up, middle, cotan, vectors, hidden, weight)
     return staged_call(
         functools.partial(norm_two_back_kernel, cols),
         args,
@@ -802,13 +814,13 @@
             jax.ShapeDtypeStruct((8, width), F32),
             jax.ShapeDtypeStruct((group, width), BF16),
         ),
-        in_specs=[VM] * 5 + [ANY],
+        in_specs=[VM] * 6 + [ANY],
         out_specs=[VM] * 3,
-        loads=[(i, args[i].shape, None) for i in (0, 1)]
-        + [(2, (own, width), own_rows)]
-        + [(i, args[i].shape, None) for i in (3, 4)],
+        loads=[(i, args[i].shape, None) for i in (0, 1, 2)]
+        + [(3, (own, width), own_rows)]
+        + [(i, args[i].shape, None) for i in (4, 5)],
         stores=(0, 2),
-        scratch_shapes=[pltpu.VMEM((width, tall), BF16), pltpu.SemaphoreType.DMA(weight.shape[:2])]
+        scratch_shapes=[pltpu.VMEM((group, width), BF16), pltpu.VMEM((width, tall), BF16), pltpu.SemaphoreType.DMA(weight.shape[:2])]
         + Reduce.scratch(cols, SUBS, group // 2, width)
         + Gather.scratch(cols, SUBS)
         + [pltpu.VMEM((group // 2 // cols // SUBS, width), F32)],
@@ -1165,7 +1177,9 @@
     own_sem,
     pair_send,
     pair_recv,
-    *sems
+    *sems,
+    load,
+    store
 ):
     half, depth = tokens.shape
     width = depth * cols
@@ -1238,6 +1252,8 @@
         if down_piece.shape[2] > tall:
             down_piece[j, :, tall:] = jnp.zeros((part, down_piece.shape[2] - tall), BF16)
 
+    store(5, 6)
+
     def across(r, s):
         where = normed.at[pl.ds(pl.multiple_of(r * half + s * step, 16), step), :]
         return send(where, where, pair_send.at[s], pair_recv.at[s], row=1 - lax.axis_index("row"))
@@ -1287,6 +1303,8 @@
 
     for s in range(cols):
         across(1 - r, s).wait_recv()
+    store(0, 1, 2, 3)
+    for s in range(cols):
         across(r, s).wait_send()
     for u in range(cols):
         own(u).wait()
@@ -1304,8 +1322,9 @@
     part, wide, tall = depth // dp, heads.shape[2], down.shape[0]
     each = tall // cols
     dma = pltpu.SemaphoreType.DMA
-    return pl.pallas_call(
+    return staged_call(
         functools.partial(start_kernel, cols),
+        (tokens, vector, heads, out, gate_up, down),
         out_shape=(
             jax.ShapeDtypeStruct((2 * half, width), BF16),
             jax.ShapeDtypeStruct((half // cols, width), BF16),
@@ -1317,7 +1336,9 @@
             jax.ShapeDtypeStruct((dp, cols, part, 4 * wide // cols), BF16),
         ),
         in_specs=[VM] * 2 + [ANY] * 4,
-        out_specs=(VM,) * 7 + (ANY,),
+        out_specs=[VM] * 7 + [ANY],
+        loads=(),
+        stores=(0, 1, 2, 3, 5, 6),
         scratch_shapes=[
             pltpu.VMEM((3, part, wide), BF16),
             pltpu.VMEM((wide, part), BF16),
@@ -1338,7 +1359,7 @@
         compiler_params=params(1),
         cost_estimate=cost(60),
         name="tokens_norm_weights",
-    )(tokens, vector, heads, out, gate_up, down)
+    )
 
 
 def rope_tables(length):
@@ -1669,22 +1690,18 @@
     gate_from,
     up_from,
     cotan_from,
-    gate_up_from,
     down_from,
     normed_from,
     weight_to,
-    normed_to,
+    grads_to,
     hidden,
     gate_part,
     up_part,
     cotan,
-    gate_up,
     down,
     normed,
     grads,
     weight_grad,
-    normed_grad,
-    gate_up_sem,
     down_sem,
     block_sem,
     whole_sem,
@@ -1711,8 +1728,6 @@
     down_copies = load_columns(down_from, down, down_sem)
     for copy in block_copies(0):
         copy.start()
-    gate_up_copy = pltpu.make_async_copy(gate_up_from, gate_up, gate_up_sem.at[0])
-    gate_up_copy.start()
     for m in range(1, blocks):
         for copy in block_copies(m):
             copy.start()
@@ -1725,9 +1740,9 @@
     for copy in down_copies:
         copy.wait()
 
-    def normed_out(m):
+    def grads_out(m):
         rows = rows_of(m)
-        return pltpu.make_async_copy(normed_grad.at[rows, :], normed_to.at[rows, :], out_sem.at[m])
+        return pltpu.make_async_copy(grads.at[rows, :], grads_to.at[rows, :], out_sem.at[m])
 
     def weight_out(p, j):
         return pltpu.make_async_copy(weight_grad.at[p, j], weight_to.at[p, j], grad_sem.at[p, j])
@@ -1738,16 +1753,11 @@
         for copy in block_copies(m):
             copy.wait()
         grad = dot_nn(cotan[rows, :], down[:, :narrow])
-        both = jnp.concatenate([grad * gate_part[rows, :], grad * up_part[rows, :]], axis=1)
+        both = jnp.concatenate(
+            [grad * gate_part[rows, :].astype(F32), grad * up_part[rows, :].astype(F32)], axis=1
+        )
         grads[rows, :] = both.astype(BF16)
-
-    gate_up_copy.wait()
-
-    @pl.loop(0, blocks)
-    def _(m):
-        rows = rows_of(m)
-        normed_grad[rows, :] = dot_nt(grads[rows, :], gate_up[...]).astype(BF16)
-        normed_out(m).start()
+        grads_out(m).start()
 
     for copy in whole_copies:
         copy.wait()
@@ -1766,16 +1776,16 @@
             weight_out(p, j).start()
 
     for m in range(blocks):
-        normed_out(m).wait()
+        grads_out(m).wait()
     for p in range(dp):
         for j in range(cols):
             weight_out(p, j).wait()
 
 
-def hidden_back(hidden, gate_part, up_part, cotan, gate_up, down, normed):
+def hidden_back(hidden, gate_part, up_part, cotan, down, normed):
     group, width = normed.shape
     dp, cols, part, _ = down.shape
-    double = gate_up.shape[1]
+    double = 2 * hidden.shape[1]
     grad_shape = (dp, cols, part, double + down.shape[3])
     blocks = group // BLOCK
     dma = pltpu.SemaphoreType.DMA
@@ -1783,22 +1793,19 @@
         hidden_back_kernel,
         out_shape=(
             jax.ShapeDtypeStruct(grad_shape, BF16),
-            jax.ShapeDtypeStruct((group, width), BF16),
+            jax.ShapeDtypeStruct((group, double), BF16),
         ),
-        in_specs=[ANY] * 7,
+        in_specs=[ANY] * 6,
         out_specs=(ANY,) * 2,
         scratch_shapes=[
             pltpu.VMEM(hidden.shape, BF16),
-            pltpu.VMEM(gate_part.shape, F32),
-            pltpu.VMEM(up_part.shape, F32),
+            pltpu.VMEM(gate_part.shape, BF16),
+            pltpu.VMEM(up_part.shape, BF16),
             pltpu.VMEM(cotan.shape, BF16),
-            pltpu.VMEM((width, double), BF16),
             pltpu.VMEM((width, down.shape[3]), BF16),
             pltpu.VMEM(normed.shape, BF16),
             pltpu.VMEM((group, double), BF16),
             pltpu.VMEM(grad_shape, BF16),
-            pltpu.VMEM((group, width), BF16),
-            dma((1,)),
             dma((dp, cols)),
             dma((3, blocks)),
             dma((2,)),
@@ -1808,49 +1815,54 @@
         compiler_params=pltpu.CompilerParams(vmem_limit_bytes=VMEM_LIMIT),
         cost_estimate=cost(30),
         name="hidden_back",
-    )(hidden, gate_part, up_part, cotan, gate_up, down, normed)
-
-
-def split_kernel(whole, first, last):
-    count, rows = whole.shape[1] - 1, whole.shape[0] * whole.shape[2]
-    inner = first.shape[1] == count
-
-    def part(k):
-        return whole[:, k].reshape(rows, whole.shape[3]).astype(F32)
-
-    for k in range(count):
-        if inner:
-            first[:, k, :] = part(k)
-        else:
-            first[k] = part(k)
-    last[...] = part(count).T
-
-
-def weights_split(whole, inner):
-    dp, count, part, wide = whole.shape
+    )(hidden, gate_part, up_part, cotan, down, normed)
+
+
+def split_kernel(hidden, attention, gate_up, down, heads, out):
+    def part(whole, k):
+        return whole[:, k].reshape(whole.shape[0] * whole.shape[2], whole.shape[3]).astype(F32)
+
+    for k in range(2):
+        gate_up[:, k, :] = part(hidden, k)
+    down[...] = part(hidden, 2).T
+    for k in range(3):
+        heads[k] = part(attention, k)
+    out[...] = part(attention, 3).T
+
+
+def weights_split(hidden, attention):
+    dp, _, part, _ = hidden.shape
     rows = min(part, 128)
     per = 128 // rows
     depth = dp * part
-    count = count - 1
-    if inner:
-        shape, block, place = (depth, count, wide), (128, count, wide), lambda b: (b, 0, 0)
-    else:
-        shape, block, place = (count, depth, wide), (count, 128, wide), lambda b: (0, b, 0)
+    tall, wide = hidden.shape[3], attention.shape[3]
+
+    def source(count, lanes):
+        return pl.BlockSpec(
+            (per, count, rows, lanes),
+            lambda b: (b * 128 // (per * part), 0, lax.rem(b, max(part // 128, 1)), 0),
+        )
+
     return pl.pallas_call(
         split_kernel,
         grid=(depth // 128,),
-        out_shape=(jax.ShapeDtypeStruct(shape, F32), jax.ShapeDtypeStruct((wide, depth), F32)),
-        in_specs=[
-            pl.BlockSpec(
-                (per, count + 1, rows, wide),
-                lambda b: (b * 128 // (per * part), 0, lax.rem(b, max(part // 128, 1)), 0),
-            )
-        ],
-        out_specs=(pl.BlockSpec(block, place), pl.BlockSpec((wide, 128), lambda b: (0, b))),
+        out_shape=(
+            jax.ShapeDtypeStruct((depth, 2, tall), F32),
+            jax.ShapeDtypeStruct((tall, depth), F32),
+            jax.ShapeDtypeStruct((3, depth, wide), F32),
+            jax.ShapeDtypeStruct((wide, depth), F32),
+        ),
+        in_specs=[source(3, tall), source(4, wide)],
+        out_specs=(
+            pl.BlockSpec((128, 2, tall), lambda b: (b, 0, 0)),
+            pl.BlockSpec((tall, 128), lambda b: (0, b)),
+            pl.BlockSpec((3, 128, wide), lambda b: (0, b, 0)),
+            pl.BlockSpec((wide, 128), lambda b: (0, b)),
+        ),
         compiler_params=pltpu.CompilerParams(vmem_limit_bytes=VMEM_LIMIT),
-        cost_estimate=cost(8),
+        cost_estimate=cost(15),
         name="weight_gradients",
-    )(whole)
+    )(hidden, attention)
 
 
 def weights_whole(piece):
@@ -1925,12 +1937,12 @@
         normed_two, middle, hidden, gate_part, up_part, gate_up_w, cotan_rows = middle_part(
             cols, branch_part, tokens_own, vectors, gate_up_piece, cotangent, sizes["dp"]
         )
-        hidden_grad, normed_part = hidden_back(
-            hidden, gate_part, up_part, cotan_rows, gate_up_w, down_w, normed_two
+        hidden_grad, gate_up_grad = hidden_back(
+            hidden, gate_part, up_part, cotan_rows, down_w, normed_two
         )
         hidden_sum = weights_sum(hidden_grad)
         grad_middle, second, mixed_part = norm_two_back(
-            cols, normed_part, middle, cotan_rows, vectors, hidden, down_w
+            cols, gate_up_grad, gate_up_w, middle, cotan_rows, vectors, hidden, down_w
         )
         second = second.reshape(8, cols, depth).transpose(1, 0, 2)
         heads_grad, out_grad, normed_part, bias_part, hidden_sum = attend_back(
@@ -1960,8 +1972,7 @@
             hidden_sum,
             bias_part,
         )
-        grad_gate_up, grad_down = weights_split(hidden_sum, True)
-        grad_qkv_weight, grad_out = weights_split(attention_sum, False)
+        grad_gate_up, grad_down, grad_qkv_weight, grad_out = weights_split(hidden_sum, attention_sum)
         grad_qkv_weight = grad_qkv_weight.transpose(1, 0, 2)
         return (
             mixed,

time: 573 us -> 554 us (0.967)
  waiting for transfers between devices: 18.6 us -> 9.18 us
  Pallas kernels: 526 us -> 517 us
    pallas_call x5 -> x6, Pallas kernels: 405 us -> 481 us  [staged_call(): pl.pallas_call(run, out_shape=tuple(out_shape), in_specs=in_specs, out_sp...]
    pallas_call x1 -> x0, Pallas kernels: 75.6 us -> none  [start_part(): pl.pallas_call(functools.partial(start_kernel, cols), out_shape=(jax.Shap...]
    reduce_scatter x1, waiting for transfers between devices: 18.6 us -> 9.13 us  [weights_sum(): lax.psum_scatter(pieces.reshape(dp * cols * part, wide), 'dp', scatter_di...]
    pallas_call x1, Pallas kernels: 29.4 us -> 21.4 us  [hidden_back(): pl.pallas_call(hidden_back_kernel, out_shape=(jax.ShapeDtypeStruct(grad_s...]
    pallas_call x2 -> x1, Pallas kernels: 16.8 us -> 14.3 us  [weights_split(): pl.pallas_call(split_kernel, grid=(depth // 128,), out_shape=(jax.ShapeDt...]
  transfers between devices with their start and end apart: 2 -> 2, of which waited for: 1 -> 1; matrix products, arithmetic and copies ran while one was open for 0% -> 0% of each run, Pallas kernels for 33% -> 34%
where the time goes in v7:
time: 554 us; the launch traced here: 548 us
  Pallas kernels  517 us (93%)
  between operations  14.4 us (3%)
  waiting for transfers between devices  9.18 us (2%)
  local copies, waits for them, and re-layouts  7.21 us (1%)
    pallas_call x6, Pallas kernels, staged_call(): pl.pallas_call(run, out_shape=tuple(out_shape), in_specs=in_specs, out_sp...  481 us
    pallas_call x1, Pallas kernels, hidden_back(): pl.pallas_call(hidden_back_kernel, out_shape=(jax.ShapeDtypeStruct(grad_s...  21.4 us
    pallas_call x1, Pallas kernels, weights_split(): pl.pallas_call(split_kernel, grid=(depth // 128,), out_shape=(jax.ShapeDt...  14.3 us
  transfers between devices with their start and end apart: 2, of which 1 were waited for; matrix products, arithmetic and copies ran while one was open for 0% of the time, Pallas kernels for 34%

profile of v7, /device:TPU:0, one launch (start us, length us, event | category | flops | bytes accessed | tf_op | source)
XLA Modules:
  0.0 548.1 jit_solution(16748213889595757658)
XLA Ops:
  7.2 0.0 all-gather.3.cloned.1.call-start
  7.2 1.3 copy.23
  8.5 1.4 concatenate.3.refs_1_
  9.8 72.9 %tokens_norm_weights.1 = (bf16[1024,2048]{1,0:T(8,128)(2,1)}, bf16[128,2048]{1,0:T(8,128)(2,1)}, f32[512,512]{1,0:T(8,128)}, f32[512,128]{1,0:T(8,128)}, f32[8,2...) custom-call(bf16[512,512]{1,0:T(8,128)(2,1)} %refs_0_.1, ...), custom_call_target="tpu_custom_call" | custom-call | flops 60000002048 | bytes 10000000 | tf_op jit(solution)/shard_map/tokens_norm_weights/pallas_call | solution.py:456
  82.8 49.4 %attention_weight_exchange.1 = (bf16[1024,768]{1,0:T(8,128)(2,1)}, bf16[1024,256]{1,0:T(8,128)(2,1)}, f32[2,2,1024,128]{3,2,1,0:T(8,128)}, bf16[1024,2048]{1,0:T...) custom-call(bf16[1024,2048]{1,0:T(8,128)(2,1)} %get-tuple-element.51.refs_0_.refs_5_, ...), custom_call_target="tpu_custom_call" | custom-call | flops 49999998976 | bytes 10000000 | tf_op jit(solution)/shard_map/attention_weight_exchange/pallas_call | solution.py:456
  132.2 0.0 all-gather.3.cloned.1.call-update
  132.2 0.2 reduce-scatter.2.cloned.1.call-start
  132.5 108.0 %middle_gate_up.1 = (bf16[1024,2048]{1,0:T(8,128)(2,1)}, f32[128,2048]{1,0:T(8,128)}, bf16[1024,704]{1,0:T(8,128)(2,1)}, bf16[1024,704]{1,0:T(8,128)(2,1)}, bf16...) custom-call(bf16[1024,2048]{1,0:T(8,128)(2,1)} %get-tuple-element.57.refs_0_, ...), custom_call_target="tpu_custom_call" | custom-call | flops 95000002560 | bytes 10000000 | tf_op jit(solution)/shard_map/middle_gate_up/pallas_call | solution.py:456
  240.5 0.0 all-gather.3.cloned.1.call-done
  240.5 21.4 %hidden_back.1 = (bf16[4,4,128,2176]{3,2,1,0:T(8,128)(2,1)}, bf16[1024,1408]{1,0:T(8,128)(2,1)}) custom-call(bf16[1024,704]{1,0:T(8,128)(2,1)} %get-tuple-element.61.hidden_from.refs_5_, bf16[1024,704]{1,0:T(8,128)(2,1)} %get-tuple-element.62.gate_from, bf16[1024,704]{1,0:T(8,128)(2,1)} %get-tuple-element.63.up_from, ...), custom_call_target="tpu_custom_call" | custom-call | flops 30000001024 | bytes 10000000 | tf_op jit(solution)/shard_map/hidden_back/pallas_call | solution.py:1792
  261.9 0.0 reduce-scatter.2.cloned.1.call-update
  261.9 79.8 %grad_sum_norm_gather.1 = (bf16[1024,2048]{1,0:T(8,128)(2,1)}, f32[8,2048]{1,0:T(8,128)}, bf16[1024,2048]{1,0:T(8,128)(2,1)}) custom-call(bf16[1024,1408]{1,0:T(8,128)(2,1)} %get-tuple-element.67.refs_0_, bf16[2048,1408]{1,0:T(8,128)(2,1)} %get-tuple-element.68.refs_1_, f32[128,2048]{1,0:T(8,128)} %get-tuple-element.69.refs_2_.refs_9_, ...), custom_call_target="tpu_custom_call" | custom-call | flops 60000002048 | bytes 10000000 | tf_op jit(solution)/shard_map/grad_sum_norm_gather/pallas_call | solution.py:456
  341.7 9.1 %reduce-scatter.2.cloned.1.call-done = bf16[512,2176]{1,0:T(8,128)(2,1)} async-done(((bf16[2048,2176]{1,0:T(8,128)(2,1)}), bf16[512,2176]{1,0:T(8,128)(2,1)}) %reduce-scatter.2.cloned.1.call-update) | async-done | bytes 2228240 | tf_op jit(solution)/shard_map/reduce_scatter | solution.py:1874
  350.8 55.1 %attention_back_exchange.1 = (bf16[2,4,4,128,384]{4,3,2,1,0:T(8,128)(2,1)}, bf16[4,4,128,256]{3,2,1,0:T(8,128)(2,1)}, bf16[1024,2048]{1,0:T(8,128)(2,1)}, f32[8,768]{1,0:T(8,128)}, bf16[3,128,2816]{2,1,0:T(8,128)(2,1)}) custom-call(bf16[1024,768]{1,0:T(8,128)(2,1)} %get-tuple-element.55.refs_0_, f32[2,2,1024,128]{3,2,1,0:T(8,128)} %get-tuple-element.56.refs_1_, ...), custom_call_target="tpu_custom_call" | custom-call | flops 49999998976 | bytes 10000000 | tf_op jit(solution)/shard_map/attention_back_exchange/pallas_call | solution.py:456
  405.9 116.2 %input_grad_mixed_sum.1 = (f32[512,512]{1,0:T(8,128)}, bf16[512,512]{1,0:T(8,128)(2,1)}, f32[8,1280]{1,0:T(8,128)}, bf16[4,4,128,1024]{3,2,1,0:T(8,128)(2,1)}, bf16[4,3,128,2816]{3,2,1,0:T(8,128)(2,1)}) custom-call(bf16[1024,2048]{1,0:T(8,128)(2,1)} %get-tuple-element.73.refs_0_, f32[512,512]{1,0:T(8,128)} %get-tuple-element.74.refs_1_, ...), custom_call_target="tpu_custom_call" | custom-call | flops 109999996928 | bytes 10000000 | tf_op jit(solution)/shard_map/input_grad_mixed_sum/pallas_call | solution.py:456
  522.1 0.8 slice_reduce_fusion
  522.9 1.5 fusion
  524.3 0.6 reshape_squeeze.3
  524.9 0.0 copy-start.1
  524.9 0.0 copy-start
  524.9 14.3 %weight_gradients.1 = (f32[512,2,2816]{2,1,0:T(2,128)}, f32[2816,512]{1,0:T(8,128)}, f32[3,512,1024]{2,1,0:T(8,128)}, f32[1024,512]{1,0:T(8,128)}) custom-call(bf16[4,3,128,2816]{3,2,1,0:T(8,128)(2,1)} %get-tuple-element.85.hidden, bf16[4,4,128,1024]{3,2,1,0:T(8,128)(2,1)} %get-tuple-element.86.attention), custom_call_target="tpu_custom_call" | custom-call | flops 15000000512 | bytes 10000000 | tf_op jit(solution)/shard_map/weight_gradients/pallas_call | solution.py:1846
  539.2 0.0 copy-done.1
  539.2 0.8 copy.26
  540.0 0.0 copy-done
  540.0 1.0 copy.27
  (1 shorter events, 0.0 us)
Async XLA Ops:
  7.2 233.3 %all-gather.3.cloned.1.call-start = ((), (), s32[]{:S(2)}) async-start(), calls=%async_computation.2 | async-start | bytes 3932160 | tf_op jit(solution)/shard_map/all_gather | solution.py:1869
  132.2 218.5 %reduce-scatter.2.cloned.1.call-start = ((), (), s32[]{:S(2)}) async-start(), calls=%async_computation.1 | async-start | bytes 11141120 | tf_op jit(solution)/shard_map/reduce_scatter | solution.py:1874
  524.9 14.3 %copy-start.1 = (bf16[512,512]{1,0:T(8,128)(2,1)S(1)}, bf16[512,512]{1,0:T(8,128)(2,1)}, u32[]{:S(2)}) copy-start(bf16[512,512]{1,0:T(8,128)(2,1)} %get-tuple-element.106) | copy-start | bytes 1572868
  524.9 15.1 %copy-start = (f32[512,512]{1,0:T(8,128)S(1)}, f32[512,512]{1,0:T(8,128)}, u32[]{:S(2)}) copy-start(f32[512,512]{1,0:T(8,128)} %get-tuple-element.107) | copy-start | bytes 3145732
Sparse Core Ops, SparseCore 0:
  132.4 70.6 all-gather.2
  262.0 88.7 reduce-scatter.1

commit v8 on v7

--- a/solution.py
+++ b/solution.py
@@ -265,7 +265,8 @@
             if self.pair:
                 self.across(self.r, self.c + k, s).start()
 
-    def slot(self, t, begin, step):
+    def slot(self, t, begin, step, first=0, count=None):
+        count = self.subs if count is None else count
         for k in range(1, self.cols):
             after = t - begin - LAG * k
 
@@ -273,9 +274,9 @@
             def _():
                 s = lax.div(after, step)
 
-                @pl.when(s < self.subs)
+                @pl.when(s < count)
                 def _():
-                    self.relay(s, k)
+                    self.relay(first + s, k)
 
     def finish(self):
         @pl.loop(0, self.subs)
@@ -519,7 +520,7 @@
     return spot
 
 
-COTANGENT_SLOT = 0
+COTANGENT_SLOTS = (0, 28)
 
 
 def middle_kernel(
@@ -597,20 +598,23 @@
         normed[spread.spot(spread.r, spread.c, s)] = result.astype(BF16)
         spread.start(s)
 
+    batch = SUBS // len(COTANGENT_SLOTS)
+
     def cotan_slot(t):
-        after = t - COTANGENT_SLOT
-
-        @pl.when((after >= 0) & (lax.rem(after + 60, 3) == 0) & (after < 3 * SUBS))
-        def _():
-            s = lax.div(after, 3)
-            rows = pl.ds(pl.multiple_of(s * rows_each, 16), rows_each)
-            cotan_rows[cotan_spot(spread.r, spread.c, s)] = cotan[rows, :]
-            cotan_spread.start(s)
-
-        cotan_spread.slot(t, COTANGENT_SLOT, 3)
+        for i, begin in enumerate(COTANGENT_SLOTS):
+            after = t - begin
+
+            @pl.when((after >= 0) & (lax.rem(after + 60, 3) == 0) & (after < 3 * batch))
+            def _():
+                s = i * batch + lax.div(after, 3)
+                rows = pl.ds(pl.multiple_of(s * rows_each, 16), rows_each)
+                cotan_rows[cotan_spot(spread.r, spread.c, s)] = cotan[rows, :]
+                cotan_spread.start(s)
+
+            cotan_spread.slot(t, begin, 3, i * batch, batch)
 
     first = summing.slots + LAG * (cols - 1)
-    last = COTANGENT_SLOT + 3 * (SUBS - 1) + LAG * (cols - 1) + 1
+    last = COTANGENT_SLOTS[-1] + 3 * (batch - 1) + LAG * (cols - 1) + 1
     blocks = group // BLOCK
 
     @pl.loop(0, first)
@@ -1153,7 +1157,10 @@
 def start_kernel(
     cols,
     tokens,
-    vector,
+    one_gain,
+    one_bias,
+    two_gain,
+    two_bias,
     heads_from,
     out_from,
     gate_up_from,
@@ -1235,7 +1242,9 @@
         sems[7:11],
         pair=False,
     )
-    vectors[:, columns(c)] = vector[...]
+    vectors[:, columns(c)] = jnp.zeros((8, depth), F32)
+    for i, values in enumerate((one_gain, one_bias, two_gain, two_bias)):
+        vectors[i : i + 1, columns(c)] = values[...]
     names.start(0)
     for s in range(cols):
         rows = pl.ds(s * step, step)
@@ -1315,7 +1324,7 @@
     spread.finish()
 
 
-def start_part(tokens, vector, heads, out, gate_up, down, sizes):
+def start_part(tokens, vectors, heads, out, gate_up, down, sizes):
     dp, cols = sizes["dp"], sizes["col"]
     half, depth = tokens.shape
     width = depth * cols
@@ -1324,7 +1333,7 @@
     dma = pltpu.SemaphoreType.DMA
     return staged_call(
         functools.partial(start_kernel, cols),
-        (tokens, vector, heads, out, gate_up, down),
+        (tokens, *vectors, heads, out, gate_up, down),
         out_shape=(
             jax.ShapeDtypeStruct((2 * half, width), BF16),
             jax.ShapeDtypeStruct((half // cols, width), BF16),
@@ -1335,7 +1344,7 @@
             jax.ShapeDtypeStruct((cols, part, each + -each % 128), BF16),
             jax.ShapeDtypeStruct((dp, cols, part, 4 * wide // cols), BF16),
         ),
-        in_specs=[VM] * 2 + [ANY] * 4,
+        in_specs=[VM] * 5 + [ANY] * 4,
         out_specs=[VM] * 7 + [ANY],
         loads=(),
         stores=(0, 1, 2, 3, 5, 6),
@@ -1427,7 +1436,7 @@
     @pl.loop(0, length // BLOCK)
     def _(m):
         rows = pl.ds(pl.multiple_of(m * BLOCK, BLOCK), BLOCK)
-        qkv[rows, :] = dot_nn(normed[rows, :], whole[:, : 3 * wide]) + bias[0:1, :]
+        qkv[rows, :] = dot_nn(normed[rows, :], whole[:, : 3 * wide])
 
     @pl.loop(0, wide // two)
     def _(pair):
@@ -1435,7 +1444,7 @@
             return pl.ds(pl.multiple_of(k * wide + pair * two, two), two)
 
         for k in range(3):
-            x = qkv[:, lanes(k)]
+            x = qkv[:, lanes(k)] + bias[k : k + 1, pl.ds(pl.multiple_of(pair * two, two), two)]
             if k < 2:
                 x = turn(x, tables)
             if k == 0:
@@ -1896,10 +1905,6 @@
         my_dp = lax.axis_index("dp")
         depth = tokens.shape[1]
         tables = rope_tables(SEQ)
-        vector = jnp.stack(
-            [attention_norm_gain, attention_norm_bias, feedforward_norm_gain, feedforward_norm_bias]
-        )
-        vector = jnp.concatenate([vector, jnp.zeros_like(vector)])
         part = depth // sizes["dp"]
 
         def share_of(rows):
@@ -1916,7 +1921,15 @@
             attention_w,
         ) = start_part(
             tokens,
-            vector,
+            [
+                values.reshape(1, -1)
+                for values in (
+                    attention_norm_gain,
+                    attention_norm_bias,
+                    feedforward_norm_gain,
+                    feedforward_norm_bias,
+                )
+            ],
             qkv_weight.transpose(1, 0, 2),
             share_of(out_weight),
             gate_up_weight,
@@ -1927,7 +1940,7 @@
             cols,
             normed_one,
             attention_w,
-            qkv_bias.reshape(1, -1),
+            qkv_bias,
             tables,
             gate_up_piece,
             down_piece,

time: 554 us -> 546 us (0.986)
  Pallas kernels: 517 us -> 511 us
    pallas_call x6, Pallas kernels: 481 us -> 476 us  [staged_call(): pl.pallas_call(run, out_shape=tuple(out_shape), in_specs=in_specs, out_sp...]
where the time goes in v8:
time: 546 us; the launch traced here: 540 us
  Pallas kernels  511 us (94%)
  between operations  14.4 us (3%)
  waiting for transfers between devices  9.55 us (2%)
    pallas_call x6, Pallas kernels, staged_call(): pl.pallas_call(run, out_shape=tuple(out_shape), in_specs=in_specs, out_sp...  476 us
    pallas_call x1, Pallas kernels, hidden_back(): pl.pallas_call(hidden_back_kernel, out_shape=(jax.ShapeDtypeStruct(grad_s...  21.4 us
    pallas_call x1, Pallas kernels, weights_split(): pl.pallas_call(split_kernel, grid=(depth // 128,), out_shape=(jax.ShapeDt...  14.3 us
  transfers between devices with their start and end apart: 2, of which 1 were waited for; matrix products, arithmetic and copies ran while one was open for 0% of the time, Pallas kernels for 34%

profile of v8, /device:TPU:0, one launch (start us, length us, event | category | flops | bytes accessed | tf_op | source)
XLA Modules:
  0.0 540.0 jit_solution(6706182803289012672)
XLA Ops:
  7.2 0.0 all-gather.3.cloned.1.call-start
  7.2 73.0 %tokens_norm_weights.1 = (bf16[1024,2048]{1,0:T(8,128)(2,1)}, bf16[128,2048]{1,0:T(8,128)(2,1)}, f32[512,512]{1,0:T(8,128)}, f32[512,128]{1,0:T(8,128)}, f32[8,2...) custom-call(bf16[512,512]{1,0:T(8,128)(2,1)} %refs_0_.1, ...), custom_call_target="tpu_custom_call" | custom-call | flops 60000002048 | bytes 10000000 | tf_op jit(solution)/shard_map/tokens_norm_weights/pallas_call | solution.py:457
  80.3 49.4 %attention_weight_exchange.1 = (bf16[1024,768]{1,0:T(8,128)(2,1)}, bf16[1024,256]{1,0:T(8,128)(2,1)}, f32[2,2,1024,128]{3,2,1,0:T(8,128)}, bf16[1024,2048]{1,0:T...) custom-call(bf16[1024,2048]{1,0:T(8,128)(2,1)} %get-tuple-element.51.refs_0_.refs_5_, ...), custom_call_target="tpu_custom_call" | custom-call | flops 49999998976 | bytes 10000000 | tf_op jit(solution)/shard_map/attention_weight_exchange/pallas_call | solution.py:457
  129.7 0.0 all-gather.3.cloned.1.call-update
  129.7 0.2 reduce-scatter.2.cloned.1.call-start
  129.9 102.4 %middle_gate_up.1 = (bf16[1024,2048]{1,0:T(8,128)(2,1)}, f32[128,2048]{1,0:T(8,128)}, bf16[1024,704]{1,0:T(8,128)(2,1)}, bf16[1024,704]{1,0:T(8,128)(2,1)}, bf16...) custom-call(bf16[1024,2048]{1,0:T(8,128)(2,1)} %get-tuple-element.57.refs_0_, ...), custom_call_target="tpu_custom_call" | custom-call | flops 95000002560 | bytes 10000000 | tf_op jit(solution)/shard_map/middle_gate_up/pallas_call | solution.py:457
  232.3 0.0 all-gather.3.cloned.1.call-done
  232.4 21.4 %hidden_back.1 = (bf16[4,4,128,2176]{3,2,1,0:T(8,128)(2,1)}, bf16[1024,1408]{1,0:T(8,128)(2,1)}) custom-call(bf16[1024,704]{1,0:T(8,128)(2,1)} %get-tuple-element.61.hidden_from.refs_5_, bf16[1024,704]{1,0:T(8,128)(2,1)} %get-tuple-element.62.gate_from, bf16[1024,704]{1,0:T(8,128)(2,1)} %get-tuple-element.63.up_from, ...), custom_call_target="tpu_custom_call" | custom-call | flops 30000001024 | bytes 10000000 | tf_op jit(solution)/shard_map/hidden_back/pallas_call | solution.py:1801
  253.7 0.0 reduce-scatter.2.cloned.1.call-update
  253.7 79.4 %grad_sum_norm_gather.1 = (bf16[1024,2048]{1,0:T(8,128)(2,1)}, f32[8,2048]{1,0:T(8,128)}, bf16[1024,2048]{1,0:T(8,128)(2,1)}) custom-call(bf16[1024,1408]{1,0:T(8,128)(2,1)} %get-tuple-element.67.refs_0_, bf16[2048,1408]{1,0:T(8,128)(2,1)} %get-tuple-element.68.refs_1_, f32[128,2048]{1,0:T(8,128)} %get-tuple-element.69.refs_2_.refs_9_, ...), custom_call_target="tpu_custom_call" | custom-call | flops 60000002048 | bytes 10000000 | tf_op jit(solution)/shard_map/grad_sum_norm_gather/pallas_call | solution.py:457
  333.2 9.5 %reduce-scatter.2.cloned.1.call-done = bf16[512,2176]{1,0:T(8,128)(2,1)} async-done(((bf16[2048,2176]{1,0:T(8,128)(2,1)}), bf16[512,2176]{1,0:T(8,128)(2,1)}) %reduce-scatter.2.cloned.1.call-update) | async-done | bytes 2228240 | tf_op jit(solution)/shard_map/reduce_scatter | solution.py:1883
  342.7 55.0 %attention_back_exchange.1 = (bf16[2,4,4,128,384]{4,3,2,1,0:T(8,128)(2,1)}, bf16[4,4,128,256]{3,2,1,0:T(8,128)(2,1)}, bf16[1024,2048]{1,0:T(8,128)(2,1)}, f32[8,768]{1,0:T(8,128)}, bf16[3,128,2816]{2,1,0:T(8,128)(2,1)}) custom-call(bf16[1024,768]{1,0:T(8,128)(2,1)} %get-tuple-element.55.refs_0_, f32[2,2,1024,128]{3,2,1,0:T(8,128)} %get-tuple-element.56.refs_1_, ...), custom_call_target="tpu_custom_call" | custom-call | flops 49999998976 | bytes 10000000 | tf_op jit(solution)/shard_map/attention_back_exchange/pallas_call | solution.py:457
  397.7 116.3 %input_grad_mixed_sum.1 = (f32[512,512]{1,0:T(8,128)}, bf16[512,512]{1,0:T(8,128)(2,1)}, f32[8,1280]{1,0:T(8,128)}, bf16[4,4,128,1024]{3,2,1,0:T(8,128)(2,1)}, bf16[4,3,128,2816]{3,2,1,0:T(8,128)(2,1)}) custom-call(bf16[1024,2048]{1,0:T(8,128)(2,1)} %get-tuple-element.73.refs_0_, f32[512,512]{1,0:T(8,128)} %get-tuple-element.74.refs_1_, ...), custom_call_target="tpu_custom_call" | custom-call | flops 109999996928 | bytes 10000000 | tf_op jit(solution)/shard_map/input_grad_mixed_sum/pallas_call | solution.py:457
  514.0 0.8 slice_reduce_fusion
  514.7 1.5 fusion
  516.2 0.6 reshape_squeeze.3
  516.8 0.0 copy-start.1
  516.8 0.0 copy-start
  516.8 14.3 %weight_gradients.1 = (f32[512,2,2816]{2,1,0:T(2,128)}, f32[2816,512]{1,0:T(8,128)}, f32[3,512,1024]{2,1,0:T(8,128)}, f32[1024,512]{1,0:T(8,128)}) custom-call(bf16[4,3,128,2816]{3,2,1,0:T(8,128)(2,1)} %get-tuple-element.85.hidden, bf16[4,4,128,1024]{3,2,1,0:T(8,128)(2,1)} %get-tuple-element.86.attention), custom_call_target="tpu_custom_call" | custom-call | flops 15000000512 | bytes 10000000 | tf_op jit(solution)/shard_map/weight_gradients/pallas_call | solution.py:1855
  531.1 0.0 copy-done.1
  531.1 0.8 copy.25
  531.9 0.0 copy-done
  531.9 1.0 copy.26
Async XLA Ops:
  7.2 225.2 %all-gather.3.cloned.1.call-start = ((), (), s32[]{:S(2)}) async-start(), calls=%async_computation.2 | async-start | bytes 3932160 | tf_op jit(solution)/shard_map/all_gather | solution.py:1878
  129.7 212.9 %reduce-scatter.2.cloned.1.call-start = ((), (), s32[]{:S(2)}) async-start(), calls=%async_computation.1 | async-start | bytes 11141120 | tf_op jit(solution)/shard_map/reduce_scatter | solution.py:1883
  516.8 14.3 %copy-start.1 = (bf16[512,512]{1,0:T(8,128)(2,1)S(1)}, bf16[512,512]{1,0:T(8,128)(2,1)}, u32[]{:S(2)}) copy-start(bf16[512,512]{1,0:T(8,128)(2,1)} %get-tuple-element.106) | copy-start | bytes 1572868
  516.8 15.1 %copy-start = (f32[512,512]{1,0:T(8,128)S(1)}, f32[512,512]{1,0:T(8,128)}, u32[]{:S(2)}) copy-start(f32[512,512]{1,0:T(8,128)} %get-tuple-element.107) | copy-start | bytes 3145732
Sparse Core Ops, SparseCore 0:
  129.8 70.6 all-gather.2
  253.9 88.7 reduce-scatter.1

commit v9 on v8

--- a/solution.py
+++ b/solution.py
@@ -71,7 +71,7 @@
         pl.semaphore_wait(barrier, 2)
 
 
-LAG = 3
+LAG = 4
 BLOCK = 256
 PACE = 6
 
@@ -520,7 +520,7 @@
     return spot
 
 
-COTANGENT_SLOTS = (0, 28)
+COTANGENT_SLOTS = (0, 34)
 
 
 def middle_kernel(
@@ -1827,7 +1827,7 @@
     )(hidden, gate_part, up_part, cotan, down, normed)
 
 
-def split_kernel(hidden, attention, gate_up, down, heads, out):
+def split_kernel(hidden, attention, small, gate_up, down, heads, out, bias, *norms):
     def part(whole, k):
         return whole[:, k].reshape(whole.shape[0] * whole.shape[2], whole.shape[3]).astype(F32)
 
@@ -1837,14 +1837,23 @@
     for k in range(3):
         heads[k] = part(attention, k)
     out[...] = part(attention, 3).T
-
-
-def weights_split(hidden, attention):
+    depth, each = norms[0].shape[1], bias.shape[1]
+    for i, norm in enumerate(norms):
+        norm[...] = small[i : i + 1, :depth]
+    for k in range(3):
+        bias[k : k + 1, :] = small[0:1, depth + k * each : depth + (k + 1) * each]
+
+
+def weights_split(hidden, attention, small):
     dp, _, part, _ = hidden.shape
     rows = min(part, 128)
     per = 128 // rows
     depth = dp * part
     tall, wide = hidden.shape[3], attention.shape[3]
+    each = (small.shape[1] - depth) // 3
+
+    def whole(shape):
+        return pl.BlockSpec(shape, lambda b: (0, 0))
 
     def source(count, lanes):
         return pl.BlockSpec(
@@ -1860,18 +1869,22 @@
             jax.ShapeDtypeStruct((tall, depth), F32),
             jax.ShapeDtypeStruct((3, depth, wide), F32),
             jax.ShapeDtypeStruct((wide, depth), F32),
-        ),
-        in_specs=[source(3, tall), source(4, wide)],
+            jax.ShapeDtypeStruct((3, each), F32),
+        )
+        + (jax.ShapeDtypeStruct((1, depth), F32),) * 4,
+        in_specs=[source(3, tall), source(4, wide), whole(small.shape)],
         out_specs=(
             pl.BlockSpec((128, 2, tall), lambda b: (b, 0, 0)),
             pl.BlockSpec((tall, 128), lambda b: (0, b)),
             pl.BlockSpec((3, 128, wide), lambda b: (0, b, 0)),
             pl.BlockSpec((wide, 128), lambda b: (0, b)),
-        ),
+            whole((3, each)),
+        )
+        + (whole((1, depth)),) * 4,
         compiler_params=pltpu.CompilerParams(vmem_limit_bytes=VMEM_LIMIT),
         cost_estimate=cost(15),
         name="weight_gradients",
-    )(hidden, attention)
+    )(hidden, attention, small)
 
 
 def weights_whole(piece):
@@ -1985,18 +1998,21 @@
             hidden_sum,
             bias_part,
         )
-        grad_gate_up, grad_down, grad_qkv_weight, grad_out = weights_split(hidden_sum, attention_sum)
+        grad_gate_up, grad_down, grad_qkv_weight, grad_out, bias, *norms = weights_split(
+            hidden_sum, attention_sum, small
+        )
+        norms = [norm.reshape(-1) for norm in norms]
         grad_qkv_weight = grad_qkv_weight.transpose(1, 0, 2)
         return (
             mixed,
             input_grad,
-            small[0, :depth],
-            small[1, :depth],
+            norms[0],
+            norms[1],
             grad_qkv_weight,
-            small[0, depth:].reshape(3, -1),
+            bias,
             grad_out,
-            small[2, :depth],
-            small[3, :depth],
+            norms[2],
+            norms[3],
             grad_gate_up,
             grad_down,
         )

time: 546 us -> 541 us (level)
  no operation moved by 1% of the time
where the time goes in v9:
time: 541 us; the launch traced here: 535 us
  Pallas kernels  512 us (95%)
  between operations  14.4 us (3%)
  waiting for transfers between devices  6.78 us (1%)
    pallas_call x6, Pallas kernels, staged_call(): pl.pallas_call(run, out_shape=tuple(out_shape), in_specs=in_specs, out_sp...  476 us
    pallas_call x1, Pallas kernels, hidden_back(): pl.pallas_call(hidden_back_kernel, out_shape=(jax.ShapeDtypeStruct(grad_s...  21.4 us
    pallas_call x1, Pallas kernels, weights_split(): pl.pallas_call(split_kernel, grid=(depth // 128,), out_shape=(jax.ShapeDt...  14.3 us
  transfers between devices with their start and end apart: 2, of which 1 were waited for; matrix products, arithmetic and copies ran while one was open for 0% of the time, Pallas kernels for 34%

profile of v9, /device:TPU:0, one launch (start us, length us, event | category | flops | bytes accessed | tf_op | source)
XLA Modules:
  0.0 535.3 jit_solution(14914787027248045172)
XLA Ops:
  7.2 0.0 all-gather.3.cloned.1.call-start
  7.2 73.0 %tokens_norm_weights.1 = (bf16[1024,2048]{1,0:T(8,128)(2,1)}, bf16[128,2048]{1,0:T(8,128)(2,1)}, f32[512,512]{1,0:T(8,128)}, f32[512,128]{1,0:T(8,128)}, f32[8,2...) custom-call(bf16[512,512]{1,0:T(8,128)(2,1)} %refs_0_.1, ...), custom_call_target="tpu_custom_call" | custom-call | flops 60000002048 | bytes 10000000 | tf_op jit(solution)/shard_map/tokens_norm_weights/pallas_call | solution.py:457
  80.3 49.4 %attention_weight_exchange.1 = (bf16[1024,768]{1,0:T(8,128)(2,1)}, bf16[1024,256]{1,0:T(8,128)(2,1)}, f32[2,2,1024,128]{3,2,1,0:T(8,128)}, bf16[1024,2048]{1,0:T...) custom-call(bf16[1024,2048]{1,0:T(8,128)(2,1)} %get-tuple-element.56.refs_0_.refs_5_, ...), custom_call_target="tpu_custom_call" | custom-call | flops 49999998976 | bytes 10000000 | tf_op jit(solution)/shard_map/attention_weight_exchange/pallas_call | solution.py:457
  129.7 0.0 all-gather.3.cloned.1.call-update
  129.7 0.2 reduce-scatter.2.cloned.1.call-start
  129.9 99.8 %middle_gate_up.1 = (bf16[1024,2048]{1,0:T(8,128)(2,1)}, f32[128,2048]{1,0:T(8,128)}, bf16[1024,704]{1,0:T(8,128)(2,1)}, bf16[1024,704]{1,0:T(8,128)(2,1)}, bf16...) custom-call(bf16[1024,2048]{1,0:T(8,128)(2,1)} %get-tuple-element.62.refs_0_, ...), custom_call_target="tpu_custom_call" | custom-call | flops 95000002560 | bytes 10000000 | tf_op jit(solution)/shard_map/middle_gate_up/pallas_call | solution.py:457
  229.8 0.0 all-gather.3.cloned.1.call-done
  229.8 21.4 %hidden_back.1 = (bf16[4,4,128,2176]{3,2,1,0:T(8,128)(2,1)}, bf16[1024,1408]{1,0:T(8,128)(2,1)}) custom-call(bf16[1024,704]{1,0:T(8,128)(2,1)} %get-tuple-element.66.hidden_from.refs_5_, bf16[1024,704]{1,0:T(8,128)(2,1)} %get-tuple-element.67.gate_from, bf16[1024,704]{1,0:T(8,128)(2,1)} %get-tuple-element.68.up_from, ...), custom_call_target="tpu_custom_call" | custom-call | flops 30000001024 | bytes 10000000 | tf_op jit(solution)/shard_map/hidden_back/pallas_call | solution.py:1801
  251.1 0.0 reduce-scatter.2.cloned.1.call-update
  251.2 82.9 %grad_sum_norm_gather.1 = (bf16[1024,2048]{1,0:T(8,128)(2,1)}, f32[8,2048]{1,0:T(8,128)}, bf16[1024,2048]{1,0:T(8,128)(2,1)}) custom-call(bf16[1024,1408]{1,0:T(8,128)(2,1)} %get-tuple-element.72.refs_0_, bf16[2048,1408]{1,0:T(8,128)(2,1)} %get-tuple-element.73.refs_1_, f32[128,2048]{1,0:T(8,128)} %get-tuple-element.74.refs_2_.refs_9_, ...), custom_call_target="tpu_custom_call" | custom-call | flops 60000002048 | bytes 10000000 | tf_op jit(solution)/shard_map/grad_sum_norm_gather/pallas_call | solution.py:457
  334.0 6.7 %reduce-scatter.2.cloned.1.call-done = bf16[512,2176]{1,0:T(8,128)(2,1)} async-done(((bf16[2048,2176]{1,0:T(8,128)(2,1)}), bf16[512,2176]{1,0:T(8,128)(2,1)}) %reduce-scatter.2.cloned.1.call-update) | async-done | bytes 2228240 | tf_op jit(solution)/shard_map/reduce_scatter | solution.py:1896
  340.8 55.1 %attention_back_exchange.1 = (bf16[2,4,4,128,384]{4,3,2,1,0:T(8,128)(2,1)}, bf16[4,4,128,256]{3,2,1,0:T(8,128)(2,1)}, bf16[1024,2048]{1,0:T(8,128)(2,1)}, f32[8,768]{1,0:T(8,128)}, bf16[3,128,2816]{2,1,0:T(8,128)(2,1)}) custom-call(bf16[1024,768]{1,0:T(8,128)(2,1)} %get-tuple-element.60.refs_0_, f32[2,2,1024,128]{3,2,1,0:T(8,128)} %get-tuple-element.61.refs_1_, ...), custom_call_target="tpu_custom_call" | custom-call | flops 49999998976 | bytes 10000000 | tf_op jit(solution)/shard_map/attention_back_exchange/pallas_call | solution.py:457
  395.9 116.1 %input_grad_mixed_sum.1 = (f32[512,512]{1,0:T(8,128)}, bf16[512,512]{1,0:T(8,128)(2,1)}, f32[8,1280]{1,0:T(8,128)}, bf16[4,4,128,1024]{3,2,1,0:T(8,128)(2,1)}, bf16[4,3,128,2816]{3,2,1,0:T(8,128)(2,1)}) custom-call(bf16[1024,2048]{1,0:T(8,128)(2,1)} %get-tuple-element.78.refs_0_, f32[512,512]{1,0:T(8,128)} %get-tuple-element.79.refs_1_, ...), custom_call_target="tpu_custom_call" | custom-call | flops 109999996928 | bytes 10000000 | tf_op jit(solution)/shard_map/input_grad_mixed_sum/pallas_call | solution.py:457
  512.0 0.0 copy-start.1
  512.1 0.0 copy-start
  512.1 14.3 %weight_gradients.1 = (f32[512,2,2816]{2,1,0:T(2,128)}, f32[2816,512]{1,0:T(8,128)}, f32[3,512,1024]{2,1,0:T(8,128)}, f32[1024,512]{1,0:T(8,128)}, f32[3,256]{1,...) custom-call(bf16[4,3,128,2816]{3,2,1,0:T(8,128)(2,1)} %get-tuple-element.89.hidden, ...), custom_call_target="tpu_custom_call" | custom-call | flops 15000000512 | bytes 10000000 | tf_op jit(solution)/shard_map/weight_gradients/pallas_call | solution.py:1864
  526.4 0.0 copy-done.1
  526.4 0.8 copy.25
  527.2 0.0 copy-done
  527.2 1.0 copy.26
Async XLA Ops:
  7.2 222.6 %all-gather.3.cloned.1.call-start = ((), (), s32[]{:S(2)}) async-start(), calls=%async_computation.2 | async-start | bytes 3932160 | tf_op jit(solution)/shard_map/all_gather | solution.py:1891
  129.7 211.1 %reduce-scatter.2.cloned.1.call-start = ((), (), s32[]{:S(2)}) async-start(), calls=%async_computation.1 | async-start | bytes 11141120 | tf_op jit(solution)/shard_map/reduce_scatter | solution.py:1896
  512.0 14.3 %copy-start.1 = (bf16[512,512]{1,0:T(8,128)(2,1)S(1)}, bf16[512,512]{1,0:T(8,128)(2,1)}, u32[]{:S(2)}) copy-start(bf16[512,512]{1,0:T(8,128)(2,1)} %get-tuple-element.112) | copy-start | bytes 1572868
  512.1 15.1 %copy-start = (f32[512,512]{1,0:T(8,128)S(1)}, f32[512,512]{1,0:T(8,128)}, u32[]{:S(2)}) copy-start(f32[512,512]{1,0:T(8,128)} %get-tuple-element.113) | copy-start | bytes 3145732
Sparse Core Ops, SparseCore 0:
  129.8 70.6 all-gather.2
  251.3 89.4 reduce-scatter.1

commit v10 on v9

--- a/solution.py
+++ b/solution.py
@@ -520,7 +520,7 @@
     return spot
 
 
-COTANGENT_SLOTS = (0, 34)
+COTANGENT_SLOTS = (0, 36)
 
 
 def middle_kernel(

time: 541 us -> 544 us (level)
  transfers between devices with their start and end apart: 2 -> 2, of which waited for: 1 -> 1; matrix products, arithmetic and copies ran while one was open for 0% -> 0% of each run, Pallas kernels for 34% -> 35%
where the time goes in v10:
time: 544 us; the launch traced here: 538 us
  Pallas kernels  515 us (95%)
  between operations  14.4 us (3%)
  waiting for transfers between devices  6.19 us (1%)
    pallas_call x6, Pallas kernels, staged_call(): pl.pallas_call(run, out_shape=tuple(out_shape), in_specs=in_specs, out_sp...  480 us
    pallas_call x1, Pallas kernels, hidden_back(): pl.pallas_call(hidden_back_kernel, out_shape=(jax.ShapeDtypeStruct(grad_s...  21.4 us
    pallas_call x1, Pallas kernels, weights_split(): pl.pallas_call(split_kernel, grid=(depth // 128,), out_shape=(jax.ShapeDt...  14.3 us
  transfers between devices with their start and end apart: 2, of which 1 were waited for; matrix products, arithmetic and copies ran while one was open for 0% of the time, Pallas kernels for 35%

profile of v10, /device:TPU:0, one launch (start us, length us, event | category | flops | bytes accessed | tf_op | source)
XLA Modules:
  0.0 537.8 jit_solution(11648209181267576226)
XLA Ops:
  7.2 0.0 all-gather.3.cloned.1.call-start
  7.2 73.0 %tokens_norm_weights.1 = (bf16[1024,2048]{1,0:T(8,128)(2,1)}, bf16[128,2048]{1,0:T(8,128)(2,1)}, f32[512,512]{1,0:T(8,128)}, f32[512,128]{1,0:T(8,128)}, f32[8,2...) custom-call(bf16[512,512]{1,0:T(8,128)(2,1)} %refs_0_.1, ...), custom_call_target="tpu_custom_call" | custom-call | flops 60000002048 | bytes 10000000 | tf_op jit(solution)/shard_map/tokens_norm_weights/pallas_call | solution.py:457
  80.3 49.4 %attention_weight_exchange.1 = (bf16[1024,768]{1,0:T(8,128)(2,1)}, bf16[1024,256]{1,0:T(8,128)(2,1)}, f32[2,2,1024,128]{3,2,1,0:T(8,128)}, bf16[1024,2048]{1,0:T...) custom-call(bf16[1024,2048]{1,0:T(8,128)(2,1)} %get-tuple-element.56.refs_0_.refs_5_, ...), custom_call_target="tpu_custom_call" | custom-call | flops 49999998976 | bytes 10000000 | tf_op jit(solution)/shard_map/attention_weight_exchange/pallas_call | solution.py:457
  129.7 0.0 all-gather.3.cloned.1.call-update
  129.7 0.2 reduce-scatter.2.cloned.1.call-start
  129.9 102.9 %middle_gate_up.1 = (bf16[1024,2048]{1,0:T(8,128)(2,1)}, f32[128,2048]{1,0:T(8,128)}, bf16[1024,704]{1,0:T(8,128)(2,1)}, bf16[1024,704]{1,0:T(8,128)(2,1)}, bf16...) custom-call(bf16[1024,2048]{1,0:T(8,128)(2,1)} %get-tuple-element.62.refs_0_, ...), custom_call_target="tpu_custom_call" | custom-call | flops 95000002560 | bytes 10000000 | tf_op jit(solution)/shard_map/middle_gate_up/pallas_call | solution.py:457
  232.8 0.0 all-gather.3.cloned.1.call-done
  232.8 21.4 %hidden_back.1 = (bf16[4,4,128,2176]{3,2,1,0:T(8,128)(2,1)}, bf16[1024,1408]{1,0:T(8,128)(2,1)}) custom-call(bf16[1024,704]{1,0:T(8,128)(2,1)} %get-tuple-element.66.hidden_from.refs_5_, bf16[1024,704]{1,0:T(8,128)(2,1)} %get-tuple-element.67.gate_from, bf16[1024,704]{1,0:T(8,128)(2,1)} %get-tuple-element.68.up_from, ...), custom_call_target="tpu_custom_call" | custom-call | flops 30000001024 | bytes 10000000 | tf_op jit(solution)/shard_map/hidden_back/pallas_call | solution.py:1801
  254.2 0.0 reduce-scatter.2.cloned.1.call-update
  254.2 82.9 %grad_sum_norm_gather.1 = (bf16[1024,2048]{1,0:T(8,128)(2,1)}, f32[8,2048]{1,0:T(8,128)}, bf16[1024,2048]{1,0:T(8,128)(2,1)}) custom-call(bf16[1024,1408]{1,0:T(8,128)(2,1)} %get-tuple-element.72.refs_0_, bf16[2048,1408]{1,0:T(8,128)(2,1)} %get-tuple-element.73.refs_1_, f32[128,2048]{1,0:T(8,128)} %get-tuple-element.74.refs_2_.refs_9_, ...), custom_call_target="tpu_custom_call" | custom-call | flops 60000002048 | bytes 10000000 | tf_op jit(solution)/shard_map/grad_sum_norm_gather/pallas_call | solution.py:457
  337.2 6.1 %reduce-scatter.2.cloned.1.call-done = bf16[512,2176]{1,0:T(8,128)(2,1)} async-done(((bf16[2048,2176]{1,0:T(8,128)(2,1)}), bf16[512,2176]{1,0:T(8,128)(2,1)}) %reduce-scatter.2.cloned.1.call-update) | async-done | bytes 2228240 | tf_op jit(solution)/shard_map/reduce_scatter | solution.py:1896
  343.3 55.1 %attention_back_exchange.1 = (bf16[2,4,4,128,384]{4,3,2,1,0:T(8,128)(2,1)}, bf16[4,4,128,256]{3,2,1,0:T(8,128)(2,1)}, bf16[1024,2048]{1,0:T(8,128)(2,1)}, f32[8,768]{1,0:T(8,128)}, bf16[3,128,2816]{2,1,0:T(8,128)(2,1)}) custom-call(bf16[1024,768]{1,0:T(8,128)(2,1)} %get-tuple-element.60.refs_0_, f32[2,2,1024,128]{3,2,1,0:T(8,128)} %get-tuple-element.61.refs_1_, ...), custom_call_target="tpu_custom_call" | custom-call | flops 49999998976 | bytes 10000000 | tf_op jit(solution)/shard_map/attention_back_exchange/pallas_call | solution.py:457
  398.4 116.2 %input_grad_mixed_sum.1 = (f32[512,512]{1,0:T(8,128)}, bf16[512,512]{1,0:T(8,128)(2,1)}, f32[8,1280]{1,0:T(8,128)}, bf16[4,4,128,1024]{3,2,1,0:T(8,128)(2,1)}, bf16[4,3,128,2816]{3,2,1,0:T(8,128)(2,1)}) custom-call(bf16[1024,2048]{1,0:T(8,128)(2,1)} %get-tuple-element.78.refs_0_, f32[512,512]{1,0:T(8,128)} %get-tuple-element.79.refs_1_, ...), custom_call_target="tpu_custom_call" | custom-call | flops 109999996928 | bytes 10000000 | tf_op jit(solution)/shard_map/input_grad_mixed_sum/pallas_call | solution.py:457
  514.6 0.0 copy-start.1
  514.6 0.0 copy-start
  514.6 14.3 %weight_gradients.1 = (f32[512,2,2816]{2,1,0:T(2,128)}, f32[2816,512]{1,0:T(8,128)}, f32[3,512,1024]{2,1,0:T(8,128)}, f32[1024,512]{1,0:T(8,128)}, f32[3,256]{1,...) custom-call(bf16[4,3,128,2816]{3,2,1,0:T(8,128)(2,1)} %get-tuple-element.89.hidden, ...), custom_call_target="tpu_custom_call" | custom-call | flops 15000000512 | bytes 10000000 | tf_op jit(solution)/shard_map/weight_gradients/pallas_call | solution.py:1864
  529.0 0.0 copy-done.1
  529.0 0.8 copy.25
  529.8 0.0 copy-done
  529.8 1.0 copy.26
Async XLA Ops:
  7.2 225.7 %all-gather.3.cloned.1.call-start = ((), (), s32[]{:S(2)}) async-start(), calls=%async_computation.2 | async-start | bytes 3932160 | tf_op jit(solution)/shard_map/all_gather | solution.py:1891
  129.7 213.6 %reduce-scatter.2.cloned.1.call-start = ((), (), s32[]{:S(2)}) async-start(), calls=%async_computation.1 | async-start | bytes 11141120 | tf_op jit(solution)/shard_map/reduce_scatter | solution.py:1896
  514.6 14.3 %copy-start.1 = (bf16[512,512]{1,0:T(8,128)(2,1)S(1)}, bf16[512,512]{1,0:T(8,128)(2,1)}, u32[]{:S(2)}) copy-start(bf16[512,512]{1,0:T(8,128)(2,1)} %get-tuple-element.112) | copy-start | bytes 1572868
  514.6 15.1 %copy-start = (f32[512,512]{1,0:T(8,128)S(1)}, f32[512,512]{1,0:T(8,128)}, u32[]{:S(2)}) copy-start(f32[512,512]{1,0:T(8,128)} %get-tuple-element.113) | copy-start | bytes 3145732
Sparse Core Ops, SparseCore 0:
  129.8 70.6 all-gather.2
  254.4 88.8 reduce-scatter.1
